TPU v7x, 32 devices: a whole 2x2x4 slice. The times are simulated.
32 devices in a mesh: group: 4 (over y, core), dev: 8 (over z, x).
Axes of the slice: x: 2, y: 2, z: 4, core: 2. Of those that a mesh axis runs over, the one named last changes fastest.
Arguments:
- hidden: bfloat16 [8192, 8192], P('group', 'dev'), may hold values from -6 to 6
- base_in_projection: bfloat16 [8192, 8192], P('group', 'dev'), may hold values from -6 to 6
- state_input_matrix: bfloat16 [8192, 128], P(('group', 'dev')), may hold values from -0.625 to 0.625
- state_output_matrix: bfloat16 [8192, 128], P(('group', 'dev')), may hold values from -1.75 to 1.75
- head_step_size: float32 [128, 8192], P('dev', 'group'), may hold values from 0.3 to 20, as said below
- head_decay_rate: float32 [128], P('dev'), may hold values from 0.0005 to 0.05
- head_skip_scale: float32 [128], P('dev'), may hold values from 0.5 to 1.5
- convolution_weight: float32 [4, 8192], P(None, 'dev'), may hold values from -3 to 3
- convolution_bias: float32 [8192], P('dev'), may hold values from -0.5 to 0.5
- adapter_down_weight: bfloat16 [32, 64, 8192], P('group', None, 'dev'), may hold values from -0.0625 to 0.0625
- adapter_up_weight: bfloat16 [32, 64, 8192], P('group', None, 'dev'), may hold values from -0.75 to 0.75
- adapter_home_group: int32 [32, 1], replicated, may hold values from 0 to 3; in each aligned block of 8 rows (0 to 7, 8 to 15, ...) at most 4 rows name the same one
- adapter_group_index: int32 [32], replicated, may hold values from 0 to 7
- state_space_cache: bfloat16 [128, 128, 64, 128], P(('group', 'dev')), may hold values from -1.75 to 1.75
- convolution_cache: bfloat16 [128, 3, 8192], P(('group', 'dev')), may hold values from -6 to 6
- prefix_holder_device: int32 [32, 1], replicated, may hold values from 0 to 7; in each aligned block of 8 rows (0 to 7, 8 to 15, ...) at most 2 rows name the same one
- prefix_cache_slot: int32 [32], replicated, may hold values from 0 to 3
- prefix_block_count: int32 [32], replicated, may hold values from 0 to 8
Outputs:
- mixer_out: bfloat16 [8192, 8192], P('group', 'dev')
- final_state: bfloat16 [32, 128, 64, 128], P('group', 'dev')
Inputs may be any that keep to these rules, and one draw needn't show every extreme that they name: `prefix_holder_device`: in each aligned block of 8 rows (one group's requests) no device index is named by more than 2 rows. `adapter_home_group`: in each aligned block of 8 rows (one group's requests) no group is named by more than 4 rows. `prefix_block_count`: 0 means that the request has no cached prefix. `head_step_size`: positive.
All inputs are finite; a program needn't handle non-finite values.
Results may differ from a plain program's by a relative error of at most 0.006.
Values may be sent and summed in bfloat16 or wider, within the bound.
No kernel may reach another device: no remote copies, remote signals or barrier semaphores. Data moves between devices by JAX's collectives and lax.ppermute only.
A program may use at most 128 MiB of HBM per device.

v0:
```python
import jax
import jax.numpy as jnp
from jax import lax
from jax.sharding import PartitionSpec as P

T_REQ = 256
CAP = 2


def rank_among(labels, classes):
    onehot = (labels[:, None] == jnp.arange(classes, dtype=jnp.int32)[None, :]).astype(jnp.int32)
    before = jnp.cumsum(onehot, axis=0) - onehot
    return jnp.sum(before * onehot, axis=1)


def conv_activate(prev_conv, lifted_rows, convolution_weight, convolution_bias):
    tap_count = convolution_weight.shape[0]
    length = lifted_rows.shape[-2]
    extended = jnp.concatenate([prev_conv.astype(jnp.float32), lifted_rows], axis=-2)
    summed = convolution_bias
    for offset in range(tap_count):
        summed = summed + convolution_weight[offset] * lax.slice_in_dim(
            extended, offset, offset + length, axis=extended.ndim - 2
        )
    return jax.nn.silu(summed)


def request_mixer(
    activated, step_rows, head_decay_rate, write_rows, read_rows, prev_state, head_skip_scale
):
    length = activated.shape[0]
    decay_sum = jnp.cumsum(-head_decay_rate[:, None] * step_rows, axis=1)
    scores = jnp.einsum("tn,sn->ts", read_rows, write_rows, preferred_element_type=jnp.float32)
    causal = (jnp.arange(length)[:, None] >= jnp.arange(length)[None, :])[None]
    exponent = jnp.where(causal, decay_sum[:, :, None] - decay_sum[:, None, :], 0.0)
    mixing = jnp.where(causal, scores[None] * jnp.exp(exponent), 0.0).astype(jnp.bfloat16)
    driven = (activated * step_rows.T[:, :, None]).astype(jnp.bfloat16)
    local_part = jnp.einsum("hts,shp->thp", mixing, driven, preferred_element_type=jnp.float32)
    carried = jnp.einsum("tn,hpn->thp", read_rows, prev_state, preferred_element_type=jnp.float32)
    result = (
        local_part
        + carried * jnp.exp(decay_sum).T[:, :, None]
        + head_skip_scale[None, :, None] * activated
    )
    to_end = jnp.exp(decay_sum[:, -1:] - decay_sum)
    factor_multiplied = (activated * (step_rows * to_end).T[:, :, None]).astype(jnp.bfloat16)
    state_new = jnp.einsum(
        "thp,tn->hpn", factor_multiplied, write_rows, preferred_element_type=jnp.float32
    )
    state_new = state_new + jnp.exp(decay_sum[:, -1])[:, None, None] * prev_state.astype(
        jnp.float32
    )
    return (result.astype(jnp.bfloat16), state_new.astype(jnp.bfloat16))


def body(
    hidden,
    base_in_projection,
    state_input_matrix,
    state_output_matrix,
    head_step_size,
    head_decay_rate,
    head_skip_scale,
    convolution_weight,
    convolution_bias,
    adapter_down_weight,
    adapter_up_weight,
    adapter_home_group,
    adapter_group_index,
    state_space_cache,
    convolution_cache,
    prefix_holder_device,
    prefix_cache_slot,
    prefix_block_count,
):
    devices = lax.axis_size("dev")
    my_group = lax.axis_index("group")
    my_index = lax.axis_index("dev")
    per_group = hidden.shape[0] // T_REQ
    local_heads = head_step_size.shape[0]
    head_size = state_space_cache.shape[2]
    width_local = base_in_projection.shape[1]
    tap_count = convolution_weight.shape[0]
    first_request = my_group * per_group
    holders = lax.dynamic_slice_in_dim(prefix_holder_device[:, 0], first_request, per_group)
    slot_rows = lax.dynamic_slice_in_dim(prefix_cache_slot, first_request, per_group)
    has_prefix = lax.dynamic_slice_in_dim(prefix_block_count, first_request, per_group) > 0
    holder_rank = rank_among(holders, devices)
    wanted = (holders == my_index)[None, :] & (
        holder_rank[None, :] == jnp.arange(CAP, dtype=jnp.int32)[:, None]
    )
    send_slot = jnp.sum(wanted.astype(jnp.int32) * slot_rows[None, :], axis=1)
    picked_state = state_space_cache[send_slot].reshape(
        CAP, devices, local_heads, head_size, state_space_cache.shape[3]
    )
    picked_conv = (
        convolution_cache[send_slot]
        .reshape(CAP, tap_count - 1, devices, width_local)
        .transpose(0, 2, 1, 3)
    )
    got_state, got_conv = (
        lax.all_to_all(picked_state, "dev", split_axis=1, concat_axis=1, tiled=True),
        lax.all_to_all(picked_conv, "dev", split_axis=1, concat_axis=1, tiled=True),
    )
    where_from = holder_rank * devices + holders
    prev_state = got_state.reshape((CAP * devices,) + got_state.shape[2:])[where_from]
    prev_state = jnp.where(has_prefix[:, None, None, None], prev_state, jnp.zeros_like(prev_state))
    prev_conv = got_conv.reshape((CAP * devices,) + got_conv.shape[2:])[where_from]
    prev_conv = jnp.where(has_prefix[:, None, None], prev_conv, jnp.zeros_like(prev_conv))
    request_home_group = lax.dynamic_slice_in_dim(
        adapter_home_group[:, 0], first_request, per_group
    )
    request_home_index = lax.dynamic_slice_in_dim(adapter_group_index, first_request, per_group)
    table_down, table_up = (
        lax.all_gather(adapter_down_weight, "group", axis=0, tiled=True),
        lax.all_gather(adapter_up_weight, "group", axis=0, tiled=True),
    )
    selected_entry = request_home_group * adapter_down_weight.shape[0] + request_home_index
    down_rows = table_down[selected_entry]
    up_rows = table_up[selected_entry]
    incoming_tokens = hidden.reshape(per_group, T_REQ, hidden.shape[1])
    partial_down = jnp.einsum(
        "rtd,rkd->rtk", incoming_tokens, down_rows, preferred_element_type=jnp.float32
    )
    shrunk_rows = lax.psum(partial_down, "dev").astype(jnp.bfloat16)
    lifted_rows = base_in_projection.reshape(per_group, T_REQ, width_local).astype(jnp.float32)
    lifted_rows = lifted_rows + jnp.einsum(
        "rtk,rkw->rtw", shrunk_rows, up_rows, preferred_element_type=jnp.float32
    )
    activated = conv_activate(prev_conv, lifted_rows, convolution_weight, convolution_bias)
    activated = activated.reshape(per_group, T_REQ, local_heads, head_size)
    write_all, read_all = (
        lax.all_gather(state_input_matrix, "dev", axis=0, tiled=True),
        lax.all_gather(state_output_matrix, "dev", axis=0, tiled=True),
    )
    write_rows = write_all.reshape(per_group, T_REQ, write_all.shape[1])
    read_rows = read_all.reshape(per_group, T_REQ, read_all.shape[1])
    step_rows = head_step_size.reshape(local_heads, per_group, T_REQ).transpose(1, 0, 2)

    def per_request(fragments):
        return request_mixer(
            fragments[0],
            fragments[1],
            head_decay_rate,
            fragments[2],
            fragments[3],
            fragments[4],
            head_skip_scale,
        )

    outputs, state_new = lax.map(
        per_request, (activated, step_rows, write_rows, read_rows, prev_state)
    )
    return (outputs.reshape(per_group * T_REQ, width_local), state_new)


def solution(mesh):
    placed = (
        P("group", "dev"),
        P("group", "dev"),
        P(("group", "dev"), None),
        P(("group", "dev"), None),
        P("dev", "group"),
        P("dev"),
        P("dev"),
        P(None, "dev"),
        P("dev"),
        P("group", None, "dev"),
        P("group", None, "dev"),
        P(),
        P(),
        P(("group", "dev"), None, None, None),
        P(("group", "dev"), None, None),
        P(),
        P(),
        P(),
    )
    return jax.shard_map(
        body,
        mesh=mesh,
        in_specs=placed,
        out_specs=(P("group", "dev"), P("group", "dev", None, None)),
        check_vma=False,
    )
```

profile of v0, /device:TPU:8, one launch (start us, length us, event | category | flops | bytes accessed | tf_op | source)
XLA Modules:
  0.0 363.3 jit_solution(12069956061467677726)
XLA Ops:
  8.7 0.7 broadcast_compare_fusion
  9.5 0.7 dynamic_slice.49
  10.6 1.3 gather_fusion
  12.6 6.3 %all-to-all-start = ((bf16[2,8,3,1024]{3,0,2,1:T(2,128)(2,1)}), bf16[2,8,3,1024]{3,0,2,1:T(2,128)(2,1)S(1)}, u32[]{:S(2)}, u32[]{:S(2)}) async-start(bf16[2,8,3,1024]{3,0,2,1:T(2,128)(2,1)} %bitcast.114), calls=%async_computation | async-start | bytes 196608 | tf_op jit(solution)/shard_map/all_to_all | solution.py:103
  18.8 8.9 %while.18 = (s32[]{:T(128)}, bf16[4,128,64,128]{3,2,1,0:T(8,128)(2,1)}, s32[2,1]{0,1:T(1,128)S(1)}, bf16[2,128,64,128]{3,2,1,0:T(8,128)(2,1)}) while((s32[]{:T(128)}, bf16[4,128,64,128]{3,2,1,0:T(8,128)(2,1)}, s32[2,1]{0,1:T(1,128)S(1)}, bf16[2,128,64,128]{3,2,1,0:T(8,128)(2,1)}) %tuple.65), condition=%wide.while_cond.clone, body=%wide.while_body.sunk.clone | while | flops 2 | bytes 4195393 | solution.py:93
  19.5 3.9 %dynamic-slice_dynamic-update-slice_fusion.3 = bf16[2,128,64,128]{3,2,1,0:T(8,128)(2,1)} fusion(bf16[2,128,64,128]{3,2,1,0:T(8,128)(2,1)} %get-tuple-element.359, s32[]{:T(128)} %get-tuple-element.356, bf16[4,128,64,128]{3,2,1,0:T(8,128)(2,1)} %get-tuple-element.361, s32[]{:T(128)} %bitcast.180), kind=kLoop, calls=%fused_computation.5.clone.1.clone | loop fusion | bytes 4195328 | tf_op jit(solution)/shard_map/gather
  24.0 3.7 %dynamic-slice_dynamic-update-slice_fusion.3 = bf16[2,128,64,128]{3,2,1,0:T(8,128)(2,1)} fusion(bf16[2,128,64,128]{3,2,1,0:T(8,128)(2,1)} %get-tuple-element.359, s32[]{:T(128)} %get-tuple-element.356, bf16[4,128,64,128]{3,2,1,0:T(8,128)(2,1)} %get-tuple-element.361, s32[]{:T(128)} %bitcast.180), kind=kLoop, calls=%fused_computation.5.clone.1.clone | loop fusion | bytes 4195328 | tf_op jit(solution)/shard_map/gather
  27.7 5.5 %copy.64 = bf16[2,8,16,64,128]{4,3,2,0,1:T(8,128)(2,1)} copy(bf16[2,8,16,64,128]{4,3,2,1,0:T(8,128)(2,1)} %bitcast.186) | data formatting | bytes 8388608 | tf_op jit(solution)/shard_map/reshape | solution.py:93
  33.3 6.2 %all-to-all-start.1 = ((bf16[2,8,16,64,128]{4,3,2,0,1:T(8,128)(2,1)}), bf16[2,8,16,64,128]{4,3,2,0,1:T(8,128)(2,1)}, u32[]{:S(2)}, u32[]{:S(2)}) async-start(bf16[2,8,16,64,128]{4,3,2,0,1:T(8,128)(2,1)} %copy.64), calls=%async_computation.1 | async-start | bytes 8388608 | tf_op jit(solution)/shard_map/all_to_all | solution.py:102
  39.8 110.8 %all_gather.14 = bf16[2048,128]{1,0:T(8,128)(2,1)S(1)} all-gather(bf16[256,128]{1,0:T(8,128)(2,1)S(1)} %copy-done.3), channel_id=1, replica_groups=mesh['group'=4,'dev'=8] {'dev'}, dimensions={0}, use_global_device_ids=true | all-gather | bytes 589824 | tf_op jit(solution)/shard_map/all_gather | solution.py:134
  150.7 31.1 %all_gather.15 = bf16[2048,128]{1,0:T(8,128)(2,1)S(1)} all-gather(bf16[256,128]{1,0:T(8,128)(2,1)S(1)} %copy-done.4), channel_id=1, replica_groups=mesh['group'=4,'dev'=8] {'dev'}, dimensions={0}, use_global_device_ids=true | all-gather | bytes 589824 | tf_op jit(solution)/shard_map/all_gather | solution.py:133
  182.5 2.8 gather_fusion.2
  185.4 3.6 convolution_bitcast_fusion
  189.0 2.8 gather_fusion.3
  191.8 41.8 %all-reduce.1 = bf16[8,256,64]{1,2,0:T(8,128)(2,1)S(1)} all-reduce(f32[8,256,64]{1,2,0:T(8,128)S(1)} %convolution_bitcast_fusion), channel_id=1, replica_groups=mesh['group'=4,'dev'=8] {'dev'}, use_global_device_ids=true, to_apply=%region_3.4 | all-reduce | flops 131072 | bytes 786432 | tf_op jit(solution)/shard_map/psum | solution.py:125
  233.6 3.5 convert_add_fusion
  237.1 6.8 %divide_multiply_fusion = f32[8,256,1024]{2,1,0:T(8,128)} fusion(f32[8,256,1024]{2,1,0:T(8,128)S(1)} %convert_add_fusion, f32[8,3,1024]{2,1,0:T(4,128)S(1)} %select_convert_fusion.4, f32[1024]{0:T(1024)S(1)} %bitcast.196, f32[1024]{0:T(1024)S(1)} %bitcast.197, f32[1024]{0:T(1024)S(1)} %bitcast.195, f32[1024]{0:T(1024)S(1)} %bitcast.194, f32[1024]{0:T(1024)S(1)} %copy-done.7), kind=kLoop, calls=%fused_computation.72 | loop fusion | flops 31457280 | bytes 16896000 | tf_op jit(solution)/shard_map/jit(silu)/mul | solution.py:25
  243.9 9.1 %copy.63 = f32[8,256,1024]{1,2,0:T(8,128)} copy(f32[8,256,1024]{2,1,0:T(8,128)} %divide_multiply_fusion) | data formatting | bytes 16777216 | tf_op jit(solution)/shard_map/jit(silu)/mul | solution.py:25
  253.0 5.5 %copy.65 = bf16[2,8,16,64,128]{4,3,2,1,0:T(8,128)(2,1)} copy(bf16[2,8,16,64,128]{4,3,2,0,1:T(8,128)(2,1)} %all-to-all-done.1) | data formatting | bytes 8388608 | tf_op jit(solution)/shard_map/all_to_all | solution.py:102
  258.5 4.3 %gather_fusion.4 = bf16[8,16,64,128]{3,2,1,0:T(8,128)(2,1)} fusion(bf16[16,16,64,128]{3,2,1,0:T(8,128)(2,1)} %bitcast.182, s32[1024]{0:T(1024)S(1)} %pad_clamp_fusion.1), kind=kCustom, calls=%fused_computation.4 | custom fusion | bytes 4194336 | tf_op jit(solution)/shard_map/gather | solution.py:106
  262.8 1.8 broadcast_select_fusion
  264.7 68.9 %while.17 = (s32[]{:T(128)}, bf16[8,256,16,64]{1,3,2,0:T(8,128)(2,1)}, bf16[8,16,64,128]{3,2,1,0:T(8,128)(2,1)}, f32[8,256,16,64]{1,3,2,0:T(8,128)}, f32[8,16,25...) while((s32[]{:T(128)}, ...), condition=%wide.region_7.8_spmd.clone, body=%wide.region_4.7_spmd.sunk.clone | while | flops 293945408 | bytes 7822385 | solution.py:151
  265.9 2.5 fusion.91
  268.7 2.4 fusion.93
  271.0 2.2 fusion.94
  274.5 2.5 fusion.91
  277.3 2.4 fusion.93
  279.6 2.2 fusion.94
  283.1 2.5 fusion.91
  285.9 2.4 fusion.93
  288.3 2.2 fusion.94
  291.7 2.5 fusion.91
  294.5 2.4 fusion.93
  296.9 2.2 fusion.94
  300.3 2.5 fusion.91
  303.1 2.4 fusion.93
  305.5 2.2 fusion.94
  309.0 2.5 fusion.91
  311.7 2.4 fusion.93
  314.1 2.2 fusion.94
  317.6 2.5 fusion.91
  320.4 2.4 fusion.93
  322.7 2.2 fusion.94
  326.2 2.5 fusion.91
  329.0 2.4 fusion.93
  331.3 2.2 fusion.94
  333.6 11.0 %copy.69 = bf16[8,256,16,64]{3,2,1,0:T(8,128)(2,1)} copy(bf16[8,256,16,64]{1,3,2,0:T(8,128)(2,1)} %get-tuple-element.119) | data formatting | bytes 8388608
  344.6 11.9 %reshape.241 = bf16[2048,1024]{1,0:T(8,128)(2,1)} reshape(bf16[8,256,16,64]{3,2,1,0:T(8,128)(2,1)} %copy.69) | data formatting | bytes 8388608
  (169 shorter events, 16.6 us)
Async XLA Ops:
  7.2 3.4 copy-start
  7.2 175.4 %all-gather.3.cloned.1.call-start = ((), (), s32[]{:S(2)}) async-start(), calls=%async_computation.2 | async-start | bytes 5242880 | tf_op jit(solution)/shard_map/all_gather | solution.py:115
  7.9 181.0 %all-gather.5.cloned.1.call-start = ((), (), s32[]{:S(2)}) async-start(), calls=%async_computation.3 | async-start | bytes 5242880 | tf_op jit(solution)/shard_map/all_gather | solution.py:116
  12.6 20.7 %all-to-all-start = ((bf16[2,8,3,1024]{3,0,2,1:T(2,128)(2,1)}), bf16[2,8,3,1024]{3,0,2,1:T(2,128)(2,1)S(1)}, u32[]{:S(2)}, u32[]{:S(2)}) async-start(bf16[2,8,3,1024]{3,0,2,1:T(2,128)(2,1)} %bitcast.114), calls=%async_computation | async-start | bytes 196608 | tf_op jit(solution)/shard_map/all_to_all | solution.py:103
  33.2 6.2 %copy-start.2 = (f32[16,2048]{1,0:T(8,128)S(1)}, f32[16,2048]{1,0:T(8,128)}, u32[]{:S(2)}) copy-start(f32[16,2048]{1,0:T(8,128)} %param.24) | copy-start | bytes 393220
  33.2 6.3 %copy-start.11 = (s32[32]{0:T(128)S(1)}, s32[32]{0:T(128)}, u32[]{:S(2)}) copy-start(s32[32]{0:T(128)} %param.37) | copy-start | bytes 388
  33.2 6.4 %copy-start.9 = (s32[32]{0:T(128)S(1)}, s32[32]{0:T(128)}, u32[]{:S(2)}) copy-start(s32[32]{0:T(128)} %param.32) | copy-start | bytes 388
  33.2 6.4 %copy-start.10 = (s32[32,1]{0,1:T(1,128)S(1)}, s32[32,1]{0,1:T(1,128)}, u32[]{:S(2)}) copy-start(s32[32,1]{0,1:T(1,128)} %param.31) | copy-start | bytes 388
  33.2 6.5 %copy-start.8 = (s32[32,1]{0,1:T(1,128)S(1)}, s32[32,1]{0,1:T(1,128)}, u32[]{:S(2)}) copy-start(s32[32,1]{0,1:T(1,128)} %param.35) | copy-start | bytes 388
  33.2 6.5 %copy-start.12 = (f32[16]{0:T(128)S(1)}, f32[16]{0:T(128)}, u32[]{:S(2)}) copy-start(f32[16]{0:T(128)} %param.25) | copy-start | bytes 196
  33.2 6.5 %copy-start.5 = (f32[4,1024]{1,0:T(4,128)S(1)}, f32[4,1024]{1,0:T(4,128)}, u32[]{:S(2)}) copy-start(f32[4,1024]{1,0:T(4,128)} %param.27) | copy-start | bytes 49156
  33.2 6.6 %copy-start.3 = (bf16[256,128]{1,0:T(8,128)(2,1)S(1)}, bf16[256,128]{1,0:T(8,128)(2,1)}, u32[]{:S(2)}) copy-start(bf16[256,128]{1,0:T(8,128)(2,1)} %param.23) | copy-start | bytes 196612
  33.3 117.4 %copy-start.4 = (bf16[256,128]{1,0:T(8,128)(2,1)S(1)}, bf16[256,128]{1,0:T(8,128)(2,1)}, u32[]{:S(2)}) copy-start(bf16[256,128]{1,0:T(8,128)(2,1)} %param.22) | copy-start | bytes 196612
  33.3 219.7 %all-to-all-start.1 = ((bf16[2,8,16,64,128]{4,3,2,0,1:T(8,128)(2,1)}), bf16[2,8,16,64,128]{4,3,2,0,1:T(8,128)(2,1)}, u32[]{:S(2)}, u32[]{:S(2)}) async-start(bf16[2,8,16,64,128]{4,3,2,0,1:T(8,128)(2,1)} %copy.64), calls=%async_computation.1 | async-start | bytes 8388608 | tf_op jit(solution)/shard_map/all_to_all | solution.py:102
  233.6 3.5 copy-start.7
  258.5 6.2 %copy-start.6 = (f32[16]{0:T(128)S(1)}, f32[16]{0:T(128)}, u32[]{:S(2)}) copy-start(f32[16]{0:T(128)} %param.26) | copy-start | bytes 196
  333.6 22.8 %copy-start.1 = (bf16[4,3,8192]{2,0,1:T(4,128)(2,1)S(1)}, bf16[4,3,8192]{2,0,1:T(4,128)(2,1)}, u32[]{:S(2)}) copy-start(bf16[4,3,8192]{2,0,1:T(4,128)(2,1)} %param.34) | copy-start | bytes 589828
Sparse Core Ops, SparseCore 0:
  9.6 35.6 all-gather.2
  46.8 34.4 all-gather.4
where the time goes:
time: 370 us; the launch traced here: 363 us
  blocking collectives  184 us (50%)
  local copies, waits for them, and re-layouts  68.2 us (18%)
  matrix products  65.4 us (18%)
  other arithmetic  17.2 us (5%)
  between operations  14.3 us (4%)
  starting transfers between devices  12.5 us (3%)
    all_gather x1, blocking collectives, body(): lax.all_gather(state_output_matrix, 'dev', axis=0, tiled=True)  111 us
    psum x1, blocking collectives, body(): shrunk_rows = lax.psum(partial_down, 'dev').astype(jnp.bfloat16)  41.8 us
    all_gather x1, blocking collectives, body(): lax.all_gather(state_input_matrix, 'dev', axis=0, tiled=True)  31.1 us
    unnamed x29, local copies, waits for them, and re-layouts  22.9 us
    dot_general x8, matrix products, request_mixer(): jnp.einsum('hts,shp->thp', mixing, driven, preferred_element_type=jnp.flo...  20 us
    dot_general x8, matrix products, request_mixer(): jnp.einsum('tn,hpn->thp', read_rows, prev_state, preferred_element_type=j...  18.9 us
    dot_general x8, matrix products, request_mixer(): jnp.einsum('thp,tn->hpn', factor_multiplied, write_rows, preferred_elemen...  17.9 us
    mul x1, local copies, waits for them, and re-layouts, conv_activate(): return jax.nn.silu(summed)  9.15 us
  transfers between devices with their start and end apart: 4, of which 0 were waited for; matrix products, arithmetic and copies ran while one was open for 13% of the time, Pallas kernels for 0%

commit v1 on v0

v1 whole, which is shorter than its diff:
```python
import functools
import math

import jax
import jax.numpy as jnp
from jax import lax
from jax.experimental import pallas as pl
from jax.experimental.pallas import tpu as pltpu
from jax.sharding import PartitionSpec as P

T_REQ = 256
CAP = 2
ACAP = 4
HEADS_PER_PIECE = 4
LOG2E = math.log2(math.e)
NT = (((1,), (1,)), ((), ()))
TN = (((0,), (0,)), ((), ()))
VMEM_LIMIT = 48 * 1024 * 1024

HOME, ADAPTER_RANK_AMONG, HOLDER, HOLDER_RANK, PRESENT = range(5)


def cost(flops, nbytes, transcendentals=0):
    return pl.CostEstimate(
        flops=int(flops), bytes_accessed=int(nbytes), transcendentals=int(transcendentals)
    )


def hbm(count):
    return [pl.BlockSpec(memory_space=pl.ANY) for _ in range(count)]


def smem(count):
    return [pl.BlockSpec(memory_space=pltpu.SMEM) for _ in range(count)]


def count_before(ref, first, position, label):
    total = jnp.int32(0)
    for q in range(position):
        total = total + (ref[first + q] == label).astype(jnp.int32)
    return total


def pick_request(labels, first, count, wanted_label, wanted_rank):
    seen = jnp.int32(0)
    chosen = jnp.int32(0)
    for q in range(count):
        hit = labels[first + q] == wanted_label
        chosen = jnp.where(hit & (seen == wanted_rank), q, chosen)
        seen = seen + hit.astype(jnp.int32)
    return chosen


def pack_adapter_kernel(groups, per_group, home, index, table, out, sems):
    mine = lax.axis_index("group")
    copies = []
    for g in range(groups):
        seen = jnp.int32(0)
        chosen = [jnp.int32(0) for _ in range(ACAP)]
        for q in range(per_group):
            hit = home[g * per_group + q] == mine
            value = index[g * per_group + q]
            for c in range(ACAP):
                chosen[c] = jnp.where(hit & (seen == c), value, chosen[c])
            seen = seen + hit.astype(jnp.int32)
        for c in range(ACAP):
            copy = pltpu.make_async_copy(table.at[chosen[c]], out.at[g, c], sems.at[g, c])
            copy.start()
            copies.append(copy)
    for copy in copies:
        copy.wait()


def pack_adapter(home, index, table, groups, per_group):
    return pl.pallas_call(
        functools.partial(pack_adapter_kernel, groups, per_group),
        out_shape=jax.ShapeDtypeStruct((groups, ACAP) + table.shape[1:], table.dtype),
        in_specs=smem(2) + hbm(1),
        out_specs=pl.BlockSpec(memory_space=pl.ANY),
        scratch_shapes=[pltpu.SemaphoreType.DMA((groups, ACAP))],
        cost_estimate=cost(0, 2 * groups * ACAP * table.shape[1] * table.shape[2] * 2),
        name="pack_adapter",
    )(home, index, table)


def pack_small_kernel(
    devices, per_group, width, home, index, holder, slot, blocks,
    write_rows, read_rows, conv, meta, rows_out, conv_out, row_sems, conv_sems,
):
    my_group = lax.axis_index("group")
    mine = lax.axis_index("dev")
    first = my_group * per_group
    row_copies = [
        pltpu.make_async_copy(write_rows, rows_out.at[0], row_sems.at[0]),
        pltpu.make_async_copy(read_rows, rows_out.at[1], row_sems.at[1]),
    ]
    for copy in row_copies:
        copy.start()
    copies = []
    for c in range(CAP):
        chosen = slot[first + pick_request(holder, first, per_group, mine, c)]
        for d in range(devices):
            copy = pltpu.make_async_copy(
                conv.at[chosen, :, pl.ds(d * width, width)], conv_out.at[d, c], conv_sems.at[c, d]
            )
            copy.start()
            copies.append(copy)
    for q in range(per_group):
        meta[HOME, q] = home[first + q]
        meta[ADAPTER_RANK_AMONG, q] = count_before(home, first, q, home[first + q])
        meta[HOLDER, q] = holder[first + q]
        meta[HOLDER_RANK, q] = count_before(holder, first, q, holder[first + q])
        meta[PRESENT, q] = (blocks[first + q] > 0).astype(jnp.int32)
    for copy in row_copies + copies:
        copy.wait()


def pack_state_kernel(devices, per_group, pieces, holder, slot, cache, *rest):
    outs, sems = rest[:pieces], rest[pieces]
    first = lax.axis_index("group") * per_group
    mine = lax.axis_index("dev")
    copies = []
    for c in range(CAP):
        chosen = slot[first + pick_request(holder, first, per_group, mine, c)]
        for p in range(pieces):
            copy = pltpu.make_async_copy(
                cache.at[chosen, :, p], outs[p].at[:, c], sems.at[c, p]
            )
            copy.start()
            copies.append(copy)
    for copy in copies:
        copy.wait()


def shrink_kernel(meta, hidden, down, out):
    part = lax.dot_general(down[0, 0], hidden[...], NT, preferred_element_type=jnp.float32)
    out[0] = part.astype(out.dtype)


def sum_kernel(parts, out):
    total = parts[0].astype(jnp.float32)
    for k in range(1, parts.shape[0]):
        total = total + parts[k].astype(jnp.float32)
    total = total.astype(out.dtype)
    for k in range(out.shape[0]):
        out[k] = total


def prep_kernel(steps, rates, row_out, column_out):
    heads, length = steps.shape
    step = steps[...]
    x = step * (rates[...] * (-LOG2E))
    high = x.astype(jnp.bfloat16)
    rest = x - high.astype(jnp.float32)
    middle = rest.astype(jnp.bfloat16)
    low = (rest - middle.astype(jnp.float32)).astype(jnp.bfloat16)
    s = lax.broadcasted_iota(jnp.int32, (length, length), 0)
    t = lax.broadcasted_iota(jnp.int32, (length, length), 1)
    ones = (s <= t).astype(jnp.float32).astype(jnp.bfloat16)
    total = jnp.dot(low, ones, preferred_element_type=jnp.float32)
    total = total + jnp.dot(middle, ones, preferred_element_type=jnp.float32)
    total = total + jnp.dot(high, ones, preferred_element_type=jnp.float32)
    row_out[...] = total - jnp.log2(step)
    column_out[...] = total.T


def mix_kernel(
    piece, meta, base, shrunk, up, conv, conv_weight, conv_bias, skip, row_decay, column_decay,
    rows_in, state, *rest,
):
    out, state_out, extended, scores = rest[-4:]
    r = pl.program_id(0)
    length, width = base.shape
    half = length // 2
    heads = state.shape[2]
    size, depth = state.shape[3], state.shape[4]
    f32, bf16 = jnp.float32, jnp.bfloat16
    present = meta[PRESENT, r] > 0

    write, read = rows_in[0, 0], rows_in[0, 1]
    all_scores = lax.dot_general(read, write, NT, preferred_element_type=f32)
    t = lax.broadcasted_iota(jnp.int32, (length, length), 0)
    s = lax.broadcasted_iota(jnp.int32, (length, length), 1)
    scores[...] = jnp.where(s <= t, all_scores, 0.0)

    lifted = base[...].astype(f32) + lax.dot_general(
        shrunk[0], up[0, 0], TN, preferred_element_type=f32
    )
    taps = conv_weight.shape[0]
    extended[8:, :] = lifted
    before = conv[0, 0].astype(f32)
    extended[8 - (taps - 1):8, :] = jnp.where(present, before, 0.0)
    v = conv_bias[...] + conv_weight[taps - 1:taps, :] * lifted
    for k in range(taps - 1):
        begin = 8 - (taps - 1) + k
        v = v + conv_weight[k:k + 1, :] * extended[begin:begin + length, :]
    activated = v * (0.5 + 0.5 * jnp.tanh(0.5 * v))
    act16 = activated.astype(bf16)
    act16_t = act16.T

    row = row_decay[...]
    column = column_decay[...]
    lane = lax.broadcasted_iota(jnp.int32, (1, 2 * size), 1)
    for pair in range(heads // 2):
        lo, hi = pair * 2 * size, (pair + 1) * 2 * size
        a = act16[:, lo:hi]
        zero = jnp.zeros_like(a)
        a_sel = (jnp.where(lane < size, a, zero), jnp.where(lane < size, zero, a))
        upper, lower, decays = [], [], []
        for i in range(2):
            h = piece * heads + pair * 2 + i
            dt = jnp.broadcast_to(column[:, h:h + 1], (length, half))
            ds0, ds1 = row[h:h + 1, :half], row[h:h + 1, half:]
            m00 = jnp.exp2(jnp.minimum(dt[:half] - ds0, 126.0)) * scores[:half, :half]
            m10 = jnp.exp2(dt[half:] - ds0) * scores[half:, :half]
            m11 = jnp.exp2(jnp.minimum(dt[half:] - ds1, 126.0)) * scores[half:, half:]
            upper.append(m00.astype(bf16))
            lower.extend([m10.astype(bf16), m11.astype(bf16)])
            decays.append(dt)
            k = pair * 2 + i
            end = dt[length - 1:length, :]
            to_end = jnp.exp2(jnp.concatenate([end, end], axis=1) - row[h:h + 1, :])
            weighted = (act16_t[k * size:(k + 1) * size, :].astype(f32) * to_end).astype(bf16)
            fresh = jnp.dot(weighted, write, preferred_element_type=f32)
            before = jnp.where(present, state[0, 0, k].astype(f32), 0.0)
            state_out[0, k] = (fresh + before * jnp.exp2(end)).astype(state_out.dtype)
        y0 = jnp.dot(
            jnp.concatenate(upper, axis=1),
            jnp.concatenate([a_sel[0][:half], a_sel[1][:half]], axis=0),
            preferred_element_type=f32,
        )
        y1 = jnp.dot(
            jnp.concatenate(lower, axis=1),
            jnp.concatenate(a_sel, axis=0),
            preferred_element_type=f32,
        )
        states = state[0, 0, 2 * pair:2 * pair + 2].reshape(2 * size, depth)
        carried = lax.dot_general(read, states, NT, preferred_element_type=f32)
        grown = jnp.exp2(jnp.where(lane < size, decays[0], decays[1]))
        carried = jnp.where(present, carried * grown, 0.0)
        direct = skip[:, lo:hi] * activated[:, lo:hi]
        out[:, lo:hi] = (jnp.concatenate([y0, y1], axis=0) + carried + direct).astype(out.dtype)


def body(
    hidden, base_in_projection, state_input_matrix, state_output_matrix, head_step_size,
    head_decay_rate, head_skip_scale, convolution_weight, convolution_bias, adapter_down_weight,
    adapter_up_weight, adapter_home_group, adapter_group_index, state_space_cache,
    convolution_cache, prefix_holder_device, prefix_cache_slot, prefix_block_count,
):
    groups, devices = lax.axis_size("group"), lax.axis_size("dev")
    tokens, width = base_in_projection.shape
    per_group = tokens // T_REQ
    heads = head_step_size.shape[0]
    size, depth = state_space_cache.shape[2:]
    rank = adapter_down_weight.shape[1]
    taps = convolution_weight.shape[0]
    pieces = heads // HEADS_PER_PIECE
    piece_width = HEADS_PER_PIECE * size
    bf16, f32 = jnp.bfloat16, jnp.float32
    share = per_group // devices

    home = adapter_home_group.reshape(-1)
    holder = prefix_holder_device.reshape(-1)

    down_send = pack_adapter(home, adapter_group_index, adapter_down_weight, groups, per_group)
    down_got = lax.all_to_all(down_send, "group", split_axis=0, concat_axis=0, tiled=True)

    meta, rows_mine, conv_send = pl.pallas_call(
        functools.partial(pack_small_kernel, devices, per_group, width),
        out_shape=(
            jax.ShapeDtypeStruct((8, per_group), jnp.int32),
            jax.ShapeDtypeStruct((2,) + state_input_matrix.shape, bf16),
            jax.ShapeDtypeStruct((devices, CAP, taps - 1, width), bf16),
        ),
        in_specs=smem(5) + hbm(3),
        out_specs=tuple(smem(1) + hbm(2)),
        scratch_shapes=[pltpu.SemaphoreType.DMA((2,)), pltpu.SemaphoreType.DMA((CAP, devices))],
        cost_estimate=cost(0, 1 << 20),
        name="pack_small",
    )(
        home, adapter_group_index, holder, prefix_cache_slot, prefix_block_count,
        state_input_matrix, state_output_matrix, convolution_cache,
    )
    rows_all = lax.all_gather(rows_mine, "dev", axis=0, tiled=False)
    conv_got = lax.all_to_all(conv_send, "dev", split_axis=0, concat_axis=0, tiled=True)

    cache = state_space_cache.reshape(
        state_space_cache.shape[0], devices, pieces, HEADS_PER_PIECE, size, depth
    )
    state_sends = pl.pallas_call(
        functools.partial(pack_state_kernel, devices, per_group, pieces),
        out_shape=tuple(
            jax.ShapeDtypeStruct((devices, CAP, HEADS_PER_PIECE, size, depth), bf16)
            for _ in range(pieces)
        ),
        in_specs=smem(2) + hbm(1),
        out_specs=tuple(hbm(pieces)),
        scratch_shapes=[pltpu.SemaphoreType.DMA((CAP, pieces))],
        cost_estimate=cost(0, 8 << 20),
        name="pack_state",
    )(holder, prefix_cache_slot, cache)
    state_gots = [
        lax.all_to_all(x, "dev", split_axis=0, concat_axis=0, tiled=True) for x in state_sends
    ]

    up_send = pack_adapter(home, adapter_group_index, adapter_up_weight, groups, per_group)
    up_got = lax.all_to_all(up_send, "group", split_axis=0, concat_axis=0, tiled=True)

    row_decay, column_decay = pl.pallas_call(
        prep_kernel,
        grid=(per_group,),
        out_shape=(
            jax.ShapeDtypeStruct((heads, tokens), f32),
            jax.ShapeDtypeStruct((tokens, heads), f32),
        ),
        in_specs=[
            pl.BlockSpec((heads, T_REQ), lambda r: (0, r)),
            pl.BlockSpec((heads, 1), lambda r: (0, 0)),
        ],
        out_specs=(
            pl.BlockSpec((heads, T_REQ), lambda r: (0, r)),
            pl.BlockSpec((T_REQ, heads), lambda r: (r, 0)),
        ),
        cost_estimate=cost(0, 4 << 20),
        name="prep",
    )(head_step_size, head_decay_rate.reshape(heads, 1))

    partial_down = pl.pallas_call(
        shrink_kernel,
        grid_spec=pltpu.PrefetchScalarGridSpec(
            num_scalar_prefetch=1,
            grid=(per_group,),
            in_specs=[
                pl.BlockSpec((T_REQ, hidden.shape[1]), lambda r, meta: (r, 0)),
                pl.BlockSpec(
                    (1, 1, rank, hidden.shape[1]),
                    lambda r, meta: (meta[HOME, r], meta[ADAPTER_RANK_AMONG, r], 0, 0),
                ),
            ],
            out_specs=pl.BlockSpec((1, rank, T_REQ), lambda r, meta: (r, 0, 0)),
        ),
        out_shape=jax.ShapeDtypeStruct((per_group, rank, T_REQ), bf16),
        cost_estimate=cost(2 * tokens * hidden.shape[1] * rank, 6 << 20),
        compiler_params=pltpu.CompilerParams(vmem_limit_bytes=VMEM_LIMIT),
        name="shrink",
    )(meta, hidden, down_got)
    parts = lax.all_to_all(partial_down, "dev", split_axis=0, concat_axis=0, tiled=True)
    summed = pl.pallas_call(
        sum_kernel,
        out_shape=jax.ShapeDtypeStruct((devices, share, rank, T_REQ), bf16),
        cost_estimate=cost(0, 1 << 19),
        name="sum_parts",
    )(parts.reshape(devices, share, rank, T_REQ))
    shrunk = lax.all_to_all(summed, "dev", split_axis=0, concat_axis=0, tiled=True)
    shrunk = shrunk.reshape(per_group, rank, T_REQ)

    skip_row = jnp.repeat(head_skip_scale, size).reshape(1, width)
    bias_row = convolution_bias.reshape(1, width)
    outs = None
    for piece in range(pieces):
        in_specs = [
            pl.BlockSpec((T_REQ, piece_width), lambda r, meta, p=piece: (r, p)),
            pl.BlockSpec((1, rank, T_REQ), lambda r, meta: (r, 0, 0)),
            pl.BlockSpec(
                (1, 1, rank, piece_width),
                lambda r, meta, p=piece: (meta[HOME, r], meta[ADAPTER_RANK_AMONG, r], 0, p),
            ),
            pl.BlockSpec(
                (1, 1, taps - 1, piece_width),
                lambda r, meta, p=piece: (meta[HOLDER, r], meta[HOLDER_RANK, r], 0, p),
            ),
            pl.BlockSpec((taps, piece_width), lambda r, meta, p=piece: (0, p)),
            pl.BlockSpec((1, piece_width), lambda r, meta, p=piece: (0, p)),
            pl.BlockSpec((1, piece_width), lambda r, meta, p=piece: (0, p)),
            pl.BlockSpec((heads, T_REQ), lambda r, meta: (0, r)),
            pl.BlockSpec((T_REQ, heads), lambda r, meta: (r, 0)),
            pl.BlockSpec((1, 2, T_REQ, depth), lambda r, meta: (r, 0, 0, 0)),
            pl.BlockSpec(
                (1, 1, HEADS_PER_PIECE, size, depth),
                lambda r, meta: (meta[HOLDER, r], meta[HOLDER_RANK, r], 0, 0, 0),
            ),
        ]
        operands = [
            meta, base_in_projection, shrunk, up_got, conv_got, convolution_weight, bias_row,
            skip_row, row_decay, column_decay, rows_all, state_gots[piece],
        ]
        aliases = {}
        if outs is not None:
            aliases = {len(operands): 0, len(operands) + 1: 1}
            operands += list(outs)
            in_specs += hbm(2)
        outs = pl.pallas_call(
            functools.partial(mix_kernel, piece),
            grid_spec=pltpu.PrefetchScalarGridSpec(
                num_scalar_prefetch=1,
                grid=(per_group,),
                in_specs=in_specs,
                out_specs=(
                    pl.BlockSpec((T_REQ, piece_width), lambda r, meta, p=piece: (r, p)),
                    pl.BlockSpec(
                        (1, HEADS_PER_PIECE, size, depth), lambda r, meta, p=piece: (r, p, 0, 0)
                    ),
                ),
                scratch_shapes=[
                    pltpu.VMEM((T_REQ + 8, piece_width), f32),
                    pltpu.VMEM((T_REQ, T_REQ), f32),
                ],
            ),
            out_shape=(
                jax.ShapeDtypeStruct((tokens, width), bf16),
                jax.ShapeDtypeStruct((per_group, heads, size, depth), bf16),
            ),
            input_output_aliases=aliases,
            cost_estimate=cost(1 << 30, 6 << 20, 8 << 20),
            compiler_params=pltpu.CompilerParams(vmem_limit_bytes=VMEM_LIMIT),
            name=f"mix_{piece}",
        )(*operands)
    return outs


def solution(mesh):
    placed = (
        P("group", "dev"),
        P("group", "dev"),
        P(("group", "dev"), None),
        P(("group", "dev"), None),
        P("dev", "group"),
        P("dev"),
        P("dev"),
        P(None, "dev"),
        P("dev"),
        P("group", None, "dev"),
        P("group", None, "dev"),
        P(),
        P(),
        P(("group", "dev"), None, None, None),
        P(("group", "dev"), None, None),
        P(),
        P(),
        P(),
    )
    return jax.shard_map(
        body,
        mesh=mesh,
        in_specs=placed,
        out_specs=(P("group", "dev"), P("group", "dev", None, None)),
        check_vma=False,
    )
```

time: 370 us -> 513 us (1.39)
  Pallas kernels: 0 us -> 320 us
  blocking collectives: 184 us -> 45.6 us
  waiting for transfers between devices: 1.42 us -> 74.3 us
  matrix products: 65.4 us -> 0 us
  local copies, waits for them, and re-layouts: 68.2 us -> 18.9 us
  starting transfers between devices: 12.5 us -> 34.1 us
  other arithmetic: 17.2 us -> 0 us
    pallas_call x0 -> x11, Pallas kernels: none -> 320 us  [the longest x2 131 us: pack_adapter(): pl.pallas_call(functools.partial(pack_adapter_kernel, groups, per_group),...]
    all_gather x2 -> x0, blocking collectives: 142 us -> none  [the longest x1 111 us: body(): lax.all_gather(state_output_matrix, 'dev', axis=0, tiled=True)]
    dot_general x34 -> x0, matrix products: 65.4 us -> none  [the longest x8 20 us: request_mixer(): jnp.einsum('hts,shp->thp', mixing, driven, preferred_element_type=jnp.flo...]
    all_to_all x0 -> x2, blocking collectives: none -> 45.6 us  [the longest x1 31.6 us: body(): lax.all_to_all(x, 'dev', split_axis=0, concat_axis=0, tiled=True)]
    all_to_all x2 -> x7, waiting for transfers between devices: 0.01 us -> 44 us  [the longest x3 36.6 us: body(): lax.all_to_all(x, 'dev', split_axis=0, concat_axis=0, tiled=True)]
    psum x1 -> x0, blocking collectives: 41.8 us -> none  [body(): shrunk_rows = lax.psum(partial_down, 'dev').astype(jnp.bfloat16)]
    all_gather x2 -> x1, waiting for transfers between devices: 0.04 us -> 29.6 us  [body(): rows_all = lax.all_gather(rows_mine, 'dev', axis=0, tiled=False)]
    all_to_all x2 -> x7, starting transfers between devices: 12.4 us -> 34.1 us  [the longest x3 14.7 us: body(): lax.all_to_all(x, 'dev', split_axis=0, concat_axis=0, tiled=True)]
  transfers between devices with their start and end apart: 4 -> 8, of which waited for: 0 -> 4; matrix products, arithmetic and copies ran while one was open for 13% -> 0% of each run, Pallas kernels for 0% -> 59%
where the time goes in v1:
time: 513 us; the launch traced here: 508 us
  Pallas kernels  320 us (62%)
  waiting for transfers between devices  74.3 us (14%)
  blocking collectives  45.6 us (9%)
  starting transfers between devices  34.1 us (7%)
  local copies, waits for them, and re-layouts  18.9 us (4%)
  between operations  14.2 us (3%)
    pallas_call x2, Pallas kernels, pack_adapter(): pl.pallas_call(functools.partial(pack_adapter_kernel, groups, per_group),...  131 us
    pallas_call x1, Pallas kernels, body(): pl.pallas_call(functools.partial(pack_state_kernel, devices, per_group, p...  129 us
    all_to_all x3, waiting for transfers between devices, body(): lax.all_to_all(x, 'dev', split_axis=0, concat_axis=0, tiled=True)  36.6 us
    pallas_call x4, Pallas kernels, body(): pl.pallas_call(functools.partial(mix_kernel, piece), grid_spec=pltpu.Pref...  36.5 us
    all_to_all x1, blocking collectives, body(): lax.all_to_all(x, 'dev', split_axis=0, concat_axis=0, tiled=True)  31.6 us
    all_gather x1, waiting for transfers between devices, body(): rows_all = lax.all_gather(rows_mine, 'dev', axis=0, tiled=False)  29.6 us
    unnamed x43, local copies, waits for them, and re-layouts  14.9 us
    all_to_all x3, starting transfers between devices, body(): lax.all_to_all(x, 'dev', split_axis=0, concat_axis=0, tiled=True)  14.7 us
  transfers between devices with their start and end apart: 8, of which 4 were waited for; matrix products, arithmetic and copies ran while one was open for 0% of the time, Pallas kernels for 59%

profile of v1, /device:TPU:8, one launch (start us, length us, event | category | flops | bytes accessed | tf_op | source)
XLA Modules:
  0.0 507.6 jit_solution(16202097167366671783)
XLA Ops:
  7.2 1.8 copy.29.conv
  9.0 10.5 %pack_small.1 = (s32[8,8]{1,0:T(8,128)}, bf16[2,256,128]{2,1,0:T(8,128)(2,1)}, bf16[8,2,3,1024]{3,2,1,0:T(4,128)(2,1)}) custom-call(s32[32]{0:T(128)} %bitcast.22, s32[32]{0:T(128)} %index.5, s32[32]{0:T(128)} %bitcast.25, s32[32]{0:T(128)} %slot.3, s32[32]{0:T(128)} %blocks.1, bf16[256,128]{1,0:T(8,128)(2,1)} %write_rows.1, bf16[256,128]{1,0:T(8,128)(2,1)} %read_rows.1, ...), custom_call_target="tpu_custom_call" | custom-call | bytes 1048576 | tf_op jit(solution)/shard_map/pack_small/pallas_call | solution.py:269
  19.5 1.6 copy.30
  21.1 6.3 %all-to-all-start.4 = ((bf16[8,2,3,1024]{3,1,2,0:T(2,128)(2,1)}), bf16[8,2,3,1024]{3,1,2,0:T(2,128)(2,1)S(1)}, u32[]{:S(2)}, u32[]{:S(2)}) async-start(bf16[8,2,3,1024]{3,1,2,0:T(2,128)(2,1)} %copy.30), calls=%async_computation.4 | async-start | bytes 196608 | tf_op jit(solution)/shard_map/all_to_all | solution.py:286
  27.3 65.5 %pack_adapter.2 = bf16[4,4,64,1024]{3,2,1,0:T(8,128)(2,1)} custom-call(s32[32]{0:T(128)} %bitcast.23, s32[32]{0:T(128)} %index.5, bf16[8,64,1024]{2,1,0:T(8,128)(2,1)} %table.2), custom_call_target="tpu_custom_call" | custom-call | bytes 4194304 | tf_op jit(solution)/shard_map/pack_adapter/pallas_call | solution.py:75
  92.8 0.0 all-to-all-done.4
  92.8 0.6 copy-done.18
  93.5 3.6 all-to-all-start
  97.1 65.5 %pack_adapter.3 = bf16[4,4,64,1024]{3,2,1,0:T(8,128)(2,1)} custom-call(s32[32]{0:T(128)} %bitcast.24, s32[32]{0:T(128)} %index.5, bf16[8,64,1024]{2,1,0:T(8,128)(2,1)} %table.3), custom_call_target="tpu_custom_call" | custom-call | bytes 4194304 | tf_op jit(solution)/shard_map/pack_adapter/pallas_call | solution.py:75
  162.6 0.0 copy-start.4
  162.6 1.3 copy-done.4
  163.9 3.6 all-to-all-start.3
  167.5 128.9 %pack_state.1 = (bf16[8,2,4,64,128]{4,3,2,1,0:T(8,128)(2,1)}, bf16[8,2,4,64,128]{4,3,2,1,0:T(8,128)(2,1)}, bf16[8,2,4,64,128]{4,3,2,1,0:T(8,128)(2,1)}, bf16[8,2,4,64,128]{4,3,2,1,0:T(8,128)(2,1)}) custom-call(s32[32]{0:T(128)} %bitcast.26, s32[32]{0:T(128)} %slot.3, bf16[4,8,4,4,64,128]{5,4,3,2,1,0:T(8,128)(2,1)} %bitcast.20), custom_call_target="tpu_custom_call" | custom-call | bytes 8388608 | tf_op jit(solution)/shard_map/pack_state/pallas_call | solution.py:291
  296.5 0.0 all-to-all-done.3.up
  296.5 31.6 %all_to_all.45.state = bf16[8,2,4,64,128]{4,3,2,1,0:T(8,128)(2,1)} all-to-all(bf16[8,2,4,64,128]{4,3,2,1,0:T(8,128)(2,1)} %get-tuple-element.23), channel_id=1, replica_groups=mesh['group'=4,'dev'=8] {'dev'}, dimensions={0} | all-to-all | bytes 2097152 | tf_op jit(solution)/shard_map/all_to_all | solution.py:304
  328.0 4.5 all-to-all-start.7
  332.6 1.6 copy-done.5
  334.2 6.3 %shrink.1 = bf16[8,64,256]{2,1,0:T(8,128)(2,1)S(1)} custom-call(s32[8,8]{1,0:T(8,128)S(1)} %copy-done.12, bf16[2048,1024]{1,0:T(8,128)(2,1)} %hidden.1, bf16[4,4,64,1024]{3,2,1,0:T(8,128)(2,1)S(1)} %copy-done.5), custom_call_target="tpu_custom_call" | custom-call | flops 268435456 | bytes 6291456 | tf_op jit(solution)/shard_map/shrink/pallas_call | solution.py:329
  340.5 15.7 %all-to-all-done.7.state = bf16[8,2,4,64,128]{4,3,2,1,0:T(8,128)(2,1)S(1)} async-done(((bf16[8,2,4,64,128]{4,3,2,1,0:T(8,128)(2,1)}), bf16[8,2,4,64,128]{4,3,2,1,0:T(8,128)(2,1)S(1)}, u32[]{:S(2)}, u32[]{:S(2)}) %all-to-all-start.7) | async-done | bytes 1048608 | tf_op jit(solution)/shard_map/all_to_all | solution.py:304
  356.2 14.1 %all_to_all.46 = bf16[8,64,256]{2,1,0:T(8,128)(2,1)} all-to-all(bf16[8,64,256]{2,1,0:T(8,128)(2,1)S(1)} %shrink.1), channel_id=1, replica_groups=mesh['group'=4,'dev'=8] {'dev'}, dimensions={0} | all-to-all | bytes 524288 | tf_op jit(solution)/shard_map/all_to_all | solution.py:348
  370.2 5.1 %all-to-all-start.8 = ((bf16[8,2,4,64,128]{4,3,2,1,0:T(8,128)(2,1)}), bf16[8,2,4,64,128]{4,3,2,1,0:T(8,128)(2,1)}, u32[]{:S(2)}, u32[]{:S(2)}) async-start(bf16[8,2,4,64,128]{4,3,2,1,0:T(8,128)(2,1)} %get-tuple-element.25), calls=%async_computation.8 | async-start | bytes 2097152 | tf_op jit(solution)/shard_map/all_to_all | solution.py:304
  375.3 1.7 sum_parts.1
  377.1 20.9 %all-to-all-done.8.state = bf16[8,2,4,64,128]{4,3,2,1,0:T(8,128)(2,1)} async-done(((bf16[8,2,4,64,128]{4,3,2,1,0:T(8,128)(2,1)}), bf16[8,2,4,64,128]{4,3,2,1,0:T(8,128)(2,1)}, u32[]{:S(2)}, u32[]{:S(2)}) %all-to-all-start.8) | async-done | bytes 1048608 | tf_op jit(solution)/shard_map/all_to_all | solution.py:304
  397.9 5.9 %all-to-all-start.2 = ((bf16[8,1,64,256]{3,2,1,0:T(8,128)(2,1)}), bf16[8,1,64,256]{3,2,1,0:T(8,128)(2,1)S(1)}, u32[]{:S(2)}, u32[]{:S(2)}) async-start(bf16[8,1,64,256]{3,2,1,0:T(8,128)(2,1)} %sum_parts.1), calls=%async_computation.2 | async-start | bytes 524288 | tf_op jit(solution)/shard_map/all_to_all | solution.py:355
  403.9 0.7 all-gather.3.cloned.1.call-update
  404.6 7.4 %all-to-all-done.2 = bf16[8,1,64,256]{3,2,1,0:T(8,128)(2,1)S(1)} async-done(((bf16[8,1,64,256]{3,2,1,0:T(8,128)(2,1)}), bf16[8,1,64,256]{3,2,1,0:T(8,128)(2,1)S(1)}, u32[]{:S(2)}, u32[]{:S(2)}) %all-to-all-start.2) | async-done | bytes 262176 | tf_op jit(solution)/shard_map/all_to_all | solution.py:355
  412.0 5.1 %all-to-all-start.5 = ((bf16[8,2,4,64,128]{4,3,2,1,0:T(8,128)(2,1)}), bf16[8,2,4,64,128]{4,3,2,1,0:T(8,128)(2,1)}, u32[]{:S(2)}, u32[]{:S(2)}) async-start(bf16[8,2,4,64,128]{4,3,2,1,0:T(8,128)(2,1)} %get-tuple-element.22), calls=%async_computation.5 | async-start | bytes 2097152 | tf_op jit(solution)/shard_map/all_to_all | solution.py:304
  417.1 0.7 copy.31.rates
  417.8 0.1 broadcast_in_dim.3
  417.9 0.7 reshape_reshape.3.skip
  418.6 5.6 %prep.1 = (f32[16,2048]{1,0:T(8,128)}, f32[2048,16]{1,0:T(8,128)}) custom-call(f32[16,2048]{1,0:T(8,128)} %steps.1, f32[16,1]{1,0:T(8,128)} %copy.31.rates), custom_call_target="tpu_custom_call" | custom-call | bytes 4194304 | tf_op jit(solution)/shard_map/prep/pallas_call | solution.py:310
  424.1 0.9 copy.35.conv
  425.1 29.6 %all-gather.3.cloned.1.call-done = bf16[16,256,128]{2,1,0:T(8,128)(2,1)} async-done(((bf16[2,256,128]{2,1,0:T(8,128)(2,1)}), bf16[16,256,128]{2,1,0:T(8,128)(2,1)}) %all-gather.3.cloned.1.call-update) | async-done | bytes 1048592 | tf_op jit(solution)/shard_map/all_gather | solution.py:285
  454.7 1.2 copy-done
  456.0 1.2 copy-done.2
  457.2 0.9 copy-done.7
  458.1 0.7 copy-done.10
  458.8 0.7 copy-done.13
  459.5 0.7 copy-done.15
  460.1 9.2 %mix_0.1 = (bf16[2048,1024]{1,0:T(8,128)(2,1)}, bf16[8,16,64,128]{3,2,1,0:T(8,128)(2,1)}) custom-call(s32[8,8]{1,0:T(8,128)S(1)} %copy-done.13, bf16[2048,1024]{1,0:T(8,128)(2,1)} %base.7, bf16[8,64,256]{2,1,0:T(8,128)(2,1)S(1)} %bitcast.12, bf16[4,4,64,1024]{3,2,1,0:T(8,128)(2,1)S(1)} %all-to-all-done.3.up, bf16[8,2,3,1024]{3,2,1,0:T(4,128)(2,1)S(1)} %copy.35.conv, ...), custom_call_target="tpu_custom_call" | custom-call | flops 1073741824 | bytes 6291456 | tf_op jit(solution)/shard_map/mix_0/pallas_call | solution.py:393
  469.3 9.1 %mix_1.1 = (bf16[2048,1024]{1,0:T(8,128)(2,1)}, bf16[8,16,64,128]{3,2,1,0:T(8,128)(2,1)}) custom-call(s32[8,8]{1,0:T(8,128)S(1)} %copy-done.13, bf16[2048,1024]{1,0:T(8,128)(2,1)} %base.7, bf16[8,64,256]{2,1,0:T(8,128)(2,1)S(1)} %bitcast.13, bf16[4,4,64,1024]{3,2,1,0:T(8,128)(2,1)S(1)} %all-to-all-done.3.up, ...), custom_call_target="tpu_custom_call", output_to_operand_aliasing={{0}: (12, {}), {1}: (13, {})} | custom-call | flops 1073741824 | bytes 6291456 | tf_op jit(solution)/shard_map/mix_1/pallas_call | solution.py:393
  478.4 9.1 %mix_2.1 = (bf16[2048,1024]{1,0:T(8,128)(2,1)}, bf16[8,16,64,128]{3,2,1,0:T(8,128)(2,1)}) custom-call(s32[8,8]{1,0:T(8,128)S(1)} %copy-done.13, bf16[2048,1024]{1,0:T(8,128)(2,1)} %base.7, bf16[8,64,256]{2,1,0:T(8,128)(2,1)S(1)} %bitcast.14, bf16[4,4,64,1024]{3,2,1,0:T(8,128)(2,1)S(1)} %all-to-all-done.3.up, ...), custom_call_target="tpu_custom_call", output_to_operand_aliasing={{0}: (12, {}), {1}: (13, {})} | custom-call | flops 1073741824 | bytes 6291456 | tf_op jit(solution)/shard_map/mix_2/pallas_call | solution.py:393
  487.5 1.2 copy-done.3
  488.7 0.9 copy-done.8
  489.6 0.7 copy-done.11
  490.3 0.7 copy-done.14
  491.0 0.7 copy-done.17
  491.7 9.1 %mix_3.1 = (bf16[2048,1024]{1,0:T(8,128)(2,1)}, bf16[8,16,64,128]{3,2,1,0:T(8,128)(2,1)}) custom-call(s32[8,8]{1,0:T(8,128)S(1)} %copy-done.14, bf16[2048,1024]{1,0:T(8,128)(2,1)} %base.7, bf16[8,64,256]{2,1,0:T(8,128)(2,1)S(1)} %bitcast.15, bf16[4,4,64,1024]{3,2,1,0:T(8,128)(2,1)S(1)} %all-to-all-done.3.up, ...), custom_call_target="tpu_custom_call", output_to_operand_aliasing={{0}: (12, {}), {1}: (13, {})} | custom-call | flops 1073741824 | bytes 6291456 | tf_op jit(solution)/shard_map/mix_3/pallas_call | solution.py:393
  (30 shorter events, 0.1 us)
Async XLA Ops:
  21.1 71.7 %all-to-all-start.4 = ((bf16[8,2,3,1024]{3,1,2,0:T(2,128)(2,1)}), bf16[8,2,3,1024]{3,1,2,0:T(2,128)(2,1)S(1)}, u32[]{:S(2)}, u32[]{:S(2)}) async-start(bf16[8,2,3,1024]{3,1,2,0:T(2,128)(2,1)} %copy.30), calls=%async_computation.4 | async-start | bytes 196608 | tf_op jit(solution)/shard_map/all_to_all | solution.py:286
  92.8 0.6 copy-start.18
  93.5 69.1 %all-to-all-start = ((bf16[4,4,64,1024]{3,2,1,0:T(8,128)(2,1)}), bf16[4,4,64,1024]{3,2,1,0:T(8,128)(2,1)S(1)}, u32[]{:S(2)}, u32[]{:S(2)}) async-start(bf16[4,4,64,1024]{3,2,1,0:T(8,128)(2,1)} %pack_adapter.2), calls=%async_computation | async-start | bytes 4194304 | tf_op jit(solution)/shard_map/all_to_all | solution.py:267
  162.6 1.3 copy-start.4
  163.9 132.6 %all-to-all-start.3 = ((bf16[4,4,64,1024]{3,2,1,0:T(8,128)(2,1)}), bf16[4,4,64,1024]{3,2,1,0:T(8,128)(2,1)S(1)}, u32[]{:S(2)}, u32[]{:S(2)}) async-start(bf16[4,4,64,1024]{3,2,1,0:T(8,128)(2,1)} %pack_adapter.3), calls=%async_computation.3 | async-start | bytes 4194304 | tf_op jit(solution)/shard_map/all_to_all | solution.py:308
  296.5 36.1 %copy-start.12 = (s32[8,8]{1,0:T(8,128)S(1)}, s32[8,8]{1,0:T(8,128)}, u32[]{:S(2)}) copy-start(s32[8,8]{1,0:T(8,128)} %get-tuple-element.17.meta) | copy-start | bytes 772
  328.0 28.1 %all-to-all-start.7 = ((bf16[8,2,4,64,128]{4,3,2,1,0:T(8,128)(2,1)}), bf16[8,2,4,64,128]{4,3,2,1,0:T(8,128)(2,1)S(1)}, u32[]{:S(2)}, u32[]{:S(2)}) async-start(bf16[8,2,4,64,128]{4,3,2,1,0:T(8,128)(2,1)} %get-tuple-element.24), calls=%async_computation.7 | async-start | bytes 2097152 | tf_op jit(solution)/shard_map/all_to_all | solution.py:304
  332.6 1.6 copy-start.5
  370.2 27.7 %all-to-all-start.8 = ((bf16[8,2,4,64,128]{4,3,2,1,0:T(8,128)(2,1)}), bf16[8,2,4,64,128]{4,3,2,1,0:T(8,128)(2,1)}, u32[]{:S(2)}, u32[]{:S(2)}) async-start(bf16[8,2,4,64,128]{4,3,2,1,0:T(8,128)(2,1)} %get-tuple-element.25), calls=%async_computation.8 | async-start | bytes 2097152 | tf_op jit(solution)/shard_map/all_to_all | solution.py:304
  375.3 41.8 %copy-start.19 = (f32[16]{0:T(128)S(1)}, f32[16]{0:T(128)}, u32[]{:S(2)}) copy-start(f32[16]{0:T(128)} %param.23) | copy-start | bytes 196
  375.3 42.5 %copy-start.20 = (f32[16]{0:T(128)S(1)}, f32[16]{0:T(128)}, u32[]{:S(2)}) copy-start(f32[16]{0:T(128)} %param.24) | copy-start | bytes 196
  375.3 79.4 %copy-start.9 = (f32[4,1024]{1,0:T(4,128)S(1)}, f32[4,1024]{1,0:T(4,128)}, u32[]{:S(2)}) copy-start(f32[4,1024]{1,0:T(4,128)} %conv_weight.7) | copy-start | bytes 49156
  397.9 14.1 %all-to-all-start.2 = ((bf16[8,1,64,256]{3,2,1,0:T(8,128)(2,1)}), bf16[8,1,64,256]{3,2,1,0:T(8,128)(2,1)S(1)}, u32[]{:S(2)}, u32[]{:S(2)}) async-start(bf16[8,1,64,256]{3,2,1,0:T(8,128)(2,1)} %sum_parts.1), calls=%async_computation.2 | async-start | bytes 524288 | tf_op jit(solution)/shard_map/all_to_all | solution.py:355
  403.9 50.9 %all-gather.3.cloned.1.call-start = ((), (), s32[]{:S(2)}) async-start(), calls=%async_computation.9 | async-start | bytes 1179648 | tf_op jit(solution)/shard_map/all_gather | solution.py:285
  412.0 75.4 %all-to-all-start.5 = ((bf16[8,2,4,64,128]{4,3,2,1,0:T(8,128)(2,1)}), bf16[8,2,4,64,128]{4,3,2,1,0:T(8,128)(2,1)}, u32[]{:S(2)}, u32[]{:S(2)}) async-start(bf16[8,2,4,64,128]{4,3,2,1,0:T(8,128)(2,1)} %get-tuple-element.22), calls=%async_computation.5 | async-start | bytes 2097152 | tf_op jit(solution)/shard_map/all_to_all | solution.py:304
  454.7 1.2 copy-start
  456.0 1.2 copy-start.2
  457.2 0.9 copy-start.7
  458.1 0.7 copy-start.10
  458.8 0.7 copy-start.13
  459.5 0.7 copy-start.15
  460.1 9.2 %copy-start.16 = (f32[1024]{0:T(1024)S(1)}, f32[1024]{0:T(1024)}, u32[]{:S(2)}) copy-start(f32[1024]{0:T(1024)} %param.26) | copy-start | bytes 12292
  469.3 9.1 %copy-start.6 = (bf16[8,2,4,64,128]{4,3,2,1,0:T(8,128)(2,1)S(1)}, bf16[8,2,4,64,128]{4,3,2,1,0:T(8,128)(2,1)}, u32[]{:S(2)}) copy-start(bf16[8,2,4,64,128]{4,3,2,1,0:T(8,128)(2,1)} %all_to_all.45.state) | copy-start | bytes 3145732
  478.4 9.1 %copy-start.1 = (bf16[16,256,128]{2,1,0:T(8,128)(2,1)S(1)}, bf16[16,256,128]{2,1,0:T(8,128)(2,1)}, u32[]{:S(2)}) copy-start(bf16[16,256,128]{2,1,0:T(8,128)(2,1)} %all-gather.3.cloned.1.call-done) | copy-start | bytes 3145732
  487.5 1.2 copy-start.3
  488.7 0.9 copy-start.8
  489.6 0.7 copy-start.11
  490.3 0.7 copy-start.14
  491.0 0.7 copy-start.17
Sparse Core Ops, SparseCore 0:
  406.8 47.8 all-gather.2

commit v2 on v1

v2 whole, which is shorter than its diff:
```python
import functools
import math

import jax
import jax.numpy as jnp
from jax import lax
from jax.experimental import pallas as pl
from jax.experimental.pallas import tpu as pltpu
from jax.sharding import PartitionSpec as P

T_REQ = 256
CAP = 2
ACAP = 4
CONV_ROWS = 16
LOG2E = math.log2(math.e)
NT = (((1,), (1,)), ((), ()))
TN = (((0,), (0,)), ((), ()))
VMEM_LIMIT = 48 * 1024 * 1024

DIST, ARANK, AINDEX, HOLDER, HRANK, PRESENT, REQ_OF, OVER, OSLOT, OHOLDER, MISC, SEND = range(12)
COUNT, MOST, ME, SLOT, SLOT_TOO = range(5)
META_SHAPE = (16, 64)


def cost(flops, nbytes, transcendentals=0):
    return pl.CostEstimate(
        flops=int(flops), bytes_accessed=int(nbytes), transcendentals=int(transcendentals)
    )


def params():
    return pltpu.CompilerParams(vmem_limit_bytes=VMEM_LIMIT)


def smem(count):
    return [pl.BlockSpec(memory_space=pltpu.SMEM) for _ in range(count)]


def as_int(flag):
    return flag.astype(jnp.int32)


def ranks_of(labels):
    ranks = []
    for q, label in enumerate(labels):
        total = jnp.int32(0)
        for other in labels[:q]:
            total = total + as_int(other == label)
        ranks.append(total)
    return ranks


def plan_kernel(groups, devices, per_group, home, index, holder, slot, blocks, meta):
    my_group = lax.axis_index("group")
    me = lax.axis_index("dev")
    first = my_group * per_group
    for j in range(per_group):
        meta[OVER, j] = jnp.int32(0)
        meta[OSLOT, j] = jnp.int32(0)
        meta[OHOLDER, j] = jnp.int32(0)

    homes = [home[first + q] for q in range(per_group)]
    for q, rank in enumerate(ranks_of(homes)):
        own = homes[q] == my_group
        meta[DIST, q] = lax.bitwise_xor(homes[q], my_group)
        meta[ARANK, q] = jnp.where(own, 0, rank)
        meta[AINDEX, q] = jnp.where(own, index[first + q], 0)
        meta[PRESENT, q] = as_int(blocks[first + q] > 0)
    for k in range(1, groups):
        theirs = lax.bitwise_xor(my_group, k) * per_group
        seen = jnp.int32(0)
        chosen = [jnp.int32(0) for _ in range(ACAP)]
        for q in range(per_group):
            hit = home[theirs + q] == my_group
            value = index[theirs + q]
            for c in range(ACAP):
                chosen[c] = jnp.where(hit & (seen == c), value, chosen[c])
            seen = seen + as_int(hit)
        for c in range(ACAP):
            meta[SEND, (k - 1) * ACAP + c] = chosen[c]

    holders = [holder[first + q] for q in range(per_group)]
    ranks = ranks_of(holders)
    count = jnp.int32(0)
    my_slots = [jnp.int32(0) for _ in range(CAP)]
    for q in range(per_group):
        meta[HOLDER, q] = holders[q]
        meta[HRANK, q] = ranks[q]
        for c in range(CAP):
            hit = (holders[q] == me) & (ranks[q] == c)
            my_slots[c] = jnp.where(hit, slot[first + q], my_slots[c])

        @pl.when(ranks[q] > 0)
        def _():
            meta[OVER, count] = jnp.int32(q)
            meta[OSLOT, count] = slot[first + q]
            meta[OHOLDER, count] = holders[q]

        count = count + as_int(ranks[q] > 0)
    empties = jnp.int32(0)
    for d in range(devices):
        source = lax.bitwise_xor(me, d)
        request = jnp.int32(-1)
        for q in range(per_group):
            request = jnp.where((holders[q] == source) & (ranks[q] == 0), q, request)
        missing = request < 0
        meta[REQ_OF, d] = jnp.where(missing, meta[OVER, empties], request)
        empties = empties + as_int(missing)
    most = jnp.int32(0)
    for g in range(groups):
        labels = [holder[g * per_group + q] for q in range(per_group)]
        total = jnp.int32(0)
        for rank in ranks_of(labels):
            total = total + as_int(rank > 0)
        most = jnp.maximum(most, total)
    meta[MISC, COUNT] = count
    meta[MISC, MOST] = most
    meta[MISC, ME] = me
    meta[MISC, SLOT] = my_slots[0]
    meta[MISC, SLOT_TOO] = my_slots[1]


def pack_adapter_kernel(groups, meta, table, *rest):
    outs, sems = rest[:-1], rest[-1]
    copies = []
    for k in range(1, groups):
        for c in range(ACAP):
            chosen = meta[SEND, (k - 1) * ACAP + c]
            copy = pltpu.make_async_copy(
                table.at[chosen], outs[k - 1].at[c], sems.at[(k - 1) * ACAP + c]
            )
            copy.start()
            copies.append(copy)
    for copy in copies:
        copy.wait()


def swap_adapters(meta, table, groups, name):
    packed = pl.pallas_call(
        functools.partial(pack_adapter_kernel, groups),
        out_shape=tuple(
            jax.ShapeDtypeStruct((ACAP,) + table.shape[1:], table.dtype) for _ in range(groups - 1)
        ),
        in_specs=smem(1) + [pl.BlockSpec(memory_space=pltpu.HBM)],
        out_specs=tuple(pl.BlockSpec(memory_space=pltpu.VMEM) for _ in range(groups - 1)),
        scratch_shapes=[pltpu.SemaphoreType.DMA(((groups - 1) * ACAP,))],
        cost_estimate=cost(0, 2 * (groups - 1) * ACAP * table.shape[1] * table.shape[2] * 2),
        compiler_params=params(),
        name=name,
    )(meta, table)
    return [
        lax.ppermute(packed[k - 1], "group", [(g, g ^ k) for g in range(groups)])
        for k in range(1, groups)
    ]


def pack_state_kernel(devices, meta, cache, *rest):
    outs, sems = rest[:-1], rest[-1]
    me = meta[MISC, ME]
    copies = []
    for d in range(1, devices):
        target = lax.bitwise_xor(me, d)
        copy = pltpu.make_async_copy(
            cache.at[meta[MISC, SLOT], target // 2, target % 2], outs[d - 1], sems.at[d - 1]
        )
        copy.start()
        copies.append(copy)
    for copy in copies:
        copy.wait()


def pack_conv_kernel(devices, width, meta, conv, out):
    half = width // 2
    for c in range(CAP):
        rows = conv[meta[MISC, (SLOT, SLOT_TOO)[c]]]
        for d in range(devices):
            for k in range(rows.shape[0]):
                for part in range(2):
                    at = c * 2 * rows.shape[0] + 2 * k + part
                    begin = d * width + part * half
                    out[d, at:at + 1, :] = rows[k:k + 1, begin:begin + half]


def copy_kernel(j, meta, source, out):
    out[0] = source[0, 0, 0]


def pick_kernel(step, lines, j, meta, own_r, over_r, own_l, over_l, *rest):
    out_r, out_l = rest[-2:]
    me = meta[MISC, ME]
    source = meta[OHOLDER, j[0]]
    same = source // 2 == me // 2
    mine = same & (source % 2 == me % 2)
    across = same & (source % 2 != me % 2)

    @pl.when(mine)
    def _():
        out_r[...] = own_r[0, 0, 0]
        out_l[...] = own_l[0, 0, 0]

    @pl.when(across)
    def _():
        out_r[...] = over_r[0]
        out_l[...] = over_l[0]

    @pl.when(jnp.logical_not(same))
    def _():
        if step > 1:
            out_r[...] = rest[0][...]
            out_l[...] = rest[1][...]
        else:
            out_r[...] = jnp.zeros_like(out_r)
            out_l[...] = jnp.zeros_like(out_l)


def right_block(meta, step, lines):
    return jnp.clip(lines + meta[MISC, ME] // 2 - step, 0, lines - 1)


def left_block(meta, step, lines):
    return jnp.clip(meta[MISC, ME] // 2 + step - lines, 0, lines - 1)


def spread_entry(j, meta, cache, devices):
    lines = devices // 2
    shape = cache.shape[3:]
    full = (1, 1, 1) + shape
    send = pl.pallas_call(
        copy_kernel,
        grid_spec=pltpu.PrefetchScalarGridSpec(
            num_scalar_prefetch=2,
            grid=(lines,),
            in_specs=[
                pl.BlockSpec(
                    full,
                    lambda m, j, meta: (
                        meta[OSLOT, j[0]], m, 1 - meta[MISC, ME] % 2, 0, 0, 0
                    ),
                )
            ],
            out_specs=pl.BlockSpec((1,) + shape, lambda m, j, meta: (m, 0, 0, 0)),
        ),
        out_shape=jax.ShapeDtypeStruct((lines,) + shape, cache.dtype),
        cost_estimate=cost(0, 2 << 20),
        compiler_params=params(),
        name="pack_across",
    )(j, meta, cache)
    across = lax.ppermute(send, "dev", [(d, d ^ 1) for d in range(devices)])
    from_left = from_right = None
    whole = pl.BlockSpec(shape, lambda g, j, meta: (0, 0, 0))
    for step in range(1, lines):
        def at_right(j, meta, step=step):
            return right_block(meta, step, lines)

        def at_left(j, meta, step=step):
            return left_block(meta, step, lines)

        operands = [cache, across, cache, across]
        in_specs = [
            pl.BlockSpec(
                full, lambda g, j, meta, at=at: (
                    meta[OSLOT, j[0]], at(j, meta), meta[MISC, ME] % 2, 0, 0, 0
                )
            ) if is_own else pl.BlockSpec(
                (1,) + shape, lambda g, j, meta, at=at: (at(j, meta), 0, 0, 0)
            )
            for at in (at_right, at_left) for is_own in (True, False)
        ]
        if step > 1:
            operands += [from_left, from_right]
            in_specs += [whole, whole]
        to_right, to_left = pl.pallas_call(
            functools.partial(pick_kernel, step, lines),
            grid_spec=pltpu.PrefetchScalarGridSpec(
                num_scalar_prefetch=2, grid=(1,), in_specs=in_specs, out_specs=(whole, whole)
            ),
            out_shape=tuple(jax.ShapeDtypeStruct(shape, cache.dtype) for _ in range(2)),
            cost_estimate=cost(0, 2 << 20),
            compiler_params=params(),
            name=f"pick_{step}",
        )(j, meta, *operands)
        from_left = lax.ppermute(
            to_right, "dev",
            [(2 * i + x, 2 * i + 2 + x) for i in range(step) for x in range(2)],
        )
        from_right = lax.ppermute(
            to_left, "dev",
            [(devices - 1 - (2 * i + x), devices - 3 - (2 * i + x))
             for i in range(step) for x in range(2)],
        )
    return across, from_left, from_right


def final_specs(shape, request):
    full = (1, 1, 1) + shape
    return [
        pl.BlockSpec(
            full, lambda g, j, meta: (
                request(g, j, meta), meta[MISC, ME] // 2, meta[MISC, ME] % 2, 0, 0, 0
            )
        ),
        pl.BlockSpec((1,) + shape, lambda g, j, meta: (meta[MISC, ME] // 2, 0, 0, 0)),
        pl.BlockSpec(shape, lambda g, j, meta: (0, 0, 0)),
        pl.BlockSpec(shape, lambda g, j, meta: (0, 0, 0)),
    ]


def which_candidate(meta, source):
    me = meta[MISC, ME]
    same = source // 2 == me // 2
    mine = same & (source % 2 == me % 2)
    return jnp.where(mine, 0, jnp.where(same, 1, jnp.where(source // 2 < me // 2, 2, 3)))


def final_kernel(j, meta, own, across, from_left, from_right, out):
    which = which_candidate(meta, meta[OHOLDER, j[0]])
    picks = (own.at[0, 0, 0], across.at[0], from_left, from_right)
    for k, pick in enumerate(picks):
        @pl.when(which == k)
        def _(pick=pick):
            out[...] = pick[...]


def spread_rest(meta, cache, devices, limit):
    shape = cache.shape[3:]

    def one(j, held):
        jj = j.reshape(1)
        got = spread_entry(jj, meta, cache, devices)
        block = pl.pallas_call(
            final_kernel,
            grid_spec=pltpu.PrefetchScalarGridSpec(
                num_scalar_prefetch=2,
                grid=(1,),
                in_specs=final_specs(shape, lambda g, j, meta: meta[OSLOT, j[0]]),
                out_specs=pl.BlockSpec(shape, lambda g, j, meta: (0, 0, 0)),
            ),
            out_shape=jax.ShapeDtypeStruct(shape, cache.dtype),
            compiler_params=params(),
            name="final_pick",
        )(jj, meta, cache, *got)
        return lax.dynamic_update_slice_in_dim(held, block[None], j - 1, 0)

    held = jnp.zeros((limit - 1,) + shape, cache.dtype)
    return lax.fori_loop(jnp.int32(1), meta[MISC, MOST], one, held)


def shrink_kernel(groups, meta, hidden, *rest):
    tables, out = rest[:groups], rest[groups]
    dist = meta[DIST, pl.program_id(0)]
    for k in range(groups):
        @pl.when(dist == k)
        def _(k=k):
            part = lax.dot_general(
                tables[k][0], hidden[...], NT, preferred_element_type=jnp.float32
            )
            out[0] = part.astype(out.dtype)


def sum_kernel(parts, out):
    total = parts[0].astype(jnp.float32)
    for k in range(1, parts.shape[0]):
        total = total + parts[k].astype(jnp.float32)
    total = total.astype(out.dtype)
    for k in range(out.shape[0]):
        out[k] = total


def prep_kernel(steps, rates, row_out, column_out):
    heads, length = steps.shape
    step = steps[...]
    x = step * (rates[...] * (-LOG2E))
    high = x.astype(jnp.bfloat16)
    rest = x - high.astype(jnp.float32)
    middle = rest.astype(jnp.bfloat16)
    low = (rest - middle.astype(jnp.float32)).astype(jnp.bfloat16)
    s = lax.broadcasted_iota(jnp.int32, (length, length), 0)
    t = lax.broadcasted_iota(jnp.int32, (length, length), 1)
    ones = (s <= t).astype(jnp.float32).astype(jnp.bfloat16)
    total = jnp.dot(low, ones, preferred_element_type=jnp.float32)
    total = total + jnp.dot(middle, ones, preferred_element_type=jnp.float32)
    total = total + jnp.dot(high, ones, preferred_element_type=jnp.float32)
    row_out[...] = total - jnp.log2(step)
    column_out[...] = total.T


def mix_kernel(groups, taps, meta, base, shrunk, *rest):
    tables, (conv, channel, row_decay, column_decay, rows_in, partial, fresh, extended, scores) = (
        rest[:groups], rest[groups:]
    )
    r = pl.program_id(0)
    length, width = base.shape
    half = length // 2
    heads, size, depth = fresh.shape[1:]
    f32, bf16 = jnp.float32, jnp.bfloat16
    dist = meta[DIST, r]
    for k in range(groups):
        @pl.when(dist == k)
        def _(k=k):
            extended[8:, :] = base[...].astype(f32) + lax.dot_general(
                shrunk[0], tables[k][0], TN, preferred_element_type=f32
            )

    write, read = rows_in[:, :depth], rows_in[:, depth:]
    all_scores = lax.dot_general(read, write, NT, preferred_element_type=f32)
    t = lax.broadcasted_iota(jnp.int32, (length, length), 0)
    s = lax.broadcasted_iota(jnp.int32, (length, length), 1)
    scores[...] = jnp.where(s <= t, all_scores, 0.0)

    present = meta[PRESENT, r] > 0
    second = meta[HRANK, r] > 0
    few = taps - 1
    carry = jnp.where(second, conv[0, 2 * few:4 * few, :], conv[0, :2 * few, :]).astype(f32)
    carry = jnp.where(present, carry, 0.0)
    for k in range(few):
        at = 8 - few + k
        extended[at:at + 1, :width // 2] = carry[2 * k:2 * k + 1, :]
        extended[at:at + 1, width // 2:] = carry[2 * k + 1:2 * k + 2, :]

    row = row_decay[...]
    column = column_decay[...]
    lane = lax.broadcasted_iota(jnp.int32, (1, 2 * size), 1)
    for pair in range(heads // 2):
        lo, hi = pair * 2 * size, (pair + 1) * 2 * size
        v = channel[taps:taps + 1, lo:hi]
        for k in range(taps):
            begin = 8 - few + k
            v = v + channel[k:k + 1, lo:hi] * extended[begin:begin + length, lo:hi]
        activated = v * (0.5 + 0.5 * jnp.tanh(0.5 * v))
        a = activated.astype(bf16)
        a_t = a.T
        zero = jnp.zeros_like(a)
        a_sel = (jnp.where(lane < size, a, zero), jnp.where(lane < size, zero, a))
        upper, lower = [], []
        for i in range(2):
            h = pair * 2 + i
            dt = jnp.broadcast_to(column[:, h:h + 1], (length, half))
            ds0, ds1 = row[h:h + 1, :half], row[h:h + 1, half:]
            m00 = jnp.exp2(jnp.minimum(dt[:half] - ds0, 126.0)) * scores[:half, :half]
            m10 = jnp.exp2(dt[half:] - ds0) * scores[half:, :half]
            m11 = jnp.exp2(jnp.minimum(dt[half:] - ds1, 126.0)) * scores[half:, half:]
            upper.append(m00.astype(bf16))
            lower.extend([m10.astype(bf16), m11.astype(bf16)])
            end = dt[length - 1:length, :]
            to_end = jnp.exp2(jnp.concatenate([end, end], axis=1) - row[h:h + 1, :])
            weighted = (a_t[i * size:(i + 1) * size, :].astype(f32) * to_end).astype(bf16)
            fresh[0, h] = jnp.dot(weighted, write, preferred_element_type=f32)
        y0 = jnp.dot(
            jnp.concatenate(upper, axis=1),
            jnp.concatenate([a_sel[0][:half], a_sel[1][:half]], axis=0),
            preferred_element_type=f32,
        )
        y1 = jnp.dot(
            jnp.concatenate(lower, axis=1),
            jnp.concatenate(a_sel, axis=0),
            preferred_element_type=f32,
        )
        direct = channel[taps + 1:taps + 2, lo:hi] * activated
        partial[:half, lo:hi] = y0 + direct[:half]
        partial[half:, lo:hi] = y1 + direct[half:]


def add_state(present, state, partial, fresh, read, column, out, final):
    heads, size, depth = state.shape
    length = partial.shape[0]
    f32 = jnp.float32
    lane = lax.broadcasted_iota(jnp.int32, (1, 2 * size), 1)
    for pair in range(heads // 2):
        lo, hi = pair * 2 * size, (pair + 1) * 2 * size
        states = state[2 * pair:2 * pair + 2]
        carried = lax.dot_general(
            read, states.reshape(2 * size, depth), NT, preferred_element_type=f32
        )
        decays = [
            jnp.broadcast_to(column[:, h:h + 1], (length, 2 * size))
            for h in (2 * pair, 2 * pair + 1)
        ]
        grown = jnp.exp2(jnp.where(lane < size, decays[0], decays[1]))
        carried = jnp.where(present, carried * grown, 0.0)
        out[:, lo:hi] = (partial[:, lo:hi] + carried).astype(out.dtype)
        for i in range(2):
            h = 2 * pair + i
            kept = states[i].astype(f32) * jnp.exp2(decays[i][length - 1:length, :depth])
            kept = jnp.where(present, kept, 0.0)
            final[0, h] = (fresh[0, h] + kept).astype(final.dtype)


def finish(begin, states, cache, j, meta, partial, fresh, rows_all, column_decay, outs):
    tokens, width = partial.shape
    per_group, heads, size, depth = fresh.shape
    shape = (heads, size, depth)
    count = len(states)
    if begin == 0:
        state_specs = [
            pl.BlockSpec(
                (1, 1, 1) + shape, lambda g, j, meta: (
                    meta[MISC, SLOT], meta[MISC, ME] // 2, meta[MISC, ME] % 2, 0, 0, 0
                )
            )
        ]
    else:
        state_specs = [pl.BlockSpec(shape, lambda g, j, meta: (0, 0, 0))]
    state_specs += [pl.BlockSpec(shape, lambda g, j, meta: (0, 0, 0))] * (count - 1)

    def kernel(j, meta, partial, fresh, rows_in, column, *rest):
        out, final = rest[-2:]
        g = pl.program_id(0)
        present = meta[PRESENT, meta[REQ_OF, begin + g]] > 0
        for k in range(count):
            state = rest[0].at[0, 0, 0] if begin == 0 and k == 0 else rest[k]

            @pl.when(g == k)
            def _(state=state):
                add_state(
                    present, state, partial, fresh, rows_in[:, depth:], column[...], out, final
                )

    return finish_call(
        kernel, count, lambda g, j, meta: meta[REQ_OF, begin + g], states, state_specs, j, meta,
        partial, fresh, rows_all, column_decay, outs, f"finish_{begin}",
    )


def finish_call(
    kernel, count, request, states, state_specs, j, meta, partial, fresh, rows_all, column_decay,
    outs, name,
):
    tokens, width = partial.shape
    per_group, heads, size, depth = fresh.shape
    in_specs = [
        pl.BlockSpec((T_REQ, width), lambda g, j, meta: (request(g, j, meta), 0)),
        pl.BlockSpec((1, heads, size, depth), lambda g, j, meta: (request(g, j, meta), 0, 0, 0)),
        pl.BlockSpec((T_REQ, 2 * depth), lambda g, j, meta: (request(g, j, meta), 0)),
        pl.BlockSpec((T_REQ, heads), lambda g, j, meta: (request(g, j, meta), 0)),
    ] + state_specs
    operands = [j, meta, partial, fresh, rows_all, column_decay] + list(states)
    aliases = {}
    if outs is not None:
        aliases = {len(operands): 0, len(operands) + 1: 1}
        operands += list(outs)
        in_specs += [pl.BlockSpec(memory_space=pl.ANY) for _ in range(2)]
    return pl.pallas_call(
        kernel,
        grid_spec=pltpu.PrefetchScalarGridSpec(
            num_scalar_prefetch=2,
            grid=(count,),
            in_specs=in_specs,
            out_specs=(
                pl.BlockSpec((T_REQ, width), lambda g, j, meta: (request(g, j, meta), 0)),
                pl.BlockSpec(
                    (1, heads, size, depth), lambda g, j, meta: (request(g, j, meta), 0, 0, 0)
                ),
            ),
        ),
        out_shape=(
            jax.ShapeDtypeStruct((tokens, width), jnp.bfloat16),
            jax.ShapeDtypeStruct((per_group, heads, size, depth), jnp.bfloat16),
        ),
        input_output_aliases=aliases,
        cost_estimate=cost(count << 26, count * (3 << 20)),
        compiler_params=params(),
        name=name,
    )(*operands)


def finish_spread(
    first, others, limit, cache, j, meta, partial, fresh, rows_all, column_decay, outs
):
    shape = fresh.shape[1:]
    depth = shape[2]

    def place(g, meta):
        return jnp.maximum(jnp.minimum(g, meta[MISC, COUNT] - 1), 0)

    def request(g, j, meta):
        return jnp.where(
            meta[MISC, COUNT] > 0, meta[OVER, place(g, meta)], meta[REQ_OF, 0]
        )

    def own_slot(g, j, meta):
        return jnp.where(meta[MISC, COUNT] > 0, meta[OSLOT, 0], meta[MISC, SLOT])

    state_specs = final_specs(shape, own_slot) + [
        pl.BlockSpec(
            (1,) + shape, lambda g, j, meta: (jnp.maximum(place(g, meta) - 1, 0), 0, 0, 0)
        )
    ]

    def kernel(j, meta, partial, fresh, rows_in, column, *rest):
        out, final = rest[-2:]
        own, across, from_left, from_right, later = rest[:5]
        g = pl.program_id(0)
        count = meta[MISC, COUNT]
        present = meta[PRESENT, request(g, j, meta)] > 0
        which = jnp.where(count > 0, which_candidate(meta, meta[OHOLDER, 0]), 0)
        which = jnp.where(g > 0, jnp.where(g < count, 4, 5), which)
        picks = (own.at[0, 0, 0], across.at[0], from_left, from_right, later.at[0])
        for k, state in enumerate(picks):
            @pl.when(which == k)
            def _(state=state):
                add_state(
                    present, state, partial, fresh, rows_in[:, depth:], column[...], out, final
                )

    return finish_call(
        kernel, limit, request, [cache, *first, others], state_specs, j, meta, partial, fresh,
        rows_all, column_decay, outs, "finish_spread",
    )


def body(
    hidden, base_in_projection, state_input_matrix, state_output_matrix, head_step_size,
    head_decay_rate, head_skip_scale, convolution_weight, convolution_bias, adapter_down_weight,
    adapter_up_weight, adapter_home_group, adapter_group_index, state_space_cache,
    convolution_cache, prefix_holder_device, prefix_cache_slot, prefix_block_count,
):
    groups, devices = lax.axis_size("group"), lax.axis_size("dev")
    tokens, width = base_in_projection.shape
    per_group = tokens // T_REQ
    assert per_group == devices and devices & (devices - 1) == 0 == groups & (groups - 1)
    heads = head_step_size.shape[0]
    size, depth = state_space_cache.shape[2:]
    rank = adapter_down_weight.shape[1]
    taps = convolution_weight.shape[0]
    bf16, f32 = jnp.bfloat16, jnp.float32
    share = per_group // devices
    shape = (heads, size, depth)

    rows_all = lax.all_gather(
        jnp.concatenate([state_input_matrix, state_output_matrix], axis=1), "dev", axis=0,
        tiled=True,
    )
    meta = pl.pallas_call(
        functools.partial(plan_kernel, groups, devices, per_group),
        out_shape=jax.ShapeDtypeStruct(META_SHAPE, jnp.int32),
        in_specs=smem(5),
        out_specs=smem(1)[0],
        cost_estimate=cost(0, 1 << 16),
        name="plan",
    )(
        adapter_home_group.reshape(-1), adapter_group_index, prefix_holder_device.reshape(-1),
        prefix_cache_slot, prefix_block_count,
    )
    zero = jnp.zeros((1,), jnp.int32)

    down_got = swap_adapters(meta, adapter_down_weight, groups, "pack_down")

    cache = state_space_cache.reshape((state_space_cache.shape[0], devices // 2, 2) + shape)
    state_sends = pl.pallas_call(
        functools.partial(pack_state_kernel, devices),
        out_shape=tuple(jax.ShapeDtypeStruct(shape, bf16) for _ in range(devices - 1)),
        in_specs=smem(1) + [pl.BlockSpec(memory_space=pltpu.HBM)],
        out_specs=tuple(pl.BlockSpec(memory_space=pltpu.VMEM) for _ in range(devices - 1)),
        scratch_shapes=[pltpu.SemaphoreType.DMA((devices - 1,))],
        cost_estimate=cost(0, 4 << 20),
        compiler_params=params(),
        name="pack_state",
    )(meta, cache)
    state_gots = [
        lax.ppermute(x, "dev", [(s, s ^ (k + 1)) for s in range(devices)])
        for k, x in enumerate(state_sends)
    ]

    conv_send = pl.pallas_call(
        functools.partial(pack_conv_kernel, devices, width),
        out_shape=jax.ShapeDtypeStruct((devices, CONV_ROWS, width // 2), bf16),
        in_specs=smem(1) + [pl.BlockSpec(memory_space=pltpu.VMEM)],
        out_specs=pl.BlockSpec(memory_space=pltpu.VMEM),
        cost_estimate=cost(0, 1 << 19),
        name="pack_conv",
    )(meta, convolution_cache)
    conv_got = lax.all_to_all(conv_send, "dev", split_axis=0, concat_axis=0, tiled=True)

    spread = spread_entry(zero, meta, cache, devices)
    limit = per_group // 2
    spread_others = spread_rest(meta, cache, devices, limit)

    row_decay, column_decay = pl.pallas_call(
        prep_kernel,
        grid=(per_group,),
        out_shape=(
            jax.ShapeDtypeStruct((heads, tokens), f32),
            jax.ShapeDtypeStruct((tokens, heads), f32),
        ),
        in_specs=[
            pl.BlockSpec((heads, T_REQ), lambda r: (0, r)),
            pl.BlockSpec((heads, 1), lambda r: (0, 0)),
        ],
        out_specs=(
            pl.BlockSpec((heads, T_REQ), lambda r: (0, r)),
            pl.BlockSpec((T_REQ, heads), lambda r: (r, 0)),
        ),
        cost_estimate=cost(0, 4 << 20),
        name="prep",
    )(head_step_size, head_decay_rate.reshape(heads, 1))

    def table_specs(table):
        return [
            pl.BlockSpec((1,) + table.shape[1:], lambda r, meta: (meta[AINDEX, r], 0, 0))
        ] + [
            pl.BlockSpec(
                (1,) + table.shape[1:],
                lambda r, meta, k=k: (jnp.where(meta[DIST, r] == k, meta[ARANK, r], 0), 0, 0),
            )
            for k in range(1, groups)
        ]

    partial_down = pl.pallas_call(
        functools.partial(shrink_kernel, groups),
        grid_spec=pltpu.PrefetchScalarGridSpec(
            num_scalar_prefetch=1,
            grid=(per_group,),
            in_specs=[pl.BlockSpec((T_REQ, hidden.shape[1]), lambda r, meta: (r, 0))]
            + table_specs(adapter_down_weight),
            out_specs=pl.BlockSpec((1, rank, T_REQ), lambda r, meta: (r, 0, 0)),
        ),
        out_shape=jax.ShapeDtypeStruct((per_group, rank, T_REQ), bf16),
        cost_estimate=cost(2 * tokens * hidden.shape[1] * rank, 6 << 20),
        compiler_params=params(),
        name="shrink",
    )(meta, hidden, adapter_down_weight, *down_got)

    meta_late, _ = lax.optimization_barrier((meta, partial_down))
    up_got = swap_adapters(meta_late, adapter_up_weight, groups, "pack_up")

    parts = lax.all_to_all(partial_down, "dev", split_axis=0, concat_axis=0, tiled=True)
    summed = pl.pallas_call(
        sum_kernel,
        out_shape=jax.ShapeDtypeStruct((devices, share, rank, T_REQ), bf16),
        cost_estimate=cost(0, 1 << 19),
        name="sum_parts",
    )(parts.reshape(devices, share, rank, T_REQ))
    shrunk = lax.all_to_all(summed, "dev", split_axis=0, concat_axis=0, tiled=True)
    shrunk = shrunk.reshape(per_group, rank, T_REQ)

    channel = jnp.concatenate(
        [
            convolution_weight,
            convolution_bias.reshape(1, width),
            jnp.repeat(head_skip_scale, size).reshape(1, width),
            jnp.zeros((8 - taps - 2, width), f32),
        ],
        axis=0,
    )
    partial, fresh = pl.pallas_call(
        functools.partial(mix_kernel, groups, taps),
        grid_spec=pltpu.PrefetchScalarGridSpec(
            num_scalar_prefetch=1,
            grid=(per_group,),
            in_specs=[
                pl.BlockSpec((T_REQ, width), lambda r, meta: (r, 0)),
                pl.BlockSpec((1, rank, T_REQ), lambda r, meta: (r, 0, 0)),
            ] + table_specs(adapter_up_weight) + [
                pl.BlockSpec(
                    (1, CONV_ROWS, width // 2), lambda r, meta: (meta[HOLDER, r], 0, 0)
                ),
                pl.BlockSpec((8, width), lambda r, meta: (0, 0)),
                pl.BlockSpec((heads, T_REQ), lambda r, meta: (0, r)),
                pl.BlockSpec((T_REQ, heads), lambda r, meta: (r, 0)),
                pl.BlockSpec((T_REQ, 2 * depth), lambda r, meta: (r, 0)),
            ],
            out_specs=(
                pl.BlockSpec((T_REQ, width), lambda r, meta: (r, 0)),
                pl.BlockSpec((1,) + shape, lambda r, meta: (r, 0, 0, 0)),
            ),
            scratch_shapes=[
                pltpu.VMEM((T_REQ + 8, width), f32),
                pltpu.VMEM((T_REQ, T_REQ), f32),
            ],
        ),
        out_shape=(
            jax.ShapeDtypeStruct((tokens, width), f32),
            jax.ShapeDtypeStruct((per_group,) + shape, f32),
        ),
        cost_estimate=cost(4 << 30, 24 << 20, 16 << 20),
        compiler_params=params(),
        name="mix",
    )(
        meta, base_in_projection, shrunk, adapter_up_weight, *up_got, conv_got, channel,
        row_decay, column_decay, rows_all,
    )

    outs = None
    half = devices // 2
    for begin, states in (
        (0, [cache] + state_gots[:half - 1]),
        (half, state_gots[half - 1:half + 1]),
        (half + 2, state_gots[half + 1:]),
    ):
        outs = finish(
            begin, states, cache, zero, meta, partial, fresh, rows_all, column_decay, outs
        )
    return finish_spread(
        spread, spread_others, limit, cache, zero, meta, partial, fresh, rows_all, column_decay,
        outs,
    )


def solution(mesh):
    placed = (
        P("group", "dev"),
        P("group", "dev"),
        P(("group", "dev"), None),
        P(("group", "dev"), None),
        P("dev", "group"),
        P("dev"),
        P("dev"),
        P(None, "dev"),
        P("dev"),
        P("group", None, "dev"),
        P("group", None, "dev"),
        P(),
        P(),
        P(("group", "dev"), None, None, None),
        P(("group", "dev"), None, None),
        P(),
        P(),
        P(),
    )
    return jax.shard_map(
        body,
        mesh=mesh,
        in_specs=placed,
        out_specs=(P("group", "dev"), P("group", "dev", None, None)),
        check_vma=False,
    )
```

time: 513 us -> 183 us (0.36)
  Pallas kernels: 320 us -> 82.1 us
  waiting for transfers between devices: 74.3 us -> 25.8 us
  blocking collectives: 45.6 us -> 0 us
  starting transfers between devices: 34.1 us -> 44.5 us
  local copies, waits for them, and re-layouts: 18.9 us -> 11.4 us
    pallas_call x9 -> x15, Pallas kernels: 313 us -> 74.8 us  [the longest x1 23.8 us: body(): pl.pallas_call(functools.partial(mix_kernel, groups, taps), grid_spec=plt...]
    all_to_all x2 -> x0, blocking collectives: 45.6 us -> none  [the longest x1 31.6 us: body(): lax.all_to_all(x, 'dev', split_axis=0, concat_axis=0, tiled=True)]
    all_to_all x5 -> x1, waiting for transfers between devices: 36.6 us -> 2.48 us  [body(): lax.all_to_all(partial_down, 'dev', split_axis=0, concat_axis=0, tiled=True)]
    all_gather x1, waiting for transfers between devices: 29.6 us -> 0.01 us  [body(): lax.all_gather(jnp.concatenate([state_input_matrix, state_output_matrix],...]
    ppermute x0 -> x20, starting transfers between devices: none -> 28.1 us  [the longest x7 9.34 us: body(): lax.ppermute(x, 'dev', [(s, s ^ k + 1) for s in range(devices)])]
    ppermute x0 -> x20, waiting for transfers between devices: none -> 23.3 us  [the longest x6 23.3 us: swap_adapters(): lax.ppermute(packed[k - 1], 'group', [(g, g ^ k) for g in range(groups)])]
    all_to_all x5 -> x1, starting transfers between devices: 21.9 us -> 5.31 us  [body(): lax.all_to_all(partial_down, 'dev', split_axis=0, concat_axis=0, tiled=True)]
    all_to_all x1, waiting for transfers between devices: 7.42 us -> 0.01 us  [body(): lax.all_to_all(summed, 'dev', split_axis=0, concat_axis=0, tiled=True)]
  transfers between devices with their start and end apart: 8 -> 24, of which waited for: 4 -> 3; matrix products, arithmetic and copies ran while one was open for 0% -> 3% of each run, Pallas kernels for 59% -> 40%
where the time goes in v2:
time: 183 us; the launch traced here: 180 us
  Pallas kernels  82.1 us (45%)
  starting transfers between devices  44.5 us (24%)
  waiting for transfers between devices  25.8 us (14%)
  between operations  14.3 us (8%)
  local copies, waits for them, and re-layouts  11.4 us (6%)
    pallas_call x1, Pallas kernels, body(): pl.pallas_call(functools.partial(mix_kernel, groups, taps), grid_spec=plt...  23.8 us
    ppermute x6, waiting for transfers between devices, swap_adapters(): lax.ppermute(packed[k - 1], 'group', [(g, g ^ k) for g in range(groups)])  23.3 us
    pallas_call x4, Pallas kernels, finish_call(): pl.pallas_call(kernel, grid_spec=pltpu.PrefetchScalarGridSpec(num_scalar_...  20.9 us
    ppermute x7, starting transfers between devices, body(): lax.ppermute(x, 'dev', [(s, s ^ k + 1) for s in range(devices)])  9.34 us
    unnamed x41, local copies, waits for them, and re-layouts  8.8 us
    ppermute x3, starting transfers between devices, spread_entry(): lax.ppermute(to_right, 'dev', [(2 * i + x, 2 * i + 2 + x) for i in range(...  8.02 us
    pallas_call x1, Pallas kernels, body(): pl.pallas_call(functools.partial(shrink_kernel, groups), grid_spec=pltpu....  7.39 us
    pallas_call x2, Pallas kernels, swap_adapters(): pl.pallas_call(functools.partial(pack_adapter_kernel, groups), out_shape=...  6.88 us
  transfers between devices with their start and end apart: 24, of which 3 were waited for; matrix products, arithmetic and copies ran while one was open for 3% of the time, Pallas kernels for 40%

profile of v2, /device:TPU:8, one launch (start us, length us, event | category | flops | bytes accessed | tf_op | source)
XLA Modules:
  0.0 180.1 jit_solution(7724337605702425381)
XLA Ops:
  7.2 1.9 %plan.1.meta = s32[16,64]{1,0:T(8,128)S(1)} custom-call(s32[32]{0:T(128)} %bitcast.28, s32[32]{0:T(128)} %index.1, s32[32]{0:T(128)} %bitcast.29, s32[32]{0:T(128)} %slot.1, s32[32]{0:T(128)} %blocks.1), custom_call_target="tpu_custom_call" | custom-call | bytes 65536 | tf_op jit(solution)/shard_map/plan/pallas_call | solution.py:633
  9.2 2.8 %pack_across.8 = bf16[4,16,64,128]{3,2,1,0:T(8,128)(2,1)S(1)} custom-call(s32[1]{0:T(128)} %constant.33.clone.1.j, s32[16,64]{1,0:T(8,128)S(1)} %plan.1.meta, bf16[4,4,2,16,64,128]{5,4,3,2,1,0:T(8,128)(2,1)} %bitcast.15), custom_call_target="tpu_custom_call" | custom-call | bytes 2097152 | tf_op jit(solution)/shard_map/pack_across/pallas_call | solution.py:228
  12.0 1.6 collective-permute-start.13
  14.2 2.9 %pack_down.1 = (bf16[4,64,1024]{2,1,0:T(8,128)(2,1)S(1)}, bf16[4,64,1024]{2,1,0:T(8,128)(2,1)S(1)}, bf16[4,64,1024]{2,1,0:T(8,128)(2,1)S(1)}) custom-call(s32[16,64]{1,0:T(8,128)S(1)} %plan.1.meta, bf16[8,64,1024]{2,1,0:T(8,128)(2,1)S(1)} %copy-done.4), custom_call_target="tpu_custom_call" | custom-call | bytes 3145728 | tf_op jit(solution)/shard_map/pack_down/pallas_call | solution.py:139
  17.2 1.6 collective-permute-start.8
  19.1 12.9 %collective-permute-done.8.rest_2_ = bf16[4,64,1024]{2,1,0:T(8,128)(2,1)S(1)} collective-permute-done((bf16[4,64,1024]{2,1,0:T(8,128)(2,1)S(1)}, bf16[4,64,1024]{2,1,0:T(8,128)(2,1)S(1)}, u32[]{:S(2)}, u32[]{:S(2)}) %collective-permute-start.8) | collective-permute-done | bytes 524320 | tf_op jit(solution)/shard_map/ppermute | solution.py:152
  32.0 10.3 %collective-permute-done.9.rest_3_ = bf16[4,64,1024]{2,1,0:T(8,128)(2,1)S(1)} collective-permute-done((bf16[4,64,1024]{2,1,0:T(8,128)(2,1)S(1)}, bf16[4,64,1024]{2,1,0:T(8,128)(2,1)S(1)}, u32[]{:S(2)}, u32[]{:S(2)}) %collective-permute-start.9) | collective-permute-done | bytes 524320 | tf_op jit(solution)/shard_map/ppermute | solution.py:152
  42.3 7.4 %shrink.1 = bf16[8,64,256]{2,1,0:T(8,128)(2,1)} custom-call(s32[16,64]{1,0:T(8,128)S(1)} %plan.1.meta, bf16[2048,1024]{1,0:T(8,128)(2,1)} %hidden.1, bf16[8,64,1024]{2,1,0:T(8,128)(2,1)S(1)} %copy-done.4, bf16[4,64,1024]{2,1,0:T(8,128)(2,1)S(1)} %collective-permute-done.7.rest_1_, bf16[4,64,1024]{2,1,0:T(8,128)(2,1)S(1)} %collective-permute-done.8.rest_2_, ...), custom_call_target="tpu_custom_call" | custom-call | flops 268435456 | bytes 6291456 | tf_op jit(solution)/shard_map/shrink/pallas_call | solution.py:708
  49.7 5.3 %all-to-all-start = ((bf16[8,64,256]{2,1,0:T(8,128)(2,1)}), bf16[8,64,256]{2,1,0:T(8,128)(2,1)S(1)}, u32[]{:S(2)}, u32[]{:S(2)}) async-start(bf16[8,64,256]{2,1,0:T(8,128)(2,1)} %shrink.1), calls=%async_computation | async-start | bytes 524288 | tf_op jit(solution)/shard_map/all_to_all | solution.py:726
  55.0 1.7 pick_1.8
  56.8 1.3 collective-permute-start.14
  58.1 0.7 collective-permute-start.15
  58.8 0.9 copy.29.conv
  59.6 1.7 pack_conv.1
  61.4 2.5 %all-to-all-done = bf16[8,64,256]{2,1,0:T(8,128)(2,1)S(1)} async-done(((bf16[8,64,256]{2,1,0:T(8,128)(2,1)}), bf16[8,64,256]{2,1,0:T(8,128)(2,1)S(1)}, u32[]{:S(2)}, u32[]{:S(2)}) %all-to-all-start) | async-done | bytes 262176 | tf_op jit(solution)/shard_map/all_to_all | solution.py:726
  63.8 4.7 %all-to-all-start.2 = ((bf16[8,16,512]{2,1,0:T(8,128)(2,1)}), bf16[8,16,512]{2,1,0:T(8,128)(2,1)S(1)}, u32[]{:S(2)}, u32[]{:S(2)}) async-start(bf16[8,16,512]{2,1,0:T(8,128)(2,1)} %pack_conv.1), calls=%async_computation.2 | async-start | bytes 262144 | tf_op jit(solution)/shard_map/all_to_all | solution.py:672
  68.6 1.7 pick_2.8
  70.4 3.4 %collective-permute-start.16 = (bf16[16,64,128]{2,1,0:T(8,128)(2,1)S(1)}, bf16[16,64,128]{2,1,0:T(8,128)(2,1)S(1)}, u32[]{:S(2)}, u32[]{:S(2)}) collective-permute-start(bf16[16,64,128]{2,1,0:T(8,128)(2,1)S(1)} %get-tuple-element.157), channel_id=1, source_target_pairs={{0,2},{1,3},{2,4},{3,5},{8,10},{9,11},{10,12},{11,13},{16,18},{17,... | collective-permute-start | bytes 786440 | tf_op jit(solution)/shard_map/ppermute | solution.py:282
  73.7 1.3 collective-permute-start.17
  75.1 4.0 %pack_up.1 = (bf16[4,64,1024]{2,1,0:T(8,128)(2,1)}, bf16[4,64,1024]{2,1,0:T(8,128)(2,1)}, bf16[4,64,1024]{2,1,0:T(8,128)(2,1)}) custom-call(s32[16,64]{1,0:T(8,128)S(1)} %plan.1.meta, bf16[8,64,1024]{2,1,0:T(8,128)(2,1)S(1)} %copy-done.5), custom_call_target="tpu_custom_call" | custom-call | bytes 3145728 | tf_op jit(solution)/shard_map/pack_up/pallas_call | solution.py:139
  79.2 1.6 collective-permute-start.11
  81.0 1.7 sum_parts.1
  82.7 6.3 %all-to-all-start.1 = ((bf16[8,1,64,256]{3,2,1,0:T(8,128)(2,1)}), bf16[8,1,64,256]{3,2,1,0:T(8,128)(2,1)}, u32[]{:S(2)}, u32[]{:S(2)}) async-start(bf16[8,1,64,256]{3,2,1,0:T(8,128)(2,1)} %sum_parts.1), calls=%async_computation.1 | async-start | bytes 524288 | tf_op jit(solution)/shard_map/all_to_all | solution.py:733
  89.0 3.5 %pack_state.1 = (bf16[16,64,128]{2,1,0:T(8,128)(2,1)}, bf16[16,64,128]{2,1,0:T(8,128)(2,1)}, bf16[16,64,128]{2,1,0:T(8,128)(2,1)}, bf16[16,64,128]{2,1,0:T(8,128...) custom-call(s32[16,64]{1,0:T(8,128)S(1)} %plan.1.meta, ...), custom_call_target="tpu_custom_call" | custom-call | bytes 4194304 | tf_op jit(solution)/shard_map/pack_state/pallas_call | solution.py:649
  92.5 0.7 copy-done.6
  93.2 1.5 collective-permute-start.24
  94.6 0.7 copy-done.8
  97.3 5.6 %prep.1 = (f32[16,2048]{1,0:T(8,128)}, f32[2048,16]{1,0:T(8,128)}) custom-call(f32[16,2048]{1,0:T(8,128)} %steps.1, f32[16,1]{1,0:T(8,128)} %copy.30.rates), custom_call_target="tpu_custom_call" | custom-call | bytes 4194304 | tf_op jit(solution)/shard_map/prep/pallas_call | solution.py:678
  103.7 0.9 copy-done.7
  104.6 0.9 copy-done.9
  105.6 2.5 %pick_3.8 = (bf16[16,64,128]{2,1,0:T(8,128)(2,1)}, bf16[16,64,128]{2,1,0:T(8,128)(2,1)}) custom-call(s32[1]{0:T(128)} %constant.33.clone.1.j, s32[16,64]{1,0:T(8,128)S(1)} %plan.1.meta, bf16[4,4,2,16,64,128]{5,4,3,2,1,0:T(8,128)(2,1)} %bitcast.21, bf16[4,16,64,128]{3,2,1,0:T(8,128)(2,1)S(1)} %collective-permute-done.13.over_r.over_l.rest_1_, ...), custom_call_target="tpu_custom_call" | custom-call | bytes 2097152 | tf_op jit(solution)/shard_map/pick_3/pallas_call | solution.py:272
  108.1 1.5 collective-permute-start.26
  109.6 2.4 %collective-permute-start.22 = (bf16[16,64,128]{2,1,0:T(8,128)(2,1)}, bf16[16,64,128]{2,1,0:T(8,128)(2,1)}, u32[]{:S(2)}, u32[]{:S(2)}) collective-permute-start(bf16[16,64,128]{2,1,0:T(8,128)(2,1)} %get-tuple-element.164), channel_id=1, source_target_pairs={{0,4},{1,5},{2,6},{3,7},{4,0},{5,1},{6,2},{7,3},{8,12},{9,13},{10,... | collective-permute-start | bytes 786440 | tf_op jit(solution)/shard_map/ppermute | solution.py:660
  111.9 1.5 collective-permute-start.23
  113.4 1.5 collective-permute-start.20
  115.4 1.2 copy-done
  116.7 0.8 copy-done.10
  117.4 0.9 copy-done.11
  118.3 23.8 %mix.1 = (f32[2048,1024]{1,0:T(8,128)}, f32[8,16,64,128]{3,2,1,0:T(8,128)}) custom-call(s32[16,64]{1,0:T(8,128)S(1)} %plan.1.meta, bf16[2048,1024]{1,0:T(8,128)(2,1)} %base.1, bf16[8,64,256]{2,1,0:T(8,128)(2,1)} %bitcast.5.shrunk, bf16[8,64,1024]{2,1,0:T(8,128)(2,1)S(1)} %copy-done.5, bf16[4,64,1024]{2,1,0:T(8,128)(2,1)} %collective-permute-done.10.rest_1_, ...), custom_call_target="tpu_custom_call" | custom-call | flops 4294967296 | bytes 25165824 | tf_op jit(solution)/shard_map/mix/pallas_call | solution.py:745
  142.1 7.2 %finish_0.1 = (bf16[2048,1024]{1,0:T(8,128)(2,1)}, bf16[8,16,64,128]{3,2,1,0:T(8,128)(2,1)}) custom-call(s32[1]{0:T(128)} %constant.33.clone.1.j, s32[16,64]{1,0:T(8,128)S(1)} %plan.1.meta, f32[2048,1024]{1,0:T(8,128)} %get-tuple-element.153.partial, f32[8,16,64,128]{3,2,1,0:T(8,128)} %get-tuple-element.154.fresh, bf16[2048,256]{1,0:T(8,128)(2,1)S(1)} %copy-done, ...), custom_call_target="tpu_custom_call" | custom-call | flops 268435456 | bytes 12582912 | tf_op jit(solution)/shard_map/finish_0/pallas_call | solution.py:542
  149.3 3.4 %collective-permute-start.18 = (bf16[16,64,128]{2,1,0:T(8,128)(2,1)}, bf16[16,64,128]{2,1,0:T(8,128)(2,1)}, u32[]{:S(2)}, u32[]{:S(2)}) collective-permute-start(bf16[16,64,128]{2,1,0:T(8,128)(2,1)} %get-tuple-element.159), channel_id=1, source_target_pairs={{0,2},{1,3},{2,4},{3,5},{4,6},{5,7},{8,10},{9,11},{10,12},{11,13},... | collective-permute-start | bytes 786440 | tf_op jit(solution)/shard_map/ppermute | solution.py:282
  152.6 3.3 %collective-permute-start.19 = (bf16[16,64,128]{2,1,0:T(8,128)(2,1)}, bf16[16,64,128]{2,1,0:T(8,128)(2,1)}, u32[]{:S(2)}, u32[]{:S(2)}) collective-permute-start(bf16[16,64,128]{2,1,0:T(8,128)(2,1)} %get-tuple-element.160), channel_id=1, source_target_pairs={{7,5},{6,4},{5,3},{4,2},{3,1},{2,0},{15,13},{14,12},{13,11},{12,10... | collective-permute-start | bytes 786440 | tf_op jit(solution)/shard_map/ppermute | solution.py:286
  156.0 4.6 %finish_4.1 = (bf16[2048,1024]{1,0:T(8,128)(2,1)}, bf16[8,16,64,128]{3,2,1,0:T(8,128)(2,1)}) custom-call(s32[1]{0:T(128)} %constant.33.clone.1.j, s32[16,64]{1,0:T(8,128)S(1)} %plan.1.meta, f32[2048,1024]{1,0:T(8,128)} %get-tuple-element.153.partial, f32[8,16,64,128]{3,2,1,0:T(8,128)} %get-tuple-element.154.fresh, ...), custom_call_target="tpu_custom_call", output_to_operand_aliasing={{0}: (8, {}), {1}: (9, {})} | custom-call | flops 134217728 | bytes 6291456 | tf_op jit(solution)/shard_map/finish_4/pallas_call | solution.py:542
  160.6 4.6 %finish_6.1 = (bf16[2048,1024]{1,0:T(8,128)(2,1)}, bf16[8,16,64,128]{3,2,1,0:T(8,128)(2,1)}) custom-call(s32[1]{0:T(128)} %constant.33.clone.1.j, s32[16,64]{1,0:T(8,128)S(1)} %plan.1.meta, f32[2048,1024]{1,0:T(8,128)} %get-tuple-element.153.partial, f32[8,16,64,128]{3,2,1,0:T(8,128)} %get-tuple-element.154.fresh, ...), custom_call_target="tpu_custom_call", output_to_operand_aliasing={{0}: (8, {}), {1}: (9, {})} | custom-call | flops 134217728 | bytes 6291456 | tf_op jit(solution)/shard_map/finish_6/pallas_call | solution.py:542
  165.2 1.1 broadcast_in_dim.20
  166.3 0.7 while.14
  167.5 1.2 copy-done.3
  168.7 4.5 %finish_spread.1 = (bf16[2048,1024]{1,0:T(8,128)(2,1)}, bf16[8,16,64,128]{3,2,1,0:T(8,128)(2,1)}) custom-call(s32[1]{0:T(128)} %constant.33.clone.1.j, s32[16,64]{1,0:T(8,128)S(1)} %get-tuple-element.288, f32[2048,1024]{1,0:T(8,128)} %get-tuple-element.153.partial, ...), custom_call_target="tpu_custom_call", output_to_operand_aliasing={{0}: (11, {}), {1}: (12, {})} | custom-call | flops 268435456 | bytes 12582912 | tf_op jit(solution)/shard_map/finish_spread/pallas_call | solution.py:542
  (69 shorter events, 5.3 us)
Async XLA Ops:
  7.2 108.3 %all-gather.2.cloned.1.call-start = ((), (), s32[]{:S(2)}) async-start(), calls=%async_computation.3 | async-start | bytes 1179648 | tf_op jit(solution)/shard_map/all_gather | solution.py:629
  9.2 4.4 %copy-start.15 = (bf16[256,128]{1,0:T(8,128)(2,1)S(1)}, bf16[256,128]{1,0:T(8,128)(2,1)}, u32[]{:S(2)}) copy-start(bf16[256,128]{1,0:T(8,128)(2,1)} %param.23) | copy-start | bytes 196612
  9.2 4.4 %copy-start.16 = (bf16[256,128]{1,0:T(8,128)(2,1)S(1)}, bf16[256,128]{1,0:T(8,128)(2,1)}, u32[]{:S(2)}) copy-start(bf16[256,128]{1,0:T(8,128)(2,1)} %param.22) | copy-start | bytes 196612
  9.2 5.0 %copy-start.4 = (bf16[8,64,1024]{2,1,0:T(8,128)(2,1)S(1)}, bf16[8,64,1024]{2,1,0:T(8,128)(2,1)}, u32[]{:S(2)}) copy-start(bf16[8,64,1024]{2,1,0:T(8,128)(2,1)} %rest_0_.2) | copy-start | bytes 3145732
  12.0 43.0 %collective-permute-start.13 = (bf16[4,16,64,128]{3,2,1,0:T(8,128)(2,1)S(1)}, bf16[4,16,64,128]{3,2,1,0:T(8,128)(2,1)S(1)}, u32[]{:S(2)}, u32[]{:S(2)}) collective-permute-start(bf16[4,16,64,128]{3,2,1,0:T(8,128)(2,1)S(1)} %pack_across.8), channel_id=1, source_target_pairs={{0,1},{1,0},{2,3},{3,2},{4,5},{5,4},{6,7},{7,6},{8,9},{9,8},{10,11... | collective-permute-start | bytes 3145736 | tf_op jit(solution)/shard_map/ppermute | solution.py:248
  17.1 2.0 %collective-permute-start.7 = (bf16[4,64,1024]{2,1,0:T(8,128)(2,1)S(1)}, bf16[4,64,1024]{2,1,0:T(8,128)(2,1)S(1)}, u32[]{:S(2)}, u32[]{:S(2)}) collective-permute-start(bf16[4,64,1024]{2,1,0:T(8,128)(2,1)S(1)} %get-tuple-element.144), channel_id=1, source_target_pairs={{0,8},{8,0},{16,24},{24,16},{1,9},{9,1},{17,25},{25,17},{2,10},{10... | collective-permute-start | bytes 1572872 | tf_op jit(solution)/shard_map/ppermute | solution.py:152
  17.2 14.8 %collective-permute-start.8 = (bf16[4,64,1024]{2,1,0:T(8,128)(2,1)S(1)}, bf16[4,64,1024]{2,1,0:T(8,128)(2,1)S(1)}, u32[]{:S(2)}, u32[]{:S(2)}) collective-permute-start(bf16[4,64,1024]{2,1,0:T(8,128)(2,1)S(1)} %get-tuple-element.145), channel_id=1, source_target_pairs={{0,16},{8,24},{16,0},{24,8},{1,17},{9,25},{17,1},{25,9},{2,18},{10... | collective-permute-start | bytes 1572872 | tf_op jit(solution)/shard_map/ppermute | solution.py:152
  18.8 23.5 %collective-permute-start.9 = (bf16[4,64,1024]{2,1,0:T(8,128)(2,1)S(1)}, bf16[4,64,1024]{2,1,0:T(8,128)(2,1)S(1)}, u32[]{:S(2)}, u32[]{:S(2)}) collective-permute-start(bf16[4,64,1024]{2,1,0:T(8,128)(2,1)S(1)} %get-tuple-element.146), channel_id=1, source_target_pairs={{0,24},{8,16},{16,8},{24,0},{1,25},{9,17},{17,9},{25,1},{2,26},{10... | collective-permute-start | bytes 1572872 | tf_op jit(solution)/shard_map/ppermute | solution.py:152
  49.7 14.1 %all-to-all-start = ((bf16[8,64,256]{2,1,0:T(8,128)(2,1)}), bf16[8,64,256]{2,1,0:T(8,128)(2,1)S(1)}, u32[]{:S(2)}, u32[]{:S(2)}) async-start(bf16[8,64,256]{2,1,0:T(8,128)(2,1)} %shrink.1), calls=%async_computation | async-start | bytes 524288 | tf_op jit(solution)/shard_map/all_to_all | solution.py:726
  55.0 3.8 %copy-start.14 = (bf16[4,3,8192]{2,0,1:T(4,128)(2,1)S(1)}, bf16[4,3,8192]{2,0,1:T(4,128)(2,1)}, u32[]{:S(2)}) copy-start(bf16[4,3,8192]{2,0,1:T(4,128)(2,1)} %param.34) | copy-start | bytes 589828
  56.8 11.8 %collective-permute-start.14 = (bf16[16,64,128]{2,1,0:T(8,128)(2,1)S(1)}, bf16[16,64,128]{2,1,0:T(8,128)(2,1)S(1)}, u32[]{:S(2)}, u32[]{:S(2)}) collective-permute-start(bf16[16,64,128]{2,1,0:T(8,128)(2,1)S(1)} %get-tuple-element.155), channel_id=1, source_target_pairs={{0,2},{1,3},{8,10},{9,11},{16,18},{17,19},{24,26},{25,27}} | collective-permute-start | bytes 786440 | tf_op jit(solution)/shard_map/ppermute | solution.py:282
  58.1 10.5 %collective-permute-start.15 = (bf16[16,64,128]{2,1,0:T(8,128)(2,1)S(1)}, bf16[16,64,128]{2,1,0:T(8,128)(2,1)S(1)}, u32[]{:S(2)}, u32[]{:S(2)}) collective-permute-start(bf16[16,64,128]{2,1,0:T(8,128)(2,1)S(1)} %get-tuple-element.156), channel_id=1, source_target_pairs={{7,5},{6,4},{15,13},{14,12},{23,21},{22,20},{31,29},{30,28}} | collective-permute-start | bytes 786440 | tf_op jit(solution)/shard_map/ppermute | solution.py:286
  63.8 6.5 %copy-start.13 = (bf16[8,64,256]{2,1,0:T(8,128)(2,1)}, bf16[8,64,256]{2,1,0:T(8,128)(2,1)S(1)}, u32[]{:S(2)}) copy-start(bf16[8,64,256]{2,1,0:T(8,128)(2,1)S(1)} %all-to-all-done) | copy-start | bytes 786436
  63.8 18.9 %all-to-all-start.2 = ((bf16[8,16,512]{2,1,0:T(8,128)(2,1)}), bf16[8,16,512]{2,1,0:T(8,128)(2,1)S(1)}, u32[]{:S(2)}, u32[]{:S(2)}) async-start(bf16[8,16,512]{2,1,0:T(8,128)(2,1)} %pack_conv.1), calls=%async_computation.2 | async-start | bytes 262144 | tf_op jit(solution)/shard_map/all_to_all | solution.py:672
  68.6 6.5 %copy-start.5 = (bf16[8,64,1024]{2,1,0:T(8,128)(2,1)S(1)}, bf16[8,64,1024]{2,1,0:T(8,128)(2,1)}, u32[]{:S(2)}) copy-start(bf16[8,64,1024]{2,1,0:T(8,128)(2,1)} %rest_0_.3) | copy-start | bytes 3145732
  70.4 22.1 %collective-permute-start.16 = (bf16[16,64,128]{2,1,0:T(8,128)(2,1)S(1)}, bf16[16,64,128]{2,1,0:T(8,128)(2,1)S(1)}, u32[]{:S(2)}, u32[]{:S(2)}) collective-permute-start(bf16[16,64,128]{2,1,0:T(8,128)(2,1)S(1)} %get-tuple-element.157), channel_id=1, source_target_pairs={{0,2},{1,3},{2,4},{3,5},{8,10},{9,11},{10,12},{11,13},{16,18},{17,... | collective-permute-start | bytes 786440 | tf_op jit(solution)/shard_map/ppermute | solution.py:282
  73.7 20.9 %collective-permute-start.17 = (bf16[16,64,128]{2,1,0:T(8,128)(2,1)S(1)}, bf16[16,64,128]{2,1,0:T(8,128)(2,1)S(1)}, u32[]{:S(2)}, u32[]{:S(2)}) collective-permute-start(bf16[16,64,128]{2,1,0:T(8,128)(2,1)S(1)} %get-tuple-element.158), channel_id=1, source_target_pairs={{7,5},{6,4},{5,3},{4,2},{15,13},{14,12},{13,11},{12,10},{23,21},{2... | collective-permute-start | bytes 786440 | tf_op jit(solution)/shard_map/ppermute | solution.py:286
  79.1 32.8 %collective-permute-start.10 = (bf16[4,64,1024]{2,1,0:T(8,128)(2,1)}, bf16[4,64,1024]{2,1,0:T(8,128)(2,1)}, u32[]{:S(2)}, u32[]{:S(2)}) collective-permute-start(bf16[4,64,1024]{2,1,0:T(8,128)(2,1)} %get-tuple-element.148), channel_id=1, source_target_pairs={{0,8},{8,0},{16,24},{24,16},{1,9},{9,1},{17,25},{25,17},{2,10},{10... | collective-permute-start | bytes 1572872 | tf_op jit(solution)/shard_map/ppermute | solution.py:152
  79.2 34.2 %collective-permute-start.11 = (bf16[4,64,1024]{2,1,0:T(8,128)(2,1)}, bf16[4,64,1024]{2,1,0:T(8,128)(2,1)}, u32[]{:S(2)}, u32[]{:S(2)}) collective-permute-start(bf16[4,64,1024]{2,1,0:T(8,128)(2,1)} %get-tuple-element.149), channel_id=1, source_target_pairs={{0,16},{8,24},{16,0},{24,8},{1,17},{9,25},{17,1},{25,9},{2,18},{10... | collective-permute-start | bytes 1572872 | tf_op jit(solution)/shard_map/ppermute | solution.py:152
  80.7 34.1 %collective-permute-start.12 = (bf16[4,64,1024]{2,1,0:T(8,128)(2,1)}, bf16[4,64,1024]{2,1,0:T(8,128)(2,1)}, u32[]{:S(2)}, u32[]{:S(2)}) collective-permute-start(bf16[4,64,1024]{2,1,0:T(8,128)(2,1)} %get-tuple-element.150), channel_id=1, source_target_pairs={{0,24},{8,16},{16,8},{24,0},{1,25},{9,17},{17,9},{25,1},{2,26},{10... | collective-permute-start | bytes 1572872 | tf_op jit(solution)/shard_map/ppermute | solution.py:152
  82.7 32.7 %all-to-all-start.1 = ((bf16[8,1,64,256]{3,2,1,0:T(8,128)(2,1)}), bf16[8,1,64,256]{3,2,1,0:T(8,128)(2,1)}, u32[]{:S(2)}, u32[]{:S(2)}) async-start(bf16[8,1,64,256]{3,2,1,0:T(8,128)(2,1)} %sum_parts.1), calls=%async_computation.1 | async-start | bytes 524288 | tf_op jit(solution)/shard_map/all_to_all | solution.py:733
  89.0 7.5 %copy-start.19 = (f32[16]{0:T(128)S(1)}, f32[16]{0:T(128)}, u32[]{:S(2)}) copy-start(f32[16]{0:T(128)} %param.25) | copy-start | bytes 196
  89.0 8.2 %copy-start.20 = (f32[16]{0:T(128)S(1)}, f32[16]{0:T(128)}, u32[]{:S(2)}) copy-start(f32[16]{0:T(128)} %param.26) | copy-start | bytes 196
  89.0 14.0 %copy-start.17 = (f32[4,1024]{1,0:T(4,128)S(1)}, f32[4,1024]{1,0:T(4,128)}, u32[]{:S(2)}) copy-start(f32[4,1024]{1,0:T(4,128)} %param.27) | copy-start | bytes 49156
  89.0 14.0 %copy-start.18 = (f32[1024]{0:T(1024)S(1)}, f32[1024]{0:T(1024)}, u32[]{:S(2)}) copy-start(f32[1024]{0:T(1024)} %param.28) | copy-start | bytes 12292
  92.5 0.7 copy-start.6
  93.2 14.9 %collective-permute-start.24 = (bf16[16,64,128]{2,1,0:T(8,128)(2,1)}, bf16[16,64,128]{2,1,0:T(8,128)(2,1)S(1)}, u32[]{:S(2)}, u32[]{:S(2)}) collective-permute-start(bf16[16,64,128]{2,1,0:T(8,128)(2,1)} %get-tuple-element.166), channel_id=1, source_target_pairs={{0,1},{1,0},{2,3},{3,2},{4,5},{5,4},{6,7},{7,6},{8,9},{9,8},{10,11... | collective-permute-start | bytes 786440 | tf_op jit(solution)/shard_map/ppermute | solution.py:660
  94.6 0.7 copy-start.8
  95.3 14.2 %collective-permute-start.25 = (bf16[16,64,128]{2,1,0:T(8,128)(2,1)}, bf16[16,64,128]{2,1,0:T(8,128)(2,1)}, u32[]{:S(2)}, u32[]{:S(2)}) collective-permute-start(bf16[16,64,128]{2,1,0:T(8,128)(2,1)} %get-tuple-element.167), channel_id=1, source_target_pairs={{0,2},{1,3},{2,0},{3,1},{4,6},{5,7},{6,4},{7,5},{8,10},{9,11},{10,... | collective-permute-start | bytes 786440 | tf_op jit(solution)/shard_map/ppermute | solution.py:660
  103.7 0.9 copy-start.7
  104.6 0.9 copy-start.9
  105.6 9.9 %copy-start.2 = (f32[2048,16]{1,0:T(8,128)S(1)}, f32[2048,16]{1,0:T(8,128)}, u32[]{:S(2)}) copy-start(f32[2048,16]{1,0:T(8,128)} %get-tuple-element.152.rest_7_.column) | copy-start | bytes 393220
  108.1 34.0 %collective-permute-start.26 = (bf16[16,64,128]{2,1,0:T(8,128)(2,1)}, bf16[16,64,128]{2,1,0:T(8,128)(2,1)}, u32[]{:S(2)}, u32[]{:S(2)}) collective-permute-start(bf16[16,64,128]{2,1,0:T(8,128)(2,1)} %get-tuple-element.168), channel_id=1, source_target_pairs={{0,3},{1,2},{2,1},{3,0},{4,7},{5,6},{6,5},{7,4},{8,11},{9,10},{10,... | collective-permute-start | bytes 786440 | tf_op jit(solution)/shard_map/ppermute | solution.py:660
  109.6 43.1 %collective-permute-start.22 = (bf16[16,64,128]{2,1,0:T(8,128)(2,1)}, bf16[16,64,128]{2,1,0:T(8,128)(2,1)}, u32[]{:S(2)}, u32[]{:S(2)}) collective-permute-start(bf16[16,64,128]{2,1,0:T(8,128)(2,1)} %get-tuple-element.164), channel_id=1, source_target_pairs={{0,4},{1,5},{2,6},{3,7},{4,0},{5,1},{6,2},{7,3},{8,12},{9,13},{10,... | collective-permute-start | bytes 786440 | tf_op jit(solution)/shard_map/ppermute | solution.py:660
  111.9 44.1 %collective-permute-start.23 = (bf16[16,64,128]{2,1,0:T(8,128)(2,1)}, bf16[16,64,128]{2,1,0:T(8,128)(2,1)}, u32[]{:S(2)}, u32[]{:S(2)}) collective-permute-start(bf16[16,64,128]{2,1,0:T(8,128)(2,1)} %get-tuple-element.165), channel_id=1, source_target_pairs={{0,5},{1,4},{2,7},{3,6},{4,1},{5,0},{6,3},{7,2},{8,13},{9,12},{10,... | collective-permute-start | bytes 786440 | tf_op jit(solution)/shard_map/ppermute | solution.py:660
  113.4 47.2 %collective-permute-start.20 = (bf16[16,64,128]{2,1,0:T(8,128)(2,1)}, bf16[16,64,128]{2,1,0:T(8,128)(2,1)}, u32[]{:S(2)}, u32[]{:S(2)}) collective-permute-start(bf16[16,64,128]{2,1,0:T(8,128)(2,1)} %get-tuple-element.162), channel_id=1, source_target_pairs={{0,6},{1,7},{2,4},{3,5},{4,2},{5,3},{6,0},{7,1},{8,14},{9,15},{10,... | collective-permute-start | bytes 786440 | tf_op jit(solution)/shard_map/ppermute | solution.py:660
  114.9 45.7 %collective-permute-start.21 = (bf16[16,64,128]{2,1,0:T(8,128)(2,1)}, bf16[16,64,128]{2,1,0:T(8,128)(2,1)}, u32[]{:S(2)}, u32[]{:S(2)}) collective-permute-start(bf16[16,64,128]{2,1,0:T(8,128)(2,1)} %get-tuple-element.163), channel_id=1, source_target_pairs={{0,7},{1,6},{2,5},{3,4},{4,3},{5,2},{6,1},{7,0},{8,15},{9,14},{10,... | collective-permute-start | bytes 786440 | tf_op jit(solution)/shard_map/ppermute | solution.py:660
  115.4 1.2 copy-start
  116.7 0.8 copy-start.10
  117.4 0.9 copy-start.11
  149.3 17.7 %collective-permute-start.18 = (bf16[16,64,128]{2,1,0:T(8,128)(2,1)}, bf16[16,64,128]{2,1,0:T(8,128)(2,1)}, u32[]{:S(2)}, u32[]{:S(2)}) collective-permute-start(bf16[16,64,128]{2,1,0:T(8,128)(2,1)} %get-tuple-element.159), channel_id=1, source_target_pairs={{0,2},{1,3},{2,4},{3,5},{4,6},{5,7},{8,10},{9,11},{10,12},{11,13},... | collective-permute-start | bytes 786440 | tf_op jit(solution)/shard_map/ppermute | solution.py:282
  152.6 14.4 %collective-permute-start.19 = (bf16[16,64,128]{2,1,0:T(8,128)(2,1)}, bf16[16,64,128]{2,1,0:T(8,128)(2,1)}, u32[]{:S(2)}, u32[]{:S(2)}) collective-permute-start(bf16[16,64,128]{2,1,0:T(8,128)(2,1)} %get-tuple-element.160), channel_id=1, source_target_pairs={{7,5},{6,4},{5,3},{4,2},{3,1},{2,0},{15,13},{14,12},{13,11},{12,10... | collective-permute-start | bytes 786440 | tf_op jit(solution)/shard_map/ppermute | solution.py:286
  166.3 1.2 copy-start.1
  167.5 1.2 copy-start.3
Sparse Core Ops, SparseCore 0:
  14.3 40.6 all-gather.1

commit v3 on v0

v3 whole, which is shorter than its diff:
```python
import functools
import math

import jax
import jax.numpy as jnp
from jax import lax
from jax.experimental import pallas as pl
from jax.experimental.pallas import tpu as pltpu
from jax.sharding import PartitionSpec as P

T_REQ = 256
CAP = 2
ACAP = 4
LOG2E = math.log2(math.e)
NT = (((1,), (1,)), ((), ()))
TN = (((0,), (0,)), ((), ()))
VMEM_LIMIT = 48 * 1024 * 1024

DIST, ARANK, AINDEX, PRESENT, POS_REQ, POS_VALID, OSLOT, OHOLDER, MISC, SEND = range(10)
MOST, ME, SLOT = range(3)
META_SHAPE = (16, 64)


def cost(flops, nbytes, transcendentals=0):
    return pl.CostEstimate(
        flops=int(flops), bytes_accessed=int(nbytes), transcendentals=int(transcendentals)
    )


def params():
    return pltpu.CompilerParams(vmem_limit_bytes=VMEM_LIMIT)


def smem(count):
    return [pl.BlockSpec(memory_space=pltpu.SMEM) for _ in range(count)]


def anywhere(count):
    return [pl.BlockSpec(memory_space=pl.ANY) for _ in range(count)]


def as_int(flag):
    return flag.astype(jnp.int32)


def ranks_of(labels):
    ranks = []
    for q, label in enumerate(labels):
        total = jnp.int32(0)
        for other in labels[:q]:
            total = total + as_int(other == label)
        ranks.append(total)
    return ranks


def plan_kernel(groups, devices, per_group, home, index, holder, slot, blocks, meta):
    my_group = lax.axis_index("group")
    me = lax.axis_index("dev")
    first = my_group * per_group
    limit = per_group // 2
    for j in range(limit):
        meta[POS_REQ, devices + j] = jnp.int32(-1)
        meta[POS_VALID, devices + j] = jnp.int32(0)
        meta[OSLOT, j] = jnp.int32(0)
        meta[OHOLDER, j] = jnp.int32(0)

    homes = [home[first + q] for q in range(per_group)]
    for q, rank in enumerate(ranks_of(homes)):
        own = homes[q] == my_group
        meta[DIST, q] = lax.bitwise_xor(homes[q], my_group)
        meta[ARANK, q] = jnp.where(own, 0, rank)
        meta[AINDEX, q] = jnp.where(own, index[first + q], 0)
        meta[PRESENT, q] = as_int(blocks[first + q] > 0)
    for k in range(1, groups):
        theirs = lax.bitwise_xor(my_group, k) * per_group
        seen = jnp.int32(0)
        chosen = [jnp.int32(0) for _ in range(ACAP)]
        for q in range(per_group):
            hit = home[theirs + q] == my_group
            value = index[theirs + q]
            for c in range(ACAP):
                chosen[c] = jnp.where(hit & (seen == c), value, chosen[c])
            seen = seen + as_int(hit)
        for c in range(ACAP):
            meta[SEND, (k - 1) * ACAP + c] = chosen[c]

    holders = [holder[first + q] for q in range(per_group)]
    ranks = ranks_of(holders)
    count = jnp.int32(0)
    my_slot = jnp.int32(0)
    for q in range(per_group):
        my_slot = jnp.where((holders[q] == me) & (ranks[q] == 0), slot[first + q], my_slot)

        @pl.when(ranks[q] > 0)
        def _():
            meta[POS_REQ, devices + count] = jnp.int32(q)
            meta[POS_VALID, devices + count] = jnp.int32(1)
            meta[OSLOT, count] = slot[first + q]
            meta[OHOLDER, count] = holders[q]

        count = count + as_int(ranks[q] > 0)
    spread = meta[POS_REQ, devices]
    requests = []
    for d in range(devices):
        source = lax.bitwise_xor(me, d)
        request = jnp.int32(-1)
        for q in range(per_group):
            request = jnp.where((holders[q] == source) & (ranks[q] == 0), q, request)
        meta[POS_VALID, d] = as_int(request >= 0)
        requests.append(request)
    requests += [meta[POS_REQ, devices + j] for j in range(limit)]
    for begin, end in ((0, devices // 2), (devices // 2, devices + limit)):
        last = jnp.int32(-1)
        filled = []
        for p in range(begin, end):
            last = jnp.where(requests[p] >= 0, requests[p], last)
            filled.append(last)
        following = jnp.maximum(spread, 0)
        for p in reversed(range(begin, end)):
            following = jnp.where(filled[p - begin] >= 0, filled[p - begin], following)
            meta[POS_REQ, p] = following
    most = jnp.int32(0)
    for g in range(groups):
        labels = [holder[g * per_group + q] for q in range(per_group)]
        total = jnp.int32(0)
        for rank in ranks_of(labels):
            total = total + as_int(rank > 0)
        most = jnp.maximum(most, total)
    meta[MISC, MOST] = most
    meta[MISC, ME] = me
    meta[MISC, SLOT] = my_slot


def pack_adapter_kernel(groups, meta, table, *rest):
    outs, sems = rest[-groups:-1], rest[-1]
    copies = []
    for k in range(1, groups):
        for c in range(ACAP):
            chosen = meta[SEND, (k - 1) * ACAP + c]
            copy = pltpu.make_async_copy(
                table.at[chosen], outs[k - 1].at[c], sems.at[(k - 1) * ACAP + c]
            )
            copy.start()
            copies.append(copy)
    for copy in copies:
        copy.wait()


def pack_adapters(meta, table, groups, name, after=()):
    return pl.pallas_call(
        functools.partial(pack_adapter_kernel, groups),
        out_shape=tuple(
            jax.ShapeDtypeStruct((ACAP,) + table.shape[1:], table.dtype) for _ in range(groups - 1)
        ),
        in_specs=smem(1) + [pl.BlockSpec(memory_space=pltpu.HBM)] + anywhere(len(after)),
        out_specs=tuple(pl.BlockSpec(memory_space=pltpu.VMEM) for _ in range(groups - 1)),
        scratch_shapes=[pltpu.SemaphoreType.DMA(((groups - 1) * ACAP,))],
        cost_estimate=cost(0, 2 * (groups - 1) * ACAP * table.shape[1] * table.shape[2] * 2),
        compiler_params=params(),
        name=name,
    )(meta, table, *after)


def swap(packed, groups):
    return [
        lax.ppermute(packed[k - 1], "group", [(g, g ^ k) for g in range(groups)])
        for k in range(1, groups)
    ]


def copy_conv(conv, slot, target, width, out, at):
    parts = width // 128
    for k in range(conv.shape[1]):
        for part in range(parts):
            begin = pl.multiple_of(target * width + part * 128, 128)
            out[at + k * parts + part:at + k * parts + part + 1, :] = (
                conv[slot, k:k + 1, pl.ds(begin, 128)]
            )


def pack_state_kernel(devices, width, meta, cache, conv, *rest):
    outs, sems = rest[-devices - 1:-1], rest[-1]
    me, slot = meta[MISC, ME], meta[MISC, SLOT]
    state_rows = cache.shape[3]
    copies = []
    for d in reversed(range(devices)):
        target = lax.bitwise_xor(me, d)
        copy = pltpu.make_async_copy(
            cache.at[slot, target // 2, target % 2], outs[d].at[pl.ds(0, state_rows)], sems.at[d]
        )
        copy.start()
        copies.append(copy)
    for d in range(devices):
        copy_conv(conv, slot, lax.bitwise_xor(me, d), width, outs[d], state_rows)
    for copy in copies:
        copy.wait()


def pack_across_kernel(lines, width, j, meta, cache, conv, *rest):
    across, own, sems = rest[-3:]
    x, slot = meta[MISC, ME] % 2, meta[OSLOT, j[0]]
    state_rows = cache.shape[3]
    copies = []
    for k, (out, place) in enumerate(((across, 1 - x), (own, x))):
        copy = pltpu.make_async_copy(
            cache.at[slot, :, place], out.at[:, pl.ds(0, state_rows)], sems.at[k]
        )
        copy.start()
        copies.append(copy)
    for out, place in ((across, 1 - x), (own, x)):
        for m in range(lines):
            copy_conv(conv, slot, 2 * m + place, width, out.at[m], state_rows)
    for copy in copies:
        copy.wait()


def pick_kernel(step, lines, j, meta, own_r, over_r, own_l, over_l, *rest):
    out_r, out_l = rest[-2:]
    me = meta[MISC, ME]
    source = meta[OHOLDER, j[0]]
    same = source // 2 == me // 2
    mine = same & (source % 2 == me % 2)
    across = same & (source % 2 != me % 2)

    @pl.when(mine)
    def _():
        out_r[...] = own_r[0]
        out_l[...] = own_l[0]

    @pl.when(across)
    def _():
        out_r[...] = over_r[0]
        out_l[...] = over_l[0]

    @pl.when(jnp.logical_not(same))
    def _():
        if step > 1:
            out_r[...] = rest[0][...]
            out_l[...] = rest[1][...]
        else:
            out_r[...] = jnp.zeros_like(out_r)
            out_l[...] = jnp.zeros_like(out_l)


def right_block(meta, step, lines):
    return jnp.clip(lines + meta[MISC, ME] // 2 - step, 0, lines - 1)


def left_block(meta, step, lines):
    return jnp.clip(meta[MISC, ME] // 2 + step - lines, 0, lines - 1)


def pack_across(j, meta, cache, conv, devices, width, after=()):
    lines = devices // 2
    shape = chunk_shape(cache, conv, width)
    return pl.pallas_call(
        functools.partial(pack_across_kernel, lines, width),
        out_shape=tuple(jax.ShapeDtypeStruct((lines,) + shape, cache.dtype) for _ in range(2)),
        in_specs=smem(2) + [
            pl.BlockSpec(memory_space=pltpu.HBM), pl.BlockSpec(memory_space=pltpu.VMEM)
        ] + anywhere(len(after)),
        out_specs=tuple(pl.BlockSpec(memory_space=pltpu.VMEM) for _ in range(2)),
        scratch_shapes=[pltpu.SemaphoreType.DMA((2,))],
        cost_estimate=cost(0, 4 << 20),
        compiler_params=params(),
        name="pack_across",
    )(j, meta, cache, conv, *after)


def spread_entry(j, meta, packed, devices):
    lines = devices // 2
    send, own = packed
    shape = own.shape[1:]
    across = lax.ppermute(send, "dev", [(d, d ^ 1) for d in range(devices)])
    from_left = from_right = None
    whole = pl.BlockSpec(shape, lambda g, j, meta: (0, 0))
    for step in range(1, lines):
        blocks = [
            pl.BlockSpec(
                (1,) + shape, lambda g, j, meta, at=at, step=step: (at(meta, step, lines), 0, 0)
            )
            for at in (right_block, left_block)
        ]
        operands = [own, across, own, across]
        in_specs = [blocks[0], blocks[0], blocks[1], blocks[1]]
        if step > 1:
            operands += [from_left, from_right]
            in_specs += [whole, whole]
        to_right, to_left = pl.pallas_call(
            functools.partial(pick_kernel, step, lines),
            grid_spec=pltpu.PrefetchScalarGridSpec(
                num_scalar_prefetch=2, grid=(1,), in_specs=in_specs, out_specs=(whole, whole)
            ),
            out_shape=tuple(jax.ShapeDtypeStruct(shape, own.dtype) for _ in range(2)),
            cost_estimate=cost(0, 2 << 20),
            compiler_params=params(),
            name=f"pick_{step}",
        )(j, meta, *operands)
        from_left = lax.ppermute(
            to_right, "dev",
            [(2 * i + x, 2 * i + 2 + x) for i in range(step) for x in range(2)],
        )
        from_right = lax.ppermute(
            to_left, "dev",
            [(devices - 1 - (2 * i + x), devices - 3 - (2 * i + x))
             for i in range(step) for x in range(2)],
        )
    return own, across, from_left, from_right


def final_specs(shape):
    line = pl.BlockSpec((1,) + shape, lambda g, j, meta: (meta[MISC, ME] // 2, 0, 0))
    whole = pl.BlockSpec(shape, lambda g, j, meta: (0, 0))
    return [line, line, whole, whole]


def which_candidate(meta, source):
    me = meta[MISC, ME]
    same = source // 2 == me // 2
    mine = same & (source % 2 == me % 2)
    return jnp.where(mine, 0, jnp.where(same, 1, jnp.where(source // 2 < me // 2, 2, 3)))


def final_kernel(j, meta, own, across, from_left, from_right, out):
    which = which_candidate(meta, meta[OHOLDER, j[0]])
    picks = (own.at[0], across.at[0], from_left, from_right)
    for k, pick in enumerate(picks):
        @pl.when(which == k)
        def _(pick=pick):
            out[...] = pick[...]


def spread_rest(meta, cache, conv, devices, width, limit):
    shape = chunk_shape(cache, conv, width)

    def one(j, held):
        jj = j.reshape(1)
        packed = pack_across(jj, meta, cache, conv, devices, width)
        got = spread_entry(jj, meta, packed, devices)
        block = pl.pallas_call(
            final_kernel,
            grid_spec=pltpu.PrefetchScalarGridSpec(
                num_scalar_prefetch=2,
                grid=(1,),
                in_specs=final_specs(shape),
                out_specs=pl.BlockSpec(shape, lambda g, j, meta: (0, 0)),
            ),
            out_shape=jax.ShapeDtypeStruct(shape, cache.dtype),
            compiler_params=params(),
            name="final_pick",
        )(jj, meta, *got)
        return lax.dynamic_update_slice_in_dim(held, block[None], j - 1, 0)

    held = jnp.zeros((limit - 1,) + shape, cache.dtype)
    return lax.fori_loop(jnp.int32(1), meta[MISC, MOST], one, held)


def shrink_kernel(groups, meta, hidden, *rest):
    tables, out = rest[:groups], rest[-1]
    dist = meta[DIST, pl.program_id(0)]
    for k in range(groups):
        @pl.when(dist == k)
        def _(k=k):
            part = lax.dot_general(
                hidden[...], tables[k][0], NT, preferred_element_type=jnp.float32
            )
            out[0] = part.T.astype(out.dtype)


def sum_kernel(parts, out):
    total = parts[0].astype(jnp.float32)
    for k in range(1, parts.shape[0]):
        total = total + parts[k].astype(jnp.float32)
    total = total.astype(out.dtype)
    for k in range(out.shape[0]):
        out[k] = total


def prep_kernel(per_group, rates, skips, steps, taps_in, bias, rows_out, column_out, channel):
    heads, tokens = steps.shape
    length = tokens // per_group
    rate = jnp.zeros((heads, length), jnp.float32)
    place = lax.broadcasted_iota(jnp.int32, rate.shape, 0)
    for h in range(heads):
        rate = jnp.where(place == h, rates[h] * (-LOG2E), rate)
    step = [steps[:, r * length:(r + 1) * length] for r in range(per_group)]
    x = jnp.concatenate([part * rate for part in step], axis=0)
    high = x.astype(jnp.bfloat16)
    rest = x - high.astype(jnp.float32)
    middle = rest.astype(jnp.bfloat16)
    low = (rest - middle.astype(jnp.float32)).astype(jnp.bfloat16)
    s = lax.broadcasted_iota(jnp.int32, (length, length), 0)
    t = lax.broadcasted_iota(jnp.int32, (length, length), 1)
    ones = (s <= t).astype(jnp.float32).astype(jnp.bfloat16)
    total = jnp.dot(low, ones, preferred_element_type=jnp.float32)
    total = total + jnp.dot(middle, ones, preferred_element_type=jnp.float32)
    total = total + jnp.dot(high, ones, preferred_element_type=jnp.float32)
    shifted = total - jnp.log2(jnp.concatenate(step, axis=0))
    columns = shifted.T
    for r in range(per_group):
        rows_out[:heads, r * length:(r + 1) * length] = total[r * heads:(r + 1) * heads]
        rows_out[heads:, r * length:(r + 1) * length] = shifted[r * heads:(r + 1) * heads]
        column_out[r] = columns[:, r * heads:(r + 1) * heads]
    taps, width = taps_in.shape
    head_of = lax.broadcasted_iota(jnp.int32, (1, width), 1) // (width // heads)
    skip = jnp.zeros((1, width), jnp.float32)
    for h in range(heads):
        skip = jnp.where(head_of == h, skips[h], skip)
    channel[:taps] = taps_in[...]
    channel[taps:taps + 1] = bias[...]
    channel[taps + 1:taps + 2] = skip


def mix_kernel(
    groups, taps, begin, direct, spread, size, meta, base, shrunk, *rest
):
    tables, rest = rest[:groups], rest[groups:]
    channel, rows_decay, column, rows_in = rest[:4]
    chunks = rest[4:4 + direct + (5 if spread else 0)]
    out, final, extended, scores, cur, carried, weighted = rest[-7:]
    g = pl.program_id(0)
    position = begin + g
    r = meta[POS_REQ, position]
    length, width = base.shape
    half = length // 2
    heads = width // size
    depth = cur.shape[1]
    few = taps - 1
    parts = width // 128
    f32, bf16 = jnp.float32, jnp.bfloat16

    which = g
    picks = list(chunks[:direct])
    if spread:
        j = g - direct
        late = jnp.where(j == 0, direct + which_candidate(meta, meta[OHOLDER, 0]), direct + 4)
        which = jnp.where(j >= 0, late, which)
        own, across, from_left, from_right, others = chunks[direct:]
        picks += [own.at[0], across.at[0], from_left, from_right, others.at[0]]

    @pl.when(meta[POS_VALID, position] > 0)
    def _():
        present = meta[PRESENT, r] > 0
        for k, pick in enumerate(picks):
            @pl.when(which == k)
            def _(pick=pick):
                cur[...] = jnp.where(present, pick[...], jnp.zeros_like(cur))

        dist = meta[DIST, r]
        for k in range(groups):
            @pl.when(dist == k)
            def _(k=k):
                extended[8:, :] = base[...].astype(f32) + lax.dot_general(
                    shrunk[0], tables[k][0], TN, preferred_element_type=f32
                )

        before = cur[width:, :].astype(f32)
        for k in range(few):
            for part in range(parts):
                extended[8 - few + k:9 - few + k, part * 128:(part + 1) * 128] = (
                    before[k * parts + part:k * parts + part + 1, :]
                )

        write, read = rows_in[:, :depth], rows_in[:, depth:]
        all_scores = lax.dot_general(write, read, NT, preferred_element_type=f32)
        s = lax.broadcasted_iota(jnp.int32, (length, length), 0)
        t = lax.broadcasted_iota(jnp.int32, (length, length), 1)
        scores[...] = jnp.where(s <= t, all_scores, 0.0)
        carried[...] = lax.dot_general(cur[:width, :], read, NT, preferred_element_type=f32)

        to_here, from_here = rows_decay[:heads, :], rows_decay[heads:, :]
        end = jnp.broadcast_to(to_here[:, length - 1:length], (heads, length))
        grown = jnp.exp2(to_here)
        to_end = jnp.exp2(end - from_here)
        kept = jnp.exp2(end[:, :depth])
        corner = jnp.zeros((half, half), bf16)
        for pair in range(heads // 2):
            lo, hi = pair * 2 * size, (pair + 1) * 2 * size
            v = channel[taps:taps + 1, lo:hi]
            for k in range(taps):
                first = 8 - few + k
                v = v + channel[k:k + 1, lo:hi] * extended[first:first + length, lo:hi]
            activated = v * (0.5 + 0.5 * jnp.tanh(0.5 * v))
            act = activated.astype(bf16).T
            sums = []
            for i in range(2):
                h = 2 * pair + i
                a = act[i * size:(i + 1) * size, :]
                ds = jnp.broadcast_to(column[0, :, h:h + 1], (length, half))
                dt0, dt1 = to_here[h:h + 1, :half], to_here[h:h + 1, half:]
                m00 = jnp.exp2(jnp.minimum(dt0 - ds[:half], 126.0)) * scores[:half, :half]
                m01 = jnp.exp2(dt1 - ds[:half]) * scores[:half, half:]
                m11 = jnp.exp2(jnp.minimum(dt1 - ds[half:], 126.0)) * scores[half:, half:]
                mixing = jnp.concatenate(
                    [
                        jnp.concatenate([m00.astype(bf16), m01.astype(bf16)], axis=1),
                        jnp.concatenate([corner, m11.astype(bf16)], axis=1),
                    ],
                    axis=0,
                )
                total = jnp.dot(a, mixing, preferred_element_type=f32)
                begin_h = h * size
                sums.append(total + carried[begin_h:begin_h + size, :] * grown[h:h + 1, :])
                weighted[begin_h:begin_h + size, :] = (
                    a.astype(f32) * to_end[h:h + 1, :]
                ).astype(bf16)
            skipped = channel[taps + 1:taps + 2, lo:hi] * activated
            out[:, lo:hi] = (jnp.concatenate(sums, axis=0).T + skipped).astype(out.dtype)
        fresh = jnp.dot(weighted[...], write, preferred_element_type=f32)
        for h in range(heads):
            rows = slice(h * size, (h + 1) * size)
            old = cur[rows, :].astype(f32) * kept[h:h + 1, :]
            final[0, rows, :] = (fresh[rows, :] + old).astype(final.dtype)


def chunk_shape(cache, conv, width):
    conv_rows = conv.shape[1] * (width // 128)
    return (cache.shape[3] + -(-conv_rows // 16) * 16, cache.shape[4])


def body(
    hidden, base_in_projection, state_input_matrix, state_output_matrix, head_step_size,
    head_decay_rate, head_skip_scale, convolution_weight, convolution_bias, adapter_down_weight,
    adapter_up_weight, adapter_home_group, adapter_group_index, state_space_cache,
    convolution_cache, prefix_holder_device, prefix_cache_slot, prefix_block_count,
):
    groups, devices = lax.axis_size("group"), lax.axis_size("dev")
    tokens, width = base_in_projection.shape
    per_group = tokens // T_REQ
    assert per_group == devices and devices & (devices - 1) == 0 == groups & (groups - 1)
    heads = head_step_size.shape[0]
    size, depth = state_space_cache.shape[2:]
    rank = adapter_down_weight.shape[1]
    taps = convolution_weight.shape[0]
    bf16, f32 = jnp.bfloat16, jnp.float32
    limit = per_group // 2
    lines = devices // 2

    rows_all = lax.all_gather(
        jnp.concatenate([state_input_matrix, state_output_matrix], axis=1), "dev", axis=0,
        tiled=True,
    )
    meta = pl.pallas_call(
        functools.partial(plan_kernel, groups, devices, per_group),
        out_shape=jax.ShapeDtypeStruct(META_SHAPE, jnp.int32),
        in_specs=smem(5),
        out_specs=smem(1)[0],
        cost_estimate=cost(0, 1 << 16),
        name="plan",
    )(
        adapter_home_group.reshape(-1), adapter_group_index, prefix_holder_device.reshape(-1),
        prefix_cache_slot, prefix_block_count,
    )
    zero = jnp.zeros((1,), jnp.int32)

    down_send = pack_adapters(meta, adapter_down_weight, groups, "pack_down")
    down_got = swap(down_send, groups)

    cache = state_space_cache.reshape(
        state_space_cache.shape[0], lines, 2, heads * size, depth
    )
    conv = convolution_cache
    shape = chunk_shape(cache, conv, width)
    chunks = pl.pallas_call(
        functools.partial(pack_state_kernel, devices, width),
        out_shape=tuple(jax.ShapeDtypeStruct(shape, bf16) for _ in range(devices)),
        in_specs=smem(1) + [
            pl.BlockSpec(memory_space=pltpu.HBM), pl.BlockSpec(memory_space=pltpu.VMEM)
        ] + anywhere(1),
        out_specs=tuple(pl.BlockSpec(memory_space=pltpu.VMEM) for _ in range(devices)),
        scratch_shapes=[pltpu.SemaphoreType.DMA((devices,))],
        cost_estimate=cost(0, 4 << 20),
        compiler_params=params(),
        name="pack_state",
    )(meta, cache, conv, down_send[0])
    got = [chunks[0]] + [
        lax.ppermute(chunks[d], "dev", [(s, s ^ d) for s in range(devices)])
        for d in range(1, devices)
    ]

    up_send = pack_adapters(meta, adapter_up_weight, groups, "pack_up", (chunks[1],))
    up_got = swap(up_send, groups)

    across = pack_across(zero, meta, cache, conv, devices, width, (up_send[0],))
    spread = spread_entry(zero, meta, across, devices)
    spread_others = spread_rest(meta, cache, conv, devices, width, limit)

    rows_decay, column_decay, channel = pl.pallas_call(
        functools.partial(prep_kernel, per_group),
        out_shape=(
            jax.ShapeDtypeStruct((2 * heads, tokens), f32),
            jax.ShapeDtypeStruct((per_group, T_REQ, heads), f32),
            jax.ShapeDtypeStruct((8, width), f32),
        ),
        in_specs=smem(2) + [pl.BlockSpec(memory_space=pltpu.VMEM) for _ in range(3)],
        out_specs=tuple(pl.BlockSpec(memory_space=pltpu.VMEM) for _ in range(3)),
        cost_estimate=cost(0, 4 << 20),
        compiler_params=params(),
        name="prep",
    )(
        head_decay_rate, head_skip_scale, head_step_size, convolution_weight,
        convolution_bias.reshape(1, width),
    )

    def table_specs(table, request):
        return [
            pl.BlockSpec(
                (1,) + table.shape[1:], lambda g, meta: (meta[AINDEX, request(g, meta)], 0, 0)
            )
        ] + [
            pl.BlockSpec(
                (1,) + table.shape[1:],
                lambda g, meta, k=k: (
                    jnp.where(
                        meta[DIST, request(g, meta)] == k, meta[ARANK, request(g, meta)], 0
                    ), 0, 0,
                ),
            )
            for k in range(1, groups)
        ]

    partial_down = pl.pallas_call(
        functools.partial(shrink_kernel, groups),
        grid_spec=pltpu.PrefetchScalarGridSpec(
            num_scalar_prefetch=1,
            grid=(per_group,),
            in_specs=[pl.BlockSpec((T_REQ, hidden.shape[1]), lambda r, meta: (r, 0))]
            + table_specs(adapter_down_weight, lambda r, meta: r) + anywhere(2),
            out_specs=pl.BlockSpec((1, rank, T_REQ), lambda r, meta: (r, 0, 0)),
        ),
        out_shape=jax.ShapeDtypeStruct((per_group, rank, T_REQ), bf16),
        cost_estimate=cost(2 * tokens * hidden.shape[1] * rank, 6 << 20),
        compiler_params=params(),
        name="shrink",
    )(meta, hidden, adapter_down_weight, *down_got, across[0], channel)

    parts = lax.all_to_all(partial_down, "dev", split_axis=0, concat_axis=0, tiled=True)
    summed = pl.pallas_call(
        sum_kernel,
        out_shape=jax.ShapeDtypeStruct((devices, 1, rank, T_REQ), bf16),
        cost_estimate=cost(0, 1 << 19),
        name="sum_parts",
    )(parts.reshape(devices, 1, rank, T_REQ))
    shrunk = lax.all_to_all(summed, "dev", split_axis=0, concat_axis=0, tiled=True)
    shrunk = shrunk.reshape(per_group, rank, T_REQ)

    outs = None
    whole = pl.BlockSpec(shape, lambda g, meta: (0, 0))
    for begin, direct, late in ((0, lines, False), (lines, devices - lines, True)):
        steps = direct + (limit if late else 0)

        def request(g, meta, begin=begin):
            return meta[POS_REQ, begin + g]

        in_specs = [
            pl.BlockSpec((T_REQ, width), lambda g, meta: (request(g, meta), 0)),
            pl.BlockSpec((1, rank, T_REQ), lambda g, meta: (request(g, meta), 0, 0)),
        ] + table_specs(adapter_up_weight, request) + [
            pl.BlockSpec((8, width), lambda g, meta: (0, 0)),
            pl.BlockSpec((2 * heads, T_REQ), lambda g, meta: (0, request(g, meta))),
            pl.BlockSpec((1, T_REQ, heads), lambda g, meta: (request(g, meta), 0, 0)),
            pl.BlockSpec((T_REQ, 2 * depth), lambda g, meta: (request(g, meta), 0)),
        ] + [whole] * direct
        operands = [
            meta, base_in_projection, shrunk, adapter_up_weight, *up_got, channel, rows_decay,
            column_decay, rows_all, *got[begin:begin + direct],
        ]
        if late:
            line = pl.BlockSpec((1,) + shape, lambda g, meta: (meta[MISC, ME] // 2, 0, 0))
            in_specs += [
                line, line, whole, whole,
                pl.BlockSpec(
                    (1,) + shape,
                    lambda g, meta, d=direct: (jnp.clip(g - d - 1, 0, limit - 2), 0, 0),
                ),
            ]
            operands += [*spread, spread_others]
        aliases = {}
        if outs is not None:
            aliases = {len(operands): 0, len(operands) + 1: 1}
            operands += list(outs)
            in_specs += anywhere(2)
        outs = pl.pallas_call(
            functools.partial(mix_kernel, groups, taps, begin, direct, late, size),
            grid_spec=pltpu.PrefetchScalarGridSpec(
                num_scalar_prefetch=1,
                grid=(steps,),
                in_specs=in_specs,
                out_specs=(
                    pl.BlockSpec((T_REQ, width), lambda g, meta: (request(g, meta), 0)),
                    pl.BlockSpec(
                        (1, heads * size, depth), lambda g, meta: (request(g, meta), 0, 0)
                    ),
                ),
                scratch_shapes=[
                    pltpu.VMEM((T_REQ + 8, width), f32),
                    pltpu.VMEM((T_REQ, T_REQ), f32),
                    pltpu.VMEM(shape, bf16),
                    pltpu.VMEM((width, T_REQ), f32),
                    pltpu.VMEM((width, T_REQ), bf16),
                ],
            ),
            out_shape=(
                jax.ShapeDtypeStruct((tokens, width), bf16),
                jax.ShapeDtypeStruct((per_group, heads * size, depth), bf16),
            ),
            input_output_aliases=aliases,
            cost_estimate=cost(2 << 30, 12 << 20, 8 << 20),
            compiler_params=params(),
            name=f"mix_{begin}",
        )(*operands)
    return outs[0], outs[1].reshape(per_group, heads, size, depth)


def solution(mesh):
    placed = (
        P("group", "dev"),
        P("group", "dev"),
        P(("group", "dev"), None),
        P(("group", "dev"), None),
        P("dev", "group"),
        P("dev"),
        P("dev"),
        P(None, "dev"),
        P("dev"),
        P("group", None, "dev"),
        P("group", None, "dev"),
        P(),
        P(),
        P(("group", "dev"), None, None, None),
        P(("group", "dev"), None, None),
        P(),
        P(),
        P(),
    )
    return jax.shard_map(
        body,
        mesh=mesh,
        in_specs=placed,
        out_specs=(P("group", "dev"), P("group", "dev", None, None)),
        check_vma=False,
    )
```

time: 370 us -> 183 us (0.49); the launches traced: 363 us -> 180 us
  blocking collectives: 184 us -> 0 us
  matrix products: 65.4 us -> 0 us
  Pallas kernels: 0 us -> 61.6 us
  local copies, waits for them, and re-layouts: 68.2 us -> 17 us
  waiting for transfers between devices: 1.42 us -> 49 us
  starting transfers between devices: 12.5 us -> 37 us
  other arithmetic: 17.2 us -> 0.66 us
    all_gather x2 -> x0, blocking collectives: 142 us -> none  [the longest x1 111 us: body(): lax.all_gather(state_output_matrix, 'dev', axis=0, tiled=True)]
    dot_general x34 -> x0, matrix products: 65.4 us -> none  [the longest x8 20 us: request_mixer(): jnp.einsum('hts,shp->thp', mixing, driven, preferred_element_type=jnp.flo...]
    pallas_call x0 -> x13, Pallas kernels: none -> 61.6 us  [the longest x2 32.2 us: body(): pl.pallas_call(functools.partial(mix_kernel, groups, taps, begin, direct,...]
    ppermute x0 -> x20, waiting for transfers between devices: none -> 48.9 us  [the longest x7 19.9 us: body(): lax.ppermute(chunks[d], 'dev', [(s, s ^ d) for s in range(devices)])]
    psum x1 -> x0, blocking collectives: 41.8 us -> none  [body(): shrunk_rows = lax.psum(partial_down, 'dev').astype(jnp.bfloat16)]
    ppermute x0 -> x20, starting transfers between devices: none -> 25.4 us  [the longest x3 9.64 us: spread_entry(): lax.ppermute(to_right, 'dev', [(2 * i + x, 2 * i + 2 + x) for i in range(...]
    gather x9 -> x0, local copies, waits for them, and re-layouts: 20.7 us -> none
    mul x9 -> x0, local copies, waits for them, and re-layouts: 9.17 us -> none  [the longest x1 9.15 us: conv_activate(): return jax.nn.silu(summed)]
  transfers between devices with their start and end apart: 4 -> 23, of which waited for: 0 -> 9; matrix products, arithmetic and copies ran while one was open for 13% -> 1% of each run, Pallas kernels for 0% -> 16%
where the time goes in v3:
time: 183 us; the launch traced here: 180 us
  Pallas kernels  61.6 us (34%)
  waiting for transfers between devices  49 us (27%)
  starting transfers between devices  37 us (20%)
  local copies, waits for them, and re-layouts  17 us (9%)
  between operations  14.4 us (8%)
    pallas_call x2, Pallas kernels, body(): pl.pallas_call(functools.partial(mix_kernel, groups, taps, begin, direct,...  32.2 us
    ppermute x7, waiting for transfers between devices, body(): lax.ppermute(chunks[d], 'dev', [(s, s ^ d) for s in range(devices)])  19.9 us
    ppermute x6, waiting for transfers between devices, swap(): lax.ppermute(packed[k - 1], 'group', [(g, g ^ k) for g in range(groups)])  19 us
    unnamed x75, local copies, waits for them, and re-layouts  15.5 us
    ppermute x3, starting transfers between devices, spread_entry(): lax.ppermute(to_right, 'dev', [(2 * i + x, 2 * i + 2 + x) for i in range(...  9.64 us
    ppermute x3, waiting for transfers between devices, spread_entry(): lax.ppermute(to_right, 'dev', [(2 * i + x, 2 * i + 2 + x) for i in range(...  8.7 us
    pallas_call x1, Pallas kernels, body(): pl.pallas_call(functools.partial(shrink_kernel, groups), grid_spec=pltpu....  7.61 us
    ppermute x7, starting transfers between devices, body(): lax.ppermute(chunks[d], 'dev', [(s, s ^ d) for s in range(devices)])  6.99 us
  transfers between devices with their start and end apart: 23, of which 9 were waited for; matrix products, arithmetic and copies ran while one was open for 1% of the time, Pallas kernels for 16%

profile of v3, /device:TPU:8, one launch (start us, length us, event | category | flops | bytes accessed | tf_op | source)
XLA Modules:
  0.0 180.3 jit_solution(7230203392080004)
XLA Ops:
  7.2 1.8 %copy.27.conv = bf16[4,3,8192]{2,1,0:T(4,128)(2,1)} copy(bf16[4,3,8192]{2,0,1:T(4,128)(2,1)} %param.34) | data formatting | bytes 393216 | tf_op args[14]
  9.0 1.9 %plan.1.meta = s32[16,64]{1,0:T(8,128)S(1)} custom-call(s32[32]{0:T(128)} %bitcast.22, s32[32]{0:T(128)} %index.1, s32[32]{0:T(128)} %bitcast.23, s32[32]{0:T(128)} %slot.1, s32[32]{0:T(128)} %blocks.1), custom_call_target="tpu_custom_call" | custom-call | bytes 65536 | tf_op jit(solution)/shard_map/plan/pallas_call | solution.py:543
  11.0 1.2 copy-done.3
  12.2 2.9 %pack_down.1 = (bf16[4,64,1024]{2,1,0:T(8,128)(2,1)S(1)}, bf16[4,64,1024]{2,1,0:T(8,128)(2,1)S(1)}, bf16[4,64,1024]{2,1,0:T(8,128)(2,1)S(1)}) custom-call(s32[16,64]{1,0:T(8,128)S(1)} %plan.1.meta, bf16[8,64,1024]{2,1,0:T(8,128)(2,1)S(1)} %copy-done.3), custom_call_target="tpu_custom_call" | custom-call | bytes 3145728 | tf_op jit(solution)/shard_map/pack_down/pallas_call | solution.py:150
  15.1 0.8 copy-done.23
  15.9 0.8 copy-done.24
  16.6 4.6 %pack_state.1 = (bf16[1056,128]{1,0:T(8,128)(2,1)S(1)}, bf16[1056,128]{1,0:T(8,128)(2,1)S(1)}, bf16[1056,128]{1,0:T(8,128)(2,1)}, bf16[1056,128]{1,0:T(8,128)(2,...) custom-call(s32[16,64]{1,0:T(8,128)S(1)} %plan.1.meta, ...), custom_call_target="tpu_custom_call" | custom-call | bytes 4194304 | tf_op jit(solution)/shard_map/pack_state/pallas_call | solution.py:564
  22.0 2.9 %pack_up.1 = (bf16[4,64,1024]{2,1,0:T(8,128)(2,1)S(1)}, bf16[4,64,1024]{2,1,0:T(8,128)(2,1)S(1)}, bf16[4,64,1024]{2,1,0:T(8,128)(2,1)S(1)}) custom-call(s32[16,64]{1,0:T(8,128)S(1)} %plan.1.meta, bf16[8,64,1024]{2,1,0:T(8,128)(2,1)S(1)} %copy-done.5, bf16[1056,128]{1,0:T(8,128)(2,1)S(1)} %get-tuple-element.166.rest_0_), custom_call_target="tpu_custom_call" | custom-call | bytes 3145728 | tf_op jit(solution)/shard_map/pack_up/pallas_call | solution.py:150
  25.0 3.0 %pack_across.8 = (bf16[4,1056,128]{2,1,0:T(8,128)(2,1)}, bf16[4,1056,128]{2,1,0:T(8,128)(2,1)S(1)}) custom-call(s32[1]{0:T(128)} %constant.32.clone.1.j, s32[16,64]{1,0:T(8,128)S(1)} %plan.1.meta, bf16[4,4,2,1024,128]{4,3,2,1,0:T(8,128)(2,1)S(1)} %bitcast.20, bf16[4,3,8192]{2,1,0:T(4,128)(2,1)} %copy.27.conv, bf16[4,64,1024]{2,1,0:T(8,128)(2,1)S(1)} %get-tuple-element.167.rest_0_), custom_call_target="tpu_custom_call" | custom-call | bytes 4194304 | tf_op jit(solution)/shard_map/pack_across/pallas_call | solution.py:256
  28.0 1.6 collective-permute-start.17
  30.3 1.6 collective-permute-start.8
  32.5 1.1 prep.1
  33.7 1.0 copy-done.7
  34.7 0.7 copy-done.13
  35.4 10.1 %collective-permute-done.8.rest_2_ = bf16[4,64,1024]{2,1,0:T(8,128)(2,1)S(1)} collective-permute-done((bf16[4,64,1024]{2,1,0:T(8,128)(2,1)}, bf16[4,64,1024]{2,1,0:T(8,128)(2,1)S(1)}, u32[]{:S(2)}, u32[]{:S(2)}) %collective-permute-start.8) | collective-permute-done | bytes 524320 | tf_op jit(solution)/shard_map/ppermute | solution.py:166
  45.4 8.9 %collective-permute-done.9.rest_3_ = bf16[4,64,1024]{2,1,0:T(8,128)(2,1)S(1)} collective-permute-done((bf16[4,64,1024]{2,1,0:T(8,128)(2,1)}, bf16[4,64,1024]{2,1,0:T(8,128)(2,1)S(1)}, u32[]{:S(2)}, u32[]{:S(2)}) %collective-permute-start.9) | collective-permute-done | bytes 524320 | tf_op jit(solution)/shard_map/ppermute | solution.py:166
  54.3 7.6 %shrink.1 = bf16[8,64,256]{2,1,0:T(8,128)(2,1)} custom-call(s32[16,64]{1,0:T(8,128)S(1)} %plan.1.meta, bf16[2048,1024]{1,0:T(8,128)(2,1)} %hidden.1, bf16[8,64,1024]{2,1,0:T(8,128)(2,1)S(1)} %copy-done.4, bf16[4,64,1024]{2,1,0:T(8,128)(2,1)S(1)} %collective-permute-done.7.rest_1_, bf16[4,64,1024]{2,1,0:T(8,128)(2,1)S(1)} %collective-permute-done.8.rest_2_, ...), custom_call_target="tpu_custom_call" | custom-call | flops 268435456 | bytes 6291456 | tf_op jit(solution)/shard_map/shrink/pallas_call | solution.py:622
  61.9 5.4 %all-to-all-start = ((bf16[8,64,256]{2,1,0:T(8,128)(2,1)}), bf16[8,64,256]{2,1,0:T(8,128)(2,1)}, u32[]{:S(2)}, u32[]{:S(2)}) async-start(bf16[8,64,256]{2,1,0:T(8,128)(2,1)} %shrink.1), calls=%async_computation | async-start | bytes 524288 | tf_op jit(solution)/shard_map/all_to_all | solution.py:637
  67.3 0.7 pick_1.8
  68.0 1.3 collective-permute-start.18
  70.0 3.7 %collective-permute-start.13 = (bf16[1056,128]{1,0:T(8,128)(2,1)}, bf16[1056,128]{1,0:T(8,128)(2,1)}, u32[]{:S(2)}, u32[]{:S(2)}) collective-permute-start(bf16[1056,128]{1,0:T(8,128)(2,1)} %get-tuple-element.174), channel_id=1, source_target_pairs={{0,4},{1,5},{2,6},{3,7},{4,0},{5,1},{6,2},{7,3},{8,12},{9,13},{10,... | collective-permute-start | bytes 811016 | tf_op jit(solution)/shard_map/ppermute | solution.py:577
  74.3 5.2 %collective-permute-done.18.rest_0_ = bf16[1056,128]{1,0:T(8,128)(2,1)S(1)} collective-permute-done((bf16[1056,128]{1,0:T(8,128)(2,1)S(1)}, bf16[1056,128]{1,0:T(8,128)(2,1)S(1)}, u32[]{:S(2)}, u32[]{:S(2)}) %collective-permute-start.18) | collective-permute-done | bytes 270368 | tf_op jit(solution)/shard_map/ppermute | solution.py:299
  79.4 1.4 pick_2.8
  81.6 4.4 %collective-permute-start.20 = (bf16[1056,128]{1,0:T(8,128)(2,1)}, bf16[1056,128]{1,0:T(8,128)(2,1)S(1)}, u32[]{:S(2)}, u32[]{:S(2)}) collective-permute-start(bf16[1056,128]{1,0:T(8,128)(2,1)} %get-tuple-element.181), channel_id=1, source_target_pairs={{0,2},{1,3},{2,4},{3,5},{8,10},{9,11},{10,12},{11,13},{16,18},{17,... | collective-permute-start | bytes 811016 | tf_op jit(solution)/shard_map/ppermute | solution.py:299
  86.0 1.0 broadcast_in_dim.12
  87.6 1.3 collective-permute-start.21
  89.8 1.4 collective-permute-done.25.rest_10_
  91.2 1.7 sum_parts.1
  92.9 6.2 %all-to-all-start.1 = ((bf16[8,1,64,256]{3,2,1,0:T(8,128)(2,1)}), bf16[8,1,64,256]{3,2,1,0:T(8,128)(2,1)S(1)}, u32[]{:S(2)}, u32[]{:S(2)}) async-start(bf16[8,1,64,256]{3,2,1,0:T(8,128)(2,1)} %sum_parts.1), calls=%async_computation.1 | async-start | bytes 524288 | tf_op jit(solution)/shard_map/all_to_all | solution.py:644
  99.1 1.5 collective-permute-start.26
  100.7 1.2 copy-done.2
  101.9 1.5 pick_3.8
  103.4 8.4 %collective-permute-done.26.rest_11_ = bf16[1056,128]{1,0:T(8,128)(2,1)S(1)} collective-permute-done((bf16[1056,128]{1,0:T(8,128)(2,1)}, bf16[1056,128]{1,0:T(8,128)(2,1)S(1)}, u32[]{:S(2)}, u32[]{:S(2)}) %collective-permute-start.26) | collective-permute-done | bytes 270368 | tf_op jit(solution)/shard_map/ppermute | solution.py:577
  111.9 0.7 copy-done.29
  112.6 1.8 collective-permute-start.14
  114.4 6.8 %collective-permute-done.24.rest_9_ = bf16[1056,128]{1,0:T(8,128)(2,1)S(1)} collective-permute-done((bf16[1056,128]{1,0:T(8,128)(2,1)}, bf16[1056,128]{1,0:T(8,128)(2,1)S(1)}, u32[]{:S(2)}, u32[]{:S(2)}) %collective-permute-start.24) | collective-permute-done | bytes 270368 | tf_op jit(solution)/shard_map/ppermute | solution.py:577
  121.9 3.9 %collective-permute-start.22 = (bf16[1056,128]{1,0:T(8,128)(2,1)}, bf16[1056,128]{1,0:T(8,128)(2,1)S(1)}, u32[]{:S(2)}, u32[]{:S(2)}) collective-permute-start(bf16[1056,128]{1,0:T(8,128)(2,1)} %get-tuple-element.183), channel_id=1, source_target_pairs={{0,2},{1,3},{2,4},{3,5},{4,6},{5,7},{8,10},{9,11},{10,12},{11,13},... | collective-permute-start | bytes 811016 | tf_op jit(solution)/shard_map/ppermute | solution.py:299
  125.8 2.1 %collective-permute-start.23 = (bf16[1056,128]{1,0:T(8,128)(2,1)}, bf16[1056,128]{1,0:T(8,128)(2,1)S(1)}, u32[]{:S(2)}, u32[]{:S(2)}) collective-permute-start(bf16[1056,128]{1,0:T(8,128)(2,1)} %get-tuple-element.184), channel_id=1, source_target_pairs={{7,5},{6,4},{5,3},{4,2},{3,1},{2,0},{15,13},{14,12},{13,11},{12,10... | collective-permute-start | bytes 811016 | tf_op jit(solution)/shard_map/ppermute | solution.py:303
  128.0 1.2 copy-done.8
  129.2 0.9 copy-done.14
  130.2 1.0 copy-done.26
  131.1 1.0 copy-done.30
  132.1 1.0 copy-done.32
  133.1 15.1 %mix_0.1 = (bf16[2048,1024]{1,0:T(8,128)(2,1)}, bf16[8,1024,128]{2,1,0:T(8,128)(2,1)}) custom-call(s32[16,64]{1,0:T(8,128)S(1)} %get-tuple-element.340, bf16[2048,1024]{1,0:T(8,128)(2,1)} %base.3, bf16[8,64,256]{2,1,0:T(8,128)(2,1)S(1)} %bitcast.15, bf16[8,64,1024]{2,1,0:T(8,128)(2,1)S(1)} %copy-done.6, ...), custom_call_target="tpu_custom_call" | custom-call | flops 2147483648 | bytes 12582912 | tf_op jit(solution)/shard_map/mix_0/pallas_call | solution.py:683
  148.2 3.3 %collective-permute-done.16.rest_11_ = bf16[1056,128]{1,0:T(8,128)(2,1)S(1)} collective-permute-done((bf16[1056,128]{1,0:T(8,128)(2,1)}, bf16[1056,128]{1,0:T(8,128)(2,1)S(1)}, u32[]{:S(2)}, u32[]{:S(2)}) %collective-permute-start.16) | collective-permute-done | bytes 270368 | tf_op jit(solution)/shard_map/ppermute | solution.py:577
  151.4 3.5 %collective-permute-done.22.rest_14_ = bf16[1056,128]{1,0:T(8,128)(2,1)S(1)} collective-permute-done((bf16[1056,128]{1,0:T(8,128)(2,1)}, bf16[1056,128]{1,0:T(8,128)(2,1)S(1)}, u32[]{:S(2)}, u32[]{:S(2)}) %collective-permute-start.22) | collective-permute-done | bytes 270368 | tf_op jit(solution)/shard_map/ppermute | solution.py:299
  154.9 1.4 collective-permute-done.23.rest_15_
  156.3 17.1 %mix_4.1 = (bf16[2048,1024]{1,0:T(8,128)(2,1)}, bf16[8,1024,128]{2,1,0:T(8,128)(2,1)}) custom-call(s32[16,64]{1,0:T(8,128)S(1)} %get-tuple-element.340, bf16[2048,1024]{1,0:T(8,128)(2,1)} %base.3, bf16[8,64,256]{2,1,0:T(8,128)(2,1)S(1)} %bitcast.16, bf16[8,64,1024]{2,1,0:T(8,128)(2,1)S(1)} %copy-done.6, ...), custom_call_target="tpu_custom_call", output_to_operand_aliasing={{0}: (20, {}), {1}: (21, {})} | custom-call | flops 2147483648 | bytes 12582912 | tf_op jit(solution)/shard_map/mix_4/pallas_call | solution.py:683
  (91 shorter events, 6.5 us)
Async XLA Ops:
  7.2 120.8 %all-gather.2.cloned.1.call-start = ((), (), s32[]{:S(2)}) async-start(), calls=%async_computation.2 | async-start | bytes 1179648 | tf_op jit(solution)/shard_map/all_gather | solution.py:539
  11.0 1.2 copy-start.3
  16.6 4.6 %copy-start.11 = (bf16[4,64,1024]{2,1,0:T(8,128)(2,1)}, bf16[4,64,1024]{2,1,0:T(8,128)(2,1)S(1)}, u32[]{:S(2)}) copy-start(bf16[4,64,1024]{2,1,0:T(8,128)(2,1)S(1)} %get-tuple-element.163.rest_0_) | copy-start | bytes 1572868
  16.6 5.4 %copy-start.5 = (bf16[8,64,1024]{2,1,0:T(8,128)(2,1)S(1)}, bf16[8,64,1024]{2,1,0:T(8,128)(2,1)}, u32[]{:S(2)}) copy-start(bf16[8,64,1024]{2,1,0:T(8,128)(2,1)} %rest_0_.5) | copy-start | bytes 3145732
  16.6 8.3 %copy-start.33 = (bf16[4,128,64,128]{3,2,1,0:T(8,128)(2,1)S(1)}, bf16[4,128,64,128]{3,2,1,0:T(8,128)(2,1)}, u32[]{:S(2)}) copy-start(bf16[4,128,64,128]{3,2,1,0:T(8,128)(2,1)} %param.33) | copy-start | bytes 25165828
  22.0 2.9 %copy-start.12 = (bf16[1056,128]{1,0:T(8,128)(2,1)}, bf16[1056,128]{1,0:T(8,128)(2,1)S(1)}, u32[]{:S(2)}) copy-start(bf16[1056,128]{1,0:T(8,128)(2,1)S(1)} %get-tuple-element.166.rest_0_) | copy-start | bytes 811012
  22.0 2.9 %copy-start.27 = (bf16[1056,128]{1,0:T(8,128)(2,1)}, bf16[1056,128]{1,0:T(8,128)(2,1)S(1)}, u32[]{:S(2)}) copy-start(bf16[1056,128]{1,0:T(8,128)(2,1)S(1)} %get-tuple-element.188) | copy-start | bytes 811012
  24.9 3.1 %copy-start.10 = (bf16[4,64,1024]{2,1,0:T(8,128)(2,1)}, bf16[4,64,1024]{2,1,0:T(8,128)(2,1)S(1)}, u32[]{:S(2)}) copy-start(bf16[4,64,1024]{2,1,0:T(8,128)(2,1)S(1)} %get-tuple-element.167.rest_0_) | copy-start | bytes 1572868
  24.9 3.1 %copy-start.21 = (bf16[4,64,1024]{2,1,0:T(8,128)(2,1)}, bf16[4,64,1024]{2,1,0:T(8,128)(2,1)S(1)}, u32[]{:S(2)}) copy-start(bf16[4,64,1024]{2,1,0:T(8,128)(2,1)S(1)} %get-tuple-element.171) | copy-start | bytes 1572868
  24.9 3.1 %copy-start.22 = (bf16[4,64,1024]{2,1,0:T(8,128)(2,1)}, bf16[4,64,1024]{2,1,0:T(8,128)(2,1)S(1)}, u32[]{:S(2)}) copy-start(bf16[4,64,1024]{2,1,0:T(8,128)(2,1)S(1)} %get-tuple-element.170) | copy-start | bytes 1572868
  24.9 4.7 %copy-start.35 = (bf16[256,128]{1,0:T(8,128)(2,1)S(1)}, bf16[256,128]{1,0:T(8,128)(2,1)}, u32[]{:S(2)}) copy-start(bf16[256,128]{1,0:T(8,128)(2,1)} %param.23) | copy-start | bytes 196612
  24.9 4.7 %copy-start.36 = (bf16[256,128]{1,0:T(8,128)(2,1)S(1)}, bf16[256,128]{1,0:T(8,128)(2,1)}, u32[]{:S(2)}) copy-start(bf16[256,128]{1,0:T(8,128)(2,1)} %param.22) | copy-start | bytes 196612
  24.9 7.6 %copy-start.16 = (f32[16,2048]{1,0:T(8,128)S(1)}, f32[16,2048]{1,0:T(8,128)}, u32[]{:S(2)}) copy-start(f32[16,2048]{1,0:T(8,128)} %steps.1) | copy-start | bytes 393220
  24.9 7.6 %copy-start.17 = (f32[4,1024]{1,0:T(4,128)S(1)}, f32[4,1024]{1,0:T(4,128)}, u32[]{:S(2)}) copy-start(f32[4,1024]{1,0:T(4,128)} %taps_in.1) | copy-start | bytes 49156
  25.0 7.5 %copy-start.18 = (f32[1024]{0:T(1024)S(1)}, f32[1024]{0:T(1024)}, u32[]{:S(2)}) copy-start(f32[1024]{0:T(1024)} %param.28) | copy-start | bytes 12292
  25.0 7.5 %copy-start.19 = (f32[16]{0:T(128)S(1)}, f32[16]{0:T(128)}, u32[]{:S(2)}) copy-start(f32[16]{0:T(128)} %rates.1) | copy-start | bytes 196
  25.0 7.5 %copy-start.20 = (f32[16]{0:T(128)S(1)}, f32[16]{0:T(128)}, u32[]{:S(2)}) copy-start(f32[16]{0:T(128)} %skips.1) | copy-start | bytes 196
  25.0 29.3 %copy-start.4 = (bf16[8,64,1024]{2,1,0:T(8,128)(2,1)S(1)}, bf16[8,64,1024]{2,1,0:T(8,128)(2,1)}, u32[]{:S(2)}) copy-start(bf16[8,64,1024]{2,1,0:T(8,128)(2,1)} %rest_0_.3) | copy-start | bytes 3145732
  28.0 72.7 %copy-start = (bf16[4,1056,128]{2,1,0:T(8,128)(2,1)}, bf16[4,1056,128]{2,1,0:T(8,128)(2,1)S(1)}, u32[]{:S(2)}) copy-start(bf16[4,1056,128]{2,1,0:T(8,128)(2,1)S(1)} %get-tuple-element.178.own_r.own_l.rest_12_) | copy-start | bytes 3244036
  28.0 39.3 %collective-permute-start.17 = (bf16[4,1056,128]{2,1,0:T(8,128)(2,1)}, bf16[4,1056,128]{2,1,0:T(8,128)(2,1)S(1)}, u32[]{:S(2)}, u32[]{:S(2)}) collective-permute-start(bf16[4,1056,128]{2,1,0:T(8,128)(2,1)} %get-tuple-element.168.rest_4_), channel_id=1, source_target_pairs={{0,1},{1,0},{2,3},{3,2},{4,5},{5,4},{6,7},{7,6},{8,9},{9,8},{10,11... | collective-permute-start | bytes 3244040 | tf_op jit(solution)/shard_map/ppermute | solution.py:274
  30.3 15.1 %collective-permute-start.8 = (bf16[4,64,1024]{2,1,0:T(8,128)(2,1)}, bf16[4,64,1024]{2,1,0:T(8,128)(2,1)S(1)}, u32[]{:S(2)}, u32[]{:S(2)}) collective-permute-start(bf16[4,64,1024]{2,1,0:T(8,128)(2,1)} %copy-done.24), channel_id=1, source_target_pairs={{0,16},{8,24},{16,0},{24,8},{1,17},{9,25},{17,1},{25,9},{2,18},{10... | collective-permute-start | bytes 1572872 | tf_op jit(solution)/shard_map/ppermute | solution.py:166
  31.9 22.5 %collective-permute-start.9 = (bf16[4,64,1024]{2,1,0:T(8,128)(2,1)}, bf16[4,64,1024]{2,1,0:T(8,128)(2,1)S(1)}, u32[]{:S(2)}, u32[]{:S(2)}) collective-permute-start(bf16[4,64,1024]{2,1,0:T(8,128)(2,1)} %copy-done.23), channel_id=1, source_target_pairs={{0,24},{8,16},{16,8},{24,0},{1,25},{9,17},{17,9},{25,1},{2,26},{10... | collective-permute-start | bytes 1572872 | tf_op jit(solution)/shard_map/ppermute | solution.py:166
  31.9 22.5 %collective-permute-start.7 = (bf16[4,64,1024]{2,1,0:T(8,128)(2,1)}, bf16[4,64,1024]{2,1,0:T(8,128)(2,1)S(1)}, u32[]{:S(2)}, u32[]{:S(2)}) collective-permute-start(bf16[4,64,1024]{2,1,0:T(8,128)(2,1)} %copy-done.11), channel_id=1, source_target_pairs={{0,8},{8,0},{16,24},{24,16},{1,9},{9,1},{17,25},{25,17},{2,10},{10... | collective-permute-start | bytes 1572872 | tf_op jit(solution)/shard_map/ppermute | solution.py:166
  61.9 29.3 %all-to-all-start = ((bf16[8,64,256]{2,1,0:T(8,128)(2,1)}), bf16[8,64,256]{2,1,0:T(8,128)(2,1)}, u32[]{:S(2)}, u32[]{:S(2)}) async-start(bf16[8,64,256]{2,1,0:T(8,128)(2,1)} %shrink.1), calls=%async_computation | async-start | bytes 524288 | tf_op jit(solution)/shard_map/all_to_all | solution.py:637
  67.3 12.1 %copy-start.1 = (bf16[4,1056,128]{2,1,0:T(8,128)(2,1)}, bf16[4,1056,128]{2,1,0:T(8,128)(2,1)S(1)}, u32[]{:S(2)}) copy-start(bf16[4,1056,128]{2,1,0:T(8,128)(2,1)S(1)} %collective-permute-done.17.over_r.over_l.rest_13_) | copy-start | bytes 3244036
  68.0 11.4 %collective-permute-start.18 = (bf16[1056,128]{1,0:T(8,128)(2,1)S(1)}, bf16[1056,128]{1,0:T(8,128)(2,1)S(1)}, u32[]{:S(2)}, u32[]{:S(2)}) collective-permute-start(bf16[1056,128]{1,0:T(8,128)(2,1)S(1)} %get-tuple-element.179), channel_id=1, source_target_pairs={{0,2},{1,3},{8,10},{9,11},{16,18},{17,19},{24,26},{25,27}} | collective-permute-start | bytes 811016 | tf_op jit(solution)/shard_map/ppermute | solution.py:299
  69.3 10.1 %collective-permute-start.19 = (bf16[1056,128]{1,0:T(8,128)(2,1)S(1)}, bf16[1056,128]{1,0:T(8,128)(2,1)S(1)}, u32[]{:S(2)}, u32[]{:S(2)}) collective-permute-start(bf16[1056,128]{1,0:T(8,128)(2,1)S(1)} %get-tuple-element.180), channel_id=1, source_target_pairs={{7,5},{6,4},{15,13},{14,12},{23,21},{22,20},{31,29},{30,28}} | collective-permute-start | bytes 811016 | tf_op jit(solution)/shard_map/ppermute | solution.py:303
  70.0 19.6 %collective-permute-start.13 = (bf16[1056,128]{1,0:T(8,128)(2,1)}, bf16[1056,128]{1,0:T(8,128)(2,1)}, u32[]{:S(2)}, u32[]{:S(2)}) collective-permute-start(bf16[1056,128]{1,0:T(8,128)(2,1)} %get-tuple-element.174), channel_id=1, source_target_pairs={{0,4},{1,5},{2,6},{3,7},{4,0},{5,1},{6,2},{7,3},{8,12},{9,13},{10,... | collective-permute-start | bytes 811016 | tf_op jit(solution)/shard_map/ppermute | solution.py:577
  73.7 17.5 %collective-permute-start.25 = (bf16[1056,128]{1,0:T(8,128)(2,1)}, bf16[1056,128]{1,0:T(8,128)(2,1)}, u32[]{:S(2)}, u32[]{:S(2)}) collective-permute-start(bf16[1056,128]{1,0:T(8,128)(2,1)} %get-tuple-element.187), channel_id=1, source_target_pairs={{0,2},{1,3},{2,0},{3,1},{4,6},{5,7},{6,4},{7,5},{8,10},{9,11},{10,... | collective-permute-start | bytes 811016 | tf_op jit(solution)/shard_map/ppermute | solution.py:577
  81.6 17.5 %collective-permute-start.20 = (bf16[1056,128]{1,0:T(8,128)(2,1)}, bf16[1056,128]{1,0:T(8,128)(2,1)S(1)}, u32[]{:S(2)}, u32[]{:S(2)}) collective-permute-start(bf16[1056,128]{1,0:T(8,128)(2,1)} %get-tuple-element.181), channel_id=1, source_target_pairs={{0,2},{1,3},{2,4},{3,5},{8,10},{9,11},{10,12},{11,13},{16,18},{17,... | collective-permute-start | bytes 811016 | tf_op jit(solution)/shard_map/ppermute | solution.py:299
  87.6 13.0 %collective-permute-start.21 = (bf16[1056,128]{1,0:T(8,128)(2,1)}, bf16[1056,128]{1,0:T(8,128)(2,1)S(1)}, u32[]{:S(2)}, u32[]{:S(2)}) collective-permute-start(bf16[1056,128]{1,0:T(8,128)(2,1)} %copy-done.28), channel_id=1, source_target_pairs={{7,5},{6,4},{5,3},{4,2},{15,13},{14,12},{13,11},{12,10},{23,21},{2... | collective-permute-start | bytes 811016 | tf_op jit(solution)/shard_map/ppermute | solution.py:303
  88.9 32.9 %collective-permute-start.11 = (bf16[4,64,1024]{2,1,0:T(8,128)(2,1)}, bf16[4,64,1024]{2,1,0:T(8,128)(2,1)S(1)}, u32[]{:S(2)}, u32[]{:S(2)}) collective-permute-start(bf16[4,64,1024]{2,1,0:T(8,128)(2,1)} %copy-done.22), channel_id=1, source_target_pairs={{0,16},{8,24},{16,0},{24,8},{1,17},{9,25},{17,1},{25,9},{2,18},{10... | collective-permute-start | bytes 1572872 | tf_op jit(solution)/shard_map/ppermute | solution.py:166
  89.6 32.3 %collective-permute-start.12 = (bf16[4,64,1024]{2,1,0:T(8,128)(2,1)}, bf16[4,64,1024]{2,1,0:T(8,128)(2,1)}, u32[]{:S(2)}, u32[]{:S(2)}) collective-permute-start(bf16[4,64,1024]{2,1,0:T(8,128)(2,1)} %copy-done.21), channel_id=1, source_target_pairs={{0,24},{8,16},{16,8},{24,0},{1,25},{9,17},{17,9},{25,1},{2,26},{10... | collective-permute-start | bytes 1572872 | tf_op jit(solution)/shard_map/ppermute | solution.py:166
  91.2 34.7 %collective-permute-start.10 = (bf16[4,64,1024]{2,1,0:T(8,128)(2,1)}, bf16[4,64,1024]{2,1,0:T(8,128)(2,1)}, u32[]{:S(2)}, u32[]{:S(2)}) collective-permute-start(bf16[4,64,1024]{2,1,0:T(8,128)(2,1)} %copy-done.10), channel_id=1, source_target_pairs={{0,8},{8,0},{16,24},{24,16},{1,9},{9,1},{17,25},{25,17},{2,10},{10... | collective-permute-start | bytes 1572872 | tf_op jit(solution)/shard_map/ppermute | solution.py:166
  92.9 35.1 %all-to-all-start.1 = ((bf16[8,1,64,256]{3,2,1,0:T(8,128)(2,1)}), bf16[8,1,64,256]{3,2,1,0:T(8,128)(2,1)S(1)}, u32[]{:S(2)}, u32[]{:S(2)}) async-start(bf16[8,1,64,256]{3,2,1,0:T(8,128)(2,1)} %sum_parts.1), calls=%async_computation.1 | async-start | bytes 524288 | tf_op jit(solution)/shard_map/all_to_all | solution.py:644
  99.1 12.8 %collective-permute-start.26 = (bf16[1056,128]{1,0:T(8,128)(2,1)}, bf16[1056,128]{1,0:T(8,128)(2,1)S(1)}, u32[]{:S(2)}, u32[]{:S(2)}) collective-permute-start(bf16[1056,128]{1,0:T(8,128)(2,1)} %copy-done.27), channel_id=1, source_target_pairs={{0,3},{1,2},{2,1},{3,0},{4,7},{5,6},{6,5},{7,4},{8,11},{9,10},{10,... | collective-permute-start | bytes 811016 | tf_op jit(solution)/shard_map/ppermute | solution.py:577
  100.6 20.6 %collective-permute-start.24 = (bf16[1056,128]{1,0:T(8,128)(2,1)}, bf16[1056,128]{1,0:T(8,128)(2,1)S(1)}, u32[]{:S(2)}, u32[]{:S(2)}) collective-permute-start(bf16[1056,128]{1,0:T(8,128)(2,1)} %copy-done.12), channel_id=1, source_target_pairs={{0,1},{1,0},{2,3},{3,2},{4,5},{5,4},{6,7},{7,6},{8,9},{9,8},{10,11... | collective-permute-start | bytes 811016 | tf_op jit(solution)/shard_map/ppermute | solution.py:577
  100.7 1.2 copy-start.2
  101.9 26.1 %copy-start.6 = (bf16[8,64,1024]{2,1,0:T(8,128)(2,1)S(1)}, bf16[8,64,1024]{2,1,0:T(8,128)(2,1)}, u32[]{:S(2)}) copy-start(bf16[8,64,1024]{2,1,0:T(8,128)(2,1)} %rest_0_.5) | copy-start | bytes 3145732
  112.6 35.5 %collective-permute-start.14 = (bf16[1056,128]{1,0:T(8,128)(2,1)}, bf16[1056,128]{1,0:T(8,128)(2,1)S(1)}, u32[]{:S(2)}, u32[]{:S(2)}) collective-permute-start(bf16[1056,128]{1,0:T(8,128)(2,1)} %get-tuple-element.175), channel_id=1, source_target_pairs={{0,5},{1,4},{2,7},{3,6},{4,1},{5,0},{6,3},{7,2},{8,13},{9,12},{10,... | collective-permute-start | bytes 811016 | tf_op jit(solution)/shard_map/ppermute | solution.py:577
  121.9 26.3 %collective-permute-start.15 = (bf16[1056,128]{1,0:T(8,128)(2,1)}, bf16[1056,128]{1,0:T(8,128)(2,1)S(1)}, u32[]{:S(2)}, u32[]{:S(2)}) collective-permute-start(bf16[1056,128]{1,0:T(8,128)(2,1)} %get-tuple-element.176), channel_id=1, source_target_pairs={{0,6},{1,7},{2,4},{3,5},{4,2},{5,3},{6,0},{7,1},{8,14},{9,15},{10,... | collective-permute-start | bytes 811016 | tf_op jit(solution)/shard_map/ppermute | solution.py:577
  121.9 29.5 %collective-permute-start.16 = (bf16[1056,128]{1,0:T(8,128)(2,1)}, bf16[1056,128]{1,0:T(8,128)(2,1)S(1)}, u32[]{:S(2)}, u32[]{:S(2)}) collective-permute-start(bf16[1056,128]{1,0:T(8,128)(2,1)} %get-tuple-element.177), channel_id=1, source_target_pairs={{0,7},{1,6},{2,5},{3,4},{4,3},{5,2},{6,1},{7,0},{8,15},{9,14},{10,... | collective-permute-start | bytes 811016 | tf_op jit(solution)/shard_map/ppermute | solution.py:577
  121.9 33.0 %collective-permute-start.22 = (bf16[1056,128]{1,0:T(8,128)(2,1)}, bf16[1056,128]{1,0:T(8,128)(2,1)S(1)}, u32[]{:S(2)}, u32[]{:S(2)}) collective-permute-start(bf16[1056,128]{1,0:T(8,128)(2,1)} %get-tuple-element.183), channel_id=1, source_target_pairs={{0,2},{1,3},{2,4},{3,5},{4,6},{5,7},{8,10},{9,11},{10,12},{11,13},... | collective-permute-start | bytes 811016 | tf_op jit(solution)/shard_map/ppermute | solution.py:299
  125.8 30.5 %collective-permute-start.23 = (bf16[1056,128]{1,0:T(8,128)(2,1)}, bf16[1056,128]{1,0:T(8,128)(2,1)S(1)}, u32[]{:S(2)}, u32[]{:S(2)}) collective-permute-start(bf16[1056,128]{1,0:T(8,128)(2,1)} %get-tuple-element.184), channel_id=1, source_target_pairs={{7,5},{6,4},{5,3},{4,2},{3,1},{2,0},{15,13},{14,12},{13,11},{12,10... | collective-permute-start | bytes 811016 | tf_op jit(solution)/shard_map/ppermute | solution.py:303
  128.0 1.2 copy-start.8
  133.0 23.3 %copy-start.9 = (f32[8,256,16]{2,1,0:T(8,128)S(1)}, f32[8,256,16]{2,1,0:T(8,128)}, u32[]{:S(2)}) copy-start(f32[8,256,16]{2,1,0:T(8,128)} %copy-done.7) | copy-start | bytes 393220
  133.0 23.3 %copy-start.15 = (f32[32,2048]{1,0:T(8,128)S(1)}, f32[32,2048]{1,0:T(8,128)}, u32[]{:S(2)}) copy-start(f32[32,2048]{1,0:T(8,128)} %copy-done.13) | copy-start | bytes 786436
  133.0 23.3 %copy-start.34 = (bf16[3,1056,128]{2,1,0:T(8,128)(2,1)S(1)}, bf16[3,1056,128]{2,1,0:T(8,128)(2,1)}, u32[]{:S(2)}) copy-start(bf16[3,1056,128]{2,1,0:T(8,128)(2,1)} %get-tuple-element.185.rest_16_) | copy-start | bytes 2433028
  (12 other events, 9.9 us)
Sparse Core Ops, SparseCore 0:
  30.4 40.8 all-gather.1

commit v4 on v3

v4 whole, which is shorter than its diff:
```python
import functools
import math

import jax
import jax.numpy as jnp
from jax import lax
from jax.experimental import pallas as pl
from jax.experimental.pallas import tpu as pltpu
from jax.sharding import PartitionSpec as P

T_REQ = 256
CAP = 2
ACAP = 4
LOG2E = math.log2(math.e)
NT = (((1,), (1,)), ((), ()))
TN = (((0,), (0,)), ((), ()))
VMEM_LIMIT = 48 * 1024 * 1024

DIST, ARANK, AINDEX, PRESENT, POS_REQ, POS_VALID, OSLOT, OHOLDER, MISC, SEND = range(10)
MOST, ME, SLOT, SPREAD = range(4)
META_SHAPE = (16, 64)


def cost():
    return pl.CostEstimate(flops=1, bytes_accessed=1, transcendentals=0)


def params():
    return pltpu.CompilerParams(vmem_limit_bytes=VMEM_LIMIT)


def smem(count):
    return [pl.BlockSpec(memory_space=pltpu.SMEM) for _ in range(count)]


def vmem(count):
    return [pl.BlockSpec(memory_space=pltpu.VMEM) for _ in range(count)]


def pinned(count):
    return [pl.BlockSpec(memory_space=pltpu.HBM) for _ in range(count)]


def anywhere(count):
    return [pl.BlockSpec(memory_space=pl.ANY) for _ in range(count)]


def as_int(flag):
    return flag.astype(jnp.int32)


def ranks_of(labels):
    ranks = []
    for q, label in enumerate(labels):
        total = jnp.int32(0)
        for other in labels[:q]:
            total = total + as_int(other == label)
        ranks.append(total)
    return ranks


def plan(groups, devices, per_group, home, index, holder, slot, blocks, meta):
    my_group = lax.axis_index("group")
    me = lax.axis_index("dev")
    first = my_group * per_group
    limit = per_group // 2
    for j in range(limit):
        meta[POS_REQ, devices + j] = jnp.int32(-1)
        meta[POS_VALID, devices + j] = jnp.int32(0)
        meta[OSLOT, j] = jnp.int32(0)
        meta[OHOLDER, j] = jnp.int32(0)

    homes = [home[first + q] for q in range(per_group)]
    for q, rank in enumerate(ranks_of(homes)):
        own = homes[q] == my_group
        meta[DIST, q] = lax.bitwise_xor(homes[q], my_group)
        meta[ARANK, q] = jnp.where(own, 0, rank)
        meta[AINDEX, q] = jnp.where(own, index[first + q], 0)
        meta[PRESENT, q] = as_int(blocks[first + q] > 0)
    for k in range(1, groups):
        theirs = lax.bitwise_xor(my_group, k) * per_group
        seen = jnp.int32(0)
        chosen = [jnp.int32(0) for _ in range(ACAP)]
        for q in range(per_group):
            hit = home[theirs + q] == my_group
            value = index[theirs + q]
            for c in range(ACAP):
                chosen[c] = jnp.where(hit & (seen == c), value, chosen[c])
            seen = seen + as_int(hit)
        for c in range(ACAP):
            meta[SEND, (k - 1) * ACAP + c] = chosen[c]

    holders = [holder[first + q] for q in range(per_group)]
    ranks = ranks_of(holders)
    count = jnp.int32(0)
    my_slot = jnp.int32(0)
    for q in range(per_group):
        my_slot = jnp.where((holders[q] == me) & (ranks[q] == 0), slot[first + q], my_slot)

        @pl.when(ranks[q] > 0)
        def _():
            meta[POS_REQ, devices + count] = jnp.int32(q)
            meta[POS_VALID, devices + count] = jnp.int32(1)
            meta[OSLOT, count] = slot[first + q]
            meta[OHOLDER, count] = holders[q]

        count = count + as_int(ranks[q] > 0)
    spread = meta[POS_REQ, devices]
    requests = []
    for d in range(devices):
        source = lax.bitwise_xor(me, d)
        request = jnp.int32(-1)
        for q in range(per_group):
            request = jnp.where((holders[q] == source) & (ranks[q] == 0), q, request)
        meta[POS_VALID, d] = as_int(request >= 0)
        requests.append(request)
    requests += [meta[POS_REQ, devices + j] for j in range(limit)]
    for begin, end in ((0, devices // 2), (devices // 2, devices)):
        last = jnp.int32(-1)
        filled = []
        for p in range(begin, end):
            last = jnp.where(requests[p] >= 0, requests[p], last)
            filled.append(last)
        following = jnp.maximum(spread, 0)
        for p in reversed(range(begin, end)):
            following = jnp.where(filled[p - begin] >= 0, filled[p - begin], following)
            meta[POS_REQ, p] = following
    meta[MISC, SPREAD] = as_int(count > 0)
    meta[POS_VALID, devices] = jnp.int32(1)
    for j in range(limit):
        meta[POS_REQ, devices + j] = jnp.where(
            j < count, requests[devices + j],
            jnp.where(count > 0, meta[POS_REQ, devices + max(j - 1, 0)], requests[0]),
        )
    most = jnp.int32(0)
    for g in range(groups):
        labels = [holder[g * per_group + q] for q in range(per_group)]
        total = jnp.int32(0)
        for rank in ranks_of(labels):
            total = total + as_int(rank > 0)
        most = jnp.maximum(most, total)
    meta[MISC, MOST] = most
    meta[MISC, ME] = me
    meta[MISC, SLOT] = my_slot


def start_adapters(groups, meta, table, outs, sems):
    copies = []
    for k in reversed(range(1, groups)):
        for c in range(ACAP):
            chosen = meta[SEND, (k - 1) * ACAP + c]
            copy = pltpu.make_async_copy(
                table.at[chosen], outs[k - 1].at[c], sems.at[(k - 1) * ACAP + c]
            )
            copy.start()
            copies.append(copy)
    return copies


def swap(packed, groups):
    return [
        lax.ppermute(packed[k - 1], "group", [(g, g ^ k) for g in range(groups)])
        for k in range(1, groups)
    ]


def copy_conv(conv, slot, target, width, out, at):
    parts = width // 128
    begin = pl.multiple_of(target * width, 128)
    for k in range(conv.shape[0]):
        rows = conv[k, :, pl.ds(begin, width)]
        row = rows[:1, :]
        for c in range(1, conv.shape[1]):
            row = jnp.where(slot == c, rows[c:c + 1, :], row)
        for part in range(parts):
            place = at + k * parts + part
            out[place:place + 1, :] = row[:, part * 128:(part + 1) * 128]


def start_state(devices, meta, cache, outs, sems):
    copies = []
    for d in reversed(range(devices)):
        target = lax.bitwise_xor(meta[MISC, ME], d)
        copy = pltpu.make_async_copy(
            cache.at[meta[MISC, SLOT], target // 2, target % 2],
            outs[d].at[pl.ds(0, cache.shape[3])], sems.at[d],
        )
        copy.start()
        copies.append(copy)
    return copies


def start_across(j, meta, cache, across, own, sems):
    x = meta[MISC, ME] % 2
    copies = []
    for k, (out, place) in enumerate(((across, 1 - x), (own, x))):
        copy = pltpu.make_async_copy(
            cache.at[meta[OSLOT, j], :, place], out.at[:, pl.ds(0, cache.shape[3])], sems.at[k]
        )
        copy.start()
        copies.append(copy)
    return copies


def conv_across(lines, width, j, meta, conv, state_rows, across, own):
    x = meta[MISC, ME] % 2
    for out, place in ((across, 1 - x), (own, x)):
        for m in range(lines):
            copy_conv(conv, meta[OSLOT, j], 2 * m + place, width, out.at[m], state_rows)


def pack_kernel(
    groups, devices, per_group, width, home, index, holder, slot, blocks, down, up, cache, write,
    read, conv, meta, rows_out, *rest
):
    downs, rest = rest[:groups - 1], rest[groups - 1:]
    ups, rest = rest[:groups - 1], rest[groups - 1:]
    chunks, (across, own, down_sems, up_sems, chunk_sems, across_sems) = (
        rest[:devices], rest[devices:]
    )
    plan(groups, devices, per_group, home, index, holder, slot, blocks, meta)
    copies = start_adapters(groups, meta, down, downs, down_sems)
    copies += start_state(devices, meta, cache, chunks, chunk_sems)
    copies += start_across(0, meta, cache, across, own, across_sems)
    copies += start_adapters(groups, meta, up, ups, up_sems)
    depth = write.shape[1]
    rows_out[:, :depth] = write[...]
    rows_out[:, depth:] = read[...]
    state_rows = cache.shape[3]
    for d in range(devices):
        target = lax.bitwise_xor(meta[MISC, ME], d)
        copy_conv(conv, meta[MISC, SLOT], target, width, chunks[d], state_rows)
    conv_across(devices // 2, width, 0, meta, conv, state_rows, across, own)
    for copy in copies:
        copy.wait()


def pack_across_kernel(lines, width, j, meta, cache, conv, across, own, sems):
    copies = start_across(j[0], meta, cache, across, own, sems)
    conv_across(lines, width, j[0], meta, conv, cache.shape[3], across, own)
    for copy in copies:
        copy.wait()


def pick_kernel(step, lines, j, meta, own_r, over_r, own_l, over_l, *rest):
    out_r, out_l = rest[-2:]
    me = meta[MISC, ME]
    source = meta[OHOLDER, j[0]]
    same = source // 2 == me // 2
    mine = same & (source % 2 == me % 2)
    across = same & (source % 2 != me % 2)

    @pl.when(mine)
    def _():
        out_r[...] = own_r[0]
        out_l[...] = own_l[0]

    @pl.when(across)
    def _():
        out_r[...] = over_r[0]
        out_l[...] = over_l[0]

    @pl.when(jnp.logical_not(same))
    def _():
        if step > 1:
            out_r[...] = rest[0][...]
            out_l[...] = rest[1][...]
        else:
            out_r[...] = jnp.zeros_like(out_r)
            out_l[...] = jnp.zeros_like(out_l)


def right_block(meta, step, lines):
    return jnp.clip(lines + meta[MISC, ME] // 2 - step, 0, lines - 1)


def left_block(meta, step, lines):
    return jnp.clip(meta[MISC, ME] // 2 + step - lines, 0, lines - 1)


def pack_across(j, meta, cache, conv, devices, width):
    lines = devices // 2
    shape = chunk_shape(cache, conv, width)
    return pl.pallas_call(
        functools.partial(pack_across_kernel, lines, width),
        out_shape=tuple(jax.ShapeDtypeStruct((lines,) + shape, cache.dtype) for _ in range(2)),
        in_specs=smem(2) + pinned(1) + vmem(1),
        out_specs=tuple(vmem(2)),
        scratch_shapes=[pltpu.SemaphoreType.DMA((2,))],
        cost_estimate=cost(),
        compiler_params=params(),
        name="pack_across",
    )(j, meta, cache, conv)


def spread_steps(j, meta, packed, devices):
    lines = devices // 2
    send, own = packed
    shape = own.shape[1:]
    across = lax.ppermute(send, "dev", [(d, d ^ 1) for d in range(devices)])
    from_left = from_right = None
    after = yield across
    whole = pl.BlockSpec(shape, lambda g, j, meta: (0, 0))
    for step in range(1, lines):
        blocks = [
            pl.BlockSpec(
                (1,) + shape, lambda g, j, meta, at=at, step=step: (at(meta, step, lines), 0, 0)
            )
            for at in (right_block, left_block)
        ]
        operands = [own, across, own, across]
        in_specs = [blocks[0], blocks[0], blocks[1], blocks[1]]
        if step > 1:
            operands += [from_left, from_right]
            in_specs += [whole, whole]
        operands += after
        in_specs += anywhere(len(after))
        to_right, to_left = pl.pallas_call(
            functools.partial(pick_kernel, step, lines),
            grid_spec=pltpu.PrefetchScalarGridSpec(
                num_scalar_prefetch=2, grid=(1,), in_specs=in_specs, out_specs=(whole, whole)
            ),
            out_shape=tuple(jax.ShapeDtypeStruct(shape, own.dtype) for _ in range(2)),
            cost_estimate=cost(),
            compiler_params=params(),
            name=f"pick_{step}",
        )(j, meta, *operands)
        from_left = lax.ppermute(
            to_right, "dev",
            [(2 * i + x, 2 * i + 2 + x) for i in range(step) for x in range(2)],
        )
        from_right = lax.ppermute(
            to_left, "dev",
            [(devices - 1 - (2 * i + x), devices - 3 - (2 * i + x))
             for i in range(step) for x in range(2)],
        )
        after = yield to_right
    yield own, across, from_left, from_right


def final_specs(shape):
    line = pl.BlockSpec((1,) + shape, lambda g, j, meta: (meta[MISC, ME] // 2, 0, 0))
    whole = pl.BlockSpec(shape, lambda g, j, meta: (0, 0))
    return [line, line, whole, whole]


def which_candidate(meta, source):
    me = meta[MISC, ME]
    same = source // 2 == me // 2
    mine = same & (source % 2 == me % 2)
    return jnp.where(mine, 0, jnp.where(same, 1, jnp.where(source // 2 < me // 2, 2, 3)))


def final_kernel(j, meta, own, across, from_left, from_right, out):
    which = which_candidate(meta, meta[OHOLDER, j[0]])
    picks = (own.at[0], across.at[0], from_left, from_right)
    for k, pick in enumerate(picks):
        @pl.when(which == k)
        def _(pick=pick):
            out[...] = pick[...]


def spread_rest(meta, cache, conv, devices, width, limit):
    shape = chunk_shape(cache, conv, width)

    def one(j, held):
        jj = j.reshape(1)
        packed = pack_across(jj, meta, cache, conv, devices, width)
        steps = spread_steps(jj, meta, packed, devices)
        next(steps)
        for _ in range(devices // 2):
            got = steps.send([])
        block = pl.pallas_call(
            final_kernel,
            grid_spec=pltpu.PrefetchScalarGridSpec(
                num_scalar_prefetch=2,
                grid=(1,),
                in_specs=final_specs(shape),
                out_specs=pl.BlockSpec(shape, lambda g, j, meta: (0, 0)),
            ),
            out_shape=jax.ShapeDtypeStruct(shape, cache.dtype),
            compiler_params=params(),
            name="final_pick",
        )(jj, meta, *got)
        return lax.dynamic_update_slice_in_dim(held, block[None], j - 1, 0)

    held = jnp.zeros((limit - 1,) + shape, cache.dtype)
    return lax.fori_loop(jnp.int32(1), meta[MISC, MOST], one, held)


def fetch_table(groups, meta, r, tables, out, sem):
    dist = meta[DIST, r]
    for k in range(groups):
        row = meta[ARANK, r] if k else meta[AINDEX, r]

        @pl.when(dist == k)
        def _(k=k, row=row):
            pltpu.make_async_copy(tables[k].at[row], out, sem).start()


def shrink_kernel(groups, per_group, meta, hidden, *rest):
    tables, (out, picked, sems) = rest[:groups], rest[-3:]
    g = pl.program_id(0)
    each = out.shape[0]

    @pl.when(g == 0)
    def _():
        for r in range(per_group):
            fetch_table(groups, meta, r, tables, picked.at[r], sems.at[r])

    for i in range(each):
        r = g * each + i
        pltpu.make_async_copy(tables[0].at[0], picked.at[r], sems.at[r]).wait()
    for i in range(each):
        part = lax.dot_general(
            hidden[i * T_REQ:(i + 1) * T_REQ, :], picked[g * each + i], NT,
            preferred_element_type=jnp.float32,
        )
        out[i] = part.T.astype(out.dtype)


def sum_kernel(parts, *rest):
    out = rest[-1]
    total = parts[0].astype(jnp.float32)
    for k in range(1, parts.shape[0]):
        total = total + parts[k].astype(jnp.float32)
    total = total.astype(out.dtype)
    for k in range(out.shape[0]):
        out[k] = total


def prep_kernel(per_group, rates, skips, steps, taps_in, bias, *rest):
    rows_out, column_out, channel = rest[-3:]
    heads, tokens = steps.shape
    length = tokens // per_group
    rate = jnp.zeros((heads, length), jnp.float32)
    place = lax.broadcasted_iota(jnp.int32, rate.shape, 0)
    for h in range(heads):
        rate = jnp.where(place == h, rates[h] * (-LOG2E), rate)
    step = [steps[:, r * length:(r + 1) * length] for r in range(per_group)]
    x = jnp.concatenate([part * rate for part in step], axis=0)
    high = x.astype(jnp.bfloat16)
    rest = x - high.astype(jnp.float32)
    middle = rest.astype(jnp.bfloat16)
    low = (rest - middle.astype(jnp.float32)).astype(jnp.bfloat16)
    s = lax.broadcasted_iota(jnp.int32, (length, length), 0)
    t = lax.broadcasted_iota(jnp.int32, (length, length), 1)
    ones = (s <= t).astype(jnp.float32).astype(jnp.bfloat16)
    total = jnp.dot(low, ones, preferred_element_type=jnp.float32)
    total = total + jnp.dot(middle, ones, preferred_element_type=jnp.float32)
    total = total + jnp.dot(high, ones, preferred_element_type=jnp.float32)
    shifted = total - jnp.log2(jnp.concatenate(step, axis=0))
    columns = shifted.T
    for r in range(per_group):
        rows_out[:heads, r * length:(r + 1) * length] = total[r * heads:(r + 1) * heads]
        rows_out[heads:, r * length:(r + 1) * length] = shifted[r * heads:(r + 1) * heads]
        column_out[r] = columns[:, r * heads:(r + 1) * heads]
    taps, width = taps_in.shape
    head_of = lax.broadcasted_iota(jnp.int32, (1, width), 1) // (width // heads)
    skip = jnp.zeros((1, width), jnp.float32)
    for h in range(heads):
        skip = jnp.where(head_of == h, skips[h], skip)
    channel[:taps] = taps_in[...]
    channel[taps:taps + 1] = bias[...]
    channel[taps + 1:taps + 2] = skip


def mix_kernel(
    groups, taps, begin, steps, spread, size, meta, base, shrunk, channel, rows_decay, column,
    rows_in, *rest
):
    tables, chunks = rest[:groups], rest[groups:]
    out, final, done, extended, scores, carried, weighted, ups, curs, table_sems, chunk_sems = (
        rest[-11:]
    )
    g = pl.program_id(0)
    position = begin + g
    r = meta[POS_REQ, position]
    length, width = base.shape
    half = length // 2
    heads = width // size
    depth = curs.shape[2]
    few = taps - 1
    parts = width // 128
    f32, bf16 = jnp.float32, jnp.bfloat16

    done[...] = jnp.zeros_like(done)

    def fetch_chunk(source, i):
        pltpu.make_async_copy(source, curs.at[i], chunk_sems.at[i]).start()

    @pl.when(g == 0)
    def _():
        for i in range(steps):
            @pl.when(meta[POS_VALID, begin + i] > 0)
            def _(i=i):
                request = meta[POS_REQ, begin + i]
                fetch_table(groups, meta, request, tables, ups.at[i], table_sems.at[i])
                if not spread:
                    fetch_chunk(chunks[i], i)
                elif i > 0:
                    fetch_chunk(chunks[4].at[i - 1], i)
                else:
                    line = meta[MISC, ME] // 2
                    candidates = [
                        chunks[0].at[line], chunks[1].at[line], chunks[2], chunks[3], chunks[5]
                    ]
                    which = jnp.where(
                        meta[MISC, SPREAD] > 0, which_candidate(meta, meta[OHOLDER, 0]), 4
                    )
                    for k, candidate in enumerate(candidates):
                        @pl.when(which == k)
                        def _(candidate=candidate):
                            fetch_chunk(candidate, 0)

    @pl.when(meta[POS_VALID, position] > 0)
    def _():
        present = meta[PRESENT, r] > 0
        write, read = rows_in[:, :depth], rows_in[:, depth:]
        all_scores = lax.dot_general(write, read, NT, preferred_element_type=f32)
        s = lax.broadcasted_iota(jnp.int32, (half, half), 0)
        t = lax.broadcasted_iota(jnp.int32, (half, half), 1)
        scores[:half] = jnp.where(s <= t, all_scores[:half, :half], 0.0)
        scores[half:] = jnp.where(s <= t, all_scores[half:, half:], 0.0)
        late_scores = all_scores[:half, half:].astype(bf16)

        to_here, from_here = rows_decay[:heads, :], rows_decay[heads:, :]
        end = jnp.broadcast_to(to_here[:, length - 1:length], (heads, length))
        middle = jnp.broadcast_to(to_here[:, half - 1:half], (heads, half))
        grown = jnp.exp2(to_here)
        to_end = jnp.exp2(end - from_here)
        to_middle = jnp.exp2(middle - from_here[:, :half])
        past_middle = jnp.exp2(to_here[:, half:] - middle)
        kept = jnp.exp2(end[:, :depth])

        pltpu.make_async_copy(tables[0].at[0], ups.at[g], table_sems.at[g]).wait()
        extended[8:, :] = base[...].astype(f32) + lax.dot_general(
            shrunk[0], ups[g], TN, preferred_element_type=f32
        )
        pltpu.make_async_copy(curs.at[g], curs.at[g], chunk_sems.at[g]).wait()
        before = jnp.where(present, curs[g, width:, :].astype(f32), 0.0)
        for k in range(few):
            for part in range(parts):
                extended[8 - few + k:9 - few + k, part * 128:(part + 1) * 128] = (
                    before[k * parts + part:k * parts + part + 1, :]
                )
        from_state = lax.dot_general(curs[g, :width, :], read, NT, preferred_element_type=f32)
        carried[...] = jnp.where(present, from_state, 0.0)

        corner = jnp.zeros((half, half), bf16)
        for pair in range(heads // 2):
            lo, hi = pair * 2 * size, (pair + 1) * 2 * size
            v = channel[taps:taps + 1, lo:hi]
            for k in range(taps):
                first = 8 - few + k
                v = v + channel[k:k + 1, lo:hi] * extended[first:first + length, lo:hi]
            activated = v * (0.5 + 0.5 * jnp.tanh(0.5 * v))
            act = activated.astype(bf16).T
            wide = act.astype(f32)
            sums, early = [], []
            for i in range(2):
                h = 2 * pair + i
                a = act[i * size:(i + 1) * size, :]
                a32 = wide[i * size:(i + 1) * size, :]
                ds = jnp.broadcast_to(column[0, :, h:h + 1], (length, half))
                dt0, dt1 = to_here[h:h + 1, :half], to_here[h:h + 1, half:]
                m0 = jnp.exp2(jnp.minimum(dt0 - ds[:half], 126.0)) * scores[:half]
                m1 = jnp.exp2(jnp.minimum(dt1 - ds[half:], 126.0)) * scores[half:]
                mixing = jnp.concatenate(
                    [
                        jnp.concatenate([m0.astype(bf16), corner], axis=1),
                        jnp.concatenate([corner, m1.astype(bf16)], axis=1),
                    ],
                    axis=0,
                )
                total = jnp.dot(a, mixing, preferred_element_type=f32)
                sums.append(total + carried[h * size:(h + 1) * size, :] * grown[h:h + 1, :])
                weighted[h * size:(h + 1) * size, :] = (a32 * to_end[h:h + 1, :]).astype(bf16)
                early.append((a32[:, :half] * to_middle[h:h + 1, :]).astype(bf16))
            passed = jnp.dot(
                jnp.concatenate(early, axis=0), late_scores, preferred_element_type=f32
            )
            for i in range(2):
                h = 2 * pair + i
                late = passed[i * size:(i + 1) * size, :] * past_middle[h:h + 1, :]
                sums[i] = jnp.concatenate([sums[i][:, :half], sums[i][:, half:] + late], axis=1)
            skipped = channel[taps + 1:taps + 2, lo:hi] * activated
            out[:, lo:hi] = (jnp.concatenate(sums, axis=0).T + skipped).astype(out.dtype)
        fresh = jnp.dot(weighted[...], write, preferred_element_type=f32)
        for h in range(heads):
            rows = slice(h * size, (h + 1) * size)
            old = curs[g, rows, :].astype(f32) * kept[h:h + 1, :]
            old = jnp.where(present, old, 0.0)
            final[0, rows, :] = (fresh[rows, :] + old).astype(final.dtype)


def chunk_shape(cache, conv, width):
    conv_rows = conv.shape[0] * (width // 128)
    return (cache.shape[3] + -(-conv_rows // 16) * 16, cache.shape[4])


def body(
    hidden, base_in_projection, state_input_matrix, state_output_matrix, head_step_size,
    head_decay_rate, head_skip_scale, convolution_weight, convolution_bias, adapter_down_weight,
    adapter_up_weight, adapter_home_group, adapter_group_index, state_space_cache,
    convolution_cache, prefix_holder_device, prefix_cache_slot, prefix_block_count,
):
    groups, devices = lax.axis_size("group"), lax.axis_size("dev")
    tokens, width = base_in_projection.shape
    per_group = tokens // T_REQ
    assert per_group == devices and devices & (devices - 1) == 0 == groups & (groups - 1)
    heads = head_step_size.shape[0]
    size, depth = state_space_cache.shape[2:]
    rank = adapter_down_weight.shape[1]
    taps = convolution_weight.shape[0]
    bf16, f32 = jnp.bfloat16, jnp.float32
    limit = per_group // 2
    lines = devices // 2

    cache = state_space_cache.reshape(
        state_space_cache.shape[0], lines, 2, heads * size, depth
    )
    conv = convolution_cache.transpose(1, 0, 2)
    shape = chunk_shape(cache, conv, width)
    picks = [
        jax.ShapeDtypeStruct((ACAP,) + adapter_down_weight.shape[1:], bf16)
        for _ in range(groups - 1)
    ]
    packed = pl.pallas_call(
        functools.partial(pack_kernel, groups, devices, per_group, width),
        out_shape=(
            jax.ShapeDtypeStruct(META_SHAPE, jnp.int32),
            jax.ShapeDtypeStruct((state_input_matrix.shape[0], 2 * depth), bf16),
            *picks,
            *picks,
            *[jax.ShapeDtypeStruct(shape, bf16) for _ in range(devices)],
            *[jax.ShapeDtypeStruct((lines,) + shape, bf16) for _ in range(2)],
        ),
        in_specs=smem(5) + pinned(3) + vmem(3),
        out_specs=tuple(smem(1) + vmem(1 + 2 * len(picks) + devices + 2)),
        scratch_shapes=[
            pltpu.SemaphoreType.DMA((len(picks) * ACAP,)),
            pltpu.SemaphoreType.DMA((len(picks) * ACAP,)),
            pltpu.SemaphoreType.DMA((devices,)),
            pltpu.SemaphoreType.DMA((2,)),
        ],
        cost_estimate=cost(),
        compiler_params=params(),
        name="pack",
    )(
        adapter_home_group.reshape(-1), adapter_group_index, prefix_holder_device.reshape(-1),
        prefix_cache_slot, prefix_block_count, adapter_down_weight, adapter_up_weight, cache,
        state_input_matrix, state_output_matrix, conv,
    )
    meta, rows_mine, packed = packed[0], packed[1], packed[2:]
    down_got = swap(packed[:groups - 1], groups)
    up_got = swap(packed[groups - 1:2 * groups - 2], groups)
    chunks = packed[2 * groups - 2:-2]
    rows_all = lax.all_gather(rows_mine, "dev", axis=0, tiled=True)
    zero = jnp.zeros((1,), jnp.int32)
    got = [chunks[0]] + [
        lax.ppermute(chunks[d], "dev", [(s, s ^ d) for s in range(devices)])
        for d in range(1, devices)
    ]

    rows_decay, column_decay, channel = pl.pallas_call(
        functools.partial(prep_kernel, per_group),
        out_shape=(
            jax.ShapeDtypeStruct((2 * heads, tokens), f32),
            jax.ShapeDtypeStruct((per_group, T_REQ, heads), f32),
            jax.ShapeDtypeStruct((8, width), f32),
        ),
        in_specs=smem(2) + vmem(3) + anywhere(1),
        out_specs=tuple(pl.BlockSpec(memory_space=pltpu.VMEM) for _ in range(3)),
        cost_estimate=cost(),
        compiler_params=params(),
        name="prep",
    )(
        head_decay_rate, head_skip_scale, head_step_size, convolution_weight,
        convolution_bias.reshape(1, width), meta,
    )

    each = per_group // 2
    partial_down = pl.pallas_call(
        functools.partial(shrink_kernel, groups, per_group),
        grid_spec=pltpu.PrefetchScalarGridSpec(
            num_scalar_prefetch=1,
            grid=(per_group // each,),
            in_specs=[pl.BlockSpec((each * T_REQ, hidden.shape[1]), lambda g, meta: (g, 0))]
            + pinned(groups) + anywhere(3),
            out_specs=pl.BlockSpec((each, rank, T_REQ), lambda g, meta: (g, 0, 0)),
            scratch_shapes=[
                pltpu.VMEM((per_group,) + adapter_down_weight.shape[1:], bf16),
                pltpu.SemaphoreType.DMA((per_group,)),
            ],
        ),
        out_shape=jax.ShapeDtypeStruct((per_group, rank, T_REQ), bf16),
        cost_estimate=cost(),
        compiler_params=params(),
        name="shrink",
    )(meta, hidden, adapter_down_weight, *down_got, channel, got[lines], got[1])

    parts = lax.all_to_all(partial_down, "dev", split_axis=0, concat_axis=0, tiled=True)
    summed = pl.pallas_call(
        sum_kernel,
        out_shape=jax.ShapeDtypeStruct((devices, 1, rank, T_REQ), bf16),
        in_specs=vmem(1) + anywhere(2),
        out_specs=vmem(1)[0],
        cost_estimate=cost(),
        name="sum_parts",
    )(parts.reshape(devices, 1, rank, T_REQ), got[lines + 1], up_got[groups // 2 - 1])
    shrunk = lax.all_to_all(summed, "dev", split_axis=0, concat_axis=0, tiled=True)
    shrunk = shrunk.reshape(per_group, rank, T_REQ)

    spread = spread_steps(zero, meta, packed[-2:], devices)
    next(spread)
    sent = spread.send([summed, rows_all])
    for step in range(2, lines - 1):
        sent = spread.send([up_got[-1]] if step == lines - 2 else [])
    spread_others = spread_rest(meta, cache, conv, devices, width, limit)

    outs = None
    for begin, steps in ((0, lines), (lines, lines), (devices, limit)):
        if begin == 0:
            chunks, after = got[:lines], [sent, got[lines + 2]]
        elif begin == lines:
            chunks, after = got[lines:], [spread.send([outs[2]])]
        else:
            chunks, after = [*spread.send([]), spread_others, got[0]], []

        def request(g, meta, begin=begin):
            return meta[POS_REQ, begin + g]

        in_specs = [
            pl.BlockSpec((T_REQ, width), lambda g, meta: (request(g, meta), 0)),
            pl.BlockSpec((1, rank, T_REQ), lambda g, meta: (request(g, meta), 0, 0)),
            pl.BlockSpec((8, width), lambda g, meta: (0, 0)),
            pl.BlockSpec((2 * heads, T_REQ), lambda g, meta: (0, request(g, meta))),
            pl.BlockSpec((1, T_REQ, heads), lambda g, meta: (request(g, meta), 0, 0)),
            pl.BlockSpec((T_REQ, 2 * depth), lambda g, meta: (request(g, meta), 0)),
        ] + pinned(groups + len(chunks)) + anywhere(len(after))
        operands = [
            meta, base_in_projection, shrunk, channel, rows_decay, column_decay, rows_all,
            adapter_up_weight, *up_got, *chunks, *after,
        ]
        aliases = {}
        if outs is not None:
            aliases = {len(operands): 0, len(operands) + 1: 1}
            operands += list(outs[:2])
            in_specs += anywhere(2)
        outs = pl.pallas_call(
            functools.partial(mix_kernel, groups, taps, begin, steps, begin == devices, size),
            grid_spec=pltpu.PrefetchScalarGridSpec(
                num_scalar_prefetch=1,
                grid=(steps,),
                in_specs=in_specs,
                out_specs=(
                    pl.BlockSpec((T_REQ, width), lambda g, meta: (request(g, meta), 0)),
                    pl.BlockSpec(
                        (1, heads * size, depth), lambda g, meta: (request(g, meta), 0, 0)
                    ),
                    pl.BlockSpec((8, 128), lambda g, meta: (0, 0)),
                ),
                scratch_shapes=[
                    pltpu.VMEM((T_REQ + 8, width), f32),
                    pltpu.VMEM((T_REQ, T_REQ // 2), f32),
                    pltpu.VMEM((width, T_REQ), f32),
                    pltpu.VMEM((width, T_REQ), bf16),
                    pltpu.VMEM((steps,) + adapter_up_weight.shape[1:], bf16),
                    pltpu.VMEM((steps,) + shape, bf16),
                    pltpu.SemaphoreType.DMA((steps,)),
                    pltpu.SemaphoreType.DMA((steps,)),
                ],
            ),
            out_shape=(
                jax.ShapeDtypeStruct((tokens, width), bf16),
                jax.ShapeDtypeStruct((per_group, heads * size, depth), bf16),
                jax.ShapeDtypeStruct((8, 128), f32),
            ),
            input_output_aliases=aliases,
            cost_estimate=cost(),
            compiler_params=params(),
            name=f"mix_{begin}",
        )(*operands)
    return outs[0], outs[1].reshape(per_group, heads, size, depth)


def solution(mesh):
    placed = (
        P("group", "dev"),
        P("group", "dev"),
        P(("group", "dev"), None),
        P(("group", "dev"), None),
        P("dev", "group"),
        P("dev"),
        P("dev"),
        P(None, "dev"),
        P("dev"),
        P("group", None, "dev"),
        P("group", None, "dev"),
        P(),
        P(),
        P(("group", "dev"), None, None, None),
        P(("group", "dev"), None, None),
        P(),
        P(),
        P(),
    )
    return jax.shard_map(
        body,
        mesh=mesh,
        in_specs=placed,
        out_specs=(P("group", "dev"), P("group", "dev", None, None)),
        check_vma=False,
    )
```

time: 183 us -> 213 us (1.16)
  local copies, waits for them, and re-layouts: 17 us -> 42.5 us
  starting transfers between devices: 37 us -> 45.4 us
  Pallas kernels: 61.6 us -> 56.8 us
    ppermute x7, waiting for transfers between devices: 19.9 us -> 48.9 us  [body(): lax.ppermute(chunks[d], 'dev', [(s, s ^ d) for s in range(devices)])]
    unnamed x75 -> x112, local copies, waits for them, and re-layouts: 15.5 us -> 40.9 us
    ppermute x6, waiting for transfers between devices: 19 us -> 0.02 us  [swap(): lax.ppermute(packed[k - 1], 'group', [(g, g ^ k) for g in range(groups)])]
    ppermute x7, waiting for transfers between devices: 10.1 us -> 0.02 us  [the longest x3 0.01 us: spread_steps(): lax.ppermute(to_left, 'dev', [(devices - 1 - (2 * i + x), devices - 3 - (...]
    pallas_call x11 -> x8, Pallas kernels: 58.8 us -> 54 us  [the longest x3 34.4 us: body(): pl.pallas_call(functools.partial(mix_kernel, groups, taps, begin, steps,...]
    ppermute x7, starting transfers between devices: 6.99 us -> 10.9 us  [body(): lax.ppermute(chunks[d], 'dev', [(s, s ^ d) for s in range(devices)])]
    all_to_all x1, starting transfers between devices: 6.24 us -> 8.41 us  [body(): lax.all_to_all(summed, 'dev', split_axis=0, concat_axis=0, tiled=True)]
  transfers between devices with their start and end apart: 23 -> 23, of which waited for: 9 -> 5; matrix products, arithmetic and copies ran while one was open for 1% -> 1% of each run, Pallas kernels for 16% -> 21%
where the time goes in v4:
time: 213 us; the launch traced here: 209 us
  Pallas kernels  56.8 us (27%)
  waiting for transfers between devices  49 us (23%)
  starting transfers between devices  45.4 us (21%)
  local copies, waits for them, and re-layouts  42.5 us (20%)
  between operations  14.3 us (7%)
    ppermute x7, waiting for transfers between devices, body(): lax.ppermute(chunks[d], 'dev', [(s, s ^ d) for s in range(devices)])  48.9 us
    unnamed x112, local copies, waits for them, and re-layouts  40.9 us
    pallas_call x3, Pallas kernels, body(): pl.pallas_call(functools.partial(mix_kernel, groups, taps, begin, steps,...  34.4 us
    ppermute x7, starting transfers between devices, body(): lax.ppermute(chunks[d], 'dev', [(s, s ^ d) for s in range(devices)])  10.9 us
    all_to_all x1, starting transfers between devices, body(): lax.all_to_all(summed, 'dev', split_axis=0, concat_axis=0, tiled=True)  8.41 us
    ppermute x3, starting transfers between devices, spread_steps(): lax.ppermute(to_left, 'dev', [(devices - 1 - (2 * i + x), devices - 3 - (...  7.3 us
    all_to_all x1, starting transfers between devices, body(): lax.all_to_all(partial_down, 'dev', split_axis=0, concat_axis=0, tiled=True)  7.26 us
    pallas_call x1, Pallas kernels, body(): pl.pallas_call(functools.partial(pack_kernel, groups, devices, per_group,...  6.99 us
  transfers between devices with their start and end apart: 23, of which 5 were waited for; matrix products, arithmetic and copies ran while one was open for 1% of the time, Pallas kernels for 21%

profile of v4, /device:TPU:8, one launch (start us, length us, event | category | flops | bytes accessed | tf_op | source)
XLA Modules:
  0.0 209.0 jit_solution(16038648377153999716)
XLA Ops:
  12.2 7.0 %pack.1 = (s32[16,64]{1,0:T(8,128)S(1)}, bf16[256,256]{1,0:T(8,128)(2,1)}, bf16[4,64,1024]{2,1,0:T(8,128)(2,1)}, bf16[4,64,1024]{2,1,0:T(8,128)(2,1)}, bf16[4,64...) custom-call(s32[32]{0:T(128)S(1)} %bitcast.20, ...), custom_call_target="tpu_custom_call" | custom-call | flops 1 | bytes 1 | tf_op jit(solution)/shard_map/pack/pallas_call | solution.py:629
  23.7 1.6 collective-permute-start.16
  25.3 2.6 %collective-permute-start.10 = (bf16[1056,128]{1,0:T(8,128)(2,1)}, bf16[1056,128]{1,0:T(8,128)(2,1)S(1)}, u32[]{:S(2)}, u32[]{:S(2)}) collective-permute-start(bf16[1056,128]{1,0:T(8,128)(2,1)} %get-tuple-element.173), channel_id=1, source_target_pairs={{0,4},{1,5},{2,6},{3,7},{4,0},{5,1},{6,2},{7,3},{8,12},{9,13},{10,... | collective-permute-start | bytes 811016 | tf_op jit(solution)/shard_map/ppermute | solution.py:662
  27.9 1.5 collective-permute-start.8
  29.8 13.1 %collective-permute-done.10.rest_5_.rest_4_ = bf16[1056,128]{1,0:T(8,128)(2,1)S(1)} collective-permute-done((bf16[1056,128]{1,0:T(8,128)(2,1)}, bf16[1056,128]{1,0:T(8,128)(2,1)S(1)}, u32[]{:S(2)}, u32[]{:S(2)}) %collective-permute-start.10) | collective-permute-done | bytes 270368 | tf_op jit(solution)/shard_map/ppermute | solution.py:662
  43.3 17.5 %collective-permute-done.11.rest_6_.rest_5_ = bf16[1056,128]{1,0:T(8,128)(2,1)S(1)} collective-permute-done((bf16[1056,128]{1,0:T(8,128)(2,1)S(1)}, bf16[1056,128]{1,0:T(8,128)(2,1)S(1)}, u32[]{:S(2)}, u32[]{:S(2)}) %collective-permute-start.11) | collective-permute-done | bytes 270368 | tf_op jit(solution)/shard_map/ppermute | solution.py:662
  60.8 1.6 collective-permute-start.13
  62.4 1.1 prep.1
  63.6 1.0 copy-done.6
  65.3 6.0 %shrink.1 = bf16[8,64,256]{2,1,0:T(8,128)(2,1)} custom-call(s32[16,64]{1,0:T(8,128)S(1)} %get-tuple-element.272.rest_0_.meta, bf16[2048,1024]{1,0:T(8,128)(2,1)} %hidden.1, bf16[8,64,1024]{2,1,0:T(8,128)(2,1)S(1)} %copy-done.19, bf16[4,64,1024]{2,1,0:T(8,128)(2,1)S(1)} %collective-permute-done.7.rest_1_, ...), custom_call_target="tpu_custom_call" | custom-call | flops 1 | bytes 1 | tf_op jit(solution)/shard_map/shrink/pallas_call | solution.py:684
  72.7 7.3 %all-to-all-start = ((bf16[8,64,256]{2,1,0:T(8,128)(2,1)}), bf16[8,64,256]{2,1,0:T(8,128)(2,1)}, u32[]{:S(2)}, u32[]{:S(2)}) async-start(bf16[8,64,256]{2,1,0:T(8,128)(2,1)} %shrink.1), calls=%async_computation | async-start | bytes 524288 | tf_op jit(solution)/shard_map/all_to_all | solution.py:703
  80.0 3.3 %collective-permute-start.12 = (bf16[1056,128]{1,0:T(8,128)(2,1)}, bf16[1056,128]{1,0:T(8,128)(2,1)S(1)}, u32[]{:S(2)}, u32[]{:S(2)}) collective-permute-start(bf16[1056,128]{1,0:T(8,128)(2,1)} %copy-done.55), channel_id=1, source_target_pairs={{0,5},{1,4},{2,7},{3,6},{4,1},{5,0},{6,3},{7,2},{8,13},{9,12},{10,... | collective-permute-start | bytes 811016 | tf_op jit(solution)/shard_map/ppermute | solution.py:662
  83.2 10.8 %collective-permute-done.12.rest_0_.rest_5_ = bf16[1056,128]{1,0:T(8,128)(2,1)S(1)} collective-permute-done((bf16[1056,128]{1,0:T(8,128)(2,1)}, bf16[1056,128]{1,0:T(8,128)(2,1)S(1)}, u32[]{:S(2)}, u32[]{:S(2)}) %collective-permute-start.12) | collective-permute-done | bytes 270368 | tf_op jit(solution)/shard_map/ppermute | solution.py:662
  94.9 1.7 sum_parts.1.rest_0_
  96.7 1.6 copy-done.3
  98.3 1.6 pick_1.8
  99.8 1.3 collective-permute-start.17
  101.1 1.4 collective-permute-start.18
  102.5 1.0 collective-permute-start.23
  103.5 8.4 %all-to-all-start.1 = ((bf16[8,1,64,256]{3,2,1,0:T(8,128)(2,1)}), bf16[8,1,64,256]{3,2,1,0:T(8,128)(2,1)S(1)}, u32[]{:S(2)}, u32[]{:S(2)}) async-start(bf16[8,1,64,256]{3,2,1,0:T(8,128)(2,1)} %sum_parts.1.rest_0_), calls=%async_computation.1 | async-start | bytes 524288 | tf_op jit(solution)/shard_map/all_to_all | solution.py:712
  113.4 2.9 %collective-permute-start.22 = (bf16[1056,128]{1,0:T(8,128)(2,1)}, bf16[1056,128]{1,0:T(8,128)(2,1)S(1)}, u32[]{:S(2)}, u32[]{:S(2)}) collective-permute-start(bf16[1056,128]{1,0:T(8,128)(2,1)} %copy-done.53), channel_id=1, source_target_pairs={{0,3},{1,2},{2,1},{3,0},{4,7},{5,6},{6,5},{7,4},{8,11},{9,10},{10,... | collective-permute-start | bytes 811016 | tf_op jit(solution)/shard_map/ppermute | solution.py:662
  116.4 1.0 copy-done.15
  117.4 1.0 copy-done.38
  118.3 2.5 %pick_2.8 = (bf16[1056,128]{1,0:T(8,128)(2,1)}, bf16[1056,128]{1,0:T(8,128)(2,1)}) custom-call(s32[1]{0:T(128)} %constant.32.clone.1.j, s32[16,64]{1,0:T(8,128)S(1)} %get-tuple-element.272.rest_0_.meta, bf16[4,1056,128]{2,1,0:T(8,128)(2,1)S(1)} %copy-done, bf16[4,1056,128]{2,1,0:T(8,128)(2,1)S(1)} %collective-permute-done.16.over_r.over_l.rest_5_, ...), custom_call_target="tpu_custom_call" | custom-call | flops 1 | bytes 1 | tf_op jit(solution)/shard_map/pick_2/pallas_call | solution.py:318
  120.8 3.4 %collective-permute-start.19 = (bf16[1056,128]{1,0:T(8,128)(2,1)}, bf16[1056,128]{1,0:T(8,128)(2,1)}, u32[]{:S(2)}, u32[]{:S(2)}) collective-permute-start(bf16[1056,128]{1,0:T(8,128)(2,1)} %get-tuple-element.186.rest_8_), channel_id=1, source_target_pairs={{0,2},{1,3},{2,4},{3,5},{8,10},{9,11},{10,12},{11,13},{16,18},{17,... | collective-permute-start | bytes 811016 | tf_op jit(solution)/shard_map/ppermute | solution.py:328
  124.2 1.3 collective-permute-start.20
  125.5 2.7 %collective-permute-done.21.rest_6_ = bf16[1056,128]{1,0:T(8,128)(2,1)S(1)} collective-permute-done((bf16[1056,128]{1,0:T(8,128)(2,1)}, bf16[1056,128]{1,0:T(8,128)(2,1)S(1)}, u32[]{:S(2)}, u32[]{:S(2)}) %collective-permute-start.21) | collective-permute-done | bytes 270368 | tf_op jit(solution)/shard_map/ppermute | solution.py:662
  129.5 4.8 %collective-permute-done.22.rest_7_ = bf16[1056,128]{1,0:T(8,128)(2,1)S(1)} collective-permute-done((bf16[1056,128]{1,0:T(8,128)(2,1)}, bf16[1056,128]{1,0:T(8,128)(2,1)S(1)}, u32[]{:S(2)}, u32[]{:S(2)}) %collective-permute-start.22) | collective-permute-done | bytes 270368 | tf_op jit(solution)/shard_map/ppermute | solution.py:662
  135.0 1.2 copy-done.7
  136.3 1.0 copy-done.11
  137.3 1.0 copy-done.16
  141.2 1.0 copy-done.34
  142.2 1.0 copy-done.36
  143.1 15.6 %mix_0.1 = (bf16[2048,1024]{1,0:T(8,128)(2,1)}, bf16[8,1024,128]{2,1,0:T(8,128)(2,1)}, f32[8,128]{1,0:T(8,128)S(1)}) custom-call(s32[16,64]{1,0:T(8,128)S(1)} %get-tuple-element.272.rest_0_.meta, bf16[2048,1024]{1,0:T(8,128)(2,1)} %base.5, bf16[8,64,256]{2,1,0:T(8,128)(2,1)S(1)} %bitcast.16, f32[8,1024]{1,0:T(8,128)S(1)} %get-tuple-element.172.rest_4_.channel, ...), custom_call_target="tpu_custom_call" | custom-call | flops 1 | bytes 1 | tf_op jit(solution)/shard_map/mix_0/pallas_call | solution.py:751
  158.8 2.5 %pick_3.8 = (bf16[1056,128]{1,0:T(8,128)(2,1)}, bf16[1056,128]{1,0:T(8,128)(2,1)}) custom-call(s32[1]{0:T(128)} %constant.32.clone.1.j, s32[16,64]{1,0:T(8,128)S(1)} %get-tuple-element.272.rest_0_.meta, bf16[4,1056,128]{2,1,0:T(8,128)(2,1)S(1)} %copy-done, bf16[4,1056,128]{2,1,0:T(8,128)(2,1)S(1)} %collective-permute-done.16.over_r.over_l.rest_5_, ...), custom_call_target="tpu_custom_call" | custom-call | flops 1 | bytes 1 | tf_op jit(solution)/shard_map/pick_3/pallas_call | solution.py:318
  161.3 1.9 collective-permute-start.24
  163.2 4.6 %collective-permute-start.25 = (bf16[1056,128]{1,0:T(8,128)(2,1)}, bf16[1056,128]{1,0:T(8,128)(2,1)}, u32[]{:S(2)}, u32[]{:S(2)}) collective-permute-start(bf16[1056,128]{1,0:T(8,128)(2,1)} %get-tuple-element.194), channel_id=1, source_target_pairs={{7,5},{6,4},{5,3},{4,2},{3,1},{2,0},{15,13},{14,12},{13,11},{12,10... | collective-permute-start | bytes 811016 | tf_op jit(solution)/shard_map/ppermute | solution.py:332
  168.4 1.2 copy-done.8
  169.7 1.0 copy-done.12
  170.7 1.0 copy-done.17
  174.6 12.4 %mix_4.1 = (bf16[2048,1024]{1,0:T(8,128)(2,1)}, bf16[8,1024,128]{2,1,0:T(8,128)(2,1)}, f32[8,128]{1,0:T(8,128)}) custom-call(s32[16,64]{1,0:T(8,128)S(1)} %get-tuple-element.272.rest_0_.meta, bf16[2048,1024]{1,0:T(8,128)(2,1)} %base.5, bf16[8,64,256]{2,1,0:T(8,128)(2,1)S(1)} %bitcast.17, ...), custom_call_target="tpu_custom_call", output_to_operand_aliasing={{0}: (16, {}), {1}: (17, {})} | custom-call | flops 1 | bytes 1 | tf_op jit(solution)/shard_map/mix_4/pallas_call | solution.py:751
  187.0 1.0 broadcast_in_dim.12
  188.0 1.0 while.14
  189.3 1.2 copy-done.5
  190.5 1.2 copy-done.9
  191.7 1.0 copy-done.13
  192.8 1.0 copy-done.18
  195.7 6.4 %mix_8.1 = (bf16[2048,1024]{1,0:T(8,128)(2,1)}, bf16[8,1024,128]{2,1,0:T(8,128)(2,1)}, f32[8,128]{1,0:T(8,128)}) custom-call(s32[16,64]{1,0:T(8,128)S(1)} %get-tuple-element.330, bf16[2048,1024]{1,0:T(8,128)(2,1)} %base.5, bf16[8,64,256]{2,1,0:T(8,128)(2,1)S(1)} %bitcast.18, ...), custom_call_target="tpu_custom_call", output_to_operand_aliasing={{0}: (17, {}), {1}: (18, {})} | custom-call | flops 1 | bytes 1 | tf_op jit(solution)/shard_map/mix_8/pallas_call | solution.py:751
  (124 shorter events, 25.4 us)
Async XLA Ops:
  7.2 89.5 %all-gather.2.cloned.1.call-start = ((), (), s32[]{:S(2)}) async-start(), calls=%async_computation.2 | async-start | bytes 1179648 | tf_op jit(solution)/shard_map/all_gather | solution.py:659
  12.2 50.2 %copy-start.39 = (f32[16,2048]{1,0:T(8,128)S(1)}, f32[16,2048]{1,0:T(8,128)}, u32[]{:S(2)}) copy-start(f32[16,2048]{1,0:T(8,128)} %steps.1) | copy-start | bytes 393220
  12.2 50.2 %copy-start.42 = (f32[4,1024]{1,0:T(4,128)S(1)}, f32[4,1024]{1,0:T(4,128)}, u32[]{:S(2)}) copy-start(f32[4,1024]{1,0:T(4,128)} %taps_in.1) | copy-start | bytes 49156
  12.2 50.2 %copy-start.43 = (f32[1024]{0:T(1024)S(1)}, f32[1024]{0:T(1024)}, u32[]{:S(2)}) copy-start(f32[1024]{0:T(1024)} %param.28) | copy-start | bytes 12292
  12.2 50.2 %copy-start.49 = (f32[16]{0:T(128)S(1)}, f32[16]{0:T(128)}, u32[]{:S(2)}) copy-start(f32[16]{0:T(128)} %rates.1) | copy-start | bytes 196
  12.2 50.2 %copy-start.50 = (f32[16]{0:T(128)S(1)}, f32[16]{0:T(128)}, u32[]{:S(2)}) copy-start(f32[16]{0:T(128)} %skips.1) | copy-start | bytes 196
  12.2 53.1 %copy-start.19 = (bf16[8,64,1024]{2,1,0:T(8,128)(2,1)S(1)}, bf16[8,64,1024]{2,1,0:T(8,128)(2,1)}, u32[]{:S(2)}) copy-start(bf16[8,64,1024]{2,1,0:T(8,128)(2,1)} %rest_0_.4) | copy-start | bytes 3145732
  23.7 72.9 %collective-permute-start.16 = (bf16[4,1056,128]{2,1,0:T(8,128)(2,1)}, bf16[4,1056,128]{2,1,0:T(8,128)(2,1)S(1)}, u32[]{:S(2)}, u32[]{:S(2)}) collective-permute-start(bf16[4,1056,128]{2,1,0:T(8,128)(2,1)} %get-tuple-element.183), channel_id=1, source_target_pairs={{0,1},{1,0},{2,3},{3,2},{4,5},{5,4},{6,7},{7,6},{8,9},{9,8},{10,11... | collective-permute-start | bytes 3244040 | tf_op jit(solution)/shard_map/ppermute | solution.py:300
  25.3 17.5 %collective-permute-start.10 = (bf16[1056,128]{1,0:T(8,128)(2,1)}, bf16[1056,128]{1,0:T(8,128)(2,1)S(1)}, u32[]{:S(2)}, u32[]{:S(2)}) collective-permute-start(bf16[1056,128]{1,0:T(8,128)(2,1)} %get-tuple-element.173), channel_id=1, source_target_pairs={{0,4},{1,5},{2,6},{3,7},{4,0},{5,1},{6,2},{7,3},{8,12},{9,13},{10,... | collective-permute-start | bytes 811016 | tf_op jit(solution)/shard_map/ppermute | solution.py:662
  27.9 37.4 %collective-permute-start.7 = (bf16[4,64,1024]{2,1,0:T(8,128)(2,1)}, bf16[4,64,1024]{2,1,0:T(8,128)(2,1)S(1)}, u32[]{:S(2)}, u32[]{:S(2)}) collective-permute-start(bf16[4,64,1024]{2,1,0:T(8,128)(2,1)} %get-tuple-element.169), channel_id=1, source_target_pairs={{0,8},{8,0},{16,24},{24,16},{1,9},{9,1},{17,25},{25,17},{2,10},{10... | collective-permute-start | bytes 1572872 | tf_op jit(solution)/shard_map/ppermute | solution.py:162
  27.9 37.4 %collective-permute-start.8 = (bf16[4,64,1024]{2,1,0:T(8,128)(2,1)}, bf16[4,64,1024]{2,1,0:T(8,128)(2,1)S(1)}, u32[]{:S(2)}, u32[]{:S(2)}) collective-permute-start(bf16[4,64,1024]{2,1,0:T(8,128)(2,1)} %get-tuple-element.170), channel_id=1, source_target_pairs={{0,16},{8,24},{16,0},{24,8},{1,17},{9,25},{17,1},{25,9},{2,18},{10... | collective-permute-start | bytes 1572872 | tf_op jit(solution)/shard_map/ppermute | solution.py:162
  29.4 35.9 %collective-permute-start.9 = (bf16[4,64,1024]{2,1,0:T(8,128)(2,1)}, bf16[4,64,1024]{2,1,0:T(8,128)(2,1)S(1)}, u32[]{:S(2)}, u32[]{:S(2)}) collective-permute-start(bf16[4,64,1024]{2,1,0:T(8,128)(2,1)} %get-tuple-element.171), channel_id=1, source_target_pairs={{0,24},{8,16},{16,8},{24,0},{1,25},{9,17},{17,9},{25,1},{2,26},{10... | collective-permute-start | bytes 1572872 | tf_op jit(solution)/shard_map/ppermute | solution.py:162
  42.8 18.0 %collective-permute-start.11 = (bf16[1056,128]{1,0:T(8,128)(2,1)S(1)}, bf16[1056,128]{1,0:T(8,128)(2,1)S(1)}, u32[]{:S(2)}, u32[]{:S(2)}) collective-permute-start(bf16[1056,128]{1,0:T(8,128)(2,1)S(1)} %get-tuple-element.174), channel_id=1, source_target_pairs={{0,1},{1,0},{2,3},{3,2},{4,5},{5,4},{6,7},{7,6},{8,9},{9,8},{10,11... | collective-permute-start | bytes 811016 | tf_op jit(solution)/shard_map/ppermute | solution.py:662
  60.8 33.2 %collective-permute-start.13 = (bf16[4,64,1024]{2,1,0:T(8,128)(2,1)}, bf16[4,64,1024]{2,1,0:T(8,128)(2,1)S(1)}, u32[]{:S(2)}, u32[]{:S(2)}) collective-permute-start(bf16[4,64,1024]{2,1,0:T(8,128)(2,1)} %copy-done.52), channel_id=1, source_target_pairs={{0,16},{8,24},{16,0},{24,8},{1,17},{9,25},{17,1},{25,9},{2,18},{10... | collective-permute-start | bytes 1572872 | tf_op jit(solution)/shard_map/ppermute | solution.py:162
  63.5 1.0 copy-start.6
  72.7 23.9 %copy-start = (bf16[4,1056,128]{2,1,0:T(8,128)(2,1)S(1)}, bf16[4,1056,128]{2,1,0:T(8,128)(2,1)}, u32[]{:S(2)}) copy-start(bf16[4,1056,128]{2,1,0:T(8,128)(2,1)} %get-tuple-element.182.own_r.own_l.rest_4_) | copy-start | bytes 3244036
  72.7 21.3 %all-to-all-start = ((bf16[8,64,256]{2,1,0:T(8,128)(2,1)}), bf16[8,64,256]{2,1,0:T(8,128)(2,1)}, u32[]{:S(2)}, u32[]{:S(2)}) async-start(bf16[8,64,256]{2,1,0:T(8,128)(2,1)} %shrink.1), calls=%async_computation | async-start | bytes 524288 | tf_op jit(solution)/shard_map/all_to_all | solution.py:703
  80.0 14.0 %collective-permute-start.12 = (bf16[1056,128]{1,0:T(8,128)(2,1)}, bf16[1056,128]{1,0:T(8,128)(2,1)S(1)}, u32[]{:S(2)}, u32[]{:S(2)}) collective-permute-start(bf16[1056,128]{1,0:T(8,128)(2,1)} %copy-done.55), channel_id=1, source_target_pairs={{0,5},{1,4},{2,7},{3,6},{4,1},{5,0},{6,3},{7,2},{8,13},{9,12},{10,... | collective-permute-start | bytes 811016 | tf_op jit(solution)/shard_map/ppermute | solution.py:662
  83.2 28.6 %collective-permute-start.15 = (bf16[4,64,1024]{2,1,0:T(8,128)(2,1)}, bf16[4,64,1024]{2,1,0:T(8,128)(2,1)S(1)}, u32[]{:S(2)}, u32[]{:S(2)}) collective-permute-start(bf16[4,64,1024]{2,1,0:T(8,128)(2,1)} %copy-done.51), channel_id=1, source_target_pairs={{0,24},{8,16},{16,8},{24,0},{1,25},{9,17},{17,9},{25,1},{2,26},{10... | collective-permute-start | bytes 1572872 | tf_op jit(solution)/shard_map/ppermute | solution.py:162
  96.6 62.1 %copy-start.1 = (bf16[4,1056,128]{2,1,0:T(8,128)(2,1)}, bf16[4,1056,128]{2,1,0:T(8,128)(2,1)S(1)}, u32[]{:S(2)}) copy-start(bf16[4,1056,128]{2,1,0:T(8,128)(2,1)S(1)} %collective-permute-done.16.over_r.over_l.rest_5_) | copy-start | bytes 3244036
  96.7 1.6 copy-start.3
  99.8 12.9 %collective-permute-start.17 = (bf16[1056,128]{1,0:T(8,128)(2,1)}, bf16[1056,128]{1,0:T(8,128)(2,1)S(1)}, u32[]{:S(2)}, u32[]{:S(2)}) collective-permute-start(bf16[1056,128]{1,0:T(8,128)(2,1)} %get-tuple-element.184), channel_id=1, source_target_pairs={{0,2},{1,3},{8,10},{9,11},{16,18},{17,19},{24,26},{25,27}} | collective-permute-start | bytes 811016 | tf_op jit(solution)/shard_map/ppermute | solution.py:328
  101.1 15.2 %collective-permute-start.18 = (bf16[1056,128]{1,0:T(8,128)(2,1)}, bf16[1056,128]{1,0:T(8,128)(2,1)}, u32[]{:S(2)}, u32[]{:S(2)}) collective-permute-start(bf16[1056,128]{1,0:T(8,128)(2,1)} %get-tuple-element.185), channel_id=1, source_target_pairs={{7,5},{6,4},{15,13},{14,12},{23,21},{22,20},{31,29},{30,28}} | collective-permute-start | bytes 811016 | tf_op jit(solution)/shard_map/ppermute | solution.py:332
  102.5 21.7 %collective-permute-start.23 = (bf16[1056,128]{1,0:T(8,128)(2,1)}, bf16[1056,128]{1,0:T(8,128)(2,1)}, u32[]{:S(2)}, u32[]{:S(2)}) collective-permute-start(bf16[1056,128]{1,0:T(8,128)(2,1)} %get-tuple-element.191), channel_id=1, source_target_pairs={{0,6},{1,7},{2,4},{3,5},{4,2},{5,3},{6,0},{7,1},{8,14},{9,15},{10,... | collective-permute-start | bytes 811016 | tf_op jit(solution)/shard_map/ppermute | solution.py:662
  103.5 31.5 %collective-permute-start.14 = (bf16[4,64,1024]{2,1,0:T(8,128)(2,1)}, bf16[4,64,1024]{2,1,0:T(8,128)(2,1)}, u32[]{:S(2)}, u32[]{:S(2)}) collective-permute-start(bf16[4,64,1024]{2,1,0:T(8,128)(2,1)} %get-tuple-element.180), channel_id=1, source_target_pairs={{0,8},{8,0},{16,24},{24,16},{1,9},{9,1},{17,25},{25,17},{2,10},{10... | collective-permute-start | bytes 1572872 | tf_op jit(solution)/shard_map/ppermute | solution.py:162
  103.5 31.5 %all-to-all-start.1 = ((bf16[8,1,64,256]{3,2,1,0:T(8,128)(2,1)}), bf16[8,1,64,256]{3,2,1,0:T(8,128)(2,1)S(1)}, u32[]{:S(2)}, u32[]{:S(2)}) async-start(bf16[8,1,64,256]{3,2,1,0:T(8,128)(2,1)} %sum_parts.1.rest_0_), calls=%async_computation.1 | async-start | bytes 524288 | tf_op jit(solution)/shard_map/all_to_all | solution.py:712
  112.7 15.5 %collective-permute-start.21 = (bf16[1056,128]{1,0:T(8,128)(2,1)}, bf16[1056,128]{1,0:T(8,128)(2,1)S(1)}, u32[]{:S(2)}, u32[]{:S(2)}) collective-permute-start(bf16[1056,128]{1,0:T(8,128)(2,1)} %copy-done.54), channel_id=1, source_target_pairs={{0,2},{1,3},{2,0},{3,1},{4,6},{5,7},{6,4},{7,5},{8,10},{9,11},{10,... | collective-permute-start | bytes 811016 | tf_op jit(solution)/shard_map/ppermute | solution.py:662
  113.4 21.6 %copy-start.4 = (bf16[2048,256]{1,0:T(8,128)(2,1)S(1)}, bf16[2048,256]{1,0:T(8,128)(2,1)}, u32[]{:S(2)}) copy-start(bf16[2048,256]{1,0:T(8,128)(2,1)} %all-gather.2.cloned.1.call-done.rest_1_.rows_in) | copy-start | bytes 3145732
  113.4 20.9 %collective-permute-start.22 = (bf16[1056,128]{1,0:T(8,128)(2,1)}, bf16[1056,128]{1,0:T(8,128)(2,1)S(1)}, u32[]{:S(2)}, u32[]{:S(2)}) collective-permute-start(bf16[1056,128]{1,0:T(8,128)(2,1)} %copy-done.53), channel_id=1, source_target_pairs={{0,3},{1,2},{2,1},{3,0},{4,7},{5,6},{6,5},{7,4},{8,11},{9,10},{10,... | collective-permute-start | bytes 811016 | tf_op jit(solution)/shard_map/ppermute | solution.py:662
  116.4 1.0 copy-start.15
  117.4 1.0 copy-start.38
  120.8 37.9 %collective-permute-start.19 = (bf16[1056,128]{1,0:T(8,128)(2,1)}, bf16[1056,128]{1,0:T(8,128)(2,1)}, u32[]{:S(2)}, u32[]{:S(2)}) collective-permute-start(bf16[1056,128]{1,0:T(8,128)(2,1)} %get-tuple-element.186.rest_8_), channel_id=1, source_target_pairs={{0,2},{1,3},{2,4},{3,5},{8,10},{9,11},{10,12},{11,13},{16,18},{17,... | collective-permute-start | bytes 811016 | tf_op jit(solution)/shard_map/ppermute | solution.py:328
  124.2 34.5 %collective-permute-start.20 = (bf16[1056,128]{1,0:T(8,128)(2,1)}, bf16[1056,128]{1,0:T(8,128)(2,1)}, u32[]{:S(2)}, u32[]{:S(2)}) collective-permute-start(bf16[1056,128]{1,0:T(8,128)(2,1)} %get-tuple-element.187), channel_id=1, source_target_pairs={{7,5},{6,4},{5,3},{4,2},{15,13},{14,12},{13,11},{12,10},{23,21},{2... | collective-permute-start | bytes 811016 | tf_op jit(solution)/shard_map/ppermute | solution.py:332
  128.9 39.5 %collective-permute-start.26 = (bf16[1056,128]{1,0:T(8,128)(2,1)}, bf16[1056,128]{1,0:T(8,128)(2,1)}, u32[]{:S(2)}, u32[]{:S(2)}) collective-permute-start(bf16[1056,128]{1,0:T(8,128)(2,1)} %get-tuple-element.196), channel_id=1, source_target_pairs={{0,7},{1,6},{2,5},{3,4},{4,3},{5,2},{6,1},{7,0},{8,15},{9,14},{10,... | collective-permute-start | bytes 811016 | tf_op jit(solution)/shard_map/ppermute | solution.py:662
  135.0 1.2 copy-start.7
  136.3 1.0 copy-start.11
  137.3 1.0 copy-start.16
  139.3 1.0 copy-start.25
  161.3 27.7 %collective-permute-start.24 = (bf16[1056,128]{1,0:T(8,128)(2,1)}, bf16[1056,128]{1,0:T(8,128)(2,1)}, u32[]{:S(2)}, u32[]{:S(2)}) collective-permute-start(bf16[1056,128]{1,0:T(8,128)(2,1)} %get-tuple-element.193.rest_8_), channel_id=1, source_target_pairs={{0,2},{1,3},{2,4},{3,5},{4,6},{5,7},{8,10},{9,11},{10,12},{11,13},... | collective-permute-start | bytes 811016 | tf_op jit(solution)/shard_map/ppermute | solution.py:328
  163.2 25.8 %collective-permute-start.25 = (bf16[1056,128]{1,0:T(8,128)(2,1)}, bf16[1056,128]{1,0:T(8,128)(2,1)}, u32[]{:S(2)}, u32[]{:S(2)}) collective-permute-start(bf16[1056,128]{1,0:T(8,128)(2,1)} %get-tuple-element.194), channel_id=1, source_target_pairs={{7,5},{6,4},{5,3},{4,2},{3,1},{2,0},{15,13},{14,12},{13,11},{12,10... | collective-permute-start | bytes 811016 | tf_op jit(solution)/shard_map/ppermute | solution.py:332
  168.4 1.2 copy-start.8
  169.7 1.0 copy-start.12
  170.7 1.0 copy-start.17
  188.0 1.2 copy-start.2
  189.3 1.2 copy-start.5
  190.5 1.2 copy-start.9
  191.7 1.0 copy-start.13
  192.8 1.0 copy-start.18
  (31 other events, 24.7 us)
Sparse Core Ops, SparseCore 0:
  23.9 45.9 all-gather.1

commit v5 on v4

--- a/solution.py
+++ b/solution.py
@@ -16,13 +16,13 @@
 TN = (((0,), (0,)), ((), ()))
 VMEM_LIMIT = 48 * 1024 * 1024
 
-DIST, ARANK, AINDEX, PRESENT, POS_REQ, POS_VALID, OSLOT, OHOLDER, MISC, SEND = range(10)
-MOST, ME, SLOT, SPREAD = range(4)
+HOME, DIST, ARANK, AINDEX, PRESENT, POS_REQ, POS_VALID, OSLOT, OHOLDER, MISC, SEND = range(11)
+MOST, ME, SLOT = range(3)
 META_SHAPE = (16, 64)
 
 
 def cost():
-    return pl.CostEstimate(flops=1, bytes_accessed=1, transcendentals=0)
+    return pl.CostEstimate(flops=0, bytes_accessed=1 << 16, transcendentals=0)
 
 
 def params():
@@ -72,12 +72,12 @@
 
     homes = [home[first + q] for q in range(per_group)]
     for q, rank in enumerate(ranks_of(homes)):
-        own = homes[q] == my_group
+        meta[HOME, q] = homes[q]
         meta[DIST, q] = lax.bitwise_xor(homes[q], my_group)
-        meta[ARANK, q] = jnp.where(own, 0, rank)
-        meta[AINDEX, q] = jnp.where(own, index[first + q], 0)
+        meta[ARANK, q] = rank
+        meta[AINDEX, q] = index[first + q]
         meta[PRESENT, q] = as_int(blocks[first + q] > 0)
-    for k in range(1, groups):
+    for k in range(groups):
         theirs = lax.bitwise_xor(my_group, k) * per_group
         seen = jnp.int32(0)
         chosen = [jnp.int32(0) for _ in range(ACAP)]
@@ -88,7 +88,7 @@
                 chosen[c] = jnp.where(hit & (seen == c), value, chosen[c])
             seen = seen + as_int(hit)
         for c in range(ACAP):
-            meta[SEND, (k - 1) * ACAP + c] = chosen[c]
+            meta[SEND, k * ACAP + c] = chosen[c]
 
     holders = [holder[first + q] for q in range(per_group)]
     ranks = ranks_of(holders)
@@ -115,7 +115,7 @@
         meta[POS_VALID, d] = as_int(request >= 0)
         requests.append(request)
     requests += [meta[POS_REQ, devices + j] for j in range(limit)]
-    for begin, end in ((0, devices // 2), (devices // 2, devices)):
+    for begin, end in ((0, devices // 2), (devices // 2, devices + limit)):
         last = jnp.int32(-1)
         filled = []
         for p in range(begin, end):
@@ -125,13 +125,6 @@
         for p in reversed(range(begin, end)):
             following = jnp.where(filled[p - begin] >= 0, filled[p - begin], following)
             meta[POS_REQ, p] = following
-    meta[MISC, SPREAD] = as_int(count > 0)
-    meta[POS_VALID, devices] = jnp.int32(1)
-    for j in range(limit):
-        meta[POS_REQ, devices + j] = jnp.where(
-            j < count, requests[devices + j],
-            jnp.where(count > 0, meta[POS_REQ, devices + max(j - 1, 0)], requests[0]),
-        )
     most = jnp.int32(0)
     for g in range(groups):
         labels = [holder[g * per_group + q] for q in range(per_group)]
@@ -146,12 +139,14 @@
 
 def start_adapters(groups, meta, table, outs, sems):
     copies = []
-    for k in reversed(range(1, groups)):
+    for k in reversed(range(groups) if len(outs) == 1 else range(1, groups)):
         for c in range(ACAP):
-            chosen = meta[SEND, (k - 1) * ACAP + c]
-            copy = pltpu.make_async_copy(
-                table.at[chosen], outs[k - 1].at[c], sems.at[(k - 1) * ACAP + c]
-            )
+            chosen = meta[SEND, k * ACAP + c]
+            if len(outs) == 1:
+                out = outs[0].at[lax.bitwise_xor(lax.axis_index("group"), k), c]
+            else:
+                out = outs[k - 1].at[c]
+            copy = pltpu.make_async_copy(table.at[chosen], out, sems.at[k * ACAP + c])
             copy.start()
             copies.append(copy)
     return copies
@@ -213,7 +208,7 @@
     groups, devices, per_group, width, home, index, holder, slot, blocks, down, up, cache, write,
     read, conv, meta, rows_out, *rest
 ):
-    downs, rest = rest[:groups - 1], rest[groups - 1:]
+    downs, rest = rest[:1], rest[1:]
     ups, rest = rest[:groups - 1], rest[groups - 1:]
     chunks, (across, own, down_sems, up_sems, chunk_sems, across_sems) = (
         rest[:devices], rest[devices:]
@@ -398,19 +393,21 @@
             pltpu.make_async_copy(tables[k].at[row], out, sem).start()
 
 
-def shrink_kernel(groups, per_group, meta, hidden, *rest):
-    tables, (out, picked, sems) = rest[:groups], rest[-3:]
+def shrink_kernel(per_group, meta, hidden, table, *rest):
+    out, picked, sems = rest[-3:]
     g = pl.program_id(0)
     each = out.shape[0]
 
     @pl.when(g == 0)
     def _():
         for r in range(per_group):
-            fetch_table(groups, meta, r, tables, picked.at[r], sems.at[r])
+            pltpu.make_async_copy(
+                table.at[meta[HOME, r], meta[ARANK, r]], picked.at[r], sems.at[r]
+            ).start()
 
     for i in range(each):
         r = g * each + i
-        pltpu.make_async_copy(tables[0].at[0], picked.at[r], sems.at[r]).wait()
+        pltpu.make_async_copy(table.at[0, 0], picked.at[r], sems.at[r]).wait()
     for i in range(each):
         part = lax.dot_general(
             hidden[i * T_REQ:(i + 1) * T_REQ, :], picked[g * each + i], NT,
@@ -466,12 +463,12 @@
 
 
 def mix_kernel(
-    groups, taps, begin, steps, spread, size, meta, base, shrunk, channel, rows_decay, column,
+    groups, taps, begin, steps, direct, size, meta, base, shrunk, channel, rows_decay, column,
     rows_in, *rest
 ):
     tables, chunks = rest[:groups], rest[groups:]
-    out, final, done, extended, scores, carried, weighted, ups, curs, table_sems, chunk_sems = (
-        rest[-11:]
+    out, final, extended, scores, carried, weighted, ups, curs, table_sems, chunk_sems = (
+        rest[-10:]
     )
     g = pl.program_id(0)
     position = begin + g
@@ -484,8 +481,6 @@
     parts = width // 128
     f32, bf16 = jnp.float32, jnp.bfloat16
 
-    done[...] = jnp.zeros_like(done)
-
     def fetch_chunk(source, i):
         pltpu.make_async_copy(source, curs.at[i], chunk_sems.at[i]).start()
 
@@ -496,22 +491,19 @@
             def _(i=i):
                 request = meta[POS_REQ, begin + i]
                 fetch_table(groups, meta, request, tables, ups.at[i], table_sems.at[i])
-                if not spread:
+                if i < direct:
                     fetch_chunk(chunks[i], i)
-                elif i > 0:
-                    fetch_chunk(chunks[4].at[i - 1], i)
+                elif i > direct:
+                    fetch_chunk(chunks[direct + 4].at[i - direct - 1], i)
                 else:
                     line = meta[MISC, ME] // 2
-                    candidates = [
-                        chunks[0].at[line], chunks[1].at[line], chunks[2], chunks[3], chunks[5]
-                    ]
-                    which = jnp.where(
-                        meta[MISC, SPREAD] > 0, which_candidate(meta, meta[OHOLDER, 0]), 4
-                    )
+                    own, across, from_left, from_right = chunks[direct:direct + 4]
+                    candidates = [own.at[line], across.at[line], from_left, from_right]
+                    which = which_candidate(meta, meta[OHOLDER, 0])
                     for k, candidate in enumerate(candidates):
                         @pl.when(which == k)
                         def _(candidate=candidate):
-                            fetch_chunk(candidate, 0)
+                            fetch_chunk(candidate, direct)
 
     @pl.when(meta[POS_VALID, position] > 0)
     def _():
@@ -631,16 +623,16 @@
         out_shape=(
             jax.ShapeDtypeStruct(META_SHAPE, jnp.int32),
             jax.ShapeDtypeStruct((state_input_matrix.shape[0], 2 * depth), bf16),
-            *picks,
+            jax.ShapeDtypeStruct((groups, ACAP) + adapter_down_weight.shape[1:], bf16),
             *picks,
             *[jax.ShapeDtypeStruct(shape, bf16) for _ in range(devices)],
             *[jax.ShapeDtypeStruct((lines,) + shape, bf16) for _ in range(2)],
         ),
         in_specs=smem(5) + pinned(3) + vmem(3),
-        out_specs=tuple(smem(1) + vmem(1 + 2 * len(picks) + devices + 2)),
+        out_specs=tuple(smem(1) + vmem(2 + len(picks) + devices + 2)),
         scratch_shapes=[
-            pltpu.SemaphoreType.DMA((len(picks) * ACAP,)),
-            pltpu.SemaphoreType.DMA((len(picks) * ACAP,)),
+            pltpu.SemaphoreType.DMA((groups * ACAP,)),
+            pltpu.SemaphoreType.DMA((groups * ACAP,)),
             pltpu.SemaphoreType.DMA((devices,)),
             pltpu.SemaphoreType.DMA((2,)),
         ],
@@ -653,15 +645,17 @@
         state_input_matrix, state_output_matrix, conv,
     )
     meta, rows_mine, packed = packed[0], packed[1], packed[2:]
-    down_got = swap(packed[:groups - 1], groups)
-    up_got = swap(packed[groups - 1:2 * groups - 2], groups)
-    chunks = packed[2 * groups - 2:-2]
+    down_got = lax.all_to_all(packed[0], "group", split_axis=0, concat_axis=0, tiled=True)
+    chunks = packed[groups:-2]
     rows_all = lax.all_gather(rows_mine, "dev", axis=0, tiled=True)
     zero = jnp.zeros((1,), jnp.int32)
     got = [chunks[0]] + [
         lax.ppermute(chunks[d], "dev", [(s, s ^ d) for s in range(devices)])
         for d in range(1, devices)
     ]
+
+    up_send, _ = lax.optimization_barrier((packed[1:groups], got[lines]))
+    up_got = swap(up_send, groups)
 
     rows_decay, column_decay, channel = pl.pallas_call(
         functools.partial(prep_kernel, per_group),
@@ -682,12 +676,12 @@
 
     each = per_group // 2
     partial_down = pl.pallas_call(
-        functools.partial(shrink_kernel, groups, per_group),
+        functools.partial(shrink_kernel, per_group),
         grid_spec=pltpu.PrefetchScalarGridSpec(
             num_scalar_prefetch=1,
             grid=(per_group // each,),
             in_specs=[pl.BlockSpec((each * T_REQ, hidden.shape[1]), lambda g, meta: (g, 0))]
-            + pinned(groups) + anywhere(3),
+            + anywhere(3),
             out_specs=pl.BlockSpec((each, rank, T_REQ), lambda g, meta: (g, 0, 0)),
             scratch_shapes=[
                 pltpu.VMEM((per_group,) + adapter_down_weight.shape[1:], bf16),
@@ -698,35 +692,34 @@
         cost_estimate=cost(),
         compiler_params=params(),
         name="shrink",
-    )(meta, hidden, adapter_down_weight, *down_got, channel, got[lines], got[1])
+    )(meta, hidden, down_got, channel, got[lines])
 
     parts = lax.all_to_all(partial_down, "dev", split_axis=0, concat_axis=0, tiled=True)
     summed = pl.pallas_call(
         sum_kernel,
         out_shape=jax.ShapeDtypeStruct((devices, 1, rank, T_REQ), bf16),
-        in_specs=vmem(1) + anywhere(2),
+        in_specs=vmem(1) + anywhere(1),
         out_specs=vmem(1)[0],
         cost_estimate=cost(),
         name="sum_parts",
-    )(parts.reshape(devices, 1, rank, T_REQ), got[lines + 1], up_got[groups // 2 - 1])
+    )(parts.reshape(devices, 1, rank, T_REQ), got[lines + 1])
     shrunk = lax.all_to_all(summed, "dev", split_axis=0, concat_axis=0, tiled=True)
     shrunk = shrunk.reshape(per_group, rank, T_REQ)
 
+    befores = [[partial_down], [summed, up_got[groups // 2 - 1]], [rows_all, up_got[-1]]]
     spread = spread_steps(zero, meta, packed[-2:], devices)
     next(spread)
-    sent = spread.send([summed, rows_all])
-    for step in range(2, lines - 1):
-        sent = spread.send([up_got[-1]] if step == lines - 2 else [])
+    for step in range(1, lines):
+        sent = spread.send(befores.pop(0) if befores else [])
+    spread = spread.send([])
     spread_others = spread_rest(meta, cache, conv, devices, width, limit)
 
     outs = None
-    for begin, steps in ((0, lines), (lines, lines), (devices, limit)):
+    for begin, steps in ((0, lines), (lines, devices - lines + limit)):
         if begin == 0:
             chunks, after = got[:lines], [sent, got[lines + 2]]
-        elif begin == lines:
-            chunks, after = got[lines:], [spread.send([outs[2]])]
         else:
-            chunks, after = [*spread.send([]), spread_others, got[0]], []
+            chunks, after = [*got[lines:], *spread, spread_others], []
 
         def request(g, meta, begin=begin):
             return meta[POS_REQ, begin + g]
@@ -738,7 +731,7 @@
             pl.BlockSpec((2 * heads, T_REQ), lambda g, meta: (0, request(g, meta))),
             pl.BlockSpec((1, T_REQ, heads), lambda g, meta: (request(g, meta), 0, 0)),
             pl.BlockSpec((T_REQ, 2 * depth), lambda g, meta: (request(g, meta), 0)),
-        ] + pinned(groups + len(chunks)) + anywhere(len(after))
+        ] + anywhere(groups + len(chunks) + len(after))
         operands = [
             meta, base_in_projection, shrunk, channel, rows_decay, column_decay, rows_all,
             adapter_up_weight, *up_got, *chunks, *after,
@@ -746,10 +739,10 @@
         aliases = {}
         if outs is not None:
             aliases = {len(operands): 0, len(operands) + 1: 1}
-            operands += list(outs[:2])
+            operands += list(outs)
             in_specs += anywhere(2)
         outs = pl.pallas_call(
-            functools.partial(mix_kernel, groups, taps, begin, steps, begin == devices, size),
+            functools.partial(mix_kernel, groups, taps, begin, steps, lines, size),
             grid_spec=pltpu.PrefetchScalarGridSpec(
                 num_scalar_prefetch=1,
                 grid=(steps,),
@@ -759,7 +752,6 @@
                     pl.BlockSpec(
                         (1, heads * size, depth), lambda g, meta: (request(g, meta), 0, 0)
                     ),
-                    pl.BlockSpec((8, 128), lambda g, meta: (0, 0)),
                 ),
                 scratch_shapes=[
                     pltpu.VMEM((T_REQ + 8, width), f32),
@@ -775,7 +767,6 @@
             out_shape=(
                 jax.ShapeDtypeStruct((tokens, width), bf16),
                 jax.ShapeDtypeStruct((per_group, heads * size, depth), bf16),
-                jax.ShapeDtypeStruct((8, 128), f32),
             ),
             input_output_aliases=aliases,
             cost_estimate=cost(),

time: 213 us -> 187 us (0.88)
  the two profiles are of different devices: /device:TPU:8 before, /device:TPU:0 now
where the time goes in v5:
time: 187 us; the launch traced here: 186 us
  Pallas kernels  55.5 us (30%)
  starting transfers between devices  52.7 us (28%)
  local copies, waits for them, and re-layouts  34 us (18%)
  waiting for transfers between devices  29 us (16%)
  between operations  14.3 us (8%)
    unnamed x88, local copies, waits for them, and re-layouts  32.4 us
    pallas_call x2, Pallas kernels, body(): pl.pallas_call(functools.partial(mix_kernel, groups, taps, begin, steps,...  32.1 us
    ppermute x7, waiting for transfers between devices, body(): lax.ppermute(chunks[d], 'dev', [(s, s ^ d) for s in range(devices)])  25.7 us
    ppermute x7, starting transfers between devices, body(): lax.ppermute(chunks[d], 'dev', [(s, s ^ d) for s in range(devices)])  16.5 us
    pallas_call x1, Pallas kernels, body(): pl.pallas_call(functools.partial(pack_kernel, groups, devices, per_group,...  10.2 us
    ppermute x3, starting transfers between devices, spread_steps(): lax.ppermute(to_right, 'dev', [(2 * i + x, 2 * i + 2 + x) for i in range(...  9.91 us
    all_to_all x1, starting transfers between devices, body(): lax.all_to_all(summed, 'dev', split_axis=0, concat_axis=0, tiled=True)  8.68 us
    all_to_all x1, starting transfers between devices, body(): lax.all_to_all(partial_down, 'dev', split_axis=0, concat_axis=0, tiled=True)  6.38 us
  transfers between devices with their start and end apart: 21, of which 4 were waited for; matrix products, arithmetic and copies ran while one was open for 1% of the time, Pallas kernels for 15%

profile of v5, /device:TPU:0, one launch (start us, length us, event | category | flops | bytes accessed | tf_op | source)
XLA Modules:
  0.0 186.4 jit_solution(14535235594656560520)
XLA Ops:
  7.2 1.2 copy-done.2
  8.4 1.2 copy-done.22
  14.6 10.2 %pack.1 = (s32[16,64]{1,0:T(8,128)S(1)}, bf16[256,256]{1,0:T(8,128)(2,1)}, bf16[4,4,64,1024]{3,2,1,0:T(8,128)(2,1)}, bf16[4,64,1024]{2,1,0:T(8,128)(2,1)}, bf16[...) custom-call(s32[32]{0:T(128)S(1)} %bitcast.19, ...), custom_call_target="tpu_custom_call" | custom-call | bytes 65536 | tf_op jit(solution)/shard_map/pack/pallas_call | solution.py:621
  27.7 4.4 %all-to-all-start = ((bf16[4,4,64,1024]{3,2,1,0:T(8,128)(2,1)}), bf16[4,4,64,1024]{3,2,1,0:T(8,128)(2,1)S(1)}, u32[]{:S(2)}, u32[]{:S(2)}) async-start(bf16[4,4,64,1024]{3,2,1,0:T(8,128)(2,1)} %get-tuple-element.167), calls=%async_computation | async-start | bytes 4194304 | tf_op jit(solution)/shard_map/all_to_all | solution.py:648
  32.1 2.4 %collective-permute-start.14 = (bf16[4,1056,128]{2,1,0:T(8,128)(2,1)}, bf16[4,1056,128]{2,1,0:T(8,128)(2,1)S(1)}, u32[]{:S(2)}, u32[]{:S(2)}) collective-permute-start(bf16[4,1056,128]{2,1,0:T(8,128)(2,1)} %get-tuple-element.183), channel_id=1, source_target_pairs={{0,1},{1,0},{2,3},{3,2},{4,5},{5,4},{6,7},{7,6},{8,9},{9,8},{10,11... | collective-permute-start | bytes 3244040 | tf_op jit(solution)/shard_map/ppermute | solution.py:295
  34.6 2.7 %collective-permute-start.7 = (bf16[1056,128]{1,0:T(8,128)(2,1)}, bf16[1056,128]{1,0:T(8,128)(2,1)S(1)}, u32[]{:S(2)}, u32[]{:S(2)}) collective-permute-start(bf16[1056,128]{1,0:T(8,128)(2,1)} %copy-done.43), channel_id=1, source_target_pairs={{0,4},{1,5},{2,6},{3,7},{4,0},{5,1},{6,2},{7,3},{8,12},{9,13},{10,... | collective-permute-start | bytes 811016 | tf_op jit(solution)/shard_map/ppermute | solution.py:653
  37.2 14.1 %collective-permute-done.7.rest_1_.rest_4_ = bf16[1056,128]{1,0:T(8,128)(2,1)S(1)} collective-permute-done((bf16[1056,128]{1,0:T(8,128)(2,1)}, bf16[1056,128]{1,0:T(8,128)(2,1)S(1)}, u32[]{:S(2)}, u32[]{:S(2)}) %collective-permute-start.7) | collective-permute-done | bytes 270368 | tf_op jit(solution)/shard_map/ppermute | solution.py:653
  51.4 1.7 collective-permute-start.10
  54.0 1.1 prep.1
  55.2 1.0 copy-done.12
  56.8 1.8 all-to-all-done.table
  58.6 1.3 copy-done.6
  59.9 1.6 copy-done.7
  61.5 5.9 %shrink.1.rest_0_ = bf16[8,64,256]{2,1,0:T(8,128)(2,1)} custom-call(s32[16,64]{1,0:T(8,128)S(1)} %get-tuple-element.268.rest_0_.meta, bf16[2048,1024]{1,0:T(8,128)(2,1)} %hidden.1, bf16[4,4,64,1024]{3,2,1,0:T(8,128)(2,1)S(1)} %copy-done.7, f32[8,1024]{1,0:T(8,128)S(1)} %get-tuple-element.168.rest_0_.channel, ...), custom_call_target="tpu_custom_call" | custom-call | bytes 65536 | tf_op jit(solution)/shard_map/shrink/pallas_call | solution.py:678
  68.1 6.4 %all-to-all-start.1 = ((bf16[8,64,256]{2,1,0:T(8,128)(2,1)}), bf16[8,64,256]{2,1,0:T(8,128)(2,1)}, u32[]{:S(2)}, u32[]{:S(2)}) async-start(bf16[8,64,256]{2,1,0:T(8,128)(2,1)} %shrink.1.rest_0_), calls=%async_computation.1 | async-start | bytes 524288 | tf_op jit(solution)/shard_map/all_to_all | solution.py:697
  74.5 3.8 %collective-permute-start.8 = (bf16[1056,128]{1,0:T(8,128)(2,1)}, bf16[1056,128]{1,0:T(8,128)(2,1)S(1)}, u32[]{:S(2)}, u32[]{:S(2)}) collective-permute-start(bf16[1056,128]{1,0:T(8,128)(2,1)} %get-tuple-element.170), channel_id=1, source_target_pairs={{0,5},{1,4},{2,7},{3,6},{4,1},{5,0},{6,3},{7,2},{8,13},{9,12},{10,... | collective-permute-start | bytes 811016 | tf_op jit(solution)/shard_map/ppermute | solution.py:653
  78.3 1.6 pick_1.8
  79.9 3.3 %collective-permute-start.15 = (bf16[1056,128]{1,0:T(8,128)(2,1)}, bf16[1056,128]{1,0:T(8,128)(2,1)S(1)}, u32[]{:S(2)}, u32[]{:S(2)}) collective-permute-start(bf16[1056,128]{1,0:T(8,128)(2,1)} %get-tuple-element.184), channel_id=1, source_target_pairs={{0,2},{1,3},{8,10},{9,11},{16,18},{17,19},{24,26},{25,27}} | collective-permute-start | bytes 811016 | tf_op jit(solution)/shard_map/ppermute | solution.py:323
  84.0 11.6 %collective-permute-done.8.rest_0_.rest_5_ = bf16[1056,128]{1,0:T(8,128)(2,1)S(1)} collective-permute-done((bf16[1056,128]{1,0:T(8,128)(2,1)}, bf16[1056,128]{1,0:T(8,128)(2,1)S(1)}, u32[]{:S(2)}, u32[]{:S(2)}) %collective-permute-start.8) | collective-permute-done | bytes 270368 | tf_op jit(solution)/shard_map/ppermute | solution.py:653
  96.3 1.7 sum_parts.1.rest_2_
  98.0 1.4 pick_2.8
  99.4 1.3 collective-permute-start.17
  101.4 2.2 %collective-permute-start.12 = (bf16[1056,128]{1,0:T(8,128)(2,1)}, bf16[1056,128]{1,0:T(8,128)(2,1)}, u32[]{:S(2)}, u32[]{:S(2)}) collective-permute-start(bf16[1056,128]{1,0:T(8,128)(2,1)} %get-tuple-element.180), channel_id=1, source_target_pairs={{0,6},{1,7},{2,4},{3,5},{4,2},{5,3},{6,0},{7,1},{8,14},{9,15},{10,... | collective-permute-start | bytes 811016 | tf_op jit(solution)/shard_map/ppermute | solution.py:653
  104.4 1.7 collective-permute-start.22
  106.1 1.5 collective-permute-done.17.rest_0_
  108.4 8.7 %all-to-all-start.2 = ((bf16[8,1,64,256]{3,2,1,0:T(8,128)(2,1)}), bf16[8,1,64,256]{3,2,1,0:T(8,128)(2,1)S(1)}, u32[]{:S(2)}, u32[]{:S(2)}) async-start(bf16[8,1,64,256]{3,2,1,0:T(8,128)(2,1)} %sum_parts.1.rest_2_), calls=%async_computation.2 | async-start | bytes 524288 | tf_op jit(solution)/shard_map/all_to_all | solution.py:706
  117.7 2.9 %collective-permute-start.23 = (bf16[1056,128]{1,0:T(8,128)(2,1)}, bf16[1056,128]{1,0:T(8,128)(2,1)}, u32[]{:S(2)}, u32[]{:S(2)}) collective-permute-start(bf16[1056,128]{1,0:T(8,128)(2,1)} %copy-done.42), channel_id=1, source_target_pairs={{0,3},{1,2},{2,1},{3,0},{4,7},{5,6},{6,5},{7,4},{8,11},{9,10},{10,... | collective-permute-start | bytes 811016 | tf_op jit(solution)/shard_map/ppermute | solution.py:653
  120.7 1.2 copy-done.3
  121.9 1.0 copy-done.9
  122.9 1.0 copy-done.26
  123.9 1.0 copy-done.28
  124.9 1.5 pick_3.8
  126.4 2.4 %collective-permute-start.13 = (bf16[1056,128]{1,0:T(8,128)(2,1)}, bf16[1056,128]{1,0:T(8,128)(2,1)}, u32[]{:S(2)}, u32[]{:S(2)}) collective-permute-start(bf16[1056,128]{1,0:T(8,128)(2,1)} %get-tuple-element.181), channel_id=1, source_target_pairs={{0,7},{1,6},{2,5},{3,4},{4,3},{5,2},{6,1},{7,0},{8,15},{9,14},{10,... | collective-permute-start | bytes 811016 | tf_op jit(solution)/shard_map/ppermute | solution.py:653
  128.7 1.3 collective-permute-start.20
  130.0 5.3 %collective-permute-start.19 = (bf16[1056,128]{1,0:T(8,128)(2,1)}, bf16[1056,128]{1,0:T(8,128)(2,1)}, u32[]{:S(2)}, u32[]{:S(2)}) collective-permute-start(bf16[1056,128]{1,0:T(8,128)(2,1)} %get-tuple-element.188.rest_8_), channel_id=1, source_target_pairs={{0,2},{1,3},{2,4},{3,5},{4,6},{5,7},{8,10},{9,11},{10,12},{11,13},... | collective-permute-start | bytes 811016 | tf_op jit(solution)/shard_map/ppermute | solution.py:323
  135.9 1.0 copy-done.10
  136.9 1.2 copy-done.13
  138.2 0.9 copy-done.20
  139.1 1.0 copy-done.24
  140.1 15.5 %mix_0.1 = (bf16[2048,1024]{1,0:T(8,128)(2,1)}, bf16[8,1024,128]{2,1,0:T(8,128)(2,1)}) custom-call(s32[16,64]{1,0:T(8,128)S(1)} %get-tuple-element.268.rest_0_.meta, bf16[2048,1024]{1,0:T(8,128)(2,1)} %base.3, bf16[8,64,256]{2,1,0:T(8,128)(2,1)S(1)} %bitcast.16, f32[8,1024]{1,0:T(8,128)S(1)} %get-tuple-element.168.rest_0_.channel, ...), custom_call_target="tpu_custom_call" | custom-call | bytes 65536 | tf_op jit(solution)/shard_map/mix_0/pallas_call | solution.py:744
  155.6 1.0 broadcast_in_dim.12
  156.6 0.9 while.14
  157.8 1.0 copy-done.11
  158.8 1.2 copy-done.14
  160.1 1.0 copy-done.16
  161.0 1.0 copy-done.18
  162.0 0.9 copy-done.21
  162.9 16.6 %mix_4.1 = (bf16[2048,1024]{1,0:T(8,128)(2,1)}, bf16[8,1024,128]{2,1,0:T(8,128)(2,1)}) custom-call(s32[16,64]{1,0:T(8,128)S(1)} %get-tuple-element.321, bf16[2048,1024]{1,0:T(8,128)(2,1)} %base.3, bf16[8,64,256]{2,1,0:T(8,128)(2,1)S(1)} %bitcast.17, ...), custom_call_target="tpu_custom_call", output_to_operand_aliasing={{0}: (20, {}), {1}: (21, {})} | custom-call | bytes 65536 | tf_op jit(solution)/shard_map/mix_4/pallas_call | solution.py:744
  (95 shorter events, 15.5 us)
Async XLA Ops:
  7.2 1.2 copy-start.2
  8.4 1.2 copy-start.22
  27.7 25.4 %copy-start.32 = (f32[4,1024]{1,0:T(4,128)S(1)}, f32[4,1024]{1,0:T(4,128)}, u32[]{:S(2)}) copy-start(f32[4,1024]{1,0:T(4,128)} %taps_in.1) | copy-start | bytes 49156
  27.7 25.4 %copy-start.33 = (f32[1024]{0:T(1024)S(1)}, f32[1024]{0:T(1024)}, u32[]{:S(2)}) copy-start(f32[1024]{0:T(1024)} %param.28) | copy-start | bytes 12292
  27.7 25.4 %copy-start.39 = (f32[16]{0:T(128)S(1)}, f32[16]{0:T(128)}, u32[]{:S(2)}) copy-start(f32[16]{0:T(128)} %rates.1) | copy-start | bytes 196
  27.7 25.4 %copy-start.40 = (f32[16]{0:T(128)S(1)}, f32[16]{0:T(128)}, u32[]{:S(2)}) copy-start(f32[16]{0:T(128)} %skips.1) | copy-start | bytes 196
  27.7 30.9 %all-to-all-start = ((bf16[4,4,64,1024]{3,2,1,0:T(8,128)(2,1)}), bf16[4,4,64,1024]{3,2,1,0:T(8,128)(2,1)S(1)}, u32[]{:S(2)}, u32[]{:S(2)}) async-start(bf16[4,4,64,1024]{3,2,1,0:T(8,128)(2,1)} %get-tuple-element.167), calls=%async_computation | async-start | bytes 4194304 | tf_op jit(solution)/shard_map/all_to_all | solution.py:648
  32.1 88.6 %all-gather.2.cloned.1.call-start = ((), (), s32[]{:S(2)}) async-start(), calls=%async_computation.3 | async-start | bytes 1179648 | tf_op jit(solution)/shard_map/all_gather | solution.py:650
  32.1 46.2 %collective-permute-start.14 = (bf16[4,1056,128]{2,1,0:T(8,128)(2,1)}, bf16[4,1056,128]{2,1,0:T(8,128)(2,1)S(1)}, u32[]{:S(2)}, u32[]{:S(2)}) collective-permute-start(bf16[4,1056,128]{2,1,0:T(8,128)(2,1)} %get-tuple-element.183), channel_id=1, source_target_pairs={{0,1},{1,0},{2,3},{3,2},{4,5},{5,4},{6,7},{7,6},{8,9},{9,8},{10,11... | collective-permute-start | bytes 3244040 | tf_op jit(solution)/shard_map/ppermute | solution.py:295
  34.6 16.8 %collective-permute-start.7 = (bf16[1056,128]{1,0:T(8,128)(2,1)}, bf16[1056,128]{1,0:T(8,128)(2,1)S(1)}, u32[]{:S(2)}, u32[]{:S(2)}) collective-permute-start(bf16[1056,128]{1,0:T(8,128)(2,1)} %copy-done.43), channel_id=1, source_target_pairs={{0,4},{1,5},{2,6},{3,7},{4,0},{5,1},{6,2},{7,3},{8,12},{9,13},{10,... | collective-permute-start | bytes 811016 | tf_op jit(solution)/shard_map/ppermute | solution.py:653
  51.4 46.6 %collective-permute-start.10 = (bf16[4,64,1024]{2,1,0:T(8,128)(2,1)}, bf16[4,64,1024]{2,1,0:T(8,128)(2,1)}, u32[]{:S(2)}, u32[]{:S(2)}) collective-permute-start(bf16[4,64,1024]{2,1,0:T(8,128)(2,1)} %copy-done.41), channel_id=1, source_target_pairs={{0,16},{8,24},{16,0},{24,8},{1,17},{9,25},{17,1},{25,9},{2,18},{10... | collective-permute-start | bytes 1572872 | tf_op jit(solution)/shard_map/ppermute | solution.py:157
  55.1 1.0 copy-start.12
  58.6 1.3 copy-start.6
  59.9 1.6 copy-start.7
  61.5 16.8 %copy-start = (bf16[4,1056,128]{2,1,0:T(8,128)(2,1)S(1)}, bf16[4,1056,128]{2,1,0:T(8,128)(2,1)}, u32[]{:S(2)}) copy-start(bf16[4,1056,128]{2,1,0:T(8,128)(2,1)} %get-tuple-element.182.own_r.own_l.rest_8_) | copy-start | bytes 3244036
  68.1 27.5 %all-to-all-start.1 = ((bf16[8,64,256]{2,1,0:T(8,128)(2,1)}), bf16[8,64,256]{2,1,0:T(8,128)(2,1)}, u32[]{:S(2)}, u32[]{:S(2)}) async-start(bf16[8,64,256]{2,1,0:T(8,128)(2,1)} %shrink.1.rest_0_), calls=%async_computation.1 | async-start | bytes 524288 | tf_op jit(solution)/shard_map/all_to_all | solution.py:697
  74.5 21.1 %collective-permute-start.8 = (bf16[1056,128]{1,0:T(8,128)(2,1)}, bf16[1056,128]{1,0:T(8,128)(2,1)S(1)}, u32[]{:S(2)}, u32[]{:S(2)}) collective-permute-start(bf16[1056,128]{1,0:T(8,128)(2,1)} %get-tuple-element.170), channel_id=1, source_target_pairs={{0,5},{1,4},{2,7},{3,6},{4,1},{5,0},{6,3},{7,2},{8,13},{9,12},{10,... | collective-permute-start | bytes 811016 | tf_op jit(solution)/shard_map/ppermute | solution.py:653
  78.3 42.4 %copy-start.1 = (bf16[4,1056,128]{2,1,0:T(8,128)(2,1)}, bf16[4,1056,128]{2,1,0:T(8,128)(2,1)S(1)}, u32[]{:S(2)}) copy-start(bf16[4,1056,128]{2,1,0:T(8,128)(2,1)S(1)} %collective-permute-done.14.over_r.over_l.rest_9_) | copy-start | bytes 3244036
  79.9 18.1 %collective-permute-start.15 = (bf16[1056,128]{1,0:T(8,128)(2,1)}, bf16[1056,128]{1,0:T(8,128)(2,1)S(1)}, u32[]{:S(2)}, u32[]{:S(2)}) collective-permute-start(bf16[1056,128]{1,0:T(8,128)(2,1)} %get-tuple-element.184), channel_id=1, source_target_pairs={{0,2},{1,3},{8,10},{9,11},{16,18},{17,19},{24,26},{25,27}} | collective-permute-start | bytes 811016 | tf_op jit(solution)/shard_map/ppermute | solution.py:323
  83.2 14.8 %collective-permute-start.16 = (bf16[1056,128]{1,0:T(8,128)(2,1)}, bf16[1056,128]{1,0:T(8,128)(2,1)S(1)}, u32[]{:S(2)}, u32[]{:S(2)}) collective-permute-start(bf16[1056,128]{1,0:T(8,128)(2,1)} %get-tuple-element.185), channel_id=1, source_target_pairs={{7,5},{6,4},{15,13},{14,12},{23,21},{22,20},{31,29},{30,28}} | collective-permute-start | bytes 811016 | tf_op jit(solution)/shard_map/ppermute | solution.py:327
  83.9 20.5 %collective-permute-start.11 = (bf16[4,64,1024]{2,1,0:T(8,128)(2,1)}, bf16[4,64,1024]{2,1,0:T(8,128)(2,1)S(1)}, u32[]{:S(2)}, u32[]{:S(2)}) collective-permute-start(bf16[4,64,1024]{2,1,0:T(8,128)(2,1)} %get-tuple-element.179), channel_id=1, source_target_pairs={{0,24},{8,16},{16,8},{24,0},{1,25},{9,17},{17,9},{25,1},{2,26},{10... | collective-permute-start | bytes 1572872 | tf_op jit(solution)/shard_map/ppermute | solution.py:157
  99.4 8.2 %collective-permute-start.17 = (bf16[1056,128]{1,0:T(8,128)(2,1)S(1)}, bf16[1056,128]{1,0:T(8,128)(2,1)S(1)}, u32[]{:S(2)}, u32[]{:S(2)}) collective-permute-start(bf16[1056,128]{1,0:T(8,128)(2,1)S(1)} %get-tuple-element.186), channel_id=1, source_target_pairs={{0,2},{1,3},{2,4},{3,5},{8,10},{9,11},{10,12},{11,13},{16,18},{17,... | collective-permute-start | bytes 811016 | tf_op jit(solution)/shard_map/ppermute | solution.py:323
  100.7 16.3 %collective-permute-start.18 = (bf16[1056,128]{1,0:T(8,128)(2,1)}, bf16[1056,128]{1,0:T(8,128)(2,1)S(1)}, u32[]{:S(2)}, u32[]{:S(2)}) collective-permute-start(bf16[1056,128]{1,0:T(8,128)(2,1)} %get-tuple-element.187), channel_id=1, source_target_pairs={{7,5},{6,4},{5,3},{4,2},{15,13},{14,12},{13,11},{12,10},{23,21},{2... | collective-permute-start | bytes 811016 | tf_op jit(solution)/shard_map/ppermute | solution.py:327
  101.4 24.9 %collective-permute-start.12 = (bf16[1056,128]{1,0:T(8,128)(2,1)}, bf16[1056,128]{1,0:T(8,128)(2,1)}, u32[]{:S(2)}, u32[]{:S(2)}) collective-permute-start(bf16[1056,128]{1,0:T(8,128)(2,1)} %get-tuple-element.180), channel_id=1, source_target_pairs={{0,6},{1,7},{2,4},{3,5},{4,2},{5,3},{6,0},{7,1},{8,14},{9,15},{10,... | collective-permute-start | bytes 811016 | tf_op jit(solution)/shard_map/ppermute | solution.py:653
  103.6 25.1 %collective-permute-start.21 = (bf16[1056,128]{1,0:T(8,128)(2,1)}, bf16[1056,128]{1,0:T(8,128)(2,1)}, u32[]{:S(2)}, u32[]{:S(2)}) collective-permute-start(bf16[1056,128]{1,0:T(8,128)(2,1)} %get-tuple-element.192), channel_id=1, source_target_pairs={{0,1},{1,0},{2,3},{3,2},{4,5},{5,4},{6,7},{7,6},{8,9},{9,8},{10,11... | collective-permute-start | bytes 811016 | tf_op jit(solution)/shard_map/ppermute | solution.py:653
  104.4 16.3 %copy-start.8 = (bf16[4,64,1024]{2,1,0:T(8,128)(2,1)}, bf16[4,64,1024]{2,1,0:T(8,128)(2,1)S(1)}, u32[]{:S(2)}) copy-start(bf16[4,64,1024]{2,1,0:T(8,128)(2,1)S(1)} %collective-permute-done.11.rest_3_) | copy-start | bytes 1572868
  104.4 25.6 %collective-permute-start.22 = (bf16[1056,128]{1,0:T(8,128)(2,1)}, bf16[1056,128]{1,0:T(8,128)(2,1)}, u32[]{:S(2)}, u32[]{:S(2)}) collective-permute-start(bf16[1056,128]{1,0:T(8,128)(2,1)} %get-tuple-element.193), channel_id=1, source_target_pairs={{0,2},{1,3},{2,0},{3,1},{4,6},{5,7},{6,4},{7,5},{8,10},{9,11},{10,... | collective-permute-start | bytes 811016 | tf_op jit(solution)/shard_map/ppermute | solution.py:653
  108.4 27.5 %collective-permute-start.9 = (bf16[4,64,1024]{2,1,0:T(8,128)(2,1)}, bf16[4,64,1024]{2,1,0:T(8,128)(2,1)}, u32[]{:S(2)}, u32[]{:S(2)}) collective-permute-start(bf16[4,64,1024]{2,1,0:T(8,128)(2,1)} %get-tuple-element.177), channel_id=1, source_target_pairs={{0,8},{8,0},{16,24},{24,16},{1,9},{9,1},{17,25},{25,17},{2,10},{10... | collective-permute-start | bytes 1572872 | tf_op jit(solution)/shard_map/ppermute | solution.py:157
  108.4 27.5 %all-to-all-start.2 = ((bf16[8,1,64,256]{3,2,1,0:T(8,128)(2,1)}), bf16[8,1,64,256]{3,2,1,0:T(8,128)(2,1)S(1)}, u32[]{:S(2)}, u32[]{:S(2)}) async-start(bf16[8,1,64,256]{3,2,1,0:T(8,128)(2,1)} %sum_parts.1.rest_2_), calls=%async_computation.2 | async-start | bytes 524288 | tf_op jit(solution)/shard_map/all_to_all | solution.py:706
  117.7 18.1 %collective-permute-start.23 = (bf16[1056,128]{1,0:T(8,128)(2,1)}, bf16[1056,128]{1,0:T(8,128)(2,1)}, u32[]{:S(2)}, u32[]{:S(2)}) collective-permute-start(bf16[1056,128]{1,0:T(8,128)(2,1)} %copy-done.42), channel_id=1, source_target_pairs={{0,3},{1,2},{2,1},{3,0},{4,7},{5,6},{6,5},{7,4},{8,11},{9,10},{10,... | collective-permute-start | bytes 811016 | tf_op jit(solution)/shard_map/ppermute | solution.py:653
  120.7 1.2 copy-start.3
  121.9 1.0 copy-start.9
  122.9 1.0 copy-start.26
  123.9 1.0 copy-start.28
  124.8 11.0 %copy-start.4 = (bf16[2048,256]{1,0:T(8,128)(2,1)S(1)}, bf16[2048,256]{1,0:T(8,128)(2,1)}, u32[]{:S(2)}) copy-start(bf16[2048,256]{1,0:T(8,128)(2,1)} %all-gather.2.cloned.1.call-done.rest_2_.rows_in) | copy-start | bytes 3145732
  126.4 31.1 %collective-permute-start.13 = (bf16[1056,128]{1,0:T(8,128)(2,1)}, bf16[1056,128]{1,0:T(8,128)(2,1)}, u32[]{:S(2)}, u32[]{:S(2)}) collective-permute-start(bf16[1056,128]{1,0:T(8,128)(2,1)} %get-tuple-element.181), channel_id=1, source_target_pairs={{0,7},{1,6},{2,5},{3,4},{4,3},{5,2},{6,1},{7,0},{8,15},{9,14},{10,... | collective-permute-start | bytes 811016 | tf_op jit(solution)/shard_map/ppermute | solution.py:653
  128.7 28.8 %collective-permute-start.20 = (bf16[1056,128]{1,0:T(8,128)(2,1)}, bf16[1056,128]{1,0:T(8,128)(2,1)}, u32[]{:S(2)}, u32[]{:S(2)}) collective-permute-start(bf16[1056,128]{1,0:T(8,128)(2,1)} %get-tuple-element.189), channel_id=1, source_target_pairs={{7,5},{6,4},{5,3},{4,2},{3,1},{2,0},{15,13},{14,12},{13,11},{12,10... | collective-permute-start | bytes 811016 | tf_op jit(solution)/shard_map/ppermute | solution.py:327
  130.0 27.5 %collective-permute-start.19 = (bf16[1056,128]{1,0:T(8,128)(2,1)}, bf16[1056,128]{1,0:T(8,128)(2,1)}, u32[]{:S(2)}, u32[]{:S(2)}) collective-permute-start(bf16[1056,128]{1,0:T(8,128)(2,1)} %get-tuple-element.188.rest_8_), channel_id=1, source_target_pairs={{0,2},{1,3},{2,4},{3,5},{4,6},{5,7},{8,10},{9,11},{10,12},{11,13},... | collective-permute-start | bytes 811016 | tf_op jit(solution)/shard_map/ppermute | solution.py:323
  135.9 1.0 copy-start.10
  136.9 1.2 copy-start.13
  138.2 0.9 copy-start.20
  139.1 1.0 copy-start.24
  156.6 1.2 copy-start.5
  157.8 1.0 copy-start.11
  158.8 1.2 copy-start.14
  160.1 1.0 copy-start.16
  161.0 1.0 copy-start.18
  162.0 0.9 copy-start.21
  (17 other events, 12.4 us)
Sparse Core Ops, SparseCore 0:
  35.0 44.5 all-gather.1

commit v6 on v5

--- a/solution.py
+++ b/solution.py
@@ -14,7 +14,7 @@
 LOG2E = math.log2(math.e)
 NT = (((1,), (1,)), ((), ()))
 TN = (((0,), (0,)), ((), ()))
-VMEM_LIMIT = 48 * 1024 * 1024
+VMEM_LIMIT = 63 * 1024 * 1024
 
 HOME, DIST, ARANK, AINDEX, PRESENT, POS_REQ, POS_VALID, OSLOT, OHOLDER, MISC, SEND = range(11)
 MOST, ME, SLOT = range(3)
@@ -654,6 +654,8 @@
         for d in range(1, devices)
     ]
 
+    spread_others = spread_rest(meta, cache, conv, devices, width, limit)
+
     up_send, _ = lax.optimization_barrier((packed[1:groups], got[lines]))
     up_got = swap(up_send, groups)
 
@@ -681,7 +683,7 @@
             num_scalar_prefetch=1,
             grid=(per_group // each,),
             in_specs=[pl.BlockSpec((each * T_REQ, hidden.shape[1]), lambda g, meta: (g, 0))]
-            + anywhere(3),
+            + anywhere(5),
             out_specs=pl.BlockSpec((each, rank, T_REQ), lambda g, meta: (g, 0, 0)),
             scratch_shapes=[
                 pltpu.VMEM((per_group,) + adapter_down_weight.shape[1:], bf16),
@@ -692,17 +694,18 @@
         cost_estimate=cost(),
         compiler_params=params(),
         name="shrink",
-    )(meta, hidden, down_got, channel, got[lines])
+    )(meta, hidden, down_got, channel, got[lines], got[lines + 1], spread_others)
 
     parts = lax.all_to_all(partial_down, "dev", split_axis=0, concat_axis=0, tiled=True)
     summed = pl.pallas_call(
         sum_kernel,
         out_shape=jax.ShapeDtypeStruct((devices, 1, rank, T_REQ), bf16),
-        in_specs=vmem(1) + anywhere(1),
+        in_specs=vmem(1),
         out_specs=vmem(1)[0],
         cost_estimate=cost(),
+        compiler_params=params(),
         name="sum_parts",
-    )(parts.reshape(devices, 1, rank, T_REQ), got[lines + 1])
+    )(parts.reshape(devices, 1, rank, T_REQ))
     shrunk = lax.all_to_all(summed, "dev", split_axis=0, concat_axis=0, tiled=True)
     shrunk = shrunk.reshape(per_group, rank, T_REQ)
 
@@ -712,12 +715,11 @@
     for step in range(1, lines):
         sent = spread.send(befores.pop(0) if befores else [])
     spread = spread.send([])
-    spread_others = spread_rest(meta, cache, conv, devices, width, limit)
 
     outs = None
     for begin, steps in ((0, lines), (lines, devices - lines + limit)):
         if begin == 0:
-            chunks, after = got[:lines], [sent, got[lines + 2]]
+            chunks, after = got[:lines], [sent, got[lines + 2], got[lines + 3]]
         else:
             chunks, after = [*got[lines:], *spread, spread_others], []
 

time: 187 us -> 164 us (0.88)
  the two profiles are of different devices: /device:TPU:0 before, /device:TPU:8 now
where the time goes in v6:
time: 164 us; the launch traced here: 162 us
  Pallas kernels  60.3 us (37%)
  starting transfers between devices  43.2 us (26%)
  waiting for transfers between devices  43 us (26%)
  between operations  14.2 us (9%)
    pallas_call x2, Pallas kernels, body(): pl.pallas_call(functools.partial(mix_kernel, groups, taps, begin, steps,...  33.5 us
    ppermute x7, waiting for transfers between devices, body(): lax.ppermute(chunks[d], 'dev', [(s, s ^ d) for s in range(devices)])  25.3 us
    ppermute x3, starting transfers between devices, spread_steps(): lax.ppermute(to_right, 'dev', [(2 * i + x, 2 * i + 2 + x) for i in range(...  9.88 us
    ppermute x7, starting transfers between devices, body(): lax.ppermute(chunks[d], 'dev', [(s, s ^ d) for s in range(devices)])  8.63 us
    pallas_call x3, Pallas kernels, spread_steps(): pl.pallas_call(functools.partial(pick_kernel, step, lines), grid_spec=plt...  8.48 us
    pallas_call x1, Pallas kernels, body(): pl.pallas_call(functools.partial(pack_kernel, groups, devices, per_group,...  8.47 us
    all_to_all x1, starting transfers between devices, body(): lax.all_to_all(partial_down, 'dev', split_axis=0, concat_axis=0, tiled=True)  7.14 us
    ppermute x3, waiting for transfers between devices, spread_steps(): lax.ppermute(to_left, 'dev', [(devices - 1 - (2 * i + x), devices - 3 - (...  6.4 us
  transfers between devices with their start and end apart: 21, of which 7 were waited for; matrix products, arithmetic and copies ran while one was open for 0% of the time, Pallas kernels for 21%

profile of v6, /device:TPU:8, one launch (start us, length us, event | category | flops | bytes accessed | tf_op | source)
XLA Modules:
  0.0 162.1 jit_solution(1143584832538501745)
XLA Ops:
  7.2 8.5 %pack.1 = (s32[16,64]{1,0:T(8,128)S(1)}, bf16[256,256]{1,0:T(8,128)(2,1)}, bf16[4,4,64,1024]{3,2,1,0:T(8,128)(2,1)}, bf16[4,64,1024]{2,1,0:T(8,128)(2,1)}, bf16[...) custom-call(s32[32]{0:T(128)} %bitcast.22, ...), custom_call_target="tpu_custom_call" | custom-call | bytes 65536 | tf_op jit(solution)/shard_map/pack/pallas_call | solution.py:621
  15.7 4.6 %all-to-all-start = ((bf16[4,4,64,1024]{3,2,1,0:T(8,128)(2,1)}), bf16[4,4,64,1024]{3,2,1,0:T(8,128)(2,1)}, u32[]{:S(2)}, u32[]{:S(2)}) async-start(bf16[4,4,64,1024]{3,2,1,0:T(8,128)(2,1)} %get-tuple-element.167), calls=%async_computation | async-start | bytes 4194304 | tf_op jit(solution)/shard_map/all_to_all | solution.py:648
  20.3 0.0 all-gather.2.cloned.1.call-start
  20.4 0.7 all-gather.2.cloned.1.call-update
  21.1 1.5 collective-permute-start.14
  22.6 2.5 %collective-permute-start.7 = (bf16[1056,128]{1,0:T(8,128)(2,1)S(1)}, bf16[1056,128]{1,0:T(8,128)(2,1)S(1)}, u32[]{:S(2)}, u32[]{:S(2)}) collective-permute-start(bf16[1056,128]{1,0:T(8,128)(2,1)S(1)} %copy-done.3), channel_id=1, source_target_pairs={{0,4},{1,5},{2,6},{3,7},{4,0},{5,1},{6,2},{7,3},{8,12},{9,13},{10,... | collective-permute-start | bytes 811016 | tf_op jit(solution)/shard_map/ppermute | solution.py:653
  25.1 0.4 collective-permute-start.8
  25.5 21.2 %collective-permute-done.7.rest_1_.rest_4_ = bf16[1056,128]{1,0:T(8,128)(2,1)S(1)} collective-permute-done((bf16[1056,128]{1,0:T(8,128)(2,1)S(1)}, bf16[1056,128]{1,0:T(8,128)(2,1)S(1)}, u32[]{:S(2)}, u32[]{:S(2)}) %collective-permute-start.7) | collective-permute-done | bytes 270368 | tf_op jit(solution)/shard_map/ppermute | solution.py:653
  46.7 1.9 %collective-permute-start.10 = (bf16[4,64,1024]{2,1,0:T(8,128)(2,1)}, bf16[4,64,1024]{2,1,0:T(8,128)(2,1)}, u32[]{:S(2)}, u32[]{:S(2)}) collective-permute-start(bf16[4,64,1024]{2,1,0:T(8,128)(2,1)} %get-tuple-element.179), channel_id=1, source_target_pairs={{0,16},{8,24},{16,0},{24,8},{1,17},{9,25},{17,1},{25,9},{2,18},{10... | collective-permute-start | bytes 1572872 | tf_op jit(solution)/shard_map/ppermute | solution.py:157
  48.5 0.6 slice.3
  49.1 0.1 broadcast_in_dim.12
  49.2 0.6 while.14
  49.9 0.1 collective-permute-start.11
  49.9 2.5 %prep.1 = (f32[32,2048]{1,0:T(8,128)}, f32[8,256,16]{2,1,0:T(8,128)}, f32[8,1024]{1,0:T(8,128)}) custom-call(f32[16]{0:T(128)} %rates.1, f32[16]{0:T(128)} %skips.1, f32[16,2048]{1,0:T(8,128)} %steps.1, f32[4,1024]{1,0:T(4,128)} %taps_in.1, f32[1,1024]{1,0:T(1,128)} %bitcast.21, s32[16,64]{1,0:T(8,128)S(1)} %get-tuple-element.297), custom_call_target="tpu_custom_call" | custom-call | bytes 65536 | tf_op jit(solution)/shard_map/prep/pallas_call | solution.py:662
  52.4 0.4 collective-permute-done.8.rest_2_.rest_5_
  52.8 0.0 all-to-all-done.table
  52.8 5.7 %shrink.1.rest_0_ = bf16[8,64,256]{2,1,0:T(8,128)(2,1)} custom-call(s32[16,64]{1,0:T(8,128)S(1)} %get-tuple-element.297, bf16[2048,1024]{1,0:T(8,128)(2,1)} %hidden.1, bf16[4,4,64,1024]{3,2,1,0:T(8,128)(2,1)} %all-to-all-done.table, f32[8,1024]{1,0:T(8,128)} %get-tuple-element.168.rest_0_.channel, bf16[1056,128]{1,0:T(8,128)(2,1)} %copy-done.2, ...), custom_call_target="tpu_custom_call" | custom-call | bytes 65536 | tf_op jit(solution)/shard_map/shrink/pallas_call | solution.py:680
  58.5 7.1 %all-to-all-start.1 = ((bf16[8,64,256]{2,1,0:T(8,128)(2,1)}), bf16[8,64,256]{2,1,0:T(8,128)(2,1)}, u32[]{:S(2)}, u32[]{:S(2)}) async-start(bf16[8,64,256]{2,1,0:T(8,128)(2,1)} %shrink.1.rest_0_), calls=%async_computation.1 | async-start | bytes 524288 | tf_op jit(solution)/shard_map/all_to_all | solution.py:699
  65.7 0.0 collective-permute-done.14.over_r.over_l.rest_9_
  65.7 2.7 %pick_1.8 = (bf16[1056,128]{1,0:T(8,128)(2,1)}, bf16[1056,128]{1,0:T(8,128)(2,1)}) custom-call(s32[1]{0:T(128)} %constant.34.clone.1.j, s32[16,64]{1,0:T(8,128)S(1)} %get-tuple-element.297, bf16[4,1056,128]{2,1,0:T(8,128)(2,1)} %get-tuple-element.183.own_r.own_l.rest_8_, bf16[4,1056,128]{2,1,0:T(8,128)(2,1)} %collective-permute-done.14.over_r.over_l.rest_9_, ...), custom_call_target="tpu_custom_call" | custom-call | bytes 65536 | tf_op jit(solution)/shard_map/pick_1/pallas_call | solution.py:313
  68.4 1.3 collective-permute-start.15
  69.7 1.4 collective-permute-start.16
  71.1 1.5 collective-permute-start.12
  72.6 5.4 %all-to-all-done.1 = bf16[8,64,256]{2,1,0:T(8,128)(2,1)} async-done(((bf16[8,64,256]{2,1,0:T(8,128)(2,1)}), bf16[8,64,256]{2,1,0:T(8,128)(2,1)}, u32[]{:S(2)}, u32[]{:S(2)}) %all-to-all-start.1) | async-done | bytes 262176 | tf_op jit(solution)/shard_map/all_to_all | solution.py:699
  78.0 1.7 %sum_parts.1.rest_2_ = bf16[8,1,64,256]{3,2,1,0:T(8,128)(2,1)} custom-call(bf16[8,1,64,256]{3,2,1,0:T(8,128)(2,1)} %bitcast.8.parts), custom_call_target="tpu_custom_call" | custom-call | bytes 65536 | tf_op jit(solution)/shard_map/sum_parts/pallas_call | solution.py:700
  79.7 0.0 collective-permute-done.10.rest_3_.rest_2_
  79.7 1.7 %collective-permute-done.15.rest_0_ = bf16[1056,128]{1,0:T(8,128)(2,1)} collective-permute-done((bf16[1056,128]{1,0:T(8,128)(2,1)}, bf16[1056,128]{1,0:T(8,128)(2,1)}, u32[]{:S(2)}, u32[]{:S(2)}) %collective-permute-start.15) | collective-permute-done | bytes 270368 | tf_op jit(solution)/shard_map/ppermute | solution.py:323
  81.4 0.0 collective-permute-done.16.rest_1_
  81.4 2.9 %pick_2.8 = (bf16[1056,128]{1,0:T(8,128)(2,1)}, bf16[1056,128]{1,0:T(8,128)(2,1)}) custom-call(s32[1]{0:T(128)} %constant.34.clone.1.j, s32[16,64]{1,0:T(8,128)S(1)} %get-tuple-element.297, bf16[4,1056,128]{2,1,0:T(8,128)(2,1)} %get-tuple-element.183.own_r.own_l.rest_8_, bf16[4,1056,128]{2,1,0:T(8,128)(2,1)} %collective-permute-done.14.over_r.over_l.rest_9_, ...), custom_call_target="tpu_custom_call" | custom-call | bytes 65536 | tf_op jit(solution)/shard_map/pick_2/pallas_call | solution.py:313
  84.2 4.5 %collective-permute-start.17 = (bf16[1056,128]{1,0:T(8,128)(2,1)}, bf16[1056,128]{1,0:T(8,128)(2,1)}, u32[]{:S(2)}, u32[]{:S(2)}) collective-permute-start(bf16[1056,128]{1,0:T(8,128)(2,1)} %get-tuple-element.187), channel_id=1, source_target_pairs={{0,2},{1,3},{2,4},{3,5},{8,10},{9,11},{10,12},{11,13},{16,18},{17,... | collective-permute-start | bytes 811016 | tf_op jit(solution)/shard_map/ppermute | solution.py:323
  88.8 1.3 collective-permute-start.18
  90.1 3.3 %collective-permute-start.13 = (bf16[1056,128]{1,0:T(8,128)(2,1)}, bf16[1056,128]{1,0:T(8,128)(2,1)}, u32[]{:S(2)}, u32[]{:S(2)}) collective-permute-start(bf16[1056,128]{1,0:T(8,128)(2,1)} %get-tuple-element.182), channel_id=1, source_target_pairs={{0,7},{1,6},{2,5},{3,4},{4,3},{5,2},{6,1},{7,0},{8,15},{9,14},{10,... | collective-permute-start | bytes 811016 | tf_op jit(solution)/shard_map/ppermute | solution.py:653
  93.3 0.9 collective-permute-start.21
  94.2 0.0 collective-permute-done.11.rest_3_
  94.2 0.0 collective-permute-start.9
  94.2 4.8 %all-to-all-start.2 = ((bf16[8,1,64,256]{3,2,1,0:T(8,128)(2,1)}), bf16[8,1,64,256]{3,2,1,0:T(8,128)(2,1)}, u32[]{:S(2)}, u32[]{:S(2)}) async-start(bf16[8,1,64,256]{3,2,1,0:T(8,128)(2,1)} %sum_parts.1.rest_2_), calls=%async_computation.2 | async-start | bytes 524288 | tf_op jit(solution)/shard_map/all_to_all | solution.py:709
  99.1 3.5 %collective-permute-done.17.rest_0_ = bf16[1056,128]{1,0:T(8,128)(2,1)} collective-permute-done((bf16[1056,128]{1,0:T(8,128)(2,1)}, bf16[1056,128]{1,0:T(8,128)(2,1)}, u32[]{:S(2)}, u32[]{:S(2)}) %collective-permute-start.17) | collective-permute-done | bytes 270368 | tf_op jit(solution)/shard_map/ppermute | solution.py:323
  102.6 6.4 %collective-permute-done.18.rest_1_ = bf16[1056,128]{1,0:T(8,128)(2,1)} collective-permute-done((bf16[1056,128]{1,0:T(8,128)(2,1)}, bf16[1056,128]{1,0:T(8,128)(2,1)}, u32[]{:S(2)}, u32[]{:S(2)}) %collective-permute-start.18) | collective-permute-done | bytes 270368 | tf_op jit(solution)/shard_map/ppermute | solution.py:327
  109.0 0.0 collective-permute-start.23
  109.0 2.9 %pick_3.8 = (bf16[1056,128]{1,0:T(8,128)(2,1)}, bf16[1056,128]{1,0:T(8,128)(2,1)}) custom-call(s32[1]{0:T(128)} %constant.34.clone.1.j, s32[16,64]{1,0:T(8,128)S(1)} %get-tuple-element.297, bf16[4,1056,128]{2,1,0:T(8,128)(2,1)} %get-tuple-element.183.own_r.own_l.rest_8_, bf16[4,1056,128]{2,1,0:T(8,128)(2,1)} %collective-permute-done.14.over_r.over_l.rest_9_, ...), custom_call_target="tpu_custom_call" | custom-call | bytes 65536 | tf_op jit(solution)/shard_map/pick_3/pallas_call | solution.py:313
  111.9 3.8 %collective-permute-done.13.rest_10_.rest_7_ = bf16[1056,128]{1,0:T(8,128)(2,1)} collective-permute-done((bf16[1056,128]{1,0:T(8,128)(2,1)}, bf16[1056,128]{1,0:T(8,128)(2,1)}, u32[]{:S(2)}, u32[]{:S(2)}) %collective-permute-start.13) | collective-permute-done | bytes 270368 | tf_op jit(solution)/shard_map/ppermute | solution.py:653
  115.6 1.9 %collective-permute-start.20 = (bf16[1056,128]{1,0:T(8,128)(2,1)}, bf16[1056,128]{1,0:T(8,128)(2,1)}, u32[]{:S(2)}, u32[]{:S(2)}) collective-permute-start(bf16[1056,128]{1,0:T(8,128)(2,1)} %get-tuple-element.190), channel_id=1, source_target_pairs={{7,5},{6,4},{5,3},{4,2},{3,1},{2,0},{15,13},{14,12},{13,11},{12,10... | collective-permute-start | bytes 811016 | tf_op jit(solution)/shard_map/ppermute | solution.py:327
  117.6 4.1 %collective-permute-start.19 = (bf16[1056,128]{1,0:T(8,128)(2,1)}, bf16[1056,128]{1,0:T(8,128)(2,1)}, u32[]{:S(2)}, u32[]{:S(2)}) collective-permute-start(bf16[1056,128]{1,0:T(8,128)(2,1)} %get-tuple-element.189.rest_8_), channel_id=1, source_target_pairs={{0,2},{1,3},{2,4},{3,5},{4,6},{5,7},{8,10},{9,11},{10,12},{11,13},... | collective-permute-start | bytes 811016 | tf_op jit(solution)/shard_map/ppermute | solution.py:323
  121.7 0.0 collective-permute-done.23.rest_7_
  121.7 0.0 collective-permute-done.9.rest_1_
  121.7 15.8 %mix_0.1 = (bf16[2048,1024]{1,0:T(8,128)(2,1)}, bf16[8,1024,128]{2,1,0:T(8,128)(2,1)}) custom-call(s32[16,64]{1,0:T(8,128)S(1)} %get-tuple-element.297, bf16[2048,1024]{1,0:T(8,128)(2,1)} %base.3, bf16[8,64,256]{2,1,0:T(8,128)(2,1)} %bitcast.9.shrunk, f32[8,1024]{1,0:T(8,128)} %get-tuple-element.168.rest_0_.channel, ...), custom_call_target="tpu_custom_call" | custom-call | bytes 65536 | tf_op jit(solution)/shard_map/mix_0/pallas_call | solution.py:746
  137.5 0.0 collective-permute-done.20.rest_11_
  137.6 17.6 %mix_4.1 = (bf16[2048,1024]{1,0:T(8,128)(2,1)}, bf16[8,1024,128]{2,1,0:T(8,128)(2,1)}) custom-call(s32[16,64]{1,0:T(8,128)S(1)} %get-tuple-element.297, bf16[2048,1024]{1,0:T(8,128)(2,1)} %base.3, bf16[8,64,256]{2,1,0:T(8,128)(2,1)} %bitcast.9.shrunk, f32[8,1024]{1,0:T(8,128)} %get-tuple-element.168.rest_0_.channel, ...), custom_call_target="tpu_custom_call", output_to_operand_aliasing={{0}: (20, {}), {1}: (21, {})} | custom-call | bytes 65536 | tf_op jit(solution)/shard_map/mix_4/pallas_call | solution.py:746
  (11 shorter events, 0.0 us)
Async XLA Ops:
  15.6 6.9 %copy-start.3 = (bf16[1056,128]{1,0:T(8,128)(2,1)S(1)}, bf16[1056,128]{1,0:T(8,128)(2,1)}, u32[]{:S(2)}) copy-start(bf16[1056,128]{1,0:T(8,128)(2,1)} %get-tuple-element.169) | copy-start | bytes 811012
  15.7 37.2 %all-to-all-start = ((bf16[4,4,64,1024]{3,2,1,0:T(8,128)(2,1)}), bf16[4,4,64,1024]{3,2,1,0:T(8,128)(2,1)}, u32[]{:S(2)}, u32[]{:S(2)}) async-start(bf16[4,4,64,1024]{3,2,1,0:T(8,128)(2,1)} %get-tuple-element.167), calls=%async_computation | async-start | bytes 4194304 | tf_op jit(solution)/shard_map/all_to_all | solution.py:648
  20.3 88.7 %all-gather.2.cloned.1.call-start = ((), (), s32[]{:S(2)}) async-start(), calls=%async_computation.3 | async-start | bytes 1179648 | tf_op jit(solution)/shard_map/all_gather | solution.py:650
  21.1 44.6 %collective-permute-start.14 = (bf16[4,1056,128]{2,1,0:T(8,128)(2,1)}, bf16[4,1056,128]{2,1,0:T(8,128)(2,1)}, u32[]{:S(2)}, u32[]{:S(2)}) collective-permute-start(bf16[4,1056,128]{2,1,0:T(8,128)(2,1)} %get-tuple-element.184), channel_id=1, source_target_pairs={{0,1},{1,0},{2,3},{3,2},{4,5},{5,4},{6,7},{7,6},{8,9},{9,8},{10,11... | collective-permute-start | bytes 3244040 | tf_op jit(solution)/shard_map/ppermute | solution.py:295
  22.6 24.1 %collective-permute-start.7 = (bf16[1056,128]{1,0:T(8,128)(2,1)S(1)}, bf16[1056,128]{1,0:T(8,128)(2,1)S(1)}, u32[]{:S(2)}, u32[]{:S(2)}) collective-permute-start(bf16[1056,128]{1,0:T(8,128)(2,1)S(1)} %copy-done.3), channel_id=1, source_target_pairs={{0,4},{1,5},{2,6},{3,7},{4,0},{5,1},{6,2},{7,3},{8,12},{9,13},{10,... | collective-permute-start | bytes 811016 | tf_op jit(solution)/shard_map/ppermute | solution.py:653
  25.1 27.7 %collective-permute-start.8 = (bf16[1056,128]{1,0:T(8,128)(2,1)}, bf16[1056,128]{1,0:T(8,128)(2,1)}, u32[]{:S(2)}, u32[]{:S(2)}) collective-permute-start(bf16[1056,128]{1,0:T(8,128)(2,1)} %get-tuple-element.170), channel_id=1, source_target_pairs={{0,5},{1,4},{2,7},{3,6},{4,1},{5,0},{6,3},{7,2},{8,13},{9,12},{10,... | collective-permute-start | bytes 811016 | tf_op jit(solution)/shard_map/ppermute | solution.py:653
  46.7 2.4 %copy-start.2 = (bf16[1056,128]{1,0:T(8,128)(2,1)}, bf16[1056,128]{1,0:T(8,128)(2,1)S(1)}, u32[]{:S(2)}) copy-start(bf16[1056,128]{1,0:T(8,128)(2,1)S(1)} %collective-permute-done.7.rest_1_.rest_4_) | copy-start | bytes 811012
  46.7 33.0 %collective-permute-start.10 = (bf16[4,64,1024]{2,1,0:T(8,128)(2,1)}, bf16[4,64,1024]{2,1,0:T(8,128)(2,1)}, u32[]{:S(2)}, u32[]{:S(2)}) collective-permute-start(bf16[4,64,1024]{2,1,0:T(8,128)(2,1)} %get-tuple-element.179), channel_id=1, source_target_pairs={{0,16},{8,24},{16,0},{24,8},{1,17},{9,25},{17,1},{25,9},{2,18},{10... | collective-permute-start | bytes 1572872 | tf_op jit(solution)/shard_map/ppermute | solution.py:157
  49.9 44.4 %collective-permute-start.11 = (bf16[4,64,1024]{2,1,0:T(8,128)(2,1)}, bf16[4,64,1024]{2,1,0:T(8,128)(2,1)}, u32[]{:S(2)}, u32[]{:S(2)}) collective-permute-start(bf16[4,64,1024]{2,1,0:T(8,128)(2,1)} %get-tuple-element.180), channel_id=1, source_target_pairs={{0,24},{8,16},{16,8},{24,0},{1,25},{9,17},{17,9},{25,1},{2,26},{10... | collective-permute-start | bytes 1572872 | tf_op jit(solution)/shard_map/ppermute | solution.py:157
  58.5 19.5 %all-to-all-start.1 = ((bf16[8,64,256]{2,1,0:T(8,128)(2,1)}), bf16[8,64,256]{2,1,0:T(8,128)(2,1)}, u32[]{:S(2)}, u32[]{:S(2)}) async-start(bf16[8,64,256]{2,1,0:T(8,128)(2,1)} %shrink.1.rest_0_), calls=%async_computation.1 | async-start | bytes 524288 | tf_op jit(solution)/shard_map/all_to_all | solution.py:699
  68.4 13.0 %collective-permute-start.15 = (bf16[1056,128]{1,0:T(8,128)(2,1)}, bf16[1056,128]{1,0:T(8,128)(2,1)}, u32[]{:S(2)}, u32[]{:S(2)}) collective-permute-start(bf16[1056,128]{1,0:T(8,128)(2,1)} %get-tuple-element.185), channel_id=1, source_target_pairs={{0,2},{1,3},{8,10},{9,11},{16,18},{17,19},{24,26},{25,27}} | collective-permute-start | bytes 811016 | tf_op jit(solution)/shard_map/ppermute | solution.py:323
  69.7 11.7 %collective-permute-start.16 = (bf16[1056,128]{1,0:T(8,128)(2,1)}, bf16[1056,128]{1,0:T(8,128)(2,1)}, u32[]{:S(2)}, u32[]{:S(2)}) collective-permute-start(bf16[1056,128]{1,0:T(8,128)(2,1)} %get-tuple-element.186), channel_id=1, source_target_pairs={{7,5},{6,4},{15,13},{14,12},{23,21},{22,20},{31,29},{30,28}} | collective-permute-start | bytes 811016 | tf_op jit(solution)/shard_map/ppermute | solution.py:327
  71.1 22.2 %collective-permute-start.12 = (bf16[1056,128]{1,0:T(8,128)(2,1)}, bf16[1056,128]{1,0:T(8,128)(2,1)}, u32[]{:S(2)}, u32[]{:S(2)}) collective-permute-start(bf16[1056,128]{1,0:T(8,128)(2,1)} %get-tuple-element.181), channel_id=1, source_target_pairs={{0,6},{1,7},{2,4},{3,5},{4,2},{5,3},{6,0},{7,1},{8,14},{9,15},{10,... | collective-permute-start | bytes 811016 | tf_op jit(solution)/shard_map/ppermute | solution.py:653
  84.2 18.3 %collective-permute-start.17 = (bf16[1056,128]{1,0:T(8,128)(2,1)}, bf16[1056,128]{1,0:T(8,128)(2,1)}, u32[]{:S(2)}, u32[]{:S(2)}) collective-permute-start(bf16[1056,128]{1,0:T(8,128)(2,1)} %get-tuple-element.187), channel_id=1, source_target_pairs={{0,2},{1,3},{2,4},{3,5},{8,10},{9,11},{10,12},{11,13},{16,18},{17,... | collective-permute-start | bytes 811016 | tf_op jit(solution)/shard_map/ppermute | solution.py:323
  88.8 20.2 %collective-permute-start.18 = (bf16[1056,128]{1,0:T(8,128)(2,1)}, bf16[1056,128]{1,0:T(8,128)(2,1)}, u32[]{:S(2)}, u32[]{:S(2)}) collective-permute-start(bf16[1056,128]{1,0:T(8,128)(2,1)} %get-tuple-element.188), channel_id=1, source_target_pairs={{7,5},{6,4},{5,3},{4,2},{15,13},{14,12},{13,11},{12,10},{23,21},{2... | collective-permute-start | bytes 811016 | tf_op jit(solution)/shard_map/ppermute | solution.py:327
  90.1 25.6 %collective-permute-start.13 = (bf16[1056,128]{1,0:T(8,128)(2,1)}, bf16[1056,128]{1,0:T(8,128)(2,1)}, u32[]{:S(2)}, u32[]{:S(2)}) collective-permute-start(bf16[1056,128]{1,0:T(8,128)(2,1)} %get-tuple-element.182), channel_id=1, source_target_pairs={{0,7},{1,6},{2,5},{3,4},{4,3},{5,2},{6,1},{7,0},{8,15},{9,14},{10,... | collective-permute-start | bytes 811016 | tf_op jit(solution)/shard_map/ppermute | solution.py:653
  93.3 24.2 %collective-permute-start.21 = (bf16[1056,128]{1,0:T(8,128)(2,1)}, bf16[1056,128]{1,0:T(8,128)(2,1)}, u32[]{:S(2)}, u32[]{:S(2)}) collective-permute-start(bf16[1056,128]{1,0:T(8,128)(2,1)} %get-tuple-element.192), channel_id=1, source_target_pairs={{0,1},{1,0},{2,3},{3,2},{4,5},{5,4},{6,7},{7,6},{8,9},{9,8},{10,11... | collective-permute-start | bytes 811016 | tf_op jit(solution)/shard_map/ppermute | solution.py:653
  94.2 27.5 %collective-permute-start.9 = (bf16[4,64,1024]{2,1,0:T(8,128)(2,1)}, bf16[4,64,1024]{2,1,0:T(8,128)(2,1)}, u32[]{:S(2)}, u32[]{:S(2)}) collective-permute-start(bf16[4,64,1024]{2,1,0:T(8,128)(2,1)} %get-tuple-element.178), channel_id=1, source_target_pairs={{0,8},{8,0},{16,24},{24,16},{1,9},{9,1},{17,25},{25,17},{2,10},{10... | collective-permute-start | bytes 1572872 | tf_op jit(solution)/shard_map/ppermute | solution.py:157
  94.2 27.5 %all-to-all-start.2 = ((bf16[8,1,64,256]{3,2,1,0:T(8,128)(2,1)}), bf16[8,1,64,256]{3,2,1,0:T(8,128)(2,1)}, u32[]{:S(2)}, u32[]{:S(2)}) async-start(bf16[8,1,64,256]{3,2,1,0:T(8,128)(2,1)} %sum_parts.1.rest_2_), calls=%async_computation.2 | async-start | bytes 524288 | tf_op jit(solution)/shard_map/all_to_all | solution.py:709
  102.6 19.1 %collective-permute-start.22 = (bf16[1056,128]{1,0:T(8,128)(2,1)}, bf16[1056,128]{1,0:T(8,128)(2,1)}, u32[]{:S(2)}, u32[]{:S(2)}) collective-permute-start(bf16[1056,128]{1,0:T(8,128)(2,1)} %get-tuple-element.193), channel_id=1, source_target_pairs={{0,2},{1,3},{2,0},{3,1},{4,6},{5,7},{6,4},{7,5},{8,10},{9,11},{10,... | collective-permute-start | bytes 811016 | tf_op jit(solution)/shard_map/ppermute | solution.py:653
  109.0 12.7 %collective-permute-start.23 = (bf16[1056,128]{1,0:T(8,128)(2,1)}, bf16[1056,128]{1,0:T(8,128)(2,1)}, u32[]{:S(2)}, u32[]{:S(2)}) collective-permute-start(bf16[1056,128]{1,0:T(8,128)(2,1)} %get-tuple-element.194), channel_id=1, source_target_pairs={{0,3},{1,2},{2,1},{3,0},{4,7},{5,6},{6,5},{7,4},{8,11},{9,10},{10,... | collective-permute-start | bytes 811016 | tf_op jit(solution)/shard_map/ppermute | solution.py:653
  115.6 21.9 %collective-permute-start.20 = (bf16[1056,128]{1,0:T(8,128)(2,1)}, bf16[1056,128]{1,0:T(8,128)(2,1)}, u32[]{:S(2)}, u32[]{:S(2)}) collective-permute-start(bf16[1056,128]{1,0:T(8,128)(2,1)} %get-tuple-element.190), channel_id=1, source_target_pairs={{7,5},{6,4},{5,3},{4,2},{3,1},{2,0},{15,13},{14,12},{13,11},{12,10... | collective-permute-start | bytes 811016 | tf_op jit(solution)/shard_map/ppermute | solution.py:327
  117.6 20.0 %collective-permute-start.19 = (bf16[1056,128]{1,0:T(8,128)(2,1)}, bf16[1056,128]{1,0:T(8,128)(2,1)}, u32[]{:S(2)}, u32[]{:S(2)}) collective-permute-start(bf16[1056,128]{1,0:T(8,128)(2,1)} %get-tuple-element.189.rest_8_), channel_id=1, source_target_pairs={{0,2},{1,3},{2,4},{3,5},{4,6},{5,7},{8,10},{9,11},{10,12},{11,13},... | collective-permute-start | bytes 811016 | tf_op jit(solution)/shard_map/ppermute | solution.py:323
Sparse Core Ops, SparseCore 0:
  23.3 54.0 all-gather.1

commit v7 on v6

--- a/solution.py
+++ b/solution.py
@@ -16,8 +16,8 @@
 TN = (((0,), (0,)), ((), ()))
 VMEM_LIMIT = 63 * 1024 * 1024
 
-HOME, DIST, ARANK, AINDEX, PRESENT, POS_REQ, POS_VALID, OSLOT, OHOLDER, MISC, SEND = range(11)
-MOST, ME, SLOT = range(3)
+HOME, DIST, ARANK, AINDEX, PRESENT, ENT_REQ, ENT_VALID, ENT_FROM, ENT_PLACE, MISC, SEND = range(11)
+ME, SLOT = range(2)
 META_SHAPE = (16, 64)
 
 
@@ -59,16 +59,16 @@
     return ranks
 
 
+def calls_of(devices, per_group):
+    near = devices - max(devices // 4, 1)
+    late = min(per_group, (devices - near) * CAP)
+    return (range(near), 0, per_group), (range(near, devices), per_group, late)
+
+
 def plan(groups, devices, per_group, home, index, holder, slot, blocks, meta):
     my_group = lax.axis_index("group")
     me = lax.axis_index("dev")
     first = my_group * per_group
-    limit = per_group // 2
-    for j in range(limit):
-        meta[POS_REQ, devices + j] = jnp.int32(-1)
-        meta[POS_VALID, devices + j] = jnp.int32(0)
-        meta[OSLOT, j] = jnp.int32(0)
-        meta[OHOLDER, j] = jnp.int32(0)
 
     homes = [home[first + q] for q in range(per_group)]
     for q, rank in enumerate(ranks_of(homes)):
@@ -92,49 +92,38 @@
 
     holders = [holder[first + q] for q in range(per_group)]
     ranks = ranks_of(holders)
-    count = jnp.int32(0)
-    my_slot = jnp.int32(0)
-    for q in range(per_group):
-        my_slot = jnp.where((holders[q] == me) & (ranks[q] == 0), slot[first + q], my_slot)
-
-        @pl.when(ranks[q] > 0)
-        def _():
-            meta[POS_REQ, devices + count] = jnp.int32(q)
-            meta[POS_VALID, devices + count] = jnp.int32(1)
-            meta[OSLOT, count] = slot[first + q]
-            meta[OHOLDER, count] = holders[q]
-
-        count = count + as_int(ranks[q] > 0)
-    spread = meta[POS_REQ, devices]
-    requests = []
-    for d in range(devices):
-        source = lax.bitwise_xor(me, d)
-        request = jnp.int32(-1)
+    for c in range(CAP):
+        chosen = jnp.int32(0)
         for q in range(per_group):
-            request = jnp.where((holders[q] == source) & (ranks[q] == 0), q, request)
-        meta[POS_VALID, d] = as_int(request >= 0)
-        requests.append(request)
-    requests += [meta[POS_REQ, devices + j] for j in range(limit)]
-    for begin, end in ((0, devices // 2), (devices // 2, devices + limit)):
-        last = jnp.int32(-1)
-        filled = []
-        for p in range(begin, end):
-            last = jnp.where(requests[p] >= 0, requests[p], last)
-            filled.append(last)
-        following = jnp.maximum(spread, 0)
-        for p in reversed(range(begin, end)):
-            following = jnp.where(filled[p - begin] >= 0, filled[p - begin], following)
-            meta[POS_REQ, p] = following
-    most = jnp.int32(0)
-    for g in range(groups):
-        labels = [holder[g * per_group + q] for q in range(per_group)]
-        total = jnp.int32(0)
-        for rank in ranks_of(labels):
-            total = total + as_int(rank > 0)
-        most = jnp.maximum(most, total)
-    meta[MISC, MOST] = most
+            chosen = jnp.where((holders[q] == me) & (ranks[q] == c), slot[first + q], chosen)
+        meta[MISC, SLOT + c] = chosen
     meta[MISC, ME] = me
-    meta[MISC, SLOT] = my_slot
+    for distances, begin, steps in calls_of(devices, per_group):
+        count = jnp.int32(0)
+        for d in distances:
+            for q in range(per_group):
+                hit = holders[q] == lax.bitwise_xor(me, d)
+
+                @pl.when(hit)
+                def _(d=d, q=q, count=count):
+                    meta[ENT_REQ, begin + count] = jnp.int32(q)
+                    meta[ENT_VALID, begin + count] = jnp.int32(1)
+                    meta[ENT_FROM, begin + count] = jnp.int32(d)
+                    meta[ENT_PLACE, begin + count] = ranks[q]
+
+                count = count + as_int(hit)
+
+        @pl.when(count == 0)
+        def _(begin=begin):
+            for row in (ENT_REQ, ENT_VALID, ENT_FROM, ENT_PLACE):
+                meta[row, begin] = meta[row, 0]
+
+        count = jnp.maximum(count, 1)
+        for i in range(1, steps):
+            @pl.when(i >= count)
+            def _(i=i, begin=begin):
+                meta[ENT_REQ, begin + i] = meta[ENT_REQ, begin + i - 1]
+                meta[ENT_VALID, begin + i] = jnp.int32(0)
 
 
 def start_adapters(groups, meta, table, outs, sems):
@@ -176,32 +165,14 @@
     copies = []
     for d in reversed(range(devices)):
         target = lax.bitwise_xor(meta[MISC, ME], d)
-        copy = pltpu.make_async_copy(
-            cache.at[meta[MISC, SLOT], target // 2, target % 2],
-            outs[d].at[pl.ds(0, cache.shape[3])], sems.at[d],
-        )
-        copy.start()
-        copies.append(copy)
+        for c in range(CAP):
+            copy = pltpu.make_async_copy(
+                cache.at[meta[MISC, SLOT + c], target],
+                outs[d].at[c, pl.ds(0, cache.shape[2])], sems.at[d, c],
+            )
+            copy.start()
+            copies.append(copy)
     return copies
-
-
-def start_across(j, meta, cache, across, own, sems):
-    x = meta[MISC, ME] % 2
-    copies = []
-    for k, (out, place) in enumerate(((across, 1 - x), (own, x))):
-        copy = pltpu.make_async_copy(
-            cache.at[meta[OSLOT, j], :, place], out.at[:, pl.ds(0, cache.shape[3])], sems.at[k]
-        )
-        copy.start()
-        copies.append(copy)
-    return copies
-
-
-def conv_across(lines, width, j, meta, conv, state_rows, across, own):
-    x = meta[MISC, ME] % 2
-    for out, place in ((across, 1 - x), (own, x)):
-        for m in range(lines):
-            copy_conv(conv, meta[OSLOT, j], 2 * m + place, width, out.at[m], state_rows)
 
 
 def pack_kernel(
@@ -210,177 +181,22 @@
 ):
     downs, rest = rest[:1], rest[1:]
     ups, rest = rest[:groups - 1], rest[groups - 1:]
-    chunks, (across, own, down_sems, up_sems, chunk_sems, across_sems) = (
-        rest[:devices], rest[devices:]
-    )
+    chunks, (down_sems, up_sems, chunk_sems) = rest[:devices], rest[devices:]
     plan(groups, devices, per_group, home, index, holder, slot, blocks, meta)
     copies = start_adapters(groups, meta, down, downs, down_sems)
     copies += start_state(devices, meta, cache, chunks, chunk_sems)
-    copies += start_across(0, meta, cache, across, own, across_sems)
     copies += start_adapters(groups, meta, up, ups, up_sems)
     depth = write.shape[1]
     rows_out[:, :depth] = write[...]
     rows_out[:, depth:] = read[...]
-    state_rows = cache.shape[3]
     for d in range(devices):
         target = lax.bitwise_xor(meta[MISC, ME], d)
-        copy_conv(conv, meta[MISC, SLOT], target, width, chunks[d], state_rows)
-    conv_across(devices // 2, width, 0, meta, conv, state_rows, across, own)
+        for c in range(CAP):
+            copy_conv(
+                conv, meta[MISC, SLOT + c], target, width, chunks[d].at[c], cache.shape[2]
+            )
     for copy in copies:
         copy.wait()
-
-
-def pack_across_kernel(lines, width, j, meta, cache, conv, across, own, sems):
-    copies = start_across(j[0], meta, cache, across, own, sems)
-    conv_across(lines, width, j[0], meta, conv, cache.shape[3], across, own)
-    for copy in copies:
-        copy.wait()
-
-
-def pick_kernel(step, lines, j, meta, own_r, over_r, own_l, over_l, *rest):
-    out_r, out_l = rest[-2:]
-    me = meta[MISC, ME]
-    source = meta[OHOLDER, j[0]]
-    same = source // 2 == me // 2
-    mine = same & (source % 2 == me % 2)
-    across = same & (source % 2 != me % 2)
-
-    @pl.when(mine)
-    def _():
-        out_r[...] = own_r[0]
-        out_l[...] = own_l[0]
-
-    @pl.when(across)
-    def _():
-        out_r[...] = over_r[0]
-        out_l[...] = over_l[0]
-
-    @pl.when(jnp.logical_not(same))
-    def _():
-        if step > 1:
-            out_r[...] = rest[0][...]
-            out_l[...] = rest[1][...]
-        else:
-            out_r[...] = jnp.zeros_like(out_r)
-            out_l[...] = jnp.zeros_like(out_l)
-
-
-def right_block(meta, step, lines):
-    return jnp.clip(lines + meta[MISC, ME] // 2 - step, 0, lines - 1)
-
-
-def left_block(meta, step, lines):
-    return jnp.clip(meta[MISC, ME] // 2 + step - lines, 0, lines - 1)
-
-
-def pack_across(j, meta, cache, conv, devices, width):
-    lines = devices // 2
-    shape = chunk_shape(cache, conv, width)
-    return pl.pallas_call(
-        functools.partial(pack_across_kernel, lines, width),
-        out_shape=tuple(jax.ShapeDtypeStruct((lines,) + shape, cache.dtype) for _ in range(2)),
-        in_specs=smem(2) + pinned(1) + vmem(1),
-        out_specs=tuple(vmem(2)),
-        scratch_shapes=[pltpu.SemaphoreType.DMA((2,))],
-        cost_estimate=cost(),
-        compiler_params=params(),
-        name="pack_across",
-    )(j, meta, cache, conv)
-
-
-def spread_steps(j, meta, packed, devices):
-    lines = devices // 2
-    send, own = packed
-    shape = own.shape[1:]
-    across = lax.ppermute(send, "dev", [(d, d ^ 1) for d in range(devices)])
-    from_left = from_right = None
-    after = yield across
-    whole = pl.BlockSpec(shape, lambda g, j, meta: (0, 0))
-    for step in range(1, lines):
-        blocks = [
-            pl.BlockSpec(
-                (1,) + shape, lambda g, j, meta, at=at, step=step: (at(meta, step, lines), 0, 0)
-            )
-            for at in (right_block, left_block)
-        ]
-        operands = [own, across, own, across]
-        in_specs = [blocks[0], blocks[0], blocks[1], blocks[1]]
-        if step > 1:
-            operands += [from_left, from_right]
-            in_specs += [whole, whole]
-        operands += after
-        in_specs += anywhere(len(after))
-        to_right, to_left = pl.pallas_call(
-            functools.partial(pick_kernel, step, lines),
-            grid_spec=pltpu.PrefetchScalarGridSpec(
-                num_scalar_prefetch=2, grid=(1,), in_specs=in_specs, out_specs=(whole, whole)
-            ),
-            out_shape=tuple(jax.ShapeDtypeStruct(shape, own.dtype) for _ in range(2)),
-            cost_estimate=cost(),
-            compiler_params=params(),
-            name=f"pick_{step}",
-        )(j, meta, *operands)
-        from_left = lax.ppermute(
-            to_right, "dev",
-            [(2 * i + x, 2 * i + 2 + x) for i in range(step) for x in range(2)],
-        )
-        from_right = lax.ppermute(
-            to_left, "dev",
-            [(devices - 1 - (2 * i + x), devices - 3 - (2 * i + x))
-             for i in range(step) for x in range(2)],
-        )
-        after = yield to_right
-    yield own, across, from_left, from_right
-
-
-def final_specs(shape):
-    line = pl.BlockSpec((1,) + shape, lambda g, j, meta: (meta[MISC, ME] // 2, 0, 0))
-    whole = pl.BlockSpec(shape, lambda g, j, meta: (0, 0))
-    return [line, line, whole, whole]
-
-
-def which_candidate(meta, source):
-    me = meta[MISC, ME]
-    same = source // 2 == me // 2
-    mine = same & (source % 2 == me % 2)
-    return jnp.where(mine, 0, jnp.where(same, 1, jnp.where(source // 2 < me // 2, 2, 3)))
-
-
-def final_kernel(j, meta, own, across, from_left, from_right, out):
-    which = which_candidate(meta, meta[OHOLDER, j[0]])
-    picks = (own.at[0], across.at[0], from_left, from_right)
-    for k, pick in enumerate(picks):
-        @pl.when(which == k)
-        def _(pick=pick):
-            out[...] = pick[...]
-
-
-def spread_rest(meta, cache, conv, devices, width, limit):
-    shape = chunk_shape(cache, conv, width)
-
-    def one(j, held):
-        jj = j.reshape(1)
-        packed = pack_across(jj, meta, cache, conv, devices, width)
-        steps = spread_steps(jj, meta, packed, devices)
-        next(steps)
-        for _ in range(devices // 2):
-            got = steps.send([])
-        block = pl.pallas_call(
-            final_kernel,
-            grid_spec=pltpu.PrefetchScalarGridSpec(
-                num_scalar_prefetch=2,
-                grid=(1,),
-                in_specs=final_specs(shape),
-                out_specs=pl.BlockSpec(shape, lambda g, j, meta: (0, 0)),
-            ),
-            out_shape=jax.ShapeDtypeStruct(shape, cache.dtype),
-            compiler_params=params(),
-            name="final_pick",
-        )(jj, meta, *got)
-        return lax.dynamic_update_slice_in_dim(held, block[None], j - 1, 0)
-
-    held = jnp.zeros((limit - 1,) + shape, cache.dtype)
-    return lax.fori_loop(jnp.int32(1), meta[MISC, MOST], one, held)
 
 
 def fetch_table(groups, meta, r, tables, out, sem):
@@ -463,16 +279,16 @@
 
 
 def mix_kernel(
-    groups, taps, begin, steps, direct, size, meta, base, shrunk, channel, rows_decay, column,
+    groups, taps, begin, steps, size, meta, base, shrunk, channel, rows_decay, column,
     rows_in, *rest
 ):
-    tables, chunks = rest[:groups], rest[groups:]
+    tables, chunks = rest[:groups], rest[groups:groups + lax.axis_size("dev")]
     out, final, extended, scores, carried, weighted, ups, curs, table_sems, chunk_sems = (
         rest[-10:]
     )
     g = pl.program_id(0)
-    position = begin + g
-    r = meta[POS_REQ, position]
+    entry = begin + g
+    r = meta[ENT_REQ, entry]
     length, width = base.shape
     half = length // 2
     heads = width // size
@@ -487,25 +303,17 @@
     @pl.when(g == 0)
     def _():
         for i in range(steps):
-            @pl.when(meta[POS_VALID, begin + i] > 0)
+            @pl.when(meta[ENT_VALID, begin + i] > 0)
             def _(i=i):
-                request = meta[POS_REQ, begin + i]
+                request = meta[ENT_REQ, begin + i]
                 fetch_table(groups, meta, request, tables, ups.at[i], table_sems.at[i])
-                if i < direct:
-                    fetch_chunk(chunks[i], i)
-                elif i > direct:
-                    fetch_chunk(chunks[direct + 4].at[i - direct - 1], i)
-                else:
-                    line = meta[MISC, ME] // 2
-                    own, across, from_left, from_right = chunks[direct:direct + 4]
-                    candidates = [own.at[line], across.at[line], from_left, from_right]
-                    which = which_candidate(meta, meta[OHOLDER, 0])
-                    for k, candidate in enumerate(candidates):
-                        @pl.when(which == k)
-                        def _(candidate=candidate):
-                            fetch_chunk(candidate, direct)
-
-    @pl.when(meta[POS_VALID, position] > 0)
+                source = meta[ENT_FROM, begin + i]
+                for d, chunk in enumerate(chunks):
+                    @pl.when(source == d)
+                    def _(chunk=chunk):
+                        fetch_chunk(chunk.at[meta[ENT_PLACE, begin + i]], i)
+
+    @pl.when(meta[ENT_VALID, entry] > 0)
     def _():
         present = meta[PRESENT, r] > 0
         write, read = rows_in[:, :depth], rows_in[:, depth:]
@@ -588,7 +396,7 @@
 
 def chunk_shape(cache, conv, width):
     conv_rows = conv.shape[0] * (width // 128)
-    return (cache.shape[3] + -(-conv_rows // 16) * 16, cache.shape[4])
+    return (cache.shape[2] + -(-conv_rows // 16) * 16, cache.shape[3])
 
 
 def body(
@@ -606,11 +414,9 @@
     rank = adapter_down_weight.shape[1]
     taps = convolution_weight.shape[0]
     bf16, f32 = jnp.bfloat16, jnp.float32
-    limit = per_group // 2
-    lines = devices // 2
 
     cache = state_space_cache.reshape(
-        state_space_cache.shape[0], lines, 2, heads * size, depth
+        state_space_cache.shape[0], devices, heads * size, depth
     )
     conv = convolution_cache.transpose(1, 0, 2)
     shape = chunk_shape(cache, conv, width)
@@ -625,16 +431,14 @@
             jax.ShapeDtypeStruct((state_input_matrix.shape[0], 2 * depth), bf16),
             jax.ShapeDtypeStruct((groups, ACAP) + adapter_down_weight.shape[1:], bf16),
             *picks,
-            *[jax.ShapeDtypeStruct(shape, bf16) for _ in range(devices)],
-            *[jax.ShapeDtypeStruct((lines,) + shape, bf16) for _ in range(2)],
+            *[jax.ShapeDtypeStruct((CAP,) + shape, bf16) for _ in range(devices)],
         ),
         in_specs=smem(5) + pinned(3) + vmem(3),
-        out_specs=tuple(smem(1) + vmem(2 + len(picks) + devices + 2)),
+        out_specs=tuple(smem(1) + vmem(2 + len(picks) + devices)),
         scratch_shapes=[
             pltpu.SemaphoreType.DMA((groups * ACAP,)),
             pltpu.SemaphoreType.DMA((groups * ACAP,)),
-            pltpu.SemaphoreType.DMA((devices,)),
-            pltpu.SemaphoreType.DMA((2,)),
+            pltpu.SemaphoreType.DMA((devices, CAP)),
         ],
         cost_estimate=cost(),
         compiler_params=params(),
@@ -646,17 +450,14 @@
     )
     meta, rows_mine, packed = packed[0], packed[1], packed[2:]
     down_got = lax.all_to_all(packed[0], "group", split_axis=0, concat_axis=0, tiled=True)
-    chunks = packed[groups:-2]
+    chunks = packed[groups:]
     rows_all = lax.all_gather(rows_mine, "dev", axis=0, tiled=True)
-    zero = jnp.zeros((1,), jnp.int32)
     got = [chunks[0]] + [
         lax.ppermute(chunks[d], "dev", [(s, s ^ d) for s in range(devices)])
         for d in range(1, devices)
     ]
 
-    spread_others = spread_rest(meta, cache, conv, devices, width, limit)
-
-    up_send, _ = lax.optimization_barrier((packed[1:groups], got[lines]))
+    up_send, _ = lax.optimization_barrier((packed[1:groups], got[1]))
     up_got = swap(up_send, groups)
 
     rows_decay, column_decay, channel = pl.pallas_call(
@@ -677,13 +478,14 @@
     )
 
     each = per_group // 2
+    early = [*got[1:devices // 2 + 1], up_got[0]]
     partial_down = pl.pallas_call(
         functools.partial(shrink_kernel, per_group),
         grid_spec=pltpu.PrefetchScalarGridSpec(
             num_scalar_prefetch=1,
             grid=(per_group // each,),
             in_specs=[pl.BlockSpec((each * T_REQ, hidden.shape[1]), lambda g, meta: (g, 0))]
-            + anywhere(5),
+            + anywhere(2 + len(early)),
             out_specs=pl.BlockSpec((each, rank, T_REQ), lambda g, meta: (g, 0, 0)),
             scratch_shapes=[
                 pltpu.VMEM((per_group,) + adapter_down_weight.shape[1:], bf16),
@@ -694,7 +496,7 @@
         cost_estimate=cost(),
         compiler_params=params(),
         name="shrink",
-    )(meta, hidden, down_got, channel, got[lines], got[lines + 1], spread_others)
+    )(meta, hidden, down_got, channel, *early)
 
     parts = lax.all_to_all(partial_down, "dev", split_axis=0, concat_axis=0, tiled=True)
     summed = pl.pallas_call(
@@ -709,22 +511,12 @@
     shrunk = lax.all_to_all(summed, "dev", split_axis=0, concat_axis=0, tiled=True)
     shrunk = shrunk.reshape(per_group, rank, T_REQ)
 
-    befores = [[partial_down], [summed, up_got[groups // 2 - 1]], [rows_all, up_got[-1]]]
-    spread = spread_steps(zero, meta, packed[-2:], devices)
-    next(spread)
-    for step in range(1, lines):
-        sent = spread.send(befores.pop(0) if befores else [])
-    spread = spread.send([])
-
     outs = None
-    for begin, steps in ((0, lines), (lines, devices - lines + limit)):
-        if begin == 0:
-            chunks, after = got[:lines], [sent, got[lines + 2], got[lines + 3]]
-        else:
-            chunks, after = [*got[lines:], *spread, spread_others], []
+    for distances, begin, steps in calls_of(devices, per_group):
+        ready = [got[d] if d < distances.stop else chunks[d] for d in range(devices)]
 
         def request(g, meta, begin=begin):
-            return meta[POS_REQ, begin + g]
+            return meta[ENT_REQ, begin + g]
 
         in_specs = [
             pl.BlockSpec((T_REQ, width), lambda g, meta: (request(g, meta), 0)),
@@ -733,10 +525,10 @@
             pl.BlockSpec((2 * heads, T_REQ), lambda g, meta: (0, request(g, meta))),
             pl.BlockSpec((1, T_REQ, heads), lambda g, meta: (request(g, meta), 0, 0)),
             pl.BlockSpec((T_REQ, 2 * depth), lambda g, meta: (request(g, meta), 0)),
-        ] + anywhere(groups + len(chunks) + len(after))
+        ] + anywhere(groups + devices)
         operands = [
             meta, base_in_projection, shrunk, channel, rows_decay, column_decay, rows_all,
-            adapter_up_weight, *up_got, *chunks, *after,
+            adapter_up_weight, *up_got, *ready,
         ]
         aliases = {}
         if outs is not None:
@@ -744,7 +536,7 @@
             operands += list(outs)
             in_specs += anywhere(2)
         outs = pl.pallas_call(
-            functools.partial(mix_kernel, groups, taps, begin, steps, lines, size),
+            functools.partial(mix_kernel, groups, taps, begin, steps, size),
             grid_spec=pltpu.PrefetchScalarGridSpec(
                 num_scalar_prefetch=1,
                 grid=(steps,),

time: 164 us -> 210 us (1.28)
  waiting for transfers between devices: 43 us -> 109 us
  starting transfers between devices: 43.2 us -> 30.1 us
  Pallas kernels: 60.3 us -> 51.8 us
    all_to_all x1, waiting for transfers between devices: 5.37 us -> 35.8 us  [body(): lax.all_to_all(partial_down, 'dev', split_axis=0, concat_axis=0, tiled=True)]
    all_to_all x1, waiting for transfers between devices: 0.01 us -> 27.5 us  [body(): lax.all_to_all(summed, 'dev', split_axis=0, concat_axis=0, tiled=True)]
    ppermute x7, waiting for transfers between devices: 25.3 us -> 45.8 us  [body(): lax.ppermute(chunks[d], 'dev', [(s, s ^ d) for s in range(devices)])]
    ppermute x7 -> x0, starting transfers between devices: 16 us -> none  [the longest x3 9.88 us: spread_steps(): lax.ppermute(to_right, 'dev', [(2 * i + x, 2 * i + 2 + x) for i in range(...]
    ppermute x7 -> x0, waiting for transfers between devices: 11.6 us -> none  [the longest x3 6.4 us: spread_steps(): lax.ppermute(to_left, 'dev', [(devices - 1 - (2 * i + x), devices - 3 - (...]
    pallas_call x3 -> x0, Pallas kernels: 8.48 us -> none  [spread_steps(): pl.pallas_call(functools.partial(pick_kernel, step, lines), grid_spec=plt...]
    ppermute x7, starting transfers between devices: 8.63 us -> 11.6 us  [body(): lax.ppermute(chunks[d], 'dev', [(s, s ^ d) for s in range(devices)])]
  transfers between devices with their start and end apart: 21 -> 14, of which waited for: 7 -> 7; matrix products, arithmetic and copies ran while one was open for 0% -> 0% of each run, Pallas kernels for 21% -> 16%
where the time goes in v7:
time: 210 us; the launch traced here: 207 us
  waiting for transfers between devices  109 us (52%)
  Pallas kernels  51.8 us (25%)
  starting transfers between devices  30.1 us (14%)
  between operations  14.1 us (7%)
    ppermute x7, waiting for transfers between devices, body(): lax.ppermute(chunks[d], 'dev', [(s, s ^ d) for s in range(devices)])  45.8 us
    all_to_all x1, waiting for transfers between devices, body(): lax.all_to_all(partial_down, 'dev', split_axis=0, concat_axis=0, tiled=True)  35.8 us
    pallas_call x2, Pallas kernels, body(): pl.pallas_call(functools.partial(mix_kernel, groups, taps, begin, steps,...  33 us
    all_to_all x1, waiting for transfers between devices, body(): lax.all_to_all(summed, 'dev', split_axis=0, concat_axis=0, tiled=True)  27.5 us
    ppermute x7, starting transfers between devices, body(): lax.ppermute(chunks[d], 'dev', [(s, s ^ d) for s in range(devices)])  11.6 us
    pallas_call x1, Pallas kernels, body(): pl.pallas_call(functools.partial(pack_kernel, groups, devices, per_group,...  8.62 us
    all_to_all x1, starting transfers between devices, body(): lax.all_to_all(partial_down, 'dev', split_axis=0, concat_axis=0, tiled=True)  7.43 us
    pallas_call x1, Pallas kernels, body(): pl.pallas_call(functools.partial(shrink_kernel, per_group), grid_spec=plt...  5.84 us
  transfers between devices with their start and end apart: 14, of which 7 were waited for; matrix products, arithmetic and copies ran while one was open for 0% of the time, Pallas kernels for 16%

profile of v7, /device:TPU:8, one launch (start us, length us, event | category | flops | bytes accessed | tf_op | source)
XLA Modules:
  0.0 206.6 jit_solution(7838483755948711068)
XLA Ops:
  7.2 8.6 %pack.1 = (s32[16,64]{1,0:T(8,128)}, bf16[256,256]{1,0:T(8,128)(2,1)}, bf16[4,4,64,1024]{3,2,1,0:T(8,128)(2,1)}, bf16[4,64,1024]{2,1,0:T(8,128)(2,1)}, bf16[4,64...) custom-call(s32[32]{0:T(128)} %bitcast.15, ...), custom_call_target="tpu_custom_call" | custom-call | bytes 65536 | tf_op jit(solution)/shard_map/pack/pallas_call | solution.py:427
  15.8 0.0 copy-start.4
  15.8 4.6 %all-to-all-start = ((bf16[4,4,64,1024]{3,2,1,0:T(8,128)(2,1)}), bf16[4,4,64,1024]{3,2,1,0:T(8,128)(2,1)}, u32[]{:S(2)}, u32[]{:S(2)}) async-start(bf16[4,4,64,1024]{3,2,1,0:T(8,128)(2,1)} %get-tuple-element.27), calls=%async_computation | async-start | bytes 4194304 | tf_op jit(solution)/shard_map/all_to_all | solution.py:452
  20.4 0.0 all-gather.2.cloned.1.call-start
  20.5 0.0 copy-done.4
  20.5 1.5 collective-permute-start
  22.0 0.0 all-gather.2.cloned.1.call-update
  22.0 0.7 collective-permute-start.1
  22.7 1.4 collective-permute-start.2
  24.1 2.7 %collective-permute-start.3 = (bf16[2,1056,128]{2,1,0:T(8,128)(2,1)}, bf16[2,1056,128]{2,1,0:T(8,128)(2,1)}, u32[]{:S(2)}, u32[]{:S(2)}) collective-permute-start(bf16[2,1056,128]{2,1,0:T(8,128)(2,1)} %get-tuple-element.32), channel_id=1, source_target_pairs={{0,4},{1,5},{2,6},{3,7},{4,0},{5,1},{6,2},{7,3},{8,12},{9,13},{10,... | collective-permute-start | bytes 1622024 | tf_op jit(solution)/shard_map/ppermute | solution.py:456
  26.9 8.2 %collective-permute-done.rest_1_.rest_5_ = bf16[2,1056,128]{2,1,0:T(8,128)(2,1)S(1)} collective-permute-done((bf16[2,1056,128]{2,1,0:T(8,128)(2,1)S(1)}, bf16[2,1056,128]{2,1,0:T(8,128)(2,1)S(1)}, u32[]{:S(2)}, u32[]{:S(2)}) %collective-permute-start) | collective-permute-done | bytes 540704 | tf_op jit(solution)/shard_map/ppermute | solution.py:456
  35.1 0.0 copy-start
  35.1 0.0 collective-permute-start.4
  35.1 2.7 %prep.1 = (f32[32,2048]{1,0:T(8,128)}, f32[8,256,16]{2,1,0:T(8,128)}, f32[8,1024]{1,0:T(8,128)}) custom-call(f32[16]{0:T(128)} %rates.1, f32[16]{0:T(128)} %skips.1, f32[16,2048]{1,0:T(8,128)} %steps.1, f32[4,1024]{1,0:T(4,128)} %taps_in.1, f32[1,1024]{1,0:T(1,128)} %bitcast.14, s32[16,64]{1,0:T(8,128)} %get-tuple-element.26.rest_0_.meta), custom_call_target="tpu_custom_call" | custom-call | bytes 65536 | tf_op jit(solution)/shard_map/prep/pallas_call | solution.py:463
  37.7 13.8 %collective-permute-done.1.rest_2_.rest_6_ = bf16[2,1056,128]{2,1,0:T(8,128)(2,1)} collective-permute-done((bf16[2,1056,128]{2,1,0:T(8,128)(2,1)}, bf16[2,1056,128]{2,1,0:T(8,128)(2,1)}, u32[]{:S(2)}, u32[]{:S(2)}) %collective-permute-start.1) | collective-permute-done | bytes 540704 | tf_op jit(solution)/shard_map/ppermute | solution.py:456
  51.5 16.1 %collective-permute-done.2.rest_3_.rest_7_ = bf16[2,1056,128]{2,1,0:T(8,128)(2,1)} collective-permute-done((bf16[2,1056,128]{2,1,0:T(8,128)(2,1)}, bf16[2,1056,128]{2,1,0:T(8,128)(2,1)}, u32[]{:S(2)}, u32[]{:S(2)}) %collective-permute-start.2) | collective-permute-done | bytes 540704 | tf_op jit(solution)/shard_map/ppermute | solution.py:456
  67.6 3.1 %collective-permute-done.3.rest_4_.rest_8_ = bf16[2,1056,128]{2,1,0:T(8,128)(2,1)} collective-permute-done((bf16[2,1056,128]{2,1,0:T(8,128)(2,1)}, bf16[2,1056,128]{2,1,0:T(8,128)(2,1)}, u32[]{:S(2)}, u32[]{:S(2)}) %collective-permute-start.3) | collective-permute-done | bytes 540704 | tf_op jit(solution)/shard_map/ppermute | solution.py:456
  70.7 0.0 collective-permute-done.4.rest_5_.rest_1_
  70.7 0.0 all-to-all-done.table
  70.7 0.0 copy-done
  70.7 5.8 %shrink.1 = bf16[8,64,256]{2,1,0:T(8,128)(2,1)} custom-call(s32[16,64]{1,0:T(8,128)} %get-tuple-element.26.rest_0_.meta, bf16[2048,1024]{1,0:T(8,128)(2,1)} %hidden.1, bf16[4,4,64,1024]{3,2,1,0:T(8,128)(2,1)} %all-to-all-done.table, f32[8,1024]{1,0:T(8,128)} %get-tuple-element.28.rest_0_.channel, bf16[2,1056,128]{2,1,0:T(8,128)(2,1)} %copy-done, ...), custom_call_target="tpu_custom_call" | custom-call | bytes 65536 | tf_op jit(solution)/shard_map/shrink/pallas_call | solution.py:482
  76.6 7.4 %all-to-all-start.1 = ((bf16[8,64,256]{2,1,0:T(8,128)(2,1)}), bf16[8,64,256]{2,1,0:T(8,128)(2,1)S(1)}, u32[]{:S(2)}, u32[]{:S(2)}) async-start(bf16[8,64,256]{2,1,0:T(8,128)(2,1)} %shrink.1), calls=%async_computation.1 | async-start | bytes 524288 | tf_op jit(solution)/shard_map/all_to_all | solution.py:501
  84.0 3.3 %collective-permute-start.7 = (bf16[2,1056,128]{2,1,0:T(8,128)(2,1)}, bf16[2,1056,128]{2,1,0:T(8,128)(2,1)S(1)}, u32[]{:S(2)}, u32[]{:S(2)}) collective-permute-start(bf16[2,1056,128]{2,1,0:T(8,128)(2,1)} %get-tuple-element.43), channel_id=1, source_target_pairs={{0,5},{1,4},{2,7},{3,6},{4,1},{5,0},{6,3},{7,2},{8,13},{9,12},{10,... | collective-permute-start | bytes 1622024 | tf_op jit(solution)/shard_map/ppermute | solution.py:456
  87.3 0.0 collective-permute-start.8
  87.3 2.0 collective-permute-start.9
  89.3 1.8 collective-permute-start.5
  91.1 0.0 collective-permute-start.6
  91.1 35.8 %all-to-all-done.1 = bf16[8,64,256]{2,1,0:T(8,128)(2,1)S(1)} async-done(((bf16[8,64,256]{2,1,0:T(8,128)(2,1)}), bf16[8,64,256]{2,1,0:T(8,128)(2,1)S(1)}, u32[]{:S(2)}, u32[]{:S(2)}) %all-to-all-start.1) | async-done | bytes 262176 | tf_op jit(solution)/shard_map/all_to_all | solution.py:501
  126.9 0.0 copy-start.3
  126.9 0.7 copy-done.3
  127.6 1.7 sum_parts.1
  129.3 4.6 %all-to-all-start.2 = ((bf16[8,1,64,256]{3,2,1,0:T(8,128)(2,1)}), bf16[8,1,64,256]{3,2,1,0:T(8,128)(2,1)S(1)}, u32[]{:S(2)}, u32[]{:S(2)}) async-start(bf16[8,1,64,256]{3,2,1,0:T(8,128)(2,1)} %sum_parts.1), calls=%async_computation.2 | async-start | bytes 524288 | tf_op jit(solution)/shard_map/all_to_all | solution.py:511
  133.9 4.6 %collective-permute-done.7.rest_9_ = bf16[2,1056,128]{2,1,0:T(8,128)(2,1)S(1)} collective-permute-done((bf16[2,1056,128]{2,1,0:T(8,128)(2,1)}, bf16[2,1056,128]{2,1,0:T(8,128)(2,1)S(1)}, u32[]{:S(2)}, u32[]{:S(2)}) %collective-permute-start.7) | collective-permute-done | bytes 540704 | tf_op jit(solution)/shard_map/ppermute | solution.py:456
  138.5 0.0 copy-start.2
  138.5 0.0 collective-permute-done.5.rest_2_
  138.5 0.0 collective-permute-done.6.rest_3_
  138.5 0.0 all-gather.2.cloned.1.call-done.rows_in
  138.5 27.5 %all-to-all-done.2 = bf16[8,1,64,256]{3,2,1,0:T(8,128)(2,1)S(1)} async-done(((bf16[8,1,64,256]{3,2,1,0:T(8,128)(2,1)}), bf16[8,1,64,256]{3,2,1,0:T(8,128)(2,1)S(1)}, u32[]{:S(2)}, u32[]{:S(2)}) %all-to-all-start.2) | async-done | bytes 262176 | tf_op jit(solution)/shard_map/all_to_all | solution.py:511
  166.0 0.0 copy-start.1
  166.0 0.0 copy-done.2
  166.0 0.7 copy-done.1
  166.7 22.8 %mix_0.1 = (bf16[2048,1024]{1,0:T(8,128)(2,1)}, bf16[8,1024,128]{2,1,0:T(8,128)(2,1)}) custom-call(s32[16,64]{1,0:T(8,128)} %get-tuple-element.26.rest_0_.meta, bf16[2048,1024]{1,0:T(8,128)(2,1)} %base.3, bf16[8,64,256]{2,1,0:T(8,128)(2,1)} %bitcast.9, f32[8,1024]{1,0:T(8,128)} %get-tuple-element.28.rest_0_.channel, ...), custom_call_target="tpu_custom_call" | custom-call | bytes 65536 | tf_op jit(solution)/shard_map/mix_0/pallas_call | solution.py:538
  189.5 0.0 collective-permute-done.8.rest_10_
  189.5 0.0 collective-permute-done.9.rest_11_
  189.5 10.2 %mix_8.1 = (bf16[2048,1024]{1,0:T(8,128)(2,1)}, bf16[8,1024,128]{2,1,0:T(8,128)(2,1)}) custom-call(s32[16,64]{1,0:T(8,128)} %get-tuple-element.26.rest_0_.meta, bf16[2048,1024]{1,0:T(8,128)(2,1)} %base.3, bf16[8,64,256]{2,1,0:T(8,128)(2,1)} %bitcast.10, f32[8,1024]{1,0:T(8,128)} %get-tuple-element.28.rest_0_.channel, ...), custom_call_target="tpu_custom_call", output_to_operand_aliasing={{0}: (19, {}), {1}: (20, {})} | custom-call | bytes 65536 | tf_op jit(solution)/shard_map/mix_8/pallas_call | solution.py:538
Async XLA Ops:
  15.8 4.7 %copy-start.4 = (bf16[2,1056,128]{2,1,0:T(8,128)(2,1)S(1)}, bf16[2,1056,128]{2,1,0:T(8,128)(2,1)}, u32[]{:S(2)}) copy-start(bf16[2,1056,128]{2,1,0:T(8,128)(2,1)} %get-tuple-element.29) | copy-start | bytes 1622020
  15.8 54.9 %all-to-all-start = ((bf16[4,4,64,1024]{3,2,1,0:T(8,128)(2,1)}), bf16[4,4,64,1024]{3,2,1,0:T(8,128)(2,1)}, u32[]{:S(2)}, u32[]{:S(2)}) async-start(bf16[4,4,64,1024]{3,2,1,0:T(8,128)(2,1)} %get-tuple-element.27), calls=%async_computation | async-start | bytes 4194304 | tf_op jit(solution)/shard_map/all_to_all | solution.py:452
  20.4 118.1 %all-gather.2.cloned.1.call-start = ((), (), s32[]{:S(2)}) async-start(), calls=%async_computation.3 | async-start | bytes 1179648 | tf_op jit(solution)/shard_map/all_gather | solution.py:454
  20.5 14.6 %collective-permute-start = (bf16[2,1056,128]{2,1,0:T(8,128)(2,1)S(1)}, bf16[2,1056,128]{2,1,0:T(8,128)(2,1)S(1)}, u32[]{:S(2)}, u32[]{:S(2)}) collective-permute-start(bf16[2,1056,128]{2,1,0:T(8,128)(2,1)S(1)} %copy-done.4), channel_id=1, source_target_pairs={{0,1},{1,0},{2,3},{3,2},{4,5},{5,4},{6,7},{7,6},{8,9},{9,8},{10,11... | collective-permute-start | bytes 1622024 | tf_op jit(solution)/shard_map/ppermute | solution.py:456
  22.0 29.5 %collective-permute-start.1 = (bf16[2,1056,128]{2,1,0:T(8,128)(2,1)}, bf16[2,1056,128]{2,1,0:T(8,128)(2,1)}, u32[]{:S(2)}, u32[]{:S(2)}) collective-permute-start(bf16[2,1056,128]{2,1,0:T(8,128)(2,1)} %get-tuple-element.30), channel_id=1, source_target_pairs={{0,2},{1,3},{2,0},{3,1},{4,6},{5,7},{6,4},{7,5},{8,10},{9,11},{10,... | collective-permute-start | bytes 1622024 | tf_op jit(solution)/shard_map/ppermute | solution.py:456
  22.7 44.9 %collective-permute-start.2 = (bf16[2,1056,128]{2,1,0:T(8,128)(2,1)}, bf16[2,1056,128]{2,1,0:T(8,128)(2,1)}, u32[]{:S(2)}, u32[]{:S(2)}) collective-permute-start(bf16[2,1056,128]{2,1,0:T(8,128)(2,1)} %get-tuple-element.31), channel_id=1, source_target_pairs={{0,3},{1,2},{2,1},{3,0},{4,7},{5,6},{6,5},{7,4},{8,11},{9,10},{10,... | collective-permute-start | bytes 1622024 | tf_op jit(solution)/shard_map/ppermute | solution.py:456
  24.1 46.6 %collective-permute-start.3 = (bf16[2,1056,128]{2,1,0:T(8,128)(2,1)}, bf16[2,1056,128]{2,1,0:T(8,128)(2,1)}, u32[]{:S(2)}, u32[]{:S(2)}) collective-permute-start(bf16[2,1056,128]{2,1,0:T(8,128)(2,1)} %get-tuple-element.32), channel_id=1, source_target_pairs={{0,4},{1,5},{2,6},{3,7},{4,0},{5,1},{6,2},{7,3},{8,12},{9,13},{10,... | collective-permute-start | bytes 1622024 | tf_op jit(solution)/shard_map/ppermute | solution.py:456
  35.1 35.6 %copy-start = (bf16[2,1056,128]{2,1,0:T(8,128)(2,1)}, bf16[2,1056,128]{2,1,0:T(8,128)(2,1)S(1)}, u32[]{:S(2)}) copy-start(bf16[2,1056,128]{2,1,0:T(8,128)(2,1)S(1)} %collective-permute-done.rest_1_.rest_5_) | copy-start | bytes 1622020
  35.1 35.6 %collective-permute-start.4 = (bf16[4,64,1024]{2,1,0:T(8,128)(2,1)}, bf16[4,64,1024]{2,1,0:T(8,128)(2,1)}, u32[]{:S(2)}, u32[]{:S(2)}) collective-permute-start(bf16[4,64,1024]{2,1,0:T(8,128)(2,1)} %get-tuple-element.36), channel_id=1, source_target_pairs={{0,8},{8,0},{16,24},{24,16},{1,9},{9,1},{17,25},{25,17},{2,10},{10... | collective-permute-start | bytes 1572872 | tf_op jit(solution)/shard_map/ppermute | solution.py:146
  76.6 50.3 %all-to-all-start.1 = ((bf16[8,64,256]{2,1,0:T(8,128)(2,1)}), bf16[8,64,256]{2,1,0:T(8,128)(2,1)S(1)}, u32[]{:S(2)}, u32[]{:S(2)}) async-start(bf16[8,64,256]{2,1,0:T(8,128)(2,1)} %shrink.1), calls=%async_computation.1 | async-start | bytes 524288 | tf_op jit(solution)/shard_map/all_to_all | solution.py:501
  84.0 54.5 %collective-permute-start.7 = (bf16[2,1056,128]{2,1,0:T(8,128)(2,1)}, bf16[2,1056,128]{2,1,0:T(8,128)(2,1)S(1)}, u32[]{:S(2)}, u32[]{:S(2)}) collective-permute-start(bf16[2,1056,128]{2,1,0:T(8,128)(2,1)} %get-tuple-element.43), channel_id=1, source_target_pairs={{0,5},{1,4},{2,7},{3,6},{4,1},{5,0},{6,3},{7,2},{8,13},{9,12},{10,... | collective-permute-start | bytes 1622024 | tf_op jit(solution)/shard_map/ppermute | solution.py:456
  87.3 102.3 %collective-permute-start.8 = (bf16[2,1056,128]{2,1,0:T(8,128)(2,1)}, bf16[2,1056,128]{2,1,0:T(8,128)(2,1)}, u32[]{:S(2)}, u32[]{:S(2)}) collective-permute-start(bf16[2,1056,128]{2,1,0:T(8,128)(2,1)} %get-tuple-element.44.rest_10_), channel_id=1, source_target_pairs={{0,6},{1,7},{2,4},{3,5},{4,2},{5,3},{6,0},{7,1},{8,14},{9,15},{10,... | collective-permute-start | bytes 1622024 | tf_op jit(solution)/shard_map/ppermute | solution.py:456
  87.3 102.3 %collective-permute-start.9 = (bf16[2,1056,128]{2,1,0:T(8,128)(2,1)}, bf16[2,1056,128]{2,1,0:T(8,128)(2,1)}, u32[]{:S(2)}, u32[]{:S(2)}) collective-permute-start(bf16[2,1056,128]{2,1,0:T(8,128)(2,1)} %get-tuple-element.45.rest_11_), channel_id=1, source_target_pairs={{0,7},{1,6},{2,5},{3,4},{4,3},{5,2},{6,1},{7,0},{8,15},{9,14},{10,... | collective-permute-start | bytes 1622024 | tf_op jit(solution)/shard_map/ppermute | solution.py:456
  89.3 49.2 %collective-permute-start.5 = (bf16[4,64,1024]{2,1,0:T(8,128)(2,1)}, bf16[4,64,1024]{2,1,0:T(8,128)(2,1)}, u32[]{:S(2)}, u32[]{:S(2)}) collective-permute-start(bf16[4,64,1024]{2,1,0:T(8,128)(2,1)} %get-tuple-element.40), channel_id=1, source_target_pairs={{0,16},{8,24},{16,0},{24,8},{1,17},{9,25},{17,1},{25,9},{2,18},{10... | collective-permute-start | bytes 1572872 | tf_op jit(solution)/shard_map/ppermute | solution.py:146
  91.1 47.4 %collective-permute-start.6 = (bf16[4,64,1024]{2,1,0:T(8,128)(2,1)}, bf16[4,64,1024]{2,1,0:T(8,128)(2,1)}, u32[]{:S(2)}, u32[]{:S(2)}) collective-permute-start(bf16[4,64,1024]{2,1,0:T(8,128)(2,1)} %get-tuple-element.41), channel_id=1, source_target_pairs={{0,24},{8,16},{16,8},{24,0},{1,25},{9,17},{17,9},{25,1},{2,26},{10... | collective-permute-start | bytes 1572872 | tf_op jit(solution)/shard_map/ppermute | solution.py:146
  126.9 0.7 copy-start.3
  129.3 36.7 %all-to-all-start.2 = ((bf16[8,1,64,256]{3,2,1,0:T(8,128)(2,1)}), bf16[8,1,64,256]{3,2,1,0:T(8,128)(2,1)S(1)}, u32[]{:S(2)}, u32[]{:S(2)}) async-start(bf16[8,1,64,256]{3,2,1,0:T(8,128)(2,1)} %sum_parts.1), calls=%async_computation.2 | async-start | bytes 524288 | tf_op jit(solution)/shard_map/all_to_all | solution.py:511
  138.5 27.5 %copy-start.2 = (bf16[2,1056,128]{2,1,0:T(8,128)(2,1)}, bf16[2,1056,128]{2,1,0:T(8,128)(2,1)S(1)}, u32[]{:S(2)}) copy-start(bf16[2,1056,128]{2,1,0:T(8,128)(2,1)S(1)} %collective-permute-done.7.rest_9_) | copy-start | bytes 1622020
  166.0 0.7 copy-start.1
Sparse Core Ops, SparseCore 0:
  23.4 51.9 all-gather.1

commit v8 on v6

--- a/solution.py
+++ b/solution.py
@@ -57,6 +57,10 @@
             total = total + as_int(other == label)
         ranks.append(total)
     return ranks
+
+
+def near_distances(devices):
+    return devices - max(devices // 4, 1)
 
 
 def plan(groups, devices, per_group, home, index, holder, slot, blocks, meta):
@@ -115,7 +119,8 @@
         meta[POS_VALID, d] = as_int(request >= 0)
         requests.append(request)
     requests += [meta[POS_REQ, devices + j] for j in range(limit)]
-    for begin, end in ((0, devices // 2), (devices // 2, devices + limit)):
+    near = near_distances(devices)
+    for begin, end in ((0, near), (near, devices + limit)):
         last = jnp.int32(-1)
         filled = []
         for p in range(begin, end):
@@ -467,8 +472,8 @@
     rows_in, *rest
 ):
     tables, chunks = rest[:groups], rest[groups:]
-    out, final, extended, scores, carried, weighted, ups, curs, table_sems, chunk_sems = (
-        rest[-10:]
+    out, final, done, extended, scores, carried, weighted, ups, curs, table_sems, chunk_sems = (
+        rest[-11:]
     )
     g = pl.program_id(0)
     position = begin + g
@@ -480,6 +485,8 @@
     few = taps - 1
     parts = width // 128
     f32, bf16 = jnp.float32, jnp.bfloat16
+
+    done[...] = jnp.zeros_like(done)
 
     def fetch_chunk(source, i):
         pltpu.make_async_copy(source, curs.at[i], chunk_sems.at[i]).start()
@@ -649,14 +656,15 @@
     chunks = packed[groups:-2]
     rows_all = lax.all_gather(rows_mine, "dev", axis=0, tiled=True)
     zero = jnp.zeros((1,), jnp.int32)
+    near = near_distances(devices)
     got = [chunks[0]] + [
         lax.ppermute(chunks[d], "dev", [(s, s ^ d) for s in range(devices)])
-        for d in range(1, devices)
+        for d in range(1, near)
     ]
 
     spread_others = spread_rest(meta, cache, conv, devices, width, limit)
 
-    up_send, _ = lax.optimization_barrier((packed[1:groups], got[lines]))
+    up_send, _ = lax.optimization_barrier((packed[1:groups], got[2]))
     up_got = swap(up_send, groups)
 
     rows_decay, column_decay, channel = pl.pallas_call(
@@ -677,13 +685,14 @@
     )
 
     each = per_group // 2
+    early = got[2:]
     partial_down = pl.pallas_call(
         functools.partial(shrink_kernel, per_group),
         grid_spec=pltpu.PrefetchScalarGridSpec(
             num_scalar_prefetch=1,
             grid=(per_group // each,),
             in_specs=[pl.BlockSpec((each * T_REQ, hidden.shape[1]), lambda g, meta: (g, 0))]
-            + anywhere(5),
+            + anywhere(3 + len(early)),
             out_specs=pl.BlockSpec((each, rank, T_REQ), lambda g, meta: (g, 0, 0)),
             scratch_shapes=[
                 pltpu.VMEM((per_group,) + adapter_down_weight.shape[1:], bf16),
@@ -694,7 +703,7 @@
         cost_estimate=cost(),
         compiler_params=params(),
         name="shrink",
-    )(meta, hidden, down_got, channel, got[lines], got[lines + 1], spread_others)
+    )(meta, hidden, down_got, channel, spread_others, *early)
 
     parts = lax.all_to_all(partial_down, "dev", split_axis=0, concat_axis=0, tiled=True)
     summed = pl.pallas_call(
@@ -709,19 +718,23 @@
     shrunk = lax.all_to_all(summed, "dev", split_axis=0, concat_axis=0, tiled=True)
     shrunk = shrunk.reshape(per_group, rank, T_REQ)
 
-    befores = [[partial_down], [summed, up_got[groups // 2 - 1]], [rows_all, up_got[-1]]]
+    late, _ = lax.optimization_barrier((chunks[near:], shrunk))
+    got += [
+        lax.ppermute(x, "dev", [(s, s ^ d) for s in range(devices)])
+        for d, x in zip(range(near, devices), late)
+    ]
     spread = spread_steps(zero, meta, packed[-2:], devices)
     next(spread)
-    for step in range(1, lines):
-        sent = spread.send(befores.pop(0) if befores else [])
-    spread = spread.send([])
+    for step in range(1, lines - 1):
+        sent = spread.send([partial_down] if step < lines - 2 else [shrunk])
 
     outs = None
-    for begin, steps in ((0, lines), (lines, devices - lines + limit)):
+    for begin, steps in ((0, near), (near, devices - near + limit)):
         if begin == 0:
-            chunks, after = got[:lines], [sent, got[lines + 2], got[lines + 3]]
+            chunks, after = got[:near], [sent]
         else:
-            chunks, after = [*got[lines:], *spread, spread_others], []
+            spread.send([outs[2]])
+            chunks, after = [*got[near:], *spread.send([]), spread_others], []
 
         def request(g, meta, begin=begin):
             return meta[POS_REQ, begin + g]
@@ -741,10 +754,12 @@
         aliases = {}
         if outs is not None:
             aliases = {len(operands): 0, len(operands) + 1: 1}
-            operands += list(outs)
+            operands += list(outs[:2])
             in_specs += anywhere(2)
         outs = pl.pallas_call(
-            functools.partial(mix_kernel, groups, taps, begin, steps, lines, size),
+            functools.partial(
+                mix_kernel, groups, taps, begin, steps, near if begin == 0 else devices - near, size
+            ),
             grid_spec=pltpu.PrefetchScalarGridSpec(
                 num_scalar_prefetch=1,
                 grid=(steps,),
@@ -754,6 +769,7 @@
                     pl.BlockSpec(
                         (1, heads * size, depth), lambda g, meta: (request(g, meta), 0, 0)
                     ),
+                    pl.BlockSpec((8, 128), lambda g, meta: (0, 0)),
                 ),
                 scratch_shapes=[
                     pltpu.VMEM((T_REQ + 8, width), f32),
@@ -769,6 +785,7 @@
             out_shape=(
                 jax.ShapeDtypeStruct((tokens, width), bf16),
                 jax.ShapeDtypeStruct((per_group, heads * size, depth), bf16),
+                jax.ShapeDtypeStruct((8, 128), f32),
             ),
             input_output_aliases=aliases,
             cost_estimate=cost(),

time: 164 us -> 175 us (1.067)
  waiting for transfers between devices: 43 us -> 51 us
  starting transfers between devices: 43.2 us -> 48.2 us
    ppermute x3, waiting for transfers between devices: 0.01 us -> 5.98 us  [swap(): lax.ppermute(packed[k - 1], 'group', [(g, g ^ k) for g in range(groups)])]
    all_to_all x1, waiting for transfers between devices: 0.01 us -> 3.74 us  [body(): lax.all_to_all(summed, 'dev', split_axis=0, concat_axis=0, tiled=True)]
    ppermute x0 -> x2, starting transfers between devices: none -> 2.97 us  [body(): lax.ppermute(x, 'dev', [(s, s ^ d) for s in range(devices)])]
    ppermute x3, starting transfers between devices: 4.6 us -> 7.23 us  [spread_steps(): lax.ppermute(to_left, 'dev', [(devices - 1 - (2 * i + x), devices - 3 - (...]
    ppermute x7 -> x5, waiting for transfers between devices: 25.3 us -> 24.1 us  [body(): lax.ppermute(chunks[d], 'dev', [(s, s ^ d) for s in range(devices)])]
    ppermute x7 -> x5, starting transfers between devices: 8.63 us -> 7.45 us  [body(): lax.ppermute(chunks[d], 'dev', [(s, s ^ d) for s in range(devices)])]
  transfers between devices with their start and end apart: 21 -> 21, of which waited for: 7 -> 8; matrix products, arithmetic and copies ran while one was open for 0% -> 0% of each run, Pallas kernels for 21% -> 22%
where the time goes in v8:
time: 175 us
  Pallas kernels  59.9 us (34%)
  waiting for transfers between devices  51 us (29%)
  starting transfers between devices  48.2 us (28%)
  between operations  14.2 us (8%)
    pallas_call x2, Pallas kernels, body(): pl.pallas_call(functools.partial(mix_kernel, groups, taps, begin, steps,...  33.5 us
    ppermute x5, waiting for transfers between devices, body(): lax.ppermute(chunks[d], 'dev', [(s, s ^ d) for s in range(devices)])  24.1 us
    ppermute x3, starting transfers between devices, spread_steps(): lax.ppermute(to_right, 'dev', [(2 * i + x, 2 * i + 2 + x) for i in range(...  10.2 us
    pallas_call x3, Pallas kernels, spread_steps(): pl.pallas_call(functools.partial(pick_kernel, step, lines), grid_spec=plt...  8.49 us
    pallas_call x1, Pallas kernels, body(): pl.pallas_call(functools.partial(pack_kernel, groups, devices, per_group,...  8.07 us
    ppermute x5, starting transfers between devices, body(): lax.ppermute(chunks[d], 'dev', [(s, s ^ d) for s in range(devices)])  7.45 us
    ppermute x3, starting transfers between devices, spread_steps(): lax.ppermute(to_left, 'dev', [(devices - 1 - (2 * i + x), devices - 3 - (...  7.23 us
    all_to_all x1, starting transfers between devices, body(): lax.all_to_all(partial_down, 'dev', split_axis=0, concat_axis=0, tiled=True)  7.01 us
  transfers between devices with their start and end apart: 21, of which 8 were waited for; matrix products, arithmetic and copies ran while one was open for 0% of the time, Pallas kernels for 22%

profile of v8, /device:TPU:8, one launch (start us, length us, event | category | flops | bytes accessed | tf_op | source)
XLA Modules:
  0.0 174.6 jit_solution(15133146384579982628)
XLA Ops:
  7.2 8.1 %pack.1 = (s32[16,64]{1,0:T(8,128)S(1)}, bf16[256,256]{1,0:T(8,128)(2,1)}, bf16[4,4,64,1024]{3,2,1,0:T(8,128)(2,1)}, bf16[4,64,1024]{2,1,0:T(8,128)(2,1)}, bf16[...) custom-call(s32[32]{0:T(128)} %bitcast.22, ...), custom_call_target="tpu_custom_call" | custom-call | bytes 65536 | tf_op jit(solution)/shard_map/pack/pallas_call | solution.py:628
  15.2 4.5 %all-to-all-start = ((bf16[4,4,64,1024]{3,2,1,0:T(8,128)(2,1)}), bf16[4,4,64,1024]{3,2,1,0:T(8,128)(2,1)}, u32[]{:S(2)}, u32[]{:S(2)}) async-start(bf16[4,4,64,1024]{3,2,1,0:T(8,128)(2,1)} %get-tuple-element.170), calls=%async_computation | async-start | bytes 4194304 | tf_op jit(solution)/shard_map/all_to_all | solution.py:655
  19.8 0.0 all-gather.2.cloned.1.call-start
  19.8 1.6 collective-permute-start.16
  21.4 0.0 all-gather.2.cloned.1.call-update
  21.4 0.5 collective-permute-start.7
  21.9 1.6 collective-permute-start.8
  23.5 0.5 slice.3
  24.0 0.1 broadcast_in_dim.12
  24.1 0.6 while.14
  24.8 2.7 %collective-permute-start.9 = (bf16[1056,128]{1,0:T(8,128)(2,1)}, bf16[1056,128]{1,0:T(8,128)(2,1)}, u32[]{:S(2)}, u32[]{:S(2)}) collective-permute-start(bf16[1056,128]{1,0:T(8,128)(2,1)} %get-tuple-element.175), channel_id=1, source_target_pairs={{0,4},{1,5},{2,6},{3,7},{4,0},{5,1},{6,2},{7,3},{8,12},{9,13},{10,... | collective-permute-start | bytes 811016 | tf_op jit(solution)/shard_map/ppermute | solution.py:661
  27.4 1.2 collective-permute-start.10
  28.6 2.5 %prep.1 = (f32[32,2048]{1,0:T(8,128)}, f32[8,256,16]{2,1,0:T(8,128)}, f32[8,1024]{1,0:T(8,128)}) custom-call(f32[16]{0:T(128)} %rates.1, f32[16]{0:T(128)} %skips.1, f32[16,2048]{1,0:T(8,128)} %steps.1, f32[4,1024]{1,0:T(4,128)} %taps_in.1, f32[1,1024]{1,0:T(1,128)} %bitcast.21, s32[16,64]{1,0:T(8,128)S(1)} %get-tuple-element.302), custom_call_target="tpu_custom_call" | custom-call | bytes 65536 | tf_op jit(solution)/shard_map/prep/pallas_call | solution.py:670
  31.1 9.4 %collective-permute-done.7.rest_2_.rest_6_ = bf16[1056,128]{1,0:T(8,128)(2,1)} collective-permute-done((bf16[1056,128]{1,0:T(8,128)(2,1)}, bf16[1056,128]{1,0:T(8,128)(2,1)}, u32[]{:S(2)}, u32[]{:S(2)}) %collective-permute-start.7) | collective-permute-done | bytes 270368 | tf_op jit(solution)/shard_map/ppermute | solution.py:661
  40.5 6.7 %collective-permute-done.8.rest_3_.rest_7_ = bf16[1056,128]{1,0:T(8,128)(2,1)} collective-permute-done((bf16[1056,128]{1,0:T(8,128)(2,1)}, bf16[1056,128]{1,0:T(8,128)(2,1)}, u32[]{:S(2)}, u32[]{:S(2)}) %collective-permute-start.8) | collective-permute-done | bytes 270368 | tf_op jit(solution)/shard_map/ppermute | solution.py:661
  47.2 0.0 collective-permute-done.9.rest_4_.rest_8_
  47.3 8.0 %collective-permute-done.10.rest_5_.rest_9_ = bf16[1056,128]{1,0:T(8,128)(2,1)} collective-permute-done((bf16[1056,128]{1,0:T(8,128)(2,1)}, bf16[1056,128]{1,0:T(8,128)(2,1)}, u32[]{:S(2)}, u32[]{:S(2)}) %collective-permute-start.10) | collective-permute-done | bytes 270368 | tf_op jit(solution)/shard_map/ppermute | solution.py:661
  55.2 5.7 %shrink.1.rest_0_ = bf16[8,64,256]{2,1,0:T(8,128)(2,1)} custom-call(s32[16,64]{1,0:T(8,128)S(1)} %get-tuple-element.302, bf16[2048,1024]{1,0:T(8,128)(2,1)} %hidden.1, bf16[4,4,64,1024]{3,2,1,0:T(8,128)(2,1)} %all-to-all-done.table, f32[8,1024]{1,0:T(8,128)} %get-tuple-element.171.rest_0_.channel, ...), custom_call_target="tpu_custom_call" | custom-call | bytes 65536 | tf_op jit(solution)/shard_map/shrink/pallas_call | solution.py:689
  60.9 7.0 %all-to-all-start.1 = ((bf16[8,64,256]{2,1,0:T(8,128)(2,1)}), bf16[8,64,256]{2,1,0:T(8,128)(2,1)}, u32[]{:S(2)}, u32[]{:S(2)}) async-start(bf16[8,64,256]{2,1,0:T(8,128)(2,1)} %shrink.1.rest_0_), calls=%async_computation.1 | async-start | bytes 524288 | tf_op jit(solution)/shard_map/all_to_all | solution.py:708
  67.9 0.0 collective-permute-done.16.over_r.over_l.rest_7_
  67.9 2.7 %pick_1.8 = (bf16[1056,128]{1,0:T(8,128)(2,1)}, bf16[1056,128]{1,0:T(8,128)(2,1)}) custom-call(s32[1]{0:T(128)} %constant.34.clone.1.j, s32[16,64]{1,0:T(8,128)S(1)} %get-tuple-element.302, bf16[4,1056,128]{2,1,0:T(8,128)(2,1)} %get-tuple-element.190.own_r.own_l.rest_6_, bf16[4,1056,128]{2,1,0:T(8,128)(2,1)} %collective-permute-done.16.over_r.over_l.rest_7_, ...), custom_call_target="tpu_custom_call" | custom-call | bytes 65536 | tf_op jit(solution)/shard_map/pick_1/pallas_call | solution.py:318
  70.7 1.3 collective-permute-start.17
  72.0 6.8 %all-to-all-done.1 = bf16[8,64,256]{2,1,0:T(8,128)(2,1)} async-done(((bf16[8,64,256]{2,1,0:T(8,128)(2,1)}), bf16[8,64,256]{2,1,0:T(8,128)(2,1)}, u32[]{:S(2)}, u32[]{:S(2)}) %all-to-all-start.1) | async-done | bytes 262176 | tf_op jit(solution)/shard_map/all_to_all | solution.py:708
  78.7 1.7 sum_parts.1
  80.4 5.4 %all-to-all-start.2 = ((bf16[8,1,64,256]{3,2,1,0:T(8,128)(2,1)}), bf16[8,1,64,256]{3,2,1,0:T(8,128)(2,1)}, u32[]{:S(2)}, u32[]{:S(2)}) async-start(bf16[8,1,64,256]{3,2,1,0:T(8,128)(2,1)} %sum_parts.1), calls=%async_computation.2 | async-start | bytes 524288 | tf_op jit(solution)/shard_map/all_to_all | solution.py:718
  85.8 1.4 collective-permute-start.18
  87.1 1.5 collective-permute-start.21
  88.6 0.0 collective-permute-start.11
  88.6 1.3 collective-permute-start.12
  89.9 0.0 collective-permute-done.17.rest_0_
  90.0 0.5 collective-permute-start.13
  90.5 0.0 collective-permute-done.18.rest_1_
  90.5 3.7 %all-to-all-done.2 = bf16[8,1,64,256]{3,2,1,0:T(8,128)(2,1)} async-done(((bf16[8,1,64,256]{3,2,1,0:T(8,128)(2,1)}), bf16[8,1,64,256]{3,2,1,0:T(8,128)(2,1)}, u32[]{:S(2)}, u32[]{:S(2)}) %all-to-all-start.2) | async-done | bytes 262176 | tf_op jit(solution)/shard_map/all_to_all | solution.py:718
  94.2 2.9 %pick_2.8 = (bf16[1056,128]{1,0:T(8,128)(2,1)}, bf16[1056,128]{1,0:T(8,128)(2,1)}) custom-call(s32[1]{0:T(128)} %constant.34.clone.1.j, s32[16,64]{1,0:T(8,128)S(1)} %get-tuple-element.302, bf16[4,1056,128]{2,1,0:T(8,128)(2,1)} %get-tuple-element.190.own_r.own_l.rest_6_, bf16[4,1056,128]{2,1,0:T(8,128)(2,1)} %collective-permute-done.16.over_r.over_l.rest_7_, ...), custom_call_target="tpu_custom_call" | custom-call | bytes 65536 | tf_op jit(solution)/shard_map/pick_2/pallas_call | solution.py:318
  97.1 1.3 collective-permute-start.20
  98.4 6.7 %collective-permute-start.19 = (bf16[1056,128]{1,0:T(8,128)(2,1)}, bf16[1056,128]{1,0:T(8,128)(2,1)}, u32[]{:S(2)}, u32[]{:S(2)}) collective-permute-start(bf16[1056,128]{1,0:T(8,128)(2,1)} %get-tuple-element.194.rest_10_), channel_id=1, source_target_pairs={{0,2},{1,3},{2,4},{3,5},{8,10},{9,11},{10,12},{11,13},{16,18},{17,... | collective-permute-start | bytes 811016 | tf_op jit(solution)/shard_map/ppermute | solution.py:328
  105.1 0.0 collective-permute-done.11.rest_1_
  105.1 0.1 collective-permute-start.14
  105.2 2.9 %collective-permute-start.15 = (bf16[1056,128]{1,0:T(8,128)(2,1)}, bf16[1056,128]{1,0:T(8,128)(2,1)}, u32[]{:S(2)}, u32[]{:S(2)}) collective-permute-start(bf16[1056,128]{1,0:T(8,128)(2,1)} %get-tuple-element.189), channel_id=1, source_target_pairs={{0,7},{1,6},{2,5},{3,4},{4,3},{5,2},{6,1},{7,0},{8,15},{9,14},{10,... | collective-permute-start | bytes 811016 | tf_op jit(solution)/shard_map/ppermute | solution.py:723
  108.1 6.0 %collective-permute-done.13.rest_3_ = bf16[4,64,1024]{2,1,0:T(8,128)(2,1)} collective-permute-done((bf16[4,64,1024]{2,1,0:T(8,128)(2,1)}, bf16[4,64,1024]{2,1,0:T(8,128)(2,1)}, u32[]{:S(2)}, u32[]{:S(2)}) %collective-permute-start.13) | collective-permute-done | bytes 524320 | tf_op jit(solution)/shard_map/ppermute | solution.py:162
  114.1 20.3 %mix_0.1 = (bf16[2048,1024]{1,0:T(8,128)(2,1)}, bf16[8,1024,128]{2,1,0:T(8,128)(2,1)}, f32[8,128]{1,0:T(8,128)}) custom-call(s32[16,64]{1,0:T(8,128)S(1)} %get-tuple-element.302, bf16[2048,1024]{1,0:T(8,128)(2,1)} %base.3, bf16[8,64,256]{2,1,0:T(8,128)(2,1)} %bitcast.9.rest_2_.shrunk, f32[8,1024]{1,0:T(8,128)} %get-tuple-element.171.rest_0_.channel, ...), custom_call_target="tpu_custom_call" | custom-call | bytes 65536 | tf_op jit(solution)/shard_map/mix_0/pallas_call | solution.py:759
  134.4 0.0 collective-permute-done.20.rest_1_
  134.4 2.9 %pick_3.8 = (bf16[1056,128]{1,0:T(8,128)(2,1)}, bf16[1056,128]{1,0:T(8,128)(2,1)}) custom-call(s32[1]{0:T(128)} %constant.34.clone.1.j, s32[16,64]{1,0:T(8,128)S(1)} %get-tuple-element.302, bf16[4,1056,128]{2,1,0:T(8,128)(2,1)} %get-tuple-element.190.own_r.own_l.rest_6_, bf16[4,1056,128]{2,1,0:T(8,128)(2,1)} %collective-permute-done.16.over_r.over_l.rest_7_, ...), custom_call_target="tpu_custom_call" | custom-call | bytes 65536 | tf_op jit(solution)/shard_map/pick_3/pallas_call | solution.py:318
  137.3 2.1 %collective-permute-start.22 = (bf16[1056,128]{1,0:T(8,128)(2,1)}, bf16[1056,128]{1,0:T(8,128)(2,1)}, u32[]{:S(2)}, u32[]{:S(2)}) collective-permute-start(bf16[1056,128]{1,0:T(8,128)(2,1)} %get-tuple-element.199), channel_id=1, source_target_pairs={{0,2},{1,3},{2,4},{3,5},{4,6},{5,7},{8,10},{9,11},{10,12},{11,13},... | collective-permute-start | bytes 811016 | tf_op jit(solution)/shard_map/ppermute | solution.py:328
  139.5 4.6 %collective-permute-start.23 = (bf16[1056,128]{1,0:T(8,128)(2,1)}, bf16[1056,128]{1,0:T(8,128)(2,1)}, u32[]{:S(2)}, u32[]{:S(2)}) collective-permute-start(bf16[1056,128]{1,0:T(8,128)(2,1)} %get-tuple-element.200), channel_id=1, source_target_pairs={{7,5},{6,4},{5,3},{4,2},{3,1},{2,0},{15,13},{14,12},{13,11},{12,10... | collective-permute-start | bytes 811016 | tf_op jit(solution)/shard_map/ppermute | solution.py:332
  144.1 4.3 %collective-permute-done.22.rest_8_ = bf16[1056,128]{1,0:T(8,128)(2,1)} collective-permute-done((bf16[1056,128]{1,0:T(8,128)(2,1)}, bf16[1056,128]{1,0:T(8,128)(2,1)}, u32[]{:S(2)}, u32[]{:S(2)}) %collective-permute-start.22) | collective-permute-done | bytes 270368 | tf_op jit(solution)/shard_map/ppermute | solution.py:328
  148.4 6.1 %collective-permute-done.23.rest_9_ = bf16[1056,128]{1,0:T(8,128)(2,1)} collective-permute-done((bf16[1056,128]{1,0:T(8,128)(2,1)}, bf16[1056,128]{1,0:T(8,128)(2,1)}, u32[]{:S(2)}, u32[]{:S(2)}) %collective-permute-start.23) | collective-permute-done | bytes 270368 | tf_op jit(solution)/shard_map/ppermute | solution.py:332
  154.5 13.2 %mix_6.1 = (bf16[2048,1024]{1,0:T(8,128)(2,1)}, bf16[8,1024,128]{2,1,0:T(8,128)(2,1)}, f32[8,128]{1,0:T(8,128)}) custom-call(s32[16,64]{1,0:T(8,128)S(1)} %get-tuple-element.302, bf16[2048,1024]{1,0:T(8,128)(2,1)} %base.3, bf16[8,64,256]{2,1,0:T(8,128)(2,1)} %bitcast.9.rest_2_.shrunk, ...), custom_call_target="tpu_custom_call", output_to_operand_aliasing={{0}: (18, {}), {1}: (19, {})} | custom-call | bytes 65536 | tf_op jit(solution)/shard_map/mix_6/pallas_call | solution.py:759
  (7 shorter events, 0.0 us)
Async XLA Ops:
  15.2 40.0 %all-to-all-start = ((bf16[4,4,64,1024]{3,2,1,0:T(8,128)(2,1)}), bf16[4,4,64,1024]{3,2,1,0:T(8,128)(2,1)}, u32[]{:S(2)}, u32[]{:S(2)}) async-start(bf16[4,4,64,1024]{3,2,1,0:T(8,128)(2,1)} %get-tuple-element.170), calls=%async_computation | async-start | bytes 4194304 | tf_op jit(solution)/shard_map/all_to_all | solution.py:655
  19.8 94.4 %all-gather.2.cloned.1.call-start = ((), (), s32[]{:S(2)}) async-start(), calls=%async_computation.3 | async-start | bytes 1179648 | tf_op jit(solution)/shard_map/all_gather | solution.py:657
  19.8 48.1 %collective-permute-start.16 = (bf16[4,1056,128]{2,1,0:T(8,128)(2,1)}, bf16[4,1056,128]{2,1,0:T(8,128)(2,1)}, u32[]{:S(2)}, u32[]{:S(2)}) collective-permute-start(bf16[4,1056,128]{2,1,0:T(8,128)(2,1)} %get-tuple-element.191), channel_id=1, source_target_pairs={{0,1},{1,0},{2,3},{3,2},{4,5},{5,4},{6,7},{7,6},{8,9},{9,8},{10,11... | collective-permute-start | bytes 3244040 | tf_op jit(solution)/shard_map/ppermute | solution.py:300
  21.4 19.1 %collective-permute-start.7 = (bf16[1056,128]{1,0:T(8,128)(2,1)}, bf16[1056,128]{1,0:T(8,128)(2,1)}, u32[]{:S(2)}, u32[]{:S(2)}) collective-permute-start(bf16[1056,128]{1,0:T(8,128)(2,1)} %get-tuple-element.173), channel_id=1, source_target_pairs={{0,2},{1,3},{2,0},{3,1},{4,6},{5,7},{6,4},{7,5},{8,10},{9,11},{10,... | collective-permute-start | bytes 811016 | tf_op jit(solution)/shard_map/ppermute | solution.py:661
  21.9 25.3 %collective-permute-start.8 = (bf16[1056,128]{1,0:T(8,128)(2,1)}, bf16[1056,128]{1,0:T(8,128)(2,1)}, u32[]{:S(2)}, u32[]{:S(2)}) collective-permute-start(bf16[1056,128]{1,0:T(8,128)(2,1)} %get-tuple-element.174), channel_id=1, source_target_pairs={{0,3},{1,2},{2,1},{3,0},{4,7},{5,6},{6,5},{7,4},{8,11},{9,10},{10,... | collective-permute-start | bytes 811016 | tf_op jit(solution)/shard_map/ppermute | solution.py:661
  24.8 22.5 %collective-permute-start.9 = (bf16[1056,128]{1,0:T(8,128)(2,1)}, bf16[1056,128]{1,0:T(8,128)(2,1)}, u32[]{:S(2)}, u32[]{:S(2)}) collective-permute-start(bf16[1056,128]{1,0:T(8,128)(2,1)} %get-tuple-element.175), channel_id=1, source_target_pairs={{0,4},{1,5},{2,6},{3,7},{4,0},{5,1},{6,2},{7,3},{8,12},{9,13},{10,... | collective-permute-start | bytes 811016 | tf_op jit(solution)/shard_map/ppermute | solution.py:661
  27.4 27.8 %collective-permute-start.10 = (bf16[1056,128]{1,0:T(8,128)(2,1)}, bf16[1056,128]{1,0:T(8,128)(2,1)}, u32[]{:S(2)}, u32[]{:S(2)}) collective-permute-start(bf16[1056,128]{1,0:T(8,128)(2,1)} %get-tuple-element.176), channel_id=1, source_target_pairs={{0,5},{1,4},{2,7},{3,6},{4,1},{5,0},{6,3},{7,2},{8,13},{9,12},{10,... | collective-permute-start | bytes 811016 | tf_op jit(solution)/shard_map/ppermute | solution.py:661
  60.9 17.8 %all-to-all-start.1 = ((bf16[8,64,256]{2,1,0:T(8,128)(2,1)}), bf16[8,64,256]{2,1,0:T(8,128)(2,1)}, u32[]{:S(2)}, u32[]{:S(2)}) async-start(bf16[8,64,256]{2,1,0:T(8,128)(2,1)} %shrink.1.rest_0_), calls=%async_computation.1 | async-start | bytes 524288 | tf_op jit(solution)/shard_map/all_to_all | solution.py:708
  70.7 19.3 %collective-permute-start.17 = (bf16[1056,128]{1,0:T(8,128)(2,1)}, bf16[1056,128]{1,0:T(8,128)(2,1)}, u32[]{:S(2)}, u32[]{:S(2)}) collective-permute-start(bf16[1056,128]{1,0:T(8,128)(2,1)} %get-tuple-element.192), channel_id=1, source_target_pairs={{0,2},{1,3},{8,10},{9,11},{16,18},{17,19},{24,26},{25,27}} | collective-permute-start | bytes 811016 | tf_op jit(solution)/shard_map/ppermute | solution.py:328
  80.4 13.8 %all-to-all-start.2 = ((bf16[8,1,64,256]{3,2,1,0:T(8,128)(2,1)}), bf16[8,1,64,256]{3,2,1,0:T(8,128)(2,1)}, u32[]{:S(2)}, u32[]{:S(2)}) async-start(bf16[8,1,64,256]{3,2,1,0:T(8,128)(2,1)} %sum_parts.1), calls=%async_computation.2 | async-start | bytes 524288 | tf_op jit(solution)/shard_map/all_to_all | solution.py:718
  85.8 4.7 %collective-permute-start.18 = (bf16[1056,128]{1,0:T(8,128)(2,1)}, bf16[1056,128]{1,0:T(8,128)(2,1)}, u32[]{:S(2)}, u32[]{:S(2)}) collective-permute-start(bf16[1056,128]{1,0:T(8,128)(2,1)} %get-tuple-element.193), channel_id=1, source_target_pairs={{7,5},{6,4},{15,13},{14,12},{23,21},{22,20},{31,29},{30,28}} | collective-permute-start | bytes 811016 | tf_op jit(solution)/shard_map/ppermute | solution.py:332
  87.1 11.2 %collective-permute-start.21 = (bf16[1056,128]{1,0:T(8,128)(2,1)}, bf16[1056,128]{1,0:T(8,128)(2,1)}, u32[]{:S(2)}, u32[]{:S(2)}) collective-permute-start(bf16[1056,128]{1,0:T(8,128)(2,1)} %get-tuple-element.197), channel_id=1, source_target_pairs={{0,1},{1,0},{2,3},{3,2},{4,5},{5,4},{6,7},{7,6},{8,9},{9,8},{10,11... | collective-permute-start | bytes 811016 | tf_op jit(solution)/shard_map/ppermute | solution.py:661
  88.6 16.5 %collective-permute-start.11 = (bf16[4,64,1024]{2,1,0:T(8,128)(2,1)}, bf16[4,64,1024]{2,1,0:T(8,128)(2,1)}, u32[]{:S(2)}, u32[]{:S(2)}) collective-permute-start(bf16[4,64,1024]{2,1,0:T(8,128)(2,1)} %get-tuple-element.183), channel_id=1, source_target_pairs={{0,8},{8,0},{16,24},{24,16},{1,9},{9,1},{17,25},{25,17},{2,10},{10... | collective-permute-start | bytes 1572872 | tf_op jit(solution)/shard_map/ppermute | solution.py:162
  88.6 16.6 %collective-permute-start.12 = (bf16[4,64,1024]{2,1,0:T(8,128)(2,1)}, bf16[4,64,1024]{2,1,0:T(8,128)(2,1)}, u32[]{:S(2)}, u32[]{:S(2)}) collective-permute-start(bf16[4,64,1024]{2,1,0:T(8,128)(2,1)} %get-tuple-element.184), channel_id=1, source_target_pairs={{0,16},{8,24},{16,0},{24,8},{1,17},{9,25},{17,1},{25,9},{2,18},{10... | collective-permute-start | bytes 1572872 | tf_op jit(solution)/shard_map/ppermute | solution.py:162
  90.0 24.2 %collective-permute-start.13 = (bf16[4,64,1024]{2,1,0:T(8,128)(2,1)}, bf16[4,64,1024]{2,1,0:T(8,128)(2,1)}, u32[]{:S(2)}, u32[]{:S(2)}) collective-permute-start(bf16[4,64,1024]{2,1,0:T(8,128)(2,1)} %get-tuple-element.185), channel_id=1, source_target_pairs={{0,24},{8,16},{16,8},{24,0},{1,25},{9,17},{17,9},{25,1},{2,26},{10... | collective-permute-start | bytes 1572872 | tf_op jit(solution)/shard_map/ppermute | solution.py:162
  97.1 37.3 %collective-permute-start.20 = (bf16[1056,128]{1,0:T(8,128)(2,1)}, bf16[1056,128]{1,0:T(8,128)(2,1)}, u32[]{:S(2)}, u32[]{:S(2)}) collective-permute-start(bf16[1056,128]{1,0:T(8,128)(2,1)} %get-tuple-element.195), channel_id=1, source_target_pairs={{7,5},{6,4},{5,3},{4,2},{15,13},{14,12},{13,11},{12,10},{23,21},{2... | collective-permute-start | bytes 811016 | tf_op jit(solution)/shard_map/ppermute | solution.py:332
  98.4 36.1 %collective-permute-start.19 = (bf16[1056,128]{1,0:T(8,128)(2,1)}, bf16[1056,128]{1,0:T(8,128)(2,1)}, u32[]{:S(2)}, u32[]{:S(2)}) collective-permute-start(bf16[1056,128]{1,0:T(8,128)(2,1)} %get-tuple-element.194.rest_10_), channel_id=1, source_target_pairs={{0,2},{1,3},{2,4},{3,5},{8,10},{9,11},{10,12},{11,13},{16,18},{17,... | collective-permute-start | bytes 811016 | tf_op jit(solution)/shard_map/ppermute | solution.py:328
  105.1 38.9 %collective-permute-start.14 = (bf16[1056,128]{1,0:T(8,128)(2,1)}, bf16[1056,128]{1,0:T(8,128)(2,1)}, u32[]{:S(2)}, u32[]{:S(2)}) collective-permute-start(bf16[1056,128]{1,0:T(8,128)(2,1)} %get-tuple-element.188), channel_id=1, source_target_pairs={{0,6},{1,7},{2,4},{3,5},{4,2},{5,3},{6,0},{7,1},{8,14},{9,15},{10,... | collective-permute-start | bytes 811016 | tf_op jit(solution)/shard_map/ppermute | solution.py:723
  105.2 38.9 %collective-permute-start.15 = (bf16[1056,128]{1,0:T(8,128)(2,1)}, bf16[1056,128]{1,0:T(8,128)(2,1)}, u32[]{:S(2)}, u32[]{:S(2)}) collective-permute-start(bf16[1056,128]{1,0:T(8,128)(2,1)} %get-tuple-element.189), channel_id=1, source_target_pairs={{0,7},{1,6},{2,5},{3,4},{4,3},{5,2},{6,1},{7,0},{8,15},{9,14},{10,... | collective-permute-start | bytes 811016 | tf_op jit(solution)/shard_map/ppermute | solution.py:723
  137.3 11.1 %collective-permute-start.22 = (bf16[1056,128]{1,0:T(8,128)(2,1)}, bf16[1056,128]{1,0:T(8,128)(2,1)}, u32[]{:S(2)}, u32[]{:S(2)}) collective-permute-start(bf16[1056,128]{1,0:T(8,128)(2,1)} %get-tuple-element.199), channel_id=1, source_target_pairs={{0,2},{1,3},{2,4},{3,5},{4,6},{5,7},{8,10},{9,11},{10,12},{11,13},... | collective-permute-start | bytes 811016 | tf_op jit(solution)/shard_map/ppermute | solution.py:328
  139.5 15.0 %collective-permute-start.23 = (bf16[1056,128]{1,0:T(8,128)(2,1)}, bf16[1056,128]{1,0:T(8,128)(2,1)}, u32[]{:S(2)}, u32[]{:S(2)}) collective-permute-start(bf16[1056,128]{1,0:T(8,128)(2,1)} %get-tuple-element.200), channel_id=1, source_target_pairs={{7,5},{6,4},{5,3},{4,2},{3,1},{2,0},{15,13},{14,12},{13,11},{12,10... | collective-permute-start | bytes 811016 | tf_op jit(solution)/shard_map/ppermute | solution.py:332
Sparse Core Ops, SparseCore 0:
  22.7 54.7 all-gather.1

commit v9 on v6

--- a/solution.py
+++ b/solution.py
@@ -237,32 +237,36 @@
         copy.wait()
 
 
-def pick_kernel(step, lines, j, meta, own_r, over_r, own_l, over_l, *rest):
-    out_r, out_l = rest[-2:]
+def pick_kernel(step, lines, j, meta, own, over, *rest):
+    out_r, out_l, sems = rest[-3:]
     me = meta[MISC, ME]
     source = meta[OHOLDER, j[0]]
     same = source // 2 == me // 2
     mine = same & (source % 2 == me % 2)
     across = same & (source % 2 != me % 2)
-
-    @pl.when(mine)
-    def _():
-        out_r[...] = own_r[0]
-        out_l[...] = own_l[0]
-
-    @pl.when(across)
-    def _():
-        out_r[...] = over_r[0]
-        out_l[...] = over_l[0]
-
-    @pl.when(jnp.logical_not(same))
-    def _():
+    for k, (out, block) in enumerate(((out_r, right_block), (out_l, left_block))):
+        place = block(meta, step, lines)
+
+        @pl.when(mine)
+        def _(k=k, out=out, place=place):
+            pltpu.make_async_copy(own.at[place], out, sems.at[k]).start()
+
+        @pl.when(across)
+        def _(k=k, out=out, place=place):
+            pltpu.make_async_copy(over.at[place], out, sems.at[k]).start()
+
         if step > 1:
-            out_r[...] = rest[0][...]
-            out_l[...] = rest[1][...]
+            @pl.when(jnp.logical_not(same))
+            def _(k=k, out=out):
+                pltpu.make_async_copy(rest[k], out, sems.at[k]).start()
+
+    for k, out in enumerate((out_r, out_l)):
+        if step > 1:
+            pltpu.make_async_copy(own.at[0], out, sems.at[k]).wait()
         else:
-            out_r[...] = jnp.zeros_like(out_r)
-            out_l[...] = jnp.zeros_like(out_l)
+            @pl.when(same)
+            def _(k=k, out=out):
+                pltpu.make_async_copy(own.at[0], out, sems.at[k]).wait()
 
 
 def right_block(meta, step, lines):
@@ -295,27 +299,17 @@
     across = lax.ppermute(send, "dev", [(d, d ^ 1) for d in range(devices)])
     from_left = from_right = None
     after = yield across
-    whole = pl.BlockSpec(shape, lambda g, j, meta: (0, 0))
     for step in range(1, lines):
-        blocks = [
-            pl.BlockSpec(
-                (1,) + shape, lambda g, j, meta, at=at, step=step: (at(meta, step, lines), 0, 0)
-            )
-            for at in (right_block, left_block)
-        ]
-        operands = [own, across, own, across]
-        in_specs = [blocks[0], blocks[0], blocks[1], blocks[1]]
+        operands = [own, across]
         if step > 1:
             operands += [from_left, from_right]
-            in_specs += [whole, whole]
         operands += after
-        in_specs += anywhere(len(after))
         to_right, to_left = pl.pallas_call(
             functools.partial(pick_kernel, step, lines),
-            grid_spec=pltpu.PrefetchScalarGridSpec(
-                num_scalar_prefetch=2, grid=(1,), in_specs=in_specs, out_specs=(whole, whole)
-            ),
+            in_specs=smem(2) + anywhere(len(operands)),
+            out_specs=tuple(vmem(2)),
             out_shape=tuple(jax.ShapeDtypeStruct(shape, own.dtype) for _ in range(2)),
+            scratch_shapes=[pltpu.SemaphoreType.DMA((2,))],
             cost_estimate=cost(),
             compiler_params=params(),
             name=f"pick_{step}",
@@ -656,7 +650,7 @@
 
     spread_others = spread_rest(meta, cache, conv, devices, width, limit)
 
-    up_send, _ = lax.optimization_barrier((packed[1:groups], got[lines]))
+    up_send, _ = lax.optimization_barrier((packed[1:groups], got[2]))
     up_got = swap(up_send, groups)
 
     rows_decay, column_decay, channel = pl.pallas_call(
@@ -677,13 +671,14 @@
     )
 
     each = per_group // 2
+    early = got[2:lines + 2]
     partial_down = pl.pallas_call(
         functools.partial(shrink_kernel, per_group),
         grid_spec=pltpu.PrefetchScalarGridSpec(
             num_scalar_prefetch=1,
             grid=(per_group // each,),
             in_specs=[pl.BlockSpec((each * T_REQ, hidden.shape[1]), lambda g, meta: (g, 0))]
-            + anywhere(5),
+            + anywhere(3 + len(early)),
             out_specs=pl.BlockSpec((each, rank, T_REQ), lambda g, meta: (g, 0, 0)),
             scratch_shapes=[
                 pltpu.VMEM((per_group,) + adapter_down_weight.shape[1:], bf16),
@@ -694,22 +689,22 @@
         cost_estimate=cost(),
         compiler_params=params(),
         name="shrink",
-    )(meta, hidden, down_got, channel, got[lines], got[lines + 1], spread_others)
+    )(meta, hidden, down_got, channel, spread_others, *early)
 
     parts = lax.all_to_all(partial_down, "dev", split_axis=0, concat_axis=0, tiled=True)
     summed = pl.pallas_call(
         sum_kernel,
         out_shape=jax.ShapeDtypeStruct((devices, 1, rank, T_REQ), bf16),
-        in_specs=vmem(1),
+        in_specs=vmem(1) + anywhere(1),
         out_specs=vmem(1)[0],
         cost_estimate=cost(),
         compiler_params=params(),
         name="sum_parts",
-    )(parts.reshape(devices, 1, rank, T_REQ))
+    )(parts.reshape(devices, 1, rank, T_REQ), up_got[groups // 2 - 1])
     shrunk = lax.all_to_all(summed, "dev", split_axis=0, concat_axis=0, tiled=True)
     shrunk = shrunk.reshape(per_group, rank, T_REQ)
 
-    befores = [[partial_down], [summed, up_got[groups // 2 - 1]], [rows_all, up_got[-1]]]
+    befores = [[partial_down], [summed], [rows_all, up_got[-1]]]
     spread = spread_steps(zero, meta, packed[-2:], devices)
     next(spread)
     for step in range(1, lines):

time: 164 us -> 171 us (1.043)
  waiting for transfers between devices: 43 us -> 51.5 us
  starting transfers between devices: 43.2 us -> 45.4 us
  Pallas kernels: 60.3 us -> 58.2 us
    ppermute x3, waiting for transfers between devices: 5.19 us -> 11.5 us  [spread_steps(): lax.ppermute(to_right, 'dev', [(2 * i + x, 2 * i + 2 + x) for i in range(...]
    ppermute x7, waiting for transfers between devices: 25.3 us -> 29.1 us  [body(): lax.ppermute(chunks[d], 'dev', [(s, s ^ d) for s in range(devices)])]
    ppermute x7, starting transfers between devices: 8.63 us -> 12.1 us  [body(): lax.ppermute(chunks[d], 'dev', [(s, s ^ d) for s in range(devices)])]
    ppermute x3, waiting for transfers between devices: 6.4 us -> 3.29 us  [spread_steps(): lax.ppermute(to_left, 'dev', [(devices - 1 - (2 * i + x), devices - 3 - (...]
    pallas_call x3, Pallas kernels: 8.48 us -> 6.57 us  [spread_steps(): pl.pallas_call(functools.partial(pick_kernel, step, lines), in_specs=smem...]
    ppermute x3, starting transfers between devices: 9.88 us -> 8.11 us  [spread_steps(): lax.ppermute(to_right, 'dev', [(2 * i + x, 2 * i + 2 + x) for i in range(...]
  transfers between devices with their start and end apart: 21 -> 21, of which waited for: 7 -> 9; matrix products, arithmetic and copies ran while one was open for 0% -> 0% of each run, Pallas kernels for 21% -> 18%
where the time goes in v9:
time: 171 us
  Pallas kernels  58.2 us (34%)
  waiting for transfers between devices  51.5 us (30%)
  starting transfers between devices  45.4 us (27%)
  between operations  14.2 us (8%)
    pallas_call x2, Pallas kernels, body(): pl.pallas_call(functools.partial(mix_kernel, groups, taps, begin, steps,...  33.4 us
    ppermute x7, waiting for transfers between devices, body(): lax.ppermute(chunks[d], 'dev', [(s, s ^ d) for s in range(devices)])  29.1 us
    ppermute x7, starting transfers between devices, body(): lax.ppermute(chunks[d], 'dev', [(s, s ^ d) for s in range(devices)])  12.1 us
    ppermute x3, waiting for transfers between devices, spread_steps(): lax.ppermute(to_right, 'dev', [(2 * i + x, 2 * i + 2 + x) for i in range(...  11.5 us
    pallas_call x1, Pallas kernels, body(): pl.pallas_call(functools.partial(pack_kernel, groups, devices, per_group,...  8.22 us
    ppermute x3, starting transfers between devices, spread_steps(): lax.ppermute(to_right, 'dev', [(2 * i + x, 2 * i + 2 + x) for i in range(...  8.11 us
    all_to_all x1, starting transfers between devices, body(): lax.all_to_all(partial_down, 'dev', split_axis=0, concat_axis=0, tiled=True)  7.17 us
    all_to_all x1, waiting for transfers between devices, body(): lax.all_to_all(partial_down, 'dev', split_axis=0, concat_axis=0, tiled=True)  6.93 us
  transfers between devices with their start and end apart: 21, of which 9 were waited for; matrix products, arithmetic and copies ran while one was open for 0% of the time, Pallas kernels for 18%

profile of v9, /device:TPU:8, one launch (start us, length us, event | category | flops | bytes accessed | tf_op | source)
XLA Modules:
  0.0 170.5 jit_solution(13296023400912430186)
XLA Ops:
  7.2 8.2 %pack.1 = (s32[16,64]{1,0:T(8,128)S(1)}, bf16[256,256]{1,0:T(8,128)(2,1)}, bf16[4,4,64,1024]{3,2,1,0:T(8,128)(2,1)}, bf16[4,64,1024]{2,1,0:T(8,128)(2,1)}, bf16[...) custom-call(s32[32]{0:T(128)} %bitcast.22, ...), custom_call_target="tpu_custom_call" | custom-call | bytes 65536 | tf_op jit(solution)/shard_map/pack/pallas_call | solution.py:615
  15.4 4.5 %all-to-all-start = ((bf16[4,4,64,1024]{3,2,1,0:T(8,128)(2,1)}), bf16[4,4,64,1024]{3,2,1,0:T(8,128)(2,1)}, u32[]{:S(2)}, u32[]{:S(2)}) async-start(bf16[4,4,64,1024]{3,2,1,0:T(8,128)(2,1)} %get-tuple-element.167), calls=%async_computation | async-start | bytes 4194304 | tf_op jit(solution)/shard_map/all_to_all | solution.py:642
  19.9 0.0 all-gather.2.cloned.1.call-start
  20.0 0.7 all-gather.2.cloned.1.call-update
  20.7 1.5 collective-permute-start.16
  22.2 0.3 collective-permute-start.7
  22.5 1.7 %collective-permute-start.8 = (bf16[1056,128]{1,0:T(8,128)(2,1)}, bf16[1056,128]{1,0:T(8,128)(2,1)}, u32[]{:S(2)}, u32[]{:S(2)}) collective-permute-start(bf16[1056,128]{1,0:T(8,128)(2,1)} %get-tuple-element.171), channel_id=1, source_target_pairs={{0,3},{1,2},{2,1},{3,0},{4,7},{5,6},{6,5},{7,4},{8,11},{9,10},{10,... | collective-permute-start | bytes 811016 | tf_op jit(solution)/shard_map/ppermute | solution.py:647
  24.2 0.5 slice.3
  24.7 0.1 broadcast_in_dim.12
  24.8 0.6 while.14
  25.5 2.6 %collective-permute-start.9 = (bf16[1056,128]{1,0:T(8,128)(2,1)}, bf16[1056,128]{1,0:T(8,128)(2,1)}, u32[]{:S(2)}, u32[]{:S(2)}) collective-permute-start(bf16[1056,128]{1,0:T(8,128)(2,1)} %get-tuple-element.172), channel_id=1, source_target_pairs={{0,4},{1,5},{2,6},{3,7},{4,0},{5,1},{6,2},{7,3},{8,12},{9,13},{10,... | collective-permute-start | bytes 811016 | tf_op jit(solution)/shard_map/ppermute | solution.py:647
  28.1 1.3 collective-permute-start.10
  29.4 12.6 %collective-permute-done.7.rest_2_.rest_6_ = bf16[1056,128]{1,0:T(8,128)(2,1)} collective-permute-done((bf16[1056,128]{1,0:T(8,128)(2,1)}, bf16[1056,128]{1,0:T(8,128)(2,1)}, u32[]{:S(2)}, u32[]{:S(2)}) %collective-permute-start.7) | collective-permute-done | bytes 270368 | tf_op jit(solution)/shard_map/ppermute | solution.py:647
  42.0 2.4 %collective-permute-start.11 = (bf16[4,64,1024]{2,1,0:T(8,128)(2,1)}, bf16[4,64,1024]{2,1,0:T(8,128)(2,1)}, u32[]{:S(2)}, u32[]{:S(2)}) collective-permute-start(bf16[4,64,1024]{2,1,0:T(8,128)(2,1)} %get-tuple-element.177), channel_id=1, source_target_pairs={{0,16},{8,24},{16,0},{24,8},{1,17},{9,25},{17,1},{25,9},{2,18},{10... | collective-permute-start | bytes 1572872 | tf_op jit(solution)/shard_map/ppermute | solution.py:157
  44.4 2.5 %prep.1 = (f32[32,2048]{1,0:T(8,128)}, f32[8,256,16]{2,1,0:T(8,128)}, f32[8,1024]{1,0:T(8,128)}) custom-call(f32[16]{0:T(128)} %rates.1, f32[16]{0:T(128)} %skips.1, f32[16,2048]{1,0:T(8,128)} %steps.1, f32[4,1024]{1,0:T(4,128)} %taps_in.1, f32[1,1024]{1,0:T(1,128)} %bitcast.21, s32[16,64]{1,0:T(8,128)S(1)} %get-tuple-element.297), custom_call_target="tpu_custom_call" | custom-call | bytes 65536 | tf_op jit(solution)/shard_map/prep/pallas_call | solution.py:656
  46.9 1.5 collective-permute-done.8.rest_3_.rest_7_
  48.4 0.0 collective-permute-done.9.rest_4_
  48.5 7.1 %collective-permute-done.10.rest_5_ = bf16[1056,128]{1,0:T(8,128)(2,1)} collective-permute-done((bf16[1056,128]{1,0:T(8,128)(2,1)}, bf16[1056,128]{1,0:T(8,128)(2,1)}, u32[]{:S(2)}, u32[]{:S(2)}) %collective-permute-start.10) | collective-permute-done | bytes 270368 | tf_op jit(solution)/shard_map/ppermute | solution.py:647
  55.5 5.7 %shrink.1.rest_0_ = bf16[8,64,256]{2,1,0:T(8,128)(2,1)} custom-call(s32[16,64]{1,0:T(8,128)S(1)} %get-tuple-element.297, bf16[2048,1024]{1,0:T(8,128)(2,1)} %hidden.1, bf16[4,4,64,1024]{3,2,1,0:T(8,128)(2,1)} %all-to-all-done.table, f32[8,1024]{1,0:T(8,128)} %get-tuple-element.168.rest_0_.channel, ...), custom_call_target="tpu_custom_call" | custom-call | bytes 65536 | tf_op jit(solution)/shard_map/shrink/pallas_call | solution.py:675
  61.2 7.2 %all-to-all-start.1 = ((bf16[8,64,256]{2,1,0:T(8,128)(2,1)}), bf16[8,64,256]{2,1,0:T(8,128)(2,1)}, u32[]{:S(2)}, u32[]{:S(2)}) async-start(bf16[8,64,256]{2,1,0:T(8,128)(2,1)} %shrink.1.rest_0_), calls=%async_computation.1 | async-start | bytes 524288 | tf_op jit(solution)/shard_map/all_to_all | solution.py:694
  68.4 0.0 collective-permute-done.16.over.rest_9_
  68.4 1.5 pick_1.8
  69.9 1.3 collective-permute-start.17
  71.2 1.4 collective-permute-start.18
  72.6 0.0 collective-permute-start.13
  72.6 0.0 collective-permute-done.11.rest_0_.rest_2_
  72.6 6.9 %all-to-all-done.1 = bf16[8,64,256]{2,1,0:T(8,128)(2,1)} async-done(((bf16[8,64,256]{2,1,0:T(8,128)(2,1)}), bf16[8,64,256]{2,1,0:T(8,128)(2,1)}, u32[]{:S(2)}, u32[]{:S(2)}) %all-to-all-start.1) | async-done | bytes 262176 | tf_op jit(solution)/shard_map/all_to_all | solution.py:694
  79.6 1.7 %sum_parts.1.rest_2_ = bf16[8,1,64,256]{3,2,1,0:T(8,128)(2,1)} custom-call(bf16[8,1,64,256]{3,2,1,0:T(8,128)(2,1)} %bitcast.8.parts, bf16[4,64,1024]{2,1,0:T(8,128)(2,1)} %collective-permute-done.11.rest_0_.rest_2_), custom_call_target="tpu_custom_call" | custom-call | bytes 65536 | tf_op jit(solution)/shard_map/sum_parts/pallas_call | solution.py:695
  81.3 1.2 collective-permute-done.17.rest_0_
  82.4 0.0 collective-permute-done.18.rest_1_
  82.4 2.5 %pick_2.8 = (bf16[1056,128]{1,0:T(8,128)(2,1)}, bf16[1056,128]{1,0:T(8,128)(2,1)}) custom-call(s32[1]{0:T(128)} %constant.34.clone.1.j, s32[16,64]{1,0:T(8,128)S(1)} %get-tuple-element.297, bf16[4,1056,128]{2,1,0:T(8,128)(2,1)} %get-tuple-element.185.own.rest_8_, bf16[4,1056,128]{2,1,0:T(8,128)(2,1)} %collective-permute-done.16.over.rest_9_, ...), custom_call_target="tpu_custom_call" | custom-call | bytes 65536 | tf_op jit(solution)/shard_map/pick_2/pallas_call | solution.py:307
  85.0 4.2 %collective-permute-start.19 = (bf16[1056,128]{1,0:T(8,128)(2,1)}, bf16[1056,128]{1,0:T(8,128)(2,1)}, u32[]{:S(2)}, u32[]{:S(2)}) collective-permute-start(bf16[1056,128]{1,0:T(8,128)(2,1)} %get-tuple-element.189), channel_id=1, source_target_pairs={{0,2},{1,3},{2,4},{3,5},{8,10},{9,11},{10,12},{11,13},{16,18},{17,... | collective-permute-start | bytes 811016 | tf_op jit(solution)/shard_map/ppermute | solution.py:317
  89.2 1.3 collective-permute-start.20
  90.5 2.7 %collective-permute-start.14 = (bf16[1056,128]{1,0:T(8,128)(2,1)}, bf16[1056,128]{1,0:T(8,128)(2,1)}, u32[]{:S(2)}, u32[]{:S(2)}) collective-permute-start(bf16[1056,128]{1,0:T(8,128)(2,1)} %get-tuple-element.183), channel_id=1, source_target_pairs={{0,6},{1,7},{2,4},{3,5},{4,2},{5,3},{6,0},{7,1},{8,14},{9,15},{10,... | collective-permute-start | bytes 811016 | tf_op jit(solution)/shard_map/ppermute | solution.py:647
  93.2 4.8 %all-to-all-start.2 = ((bf16[8,1,64,256]{3,2,1,0:T(8,128)(2,1)}), bf16[8,1,64,256]{3,2,1,0:T(8,128)(2,1)}, u32[]{:S(2)}, u32[]{:S(2)}) async-start(bf16[8,1,64,256]{3,2,1,0:T(8,128)(2,1)} %sum_parts.1.rest_2_), calls=%async_computation.2 | async-start | bytes 524288 | tf_op jit(solution)/shard_map/all_to_all | solution.py:704
  98.0 0.0 collective-permute-done.13.rest_3_
  98.0 2.4 %collective-permute-start.15 = (bf16[1056,128]{1,0:T(8,128)(2,1)}, bf16[1056,128]{1,0:T(8,128)(2,1)}, u32[]{:S(2)}, u32[]{:S(2)}) collective-permute-start(bf16[1056,128]{1,0:T(8,128)(2,1)} %get-tuple-element.184), channel_id=1, source_target_pairs={{0,7},{1,6},{2,5},{3,4},{4,3},{5,2},{6,1},{7,0},{8,15},{9,14},{10,... | collective-permute-start | bytes 811016 | tf_op jit(solution)/shard_map/ppermute | solution.py:647
  100.4 10.4 %collective-permute-done.19.rest_0_ = bf16[1056,128]{1,0:T(8,128)(2,1)} collective-permute-done((bf16[1056,128]{1,0:T(8,128)(2,1)}, bf16[1056,128]{1,0:T(8,128)(2,1)}, u32[]{:S(2)}, u32[]{:S(2)}) %collective-permute-start.19) | collective-permute-done | bytes 270368 | tf_op jit(solution)/shard_map/ppermute | solution.py:317
  110.8 1.1 collective-permute-start.23
  111.9 3.3 %collective-permute-done.20.rest_1_ = bf16[1056,128]{1,0:T(8,128)(2,1)} collective-permute-done((bf16[1056,128]{1,0:T(8,128)(2,1)}, bf16[1056,128]{1,0:T(8,128)(2,1)}, u32[]{:S(2)}, u32[]{:S(2)}) %collective-permute-start.20) | collective-permute-done | bytes 270368 | tf_op jit(solution)/shard_map/ppermute | solution.py:321
  115.2 2.5 %pick_3.8 = (bf16[1056,128]{1,0:T(8,128)(2,1)}, bf16[1056,128]{1,0:T(8,128)(2,1)}) custom-call(s32[1]{0:T(128)} %constant.34.clone.1.j, s32[16,64]{1,0:T(8,128)S(1)} %get-tuple-element.297, bf16[4,1056,128]{2,1,0:T(8,128)(2,1)} %get-tuple-element.185.own.rest_8_, bf16[4,1056,128]{2,1,0:T(8,128)(2,1)} %collective-permute-done.16.over.rest_9_, ...), custom_call_target="tpu_custom_call" | custom-call | bytes 65536 | tf_op jit(solution)/shard_map/pick_3/pallas_call | solution.py:307
  117.8 1.9 %collective-permute-start.22 = (bf16[1056,128]{1,0:T(8,128)(2,1)}, bf16[1056,128]{1,0:T(8,128)(2,1)}, u32[]{:S(2)}, u32[]{:S(2)}) collective-permute-start(bf16[1056,128]{1,0:T(8,128)(2,1)} %get-tuple-element.192), channel_id=1, source_target_pairs={{7,5},{6,4},{5,3},{4,2},{3,1},{2,0},{15,13},{14,12},{13,11},{12,10... | collective-permute-start | bytes 811016 | tf_op jit(solution)/shard_map/ppermute | solution.py:321
  119.7 1.3 collective-permute-done.14.rest_9_.rest_6_
  121.0 2.6 %collective-permute-start.21 = (bf16[1056,128]{1,0:T(8,128)(2,1)}, bf16[1056,128]{1,0:T(8,128)(2,1)}, u32[]{:S(2)}, u32[]{:S(2)}) collective-permute-start(bf16[1056,128]{1,0:T(8,128)(2,1)} %get-tuple-element.191.rest_8_), channel_id=1, source_target_pairs={{0,2},{1,3},{2,4},{3,5},{4,6},{5,7},{8,10},{9,11},{10,12},{11,13},... | collective-permute-start | bytes 811016 | tf_op jit(solution)/shard_map/ppermute | solution.py:317
  123.6 6.5 %collective-permute-done.15.rest_10_.rest_7_ = bf16[1056,128]{1,0:T(8,128)(2,1)} collective-permute-done((bf16[1056,128]{1,0:T(8,128)(2,1)}, bf16[1056,128]{1,0:T(8,128)(2,1)}, u32[]{:S(2)}, u32[]{:S(2)}) %collective-permute-start.15) | collective-permute-done | bytes 270368 | tf_op jit(solution)/shard_map/ppermute | solution.py:647
  130.2 14.0 %mix_0.1 = (bf16[2048,1024]{1,0:T(8,128)(2,1)}, bf16[8,1024,128]{2,1,0:T(8,128)(2,1)}) custom-call(s32[16,64]{1,0:T(8,128)S(1)} %get-tuple-element.297, bf16[2048,1024]{1,0:T(8,128)(2,1)} %base.3, bf16[8,64,256]{2,1,0:T(8,128)(2,1)} %bitcast.9.shrunk, f32[8,1024]{1,0:T(8,128)} %get-tuple-element.168.rest_0_.channel, ...), custom_call_target="tpu_custom_call" | custom-call | bytes 65536 | tf_op jit(solution)/shard_map/mix_0/pallas_call | solution.py:741
  144.2 0.0 collective-permute-done.21.rest_10_
  144.2 19.4 %mix_4.1 = (bf16[2048,1024]{1,0:T(8,128)(2,1)}, bf16[8,1024,128]{2,1,0:T(8,128)(2,1)}) custom-call(s32[16,64]{1,0:T(8,128)S(1)} %get-tuple-element.297, bf16[2048,1024]{1,0:T(8,128)(2,1)} %base.3, bf16[8,64,256]{2,1,0:T(8,128)(2,1)} %bitcast.9.shrunk, f32[8,1024]{1,0:T(8,128)} %get-tuple-element.168.rest_0_.channel, ...), custom_call_target="tpu_custom_call", output_to_operand_aliasing={{0}: (20, {}), {1}: (21, {})} | custom-call | bytes 65536 | tf_op jit(solution)/shard_map/mix_4/pallas_call | solution.py:741
  (7 shorter events, 0.0 us)
Async XLA Ops:
  15.4 40.1 %all-to-all-start = ((bf16[4,4,64,1024]{3,2,1,0:T(8,128)(2,1)}), bf16[4,4,64,1024]{3,2,1,0:T(8,128)(2,1)}, u32[]{:S(2)}, u32[]{:S(2)}) async-start(bf16[4,4,64,1024]{3,2,1,0:T(8,128)(2,1)} %get-tuple-element.167), calls=%async_computation | async-start | bytes 4194304 | tf_op jit(solution)/shard_map/all_to_all | solution.py:642
  19.9 92.0 %all-gather.2.cloned.1.call-start = ((), (), s32[]{:S(2)}) async-start(), calls=%async_computation.3 | async-start | bytes 1179648 | tf_op jit(solution)/shard_map/all_gather | solution.py:644
  20.7 47.8 %collective-permute-start.16 = (bf16[4,1056,128]{2,1,0:T(8,128)(2,1)}, bf16[4,1056,128]{2,1,0:T(8,128)(2,1)}, u32[]{:S(2)}, u32[]{:S(2)}) collective-permute-start(bf16[4,1056,128]{2,1,0:T(8,128)(2,1)} %get-tuple-element.186), channel_id=1, source_target_pairs={{0,1},{1,0},{2,3},{3,2},{4,5},{5,4},{6,7},{7,6},{8,9},{9,8},{10,11... | collective-permute-start | bytes 3244040 | tf_op jit(solution)/shard_map/ppermute | solution.py:299
  22.2 19.8 %collective-permute-start.7 = (bf16[1056,128]{1,0:T(8,128)(2,1)}, bf16[1056,128]{1,0:T(8,128)(2,1)}, u32[]{:S(2)}, u32[]{:S(2)}) collective-permute-start(bf16[1056,128]{1,0:T(8,128)(2,1)} %get-tuple-element.170), channel_id=1, source_target_pairs={{0,2},{1,3},{2,0},{3,1},{4,6},{5,7},{6,4},{7,5},{8,10},{9,11},{10,... | collective-permute-start | bytes 811016 | tf_op jit(solution)/shard_map/ppermute | solution.py:647
  22.5 26.0 %collective-permute-start.8 = (bf16[1056,128]{1,0:T(8,128)(2,1)}, bf16[1056,128]{1,0:T(8,128)(2,1)}, u32[]{:S(2)}, u32[]{:S(2)}) collective-permute-start(bf16[1056,128]{1,0:T(8,128)(2,1)} %get-tuple-element.171), channel_id=1, source_target_pairs={{0,3},{1,2},{2,1},{3,0},{4,7},{5,6},{6,5},{7,4},{8,11},{9,10},{10,... | collective-permute-start | bytes 811016 | tf_op jit(solution)/shard_map/ppermute | solution.py:647
  25.5 23.0 %collective-permute-start.9 = (bf16[1056,128]{1,0:T(8,128)(2,1)}, bf16[1056,128]{1,0:T(8,128)(2,1)}, u32[]{:S(2)}, u32[]{:S(2)}) collective-permute-start(bf16[1056,128]{1,0:T(8,128)(2,1)} %get-tuple-element.172), channel_id=1, source_target_pairs={{0,4},{1,5},{2,6},{3,7},{4,0},{5,1},{6,2},{7,3},{8,12},{9,13},{10,... | collective-permute-start | bytes 811016 | tf_op jit(solution)/shard_map/ppermute | solution.py:647
  28.1 27.4 %collective-permute-start.10 = (bf16[1056,128]{1,0:T(8,128)(2,1)}, bf16[1056,128]{1,0:T(8,128)(2,1)}, u32[]{:S(2)}, u32[]{:S(2)}) collective-permute-start(bf16[1056,128]{1,0:T(8,128)(2,1)} %get-tuple-element.173), channel_id=1, source_target_pairs={{0,5},{1,4},{2,7},{3,6},{4,1},{5,0},{6,3},{7,2},{8,13},{9,12},{10,... | collective-permute-start | bytes 811016 | tf_op jit(solution)/shard_map/ppermute | solution.py:647
  42.0 30.6 %collective-permute-start.11 = (bf16[4,64,1024]{2,1,0:T(8,128)(2,1)}, bf16[4,64,1024]{2,1,0:T(8,128)(2,1)}, u32[]{:S(2)}, u32[]{:S(2)}) collective-permute-start(bf16[4,64,1024]{2,1,0:T(8,128)(2,1)} %get-tuple-element.177), channel_id=1, source_target_pairs={{0,16},{8,24},{16,0},{24,8},{1,17},{9,25},{17,1},{25,9},{2,18},{10... | collective-permute-start | bytes 1572872 | tf_op jit(solution)/shard_map/ppermute | solution.py:157
  61.2 18.3 %all-to-all-start.1 = ((bf16[8,64,256]{2,1,0:T(8,128)(2,1)}), bf16[8,64,256]{2,1,0:T(8,128)(2,1)}, u32[]{:S(2)}, u32[]{:S(2)}) async-start(bf16[8,64,256]{2,1,0:T(8,128)(2,1)} %shrink.1.rest_0_), calls=%async_computation.1 | async-start | bytes 524288 | tf_op jit(solution)/shard_map/all_to_all | solution.py:694
  69.9 12.5 %collective-permute-start.17 = (bf16[1056,128]{1,0:T(8,128)(2,1)}, bf16[1056,128]{1,0:T(8,128)(2,1)}, u32[]{:S(2)}, u32[]{:S(2)}) collective-permute-start(bf16[1056,128]{1,0:T(8,128)(2,1)} %get-tuple-element.187), channel_id=1, source_target_pairs={{0,2},{1,3},{8,10},{9,11},{16,18},{17,19},{24,26},{25,27}} | collective-permute-start | bytes 811016 | tf_op jit(solution)/shard_map/ppermute | solution.py:317
  71.2 11.2 %collective-permute-start.18 = (bf16[1056,128]{1,0:T(8,128)(2,1)}, bf16[1056,128]{1,0:T(8,128)(2,1)}, u32[]{:S(2)}, u32[]{:S(2)}) collective-permute-start(bf16[1056,128]{1,0:T(8,128)(2,1)} %get-tuple-element.188), channel_id=1, source_target_pairs={{7,5},{6,4},{15,13},{14,12},{23,21},{22,20},{31,29},{30,28}} | collective-permute-start | bytes 811016 | tf_op jit(solution)/shard_map/ppermute | solution.py:321
  72.6 25.4 %collective-permute-start.13 = (bf16[4,64,1024]{2,1,0:T(8,128)(2,1)}, bf16[4,64,1024]{2,1,0:T(8,128)(2,1)}, u32[]{:S(2)}, u32[]{:S(2)}) collective-permute-start(bf16[4,64,1024]{2,1,0:T(8,128)(2,1)} %get-tuple-element.182), channel_id=1, source_target_pairs={{0,24},{8,16},{16,8},{24,0},{1,25},{9,17},{17,9},{25,1},{2,26},{10... | collective-permute-start | bytes 1572872 | tf_op jit(solution)/shard_map/ppermute | solution.py:157
  85.0 25.8 %collective-permute-start.19 = (bf16[1056,128]{1,0:T(8,128)(2,1)}, bf16[1056,128]{1,0:T(8,128)(2,1)}, u32[]{:S(2)}, u32[]{:S(2)}) collective-permute-start(bf16[1056,128]{1,0:T(8,128)(2,1)} %get-tuple-element.189), channel_id=1, source_target_pairs={{0,2},{1,3},{2,4},{3,5},{8,10},{9,11},{10,12},{11,13},{16,18},{17,... | collective-permute-start | bytes 811016 | tf_op jit(solution)/shard_map/ppermute | solution.py:317
  89.2 26.0 %collective-permute-start.20 = (bf16[1056,128]{1,0:T(8,128)(2,1)}, bf16[1056,128]{1,0:T(8,128)(2,1)}, u32[]{:S(2)}, u32[]{:S(2)}) collective-permute-start(bf16[1056,128]{1,0:T(8,128)(2,1)} %get-tuple-element.190), channel_id=1, source_target_pairs={{7,5},{6,4},{5,3},{4,2},{15,13},{14,12},{13,11},{12,10},{23,21},{2... | collective-permute-start | bytes 811016 | tf_op jit(solution)/shard_map/ppermute | solution.py:321
  90.5 30.5 %collective-permute-start.14 = (bf16[1056,128]{1,0:T(8,128)(2,1)}, bf16[1056,128]{1,0:T(8,128)(2,1)}, u32[]{:S(2)}, u32[]{:S(2)}) collective-permute-start(bf16[1056,128]{1,0:T(8,128)(2,1)} %get-tuple-element.183), channel_id=1, source_target_pairs={{0,6},{1,7},{2,4},{3,5},{4,2},{5,3},{6,0},{7,1},{8,14},{9,15},{10,... | collective-permute-start | bytes 811016 | tf_op jit(solution)/shard_map/ppermute | solution.py:647
  93.2 37.0 %collective-permute-start.12 = (bf16[4,64,1024]{2,1,0:T(8,128)(2,1)}, bf16[4,64,1024]{2,1,0:T(8,128)(2,1)}, u32[]{:S(2)}, u32[]{:S(2)}) collective-permute-start(bf16[4,64,1024]{2,1,0:T(8,128)(2,1)} %get-tuple-element.181), channel_id=1, source_target_pairs={{0,8},{8,0},{16,24},{24,16},{1,9},{9,1},{17,25},{25,17},{2,10},{10... | collective-permute-start | bytes 1572872 | tf_op jit(solution)/shard_map/ppermute | solution.py:157
  93.2 37.0 %all-to-all-start.2 = ((bf16[8,1,64,256]{3,2,1,0:T(8,128)(2,1)}), bf16[8,1,64,256]{3,2,1,0:T(8,128)(2,1)}, u32[]{:S(2)}, u32[]{:S(2)}) async-start(bf16[8,1,64,256]{3,2,1,0:T(8,128)(2,1)} %sum_parts.1.rest_2_), calls=%async_computation.2 | async-start | bytes 524288 | tf_op jit(solution)/shard_map/all_to_all | solution.py:704
  98.0 32.1 %collective-permute-start.15 = (bf16[1056,128]{1,0:T(8,128)(2,1)}, bf16[1056,128]{1,0:T(8,128)(2,1)}, u32[]{:S(2)}, u32[]{:S(2)}) collective-permute-start(bf16[1056,128]{1,0:T(8,128)(2,1)} %get-tuple-element.184), channel_id=1, source_target_pairs={{0,7},{1,6},{2,5},{3,4},{4,3},{5,2},{6,1},{7,0},{8,15},{9,14},{10,... | collective-permute-start | bytes 811016 | tf_op jit(solution)/shard_map/ppermute | solution.py:647
  110.8 19.3 %collective-permute-start.23 = (bf16[1056,128]{1,0:T(8,128)(2,1)}, bf16[1056,128]{1,0:T(8,128)(2,1)}, u32[]{:S(2)}, u32[]{:S(2)}) collective-permute-start(bf16[1056,128]{1,0:T(8,128)(2,1)} %get-tuple-element.194), channel_id=1, source_target_pairs={{0,1},{1,0},{2,3},{3,2},{4,5},{5,4},{6,7},{7,6},{8,9},{9,8},{10,11... | collective-permute-start | bytes 811016 | tf_op jit(solution)/shard_map/ppermute | solution.py:647
  117.8 26.4 %collective-permute-start.22 = (bf16[1056,128]{1,0:T(8,128)(2,1)}, bf16[1056,128]{1,0:T(8,128)(2,1)}, u32[]{:S(2)}, u32[]{:S(2)}) collective-permute-start(bf16[1056,128]{1,0:T(8,128)(2,1)} %get-tuple-element.192), channel_id=1, source_target_pairs={{7,5},{6,4},{5,3},{4,2},{3,1},{2,0},{15,13},{14,12},{13,11},{12,10... | collective-permute-start | bytes 811016 | tf_op jit(solution)/shard_map/ppermute | solution.py:321
  121.0 23.2 %collective-permute-start.21 = (bf16[1056,128]{1,0:T(8,128)(2,1)}, bf16[1056,128]{1,0:T(8,128)(2,1)}, u32[]{:S(2)}, u32[]{:S(2)}) collective-permute-start(bf16[1056,128]{1,0:T(8,128)(2,1)} %get-tuple-element.191.rest_8_), channel_id=1, source_target_pairs={{0,2},{1,3},{2,4},{3,5},{4,6},{5,7},{8,10},{9,11},{10,12},{11,13},... | collective-permute-start | bytes 811016 | tf_op jit(solution)/shard_map/ppermute | solution.py:317
Sparse Core Ops, SparseCore 0:
  22.9 55.6 all-gather.1

commit v10 on v9

--- a/solution.py
+++ b/solution.py
@@ -17,7 +17,7 @@
 VMEM_LIMIT = 63 * 1024 * 1024
 
 HOME, DIST, ARANK, AINDEX, PRESENT, POS_REQ, POS_VALID, OSLOT, OHOLDER, MISC, SEND = range(11)
-MOST, ME, SLOT = range(3)
+MOST, ME, SLOT, SPREAD = range(4)
 META_SHAPE = (16, 64)
 
 
@@ -57,6 +57,10 @@
             total = total + as_int(other == label)
         ranks.append(total)
     return ranks
+
+
+def near_distances(devices):
+    return devices - max(devices // 4, 1)
 
 
 def plan(groups, devices, per_group, home, index, holder, slot, blocks, meta):
@@ -115,7 +119,7 @@
         meta[POS_VALID, d] = as_int(request >= 0)
         requests.append(request)
     requests += [meta[POS_REQ, devices + j] for j in range(limit)]
-    for begin, end in ((0, devices // 2), (devices // 2, devices + limit)):
+    for begin, end in ((0, devices // 2), (devices // 2, devices)):
         last = jnp.int32(-1)
         filled = []
         for p in range(begin, end):
@@ -125,6 +129,13 @@
         for p in reversed(range(begin, end)):
             following = jnp.where(filled[p - begin] >= 0, filled[p - begin], following)
             meta[POS_REQ, p] = following
+    meta[MISC, SPREAD] = as_int(count > 0)
+    meta[POS_VALID, devices] = jnp.int32(1)
+    for j in range(limit):
+        meta[POS_REQ, devices + j] = jnp.where(
+            j < count, requests[devices + j],
+            jnp.where(count > 0, meta[POS_REQ, devices + max(j - 1, 0)], requests[0]),
+        )
     most = jnp.int32(0)
     for g in range(groups):
         labels = [holder[g * per_group + q] for q in range(per_group)]
@@ -461,8 +472,8 @@
     rows_in, *rest
 ):
     tables, chunks = rest[:groups], rest[groups:]
-    out, final, extended, scores, carried, weighted, ups, curs, table_sems, chunk_sems = (
-        rest[-10:]
+    out, final, done, extended, scores, carried, weighted, ups, curs, table_sems, chunk_sems = (
+        rest[-11:]
     )
     g = pl.program_id(0)
     position = begin + g
@@ -474,6 +485,8 @@
     few = taps - 1
     parts = width // 128
     f32, bf16 = jnp.float32, jnp.bfloat16
+
+    done[...] = jnp.zeros_like(done)
 
     def fetch_chunk(source, i):
         pltpu.make_async_copy(source, curs.at[i], chunk_sems.at[i]).start()
@@ -492,8 +505,13 @@
                 else:
                     line = meta[MISC, ME] // 2
                     own, across, from_left, from_right = chunks[direct:direct + 4]
-                    candidates = [own.at[line], across.at[line], from_left, from_right]
-                    which = which_candidate(meta, meta[OHOLDER, 0])
+                    candidates = [
+                        own.at[line], across.at[line], from_left, from_right,
+                        chunks[direct + 5],
+                    ]
+                    which = jnp.where(
+                        meta[MISC, SPREAD] > 0, which_candidate(meta, meta[OHOLDER, 0]), 4
+                    )
                     for k, candidate in enumerate(candidates):
                         @pl.when(which == k)
                         def _(candidate=candidate):
@@ -643,9 +661,10 @@
     chunks = packed[groups:-2]
     rows_all = lax.all_gather(rows_mine, "dev", axis=0, tiled=True)
     zero = jnp.zeros((1,), jnp.int32)
+    near = near_distances(devices)
     got = [chunks[0]] + [
         lax.ppermute(chunks[d], "dev", [(s, s ^ d) for s in range(devices)])
-        for d in range(1, devices)
+        for d in range(1, near)
     ]
 
     spread_others = spread_rest(meta, cache, conv, devices, width, limit)
@@ -671,7 +690,7 @@
     )
 
     each = per_group // 2
-    early = got[2:lines + 2]
+    early = got[2:]
     partial_down = pl.pallas_call(
         functools.partial(shrink_kernel, per_group),
         grid_spec=pltpu.PrefetchScalarGridSpec(
@@ -691,32 +710,39 @@
         name="shrink",
     )(meta, hidden, down_got, channel, spread_others, *early)
 
+    spread = spread_steps(zero, meta, packed[-2:], devices)
+    next(spread)
+    sent = spread.send([partial_down])
+
     parts = lax.all_to_all(partial_down, "dev", split_axis=0, concat_axis=0, tiled=True)
     summed = pl.pallas_call(
         sum_kernel,
         out_shape=jax.ShapeDtypeStruct((devices, 1, rank, T_REQ), bf16),
-        in_specs=vmem(1) + anywhere(1),
+        in_specs=vmem(1) + anywhere(2),
         out_specs=vmem(1)[0],
         cost_estimate=cost(),
         compiler_params=params(),
         name="sum_parts",
-    )(parts.reshape(devices, 1, rank, T_REQ), up_got[groups // 2 - 1])
+    )(parts.reshape(devices, 1, rank, T_REQ), up_got[groups // 2 - 1], sent)
     shrunk = lax.all_to_all(summed, "dev", split_axis=0, concat_axis=0, tiled=True)
     shrunk = shrunk.reshape(per_group, rank, T_REQ)
 
-    befores = [[partial_down], [summed], [rows_all, up_got[-1]]]
-    spread = spread_steps(zero, meta, packed[-2:], devices)
-    next(spread)
-    for step in range(1, lines):
-        sent = spread.send(befores.pop(0) if befores else [])
-    spread = spread.send([])
+    late, _ = lax.optimization_barrier((chunks[near:], partial_down))
+    got += [
+        lax.ppermute(x, "dev", [(s, s ^ d) for s in range(devices)])
+        for d, x in zip(range(near, devices), late)
+    ]
+    for step in range(2, lines - 1):
+        sent = spread.send([] if step < lines - 2 else [shrunk])
 
     outs = None
-    for begin, steps in ((0, lines), (lines, devices - lines + limit)):
+    for begin, steps in ((0, lines), (lines, lines), (devices, limit)):
         if begin == 0:
-            chunks, after = got[:lines], [sent, got[lines + 2], got[lines + 3]]
+            chunks, after = got[:lines], [sent]
+        elif begin == lines:
+            chunks, after = got[lines:], [spread.send([outs[2]])]
         else:
-            chunks, after = [*got[lines:], *spread, spread_others], []
+            chunks, after = [*spread.send([]), spread_others, got[0]], []
 
         def request(g, meta, begin=begin):
             return meta[POS_REQ, begin + g]
@@ -736,10 +762,12 @@
         aliases = {}
         if outs is not None:
             aliases = {len(operands): 0, len(operands) + 1: 1}
-            operands += list(outs)
+            operands += list(outs[:2])
             in_specs += anywhere(2)
         outs = pl.pallas_call(
-            functools.partial(mix_kernel, groups, taps, begin, steps, lines, size),
+            functools.partial(
+                mix_kernel, groups, taps, begin, steps, 0 if begin == devices else lines, size
+            ),
             grid_spec=pltpu.PrefetchScalarGridSpec(
                 num_scalar_prefetch=1,
                 grid=(steps,),
@@ -749,6 +777,7 @@
                     pl.BlockSpec(
                         (1, heads * size, depth), lambda g, meta: (request(g, meta), 0, 0)
                     ),
+                    pl.BlockSpec((8, 128), lambda g, meta: (0, 0)),
                 ),
                 scratch_shapes=[
                     pltpu.VMEM((T_REQ + 8, width), f32),
@@ -764,6 +793,7 @@
             out_shape=(
                 jax.ShapeDtypeStruct((tokens, width), bf16),
                 jax.ShapeDtypeStruct((per_group, heads * size, depth), bf16),
+                jax.ShapeDtypeStruct((8, 128), f32),
             ),
             input_output_aliases=aliases,
             cost_estimate=cost(),

time: 171 us -> 169 us (0.988)
  waiting for transfers between devices: 51.5 us -> 40.8 us
  Pallas kernels: 58.2 us -> 61.9 us
  starting transfers between devices: 45.4 us -> 47.7 us
  local copies, waits for them, and re-layouts: 0.63 us -> 2.73 us
    ppermute x7 -> x5, waiting for transfers between devices: 29.1 us -> 21.3 us  [body(): lax.ppermute(chunks[d], 'dev', [(s, s ^ d) for s in range(devices)])]
    ppermute x3, waiting for transfers between devices: 11.5 us -> 6.3 us  [spread_steps(): lax.ppermute(to_right, 'dev', [(2 * i + x, 2 * i + 2 + x) for i in range(...]
    ppermute x7 -> x5, starting transfers between devices: 12.1 us -> 7.38 us  [body(): lax.ppermute(chunks[d], 'dev', [(s, s ^ d) for s in range(devices)])]
    ppermute x3, starting transfers between devices: 8.11 us -> 11.7 us  [spread_steps(): lax.ppermute(to_right, 'dev', [(2 * i + x, 2 * i + 2 + x) for i in range(...]
    ppermute x0 -> x2, starting transfers between devices: none -> 2.97 us  [body(): lax.ppermute(x, 'dev', [(s, s ^ d) for s in range(devices)])]
    ppermute x0 -> x2, waiting for transfers between devices: none -> 2.52 us  [body(): lax.ppermute(x, 'dev', [(s, s ^ d) for s in range(devices)])]
    unnamed x0 -> x14, local copies, waits for them, and re-layouts: none -> 2.11 us
    pallas_call x2 -> x3, Pallas kernels: 33.4 us -> 35.5 us  [body(): pl.pallas_call(functools.partial(mix_kernel, groups, taps, begin, steps,...]
  transfers between devices with their start and end apart: 21 -> 21, of which waited for: 9 -> 8; matrix products, arithmetic and copies ran while one was open for 0% -> 0% of each run, Pallas kernels for 18% -> 27%
where the time goes in v10:
time: 169 us; the launch traced here: 168 us
  Pallas kernels  61.9 us (37%)
  starting transfers between devices  47.7 us (28%)
  waiting for transfers between devices  40.8 us (24%)
  between operations  14.3 us (8%)
  local copies, waits for them, and re-layouts  2.73 us (2%)
    pallas_call x3, Pallas kernels, body(): pl.pallas_call(functools.partial(mix_kernel, groups, taps, begin, steps,...  35.5 us
    ppermute x5, waiting for transfers between devices, body(): lax.ppermute(chunks[d], 'dev', [(s, s ^ d) for s in range(devices)])  21.3 us
    ppermute x3, starting transfers between devices, spread_steps(): lax.ppermute(to_right, 'dev', [(2 * i + x, 2 * i + 2 + x) for i in range(...  11.7 us
    pallas_call x1, Pallas kernels, body(): pl.pallas_call(functools.partial(pack_kernel, groups, devices, per_group,...  8.81 us
    all_to_all x1, waiting for transfers between devices, body(): lax.all_to_all(partial_down, 'dev', split_axis=0, concat_axis=0, tiled=True)  8.31 us
    pallas_call x3, Pallas kernels, spread_steps(): pl.pallas_call(functools.partial(pick_kernel, step, lines), in_specs=smem...  7.62 us
    ppermute x5, starting transfers between devices, body(): lax.ppermute(chunks[d], 'dev', [(s, s ^ d) for s in range(devices)])  7.38 us
    all_to_all x1, starting transfers between devices, body(): lax.all_to_all(partial_down, 'dev', split_axis=0, concat_axis=0, tiled=True)  7.03 us
  transfers between devices with their start and end apart: 21, of which 8 were waited for; matrix products, arithmetic and copies ran while one was open for 0% of the time, Pallas kernels for 27%

profile of v10, /device:TPU:8, one launch (start us, length us, event | category | flops | bytes accessed | tf_op | source)
XLA Modules:
  0.0 168.0 jit_solution(1408072106847401105)
XLA Ops:
  7.2 8.8 %pack.1 = (s32[16,64]{1,0:T(8,128)S(1)}, bf16[256,256]{1,0:T(8,128)(2,1)}, bf16[4,4,64,1024]{3,2,1,0:T(8,128)(2,1)}, bf16[4,64,1024]{2,1,0:T(8,128)(2,1)}, bf16[...) custom-call(s32[32]{0:T(128)} %bitcast.27, ...), custom_call_target="tpu_custom_call" | custom-call | bytes 65536 | tf_op jit(solution)/shard_map/pack/pallas_call | solution.py:633
  16.0 4.5 %all-to-all-start = ((bf16[4,4,64,1024]{3,2,1,0:T(8,128)(2,1)}), bf16[4,4,64,1024]{3,2,1,0:T(8,128)(2,1)}, u32[]{:S(2)}, u32[]{:S(2)}) async-start(bf16[4,4,64,1024]{3,2,1,0:T(8,128)(2,1)} %get-tuple-element.172), calls=%async_computation | async-start | bytes 4194304 | tf_op jit(solution)/shard_map/all_to_all | solution.py:660
  20.5 0.0 all-gather.2.cloned.1.call-start
  20.5 0.7 all-gather.2.cloned.1.call-update
  21.2 1.7 collective-permute-start.12
  22.9 0.4 collective-permute-start.7
  23.3 1.4 collective-permute-start.8
  24.8 0.5 slice.3
  25.3 0.1 broadcast_in_dim.12
  25.4 0.6 while.14
  26.0 2.8 %collective-permute-start.9 = (bf16[1056,128]{1,0:T(8,128)(2,1)}, bf16[1056,128]{1,0:T(8,128)(2,1)}, u32[]{:S(2)}, u32[]{:S(2)}) collective-permute-start(bf16[1056,128]{1,0:T(8,128)(2,1)} %get-tuple-element.177), channel_id=1, source_target_pairs={{0,4},{1,5},{2,6},{3,7},{4,0},{5,1},{6,2},{7,3},{8,12},{9,13},{10,... | collective-permute-start | bytes 811016 | tf_op jit(solution)/shard_map/ppermute | solution.py:666
  28.8 1.2 collective-permute-start.10
  30.0 13.2 %collective-permute-done.7.rest_2_.rest_6_ = bf16[1056,128]{1,0:T(8,128)(2,1)} collective-permute-done((bf16[1056,128]{1,0:T(8,128)(2,1)}, bf16[1056,128]{1,0:T(8,128)(2,1)}, u32[]{:S(2)}, u32[]{:S(2)}) %collective-permute-start.7) | collective-permute-done | bytes 270368 | tf_op jit(solution)/shard_map/ppermute | solution.py:666
  43.2 2.3 %collective-permute-start.11 = (bf16[4,64,1024]{2,1,0:T(8,128)(2,1)}, bf16[4,64,1024]{2,1,0:T(8,128)(2,1)S(1)}, u32[]{:S(2)}, u32[]{:S(2)}) collective-permute-start(bf16[4,64,1024]{2,1,0:T(8,128)(2,1)} %get-tuple-element.182), channel_id=1, source_target_pairs={{0,16},{8,24},{16,0},{24,8},{1,17},{9,25},{17,1},{25,9},{2,18},{10... | collective-permute-start | bytes 1572872 | tf_op jit(solution)/shard_map/ppermute | solution.py:168
  45.5 2.5 %prep.1 = (f32[32,2048]{1,0:T(8,128)}, f32[8,256,16]{2,1,0:T(8,128)}, f32[8,1024]{1,0:T(8,128)}) custom-call(f32[16]{0:T(128)} %rates.1, f32[16]{0:T(128)} %skips.1, f32[16,2048]{1,0:T(8,128)} %steps.1, f32[4,1024]{1,0:T(4,128)} %taps_in.1, f32[1,1024]{1,0:T(1,128)} %bitcast.26, s32[16,64]{1,0:T(8,128)S(1)} %get-tuple-element.307), custom_call_target="tpu_custom_call" | custom-call | bytes 65536 | tf_op jit(solution)/shard_map/prep/pallas_call | solution.py:675
  48.0 1.4 collective-permute-done.8.rest_3_.rest_7_
  49.4 6.7 %collective-permute-done.10.rest_5_ = bf16[1056,128]{1,0:T(8,128)(2,1)} collective-permute-done((bf16[1056,128]{1,0:T(8,128)(2,1)}, bf16[1056,128]{1,0:T(8,128)(2,1)}, u32[]{:S(2)}, u32[]{:S(2)}) %collective-permute-start.10) | collective-permute-done | bytes 270368 | tf_op jit(solution)/shard_map/ppermute | solution.py:666
  56.2 5.7 %shrink.1.rest_0_ = bf16[8,64,256]{2,1,0:T(8,128)(2,1)} custom-call(s32[16,64]{1,0:T(8,128)S(1)} %get-tuple-element.307, bf16[2048,1024]{1,0:T(8,128)(2,1)} %hidden.1, bf16[4,4,64,1024]{3,2,1,0:T(8,128)(2,1)} %all-to-all-done.table, f32[8,1024]{1,0:T(8,128)} %get-tuple-element.173.rest_0_.channel, bf16[3,1056,128]{2,1,0:T(8,128)(2,1)} %copy-done.1, ...), custom_call_target="tpu_custom_call" | custom-call | bytes 65536 | tf_op jit(solution)/shard_map/shrink/pallas_call | solution.py:694
  61.9 7.0 %all-to-all-start.1 = ((bf16[8,64,256]{2,1,0:T(8,128)(2,1)}), bf16[8,64,256]{2,1,0:T(8,128)(2,1)S(1)}, u32[]{:S(2)}, u32[]{:S(2)}) async-start(bf16[8,64,256]{2,1,0:T(8,128)(2,1)} %shrink.1.rest_0_), calls=%async_computation.1 | async-start | bytes 524288 | tf_op jit(solution)/shard_map/all_to_all | solution.py:717
  68.9 2.5 %pick_1.8 = (bf16[1056,128]{1,0:T(8,128)(2,1)}, bf16[1056,128]{1,0:T(8,128)(2,1)}) custom-call(s32[1]{0:T(128)} %constant.34.clone.1.j, s32[16,64]{1,0:T(8,128)S(1)} %get-tuple-element.307, bf16[4,1056,128]{2,1,0:T(8,128)(2,1)} %get-tuple-element.183.own.rest_4_, bf16[4,1056,128]{2,1,0:T(8,128)(2,1)} %collective-permute-done.12.over.rest_5_, ...), custom_call_target="tpu_custom_call" | custom-call | bytes 65536 | tf_op jit(solution)/shard_map/pick_1/pallas_call | solution.py:318
  71.5 0.0 collective-permute-done.11.rest_0_.rest_2_
  71.5 8.3 %all-to-all-done.1 = bf16[8,64,256]{2,1,0:T(8,128)(2,1)S(1)} async-done(((bf16[8,64,256]{2,1,0:T(8,128)(2,1)}), bf16[8,64,256]{2,1,0:T(8,128)(2,1)S(1)}, u32[]{:S(2)}, u32[]{:S(2)}) %all-to-all-start.1) | async-done | bytes 262176 | tf_op jit(solution)/shard_map/all_to_all | solution.py:717
  79.8 0.7 copy-done.7
  80.5 1.7 %sum_parts.1 = bf16[8,1,64,256]{3,2,1,0:T(8,128)(2,1)} custom-call(bf16[8,1,64,256]{3,2,1,0:T(8,128)(2,1)} %bitcast.25, bf16[4,64,1024]{2,1,0:T(8,128)(2,1)} %copy-done, bf16[1056,128]{1,0:T(8,128)(2,1)} %get-tuple-element.185.rest_1_), custom_call_target="tpu_custom_call" | custom-call | bytes 65536 | tf_op jit(solution)/shard_map/sum_parts/pallas_call | solution.py:718
  82.2 4.6 %all-to-all-start.2 = ((bf16[8,1,64,256]{3,2,1,0:T(8,128)(2,1)}), bf16[8,1,64,256]{3,2,1,0:T(8,128)(2,1)S(1)}, u32[]{:S(2)}, u32[]{:S(2)}) async-start(bf16[8,1,64,256]{3,2,1,0:T(8,128)(2,1)} %sum_parts.1), calls=%async_computation.2 | async-start | bytes 524288 | tf_op jit(solution)/shard_map/all_to_all | solution.py:727
  86.8 0.7 collective-permute-start.16
  87.5 1.3 collective-permute-start.15
  88.8 0.1 collective-permute-start.13
  88.9 1.6 collective-permute-start.14
  90.5 1.5 collective-permute-start.19
  91.9 0.7 copy-done.8
  92.6 4.8 %collective-permute-done.15.rest_0_ = bf16[1056,128]{1,0:T(8,128)(2,1)} collective-permute-done((bf16[1056,128]{1,0:T(8,128)(2,1)}, bf16[1056,128]{1,0:T(8,128)(2,1)}, u32[]{:S(2)}, u32[]{:S(2)}) %collective-permute-start.15) | collective-permute-done | bytes 270368 | tf_op jit(solution)/shard_map/ppermute | solution.py:328
  97.5 0.7 copy-done.5
  98.2 2.5 %pick_2.8 = (bf16[1056,128]{1,0:T(8,128)(2,1)}, bf16[1056,128]{1,0:T(8,128)(2,1)}) custom-call(s32[1]{0:T(128)} %constant.34.clone.1.j, s32[16,64]{1,0:T(8,128)S(1)} %get-tuple-element.307, bf16[4,1056,128]{2,1,0:T(8,128)(2,1)} %get-tuple-element.183.own.rest_4_, bf16[4,1056,128]{2,1,0:T(8,128)(2,1)} %collective-permute-done.12.over.rest_5_, ...), custom_call_target="tpu_custom_call" | custom-call | bytes 65536 | tf_op jit(solution)/shard_map/pick_2/pallas_call | solution.py:318
  100.7 1.3 collective-permute-start.18
  102.0 5.8 %collective-permute-start.17 = (bf16[1056,128]{1,0:T(8,128)(2,1)}, bf16[1056,128]{1,0:T(8,128)(2,1)}, u32[]{:S(2)}, u32[]{:S(2)}) collective-permute-start(bf16[1056,128]{1,0:T(8,128)(2,1)} %get-tuple-element.192.rest_8_), channel_id=1, source_target_pairs={{0,2},{1,3},{2,4},{3,5},{8,10},{9,11},{10,12},{11,13},{16,18},{17,... | collective-permute-start | bytes 811016 | tf_op jit(solution)/shard_map/ppermute | solution.py:328
  107.8 0.0 collective-permute-done.19.rest_5_
  107.8 0.1 collective-permute-start.22
  107.9 2.9 %collective-permute-start.23 = (bf16[1056,128]{1,0:T(8,128)(2,1)}, bf16[1056,128]{1,0:T(8,128)(2,1)}, u32[]{:S(2)}, u32[]{:S(2)}) collective-permute-start(bf16[1056,128]{1,0:T(8,128)(2,1)} %get-tuple-element.202), channel_id=1, source_target_pairs={{0,7},{1,6},{2,5},{3,4},{4,3},{5,2},{6,1},{7,0},{8,15},{9,14},{10,... | collective-permute-start | bytes 811016 | tf_op jit(solution)/shard_map/ppermute | solution.py:732
  110.8 12.7 %mix_0.1 = (bf16[2048,1024]{1,0:T(8,128)(2,1)}, bf16[8,1024,128]{2,1,0:T(8,128)(2,1)}, f32[8,128]{1,0:T(8,128)}) custom-call(s32[16,64]{1,0:T(8,128)S(1)} %get-tuple-element.307, bf16[2048,1024]{1,0:T(8,128)(2,1)} %base.5, bf16[8,64,256]{2,1,0:T(8,128)(2,1)} %bitcast.22, f32[8,1024]{1,0:T(8,128)} %get-tuple-element.173.rest_0_.channel, ...), custom_call_target="tpu_custom_call" | custom-call | bytes 65536 | tf_op jit(solution)/shard_map/mix_0/pallas_call | solution.py:767
  123.5 1.6 collective-permute-done.18.rest_1_
  125.2 1.5 collective-permute-done.17.rest_0_
  126.6 2.5 %pick_3.8 = (bf16[1056,128]{1,0:T(8,128)(2,1)}, bf16[1056,128]{1,0:T(8,128)(2,1)}) custom-call(s32[1]{0:T(128)} %constant.34.clone.1.j, s32[16,64]{1,0:T(8,128)S(1)} %get-tuple-element.307, bf16[4,1056,128]{2,1,0:T(8,128)(2,1)} %get-tuple-element.183.own.rest_4_, bf16[4,1056,128]{2,1,0:T(8,128)(2,1)} %collective-permute-done.12.over.rest_5_, ...), custom_call_target="tpu_custom_call" | custom-call | bytes 65536 | tf_op jit(solution)/shard_map/pick_3/pallas_call | solution.py:318
  129.2 1.9 %collective-permute-start.21 = (bf16[1056,128]{1,0:T(8,128)(2,1)}, bf16[1056,128]{1,0:T(8,128)(2,1)}, u32[]{:S(2)}, u32[]{:S(2)}) collective-permute-start(bf16[1056,128]{1,0:T(8,128)(2,1)} %get-tuple-element.198), channel_id=1, source_target_pairs={{7,5},{6,4},{5,3},{4,2},{3,1},{2,0},{15,13},{14,12},{13,11},{12,10... | collective-permute-start | bytes 811016 | tf_op jit(solution)/shard_map/ppermute | solution.py:332
  131.1 4.6 %collective-permute-start.20 = (bf16[1056,128]{1,0:T(8,128)(2,1)}, bf16[1056,128]{1,0:T(8,128)(2,1)}, u32[]{:S(2)}, u32[]{:S(2)}) collective-permute-start(bf16[1056,128]{1,0:T(8,128)(2,1)} %get-tuple-element.197.rest_8_), channel_id=1, source_target_pairs={{0,2},{1,3},{2,4},{3,5},{4,6},{5,7},{8,10},{9,11},{10,12},{11,13},... | collective-permute-start | bytes 811016 | tf_op jit(solution)/shard_map/ppermute | solution.py:328
  135.7 2.5 %collective-permute-done.23.rest_7_ = bf16[1056,128]{1,0:T(8,128)(2,1)} collective-permute-done((bf16[1056,128]{1,0:T(8,128)(2,1)}, bf16[1056,128]{1,0:T(8,128)(2,1)}, u32[]{:S(2)}, u32[]{:S(2)}) %collective-permute-start.23) | collective-permute-done | bytes 270368 | tf_op jit(solution)/shard_map/ppermute | solution.py:732
  138.2 15.8 %mix_4.1 = (bf16[2048,1024]{1,0:T(8,128)(2,1)}, bf16[8,1024,128]{2,1,0:T(8,128)(2,1)}, f32[8,128]{1,0:T(8,128)}) custom-call(s32[16,64]{1,0:T(8,128)S(1)} %get-tuple-element.307, bf16[2048,1024]{1,0:T(8,128)(2,1)} %base.5, bf16[8,64,256]{2,1,0:T(8,128)(2,1)} %bitcast.23, ...), custom_call_target="tpu_custom_call", output_to_operand_aliasing={{0}: (16, {}), {1}: (17, {})} | custom-call | bytes 65536 | tf_op jit(solution)/shard_map/mix_4/pallas_call | solution.py:767
  154.1 7.0 %mix_8.1 = (bf16[2048,1024]{1,0:T(8,128)(2,1)}, bf16[8,1024,128]{2,1,0:T(8,128)(2,1)}, f32[8,128]{1,0:T(8,128)}) custom-call(s32[16,64]{1,0:T(8,128)S(1)} %get-tuple-element.307, bf16[2048,1024]{1,0:T(8,128)(2,1)} %base.5, bf16[8,64,256]{2,1,0:T(8,128)(2,1)} %bitcast.24, ...), custom_call_target="tpu_custom_call", output_to_operand_aliasing={{0}: (17, {}), {1}: (18, {})} | custom-call | bytes 65536 | tf_op jit(solution)/shard_map/mix_8/pallas_call | solution.py:767
  (22 shorter events, 0.0 us)
Async XLA Ops:
  16.0 40.2 %all-to-all-start = ((bf16[4,4,64,1024]{3,2,1,0:T(8,128)(2,1)}), bf16[4,4,64,1024]{3,2,1,0:T(8,128)(2,1)}, u32[]{:S(2)}, u32[]{:S(2)}) async-start(bf16[4,4,64,1024]{3,2,1,0:T(8,128)(2,1)} %get-tuple-element.172), calls=%async_computation | async-start | bytes 4194304 | tf_op jit(solution)/shard_map/all_to_all | solution.py:660
  20.5 90.4 %all-gather.2.cloned.1.call-start = ((), (), s32[]{:S(2)}) async-start(), calls=%async_computation.3 | async-start | bytes 1179648 | tf_op jit(solution)/shard_map/all_gather | solution.py:662
  21.2 47.7 %collective-permute-start.12 = (bf16[4,1056,128]{2,1,0:T(8,128)(2,1)}, bf16[4,1056,128]{2,1,0:T(8,128)(2,1)}, u32[]{:S(2)}, u32[]{:S(2)}) collective-permute-start(bf16[4,1056,128]{2,1,0:T(8,128)(2,1)} %get-tuple-element.184), channel_id=1, source_target_pairs={{0,1},{1,0},{2,3},{3,2},{4,5},{5,4},{6,7},{7,6},{8,9},{9,8},{10,11... | collective-permute-start | bytes 3244040 | tf_op jit(solution)/shard_map/ppermute | solution.py:310
  22.9 20.3 %collective-permute-start.7 = (bf16[1056,128]{1,0:T(8,128)(2,1)}, bf16[1056,128]{1,0:T(8,128)(2,1)}, u32[]{:S(2)}, u32[]{:S(2)}) collective-permute-start(bf16[1056,128]{1,0:T(8,128)(2,1)} %get-tuple-element.175), channel_id=1, source_target_pairs={{0,2},{1,3},{2,0},{3,1},{4,6},{5,7},{6,4},{7,5},{8,10},{9,11},{10,... | collective-permute-start | bytes 811016 | tf_op jit(solution)/shard_map/ppermute | solution.py:666
  23.3 26.1 %collective-permute-start.8 = (bf16[1056,128]{1,0:T(8,128)(2,1)}, bf16[1056,128]{1,0:T(8,128)(2,1)}, u32[]{:S(2)}, u32[]{:S(2)}) collective-permute-start(bf16[1056,128]{1,0:T(8,128)(2,1)} %get-tuple-element.176), channel_id=1, source_target_pairs={{0,3},{1,2},{2,1},{3,0},{4,7},{5,6},{6,5},{7,4},{8,11},{9,10},{10,... | collective-permute-start | bytes 811016 | tf_op jit(solution)/shard_map/ppermute | solution.py:666
  26.0 17.2 %copy-start.1 = (bf16[3,1056,128]{2,1,0:T(8,128)(2,1)}, bf16[3,1056,128]{2,1,0:T(8,128)(2,1)S(1)}, u32[]{:S(2)}) copy-start(bf16[3,1056,128]{2,1,0:T(8,128)(2,1)S(1)} %get-tuple-element.174.rest_1_.rest_8_) | copy-start | bytes 2433028
  26.0 23.4 %collective-permute-start.9 = (bf16[1056,128]{1,0:T(8,128)(2,1)}, bf16[1056,128]{1,0:T(8,128)(2,1)}, u32[]{:S(2)}, u32[]{:S(2)}) collective-permute-start(bf16[1056,128]{1,0:T(8,128)(2,1)} %get-tuple-element.177), channel_id=1, source_target_pairs={{0,4},{1,5},{2,6},{3,7},{4,0},{5,1},{6,2},{7,3},{8,12},{9,13},{10,... | collective-permute-start | bytes 811016 | tf_op jit(solution)/shard_map/ppermute | solution.py:666
  28.8 27.4 %collective-permute-start.10 = (bf16[1056,128]{1,0:T(8,128)(2,1)}, bf16[1056,128]{1,0:T(8,128)(2,1)}, u32[]{:S(2)}, u32[]{:S(2)}) collective-permute-start(bf16[1056,128]{1,0:T(8,128)(2,1)} %get-tuple-element.178), channel_id=1, source_target_pairs={{0,5},{1,4},{2,7},{3,6},{4,1},{5,0},{6,3},{7,2},{8,13},{9,12},{10,... | collective-permute-start | bytes 811016 | tf_op jit(solution)/shard_map/ppermute | solution.py:666
  43.2 28.3 %collective-permute-start.11 = (bf16[4,64,1024]{2,1,0:T(8,128)(2,1)}, bf16[4,64,1024]{2,1,0:T(8,128)(2,1)S(1)}, u32[]{:S(2)}, u32[]{:S(2)}) collective-permute-start(bf16[4,64,1024]{2,1,0:T(8,128)(2,1)} %get-tuple-element.182), channel_id=1, source_target_pairs={{0,16},{8,24},{16,0},{24,8},{1,17},{9,25},{17,1},{25,9},{2,18},{10... | collective-permute-start | bytes 1572872 | tf_op jit(solution)/shard_map/ppermute | solution.py:168
  61.9 17.9 %all-to-all-start.1 = ((bf16[8,64,256]{2,1,0:T(8,128)(2,1)}), bf16[8,64,256]{2,1,0:T(8,128)(2,1)S(1)}, u32[]{:S(2)}, u32[]{:S(2)}) async-start(bf16[8,64,256]{2,1,0:T(8,128)(2,1)} %shrink.1.rest_0_), calls=%async_computation.1 | async-start | bytes 524288 | tf_op jit(solution)/shard_map/all_to_all | solution.py:717
  71.5 8.3 %copy-start = (bf16[4,64,1024]{2,1,0:T(8,128)(2,1)}, bf16[4,64,1024]{2,1,0:T(8,128)(2,1)S(1)}, u32[]{:S(2)}) copy-start(bf16[4,64,1024]{2,1,0:T(8,128)(2,1)S(1)} %collective-permute-done.11.rest_0_.rest_2_) | copy-start | bytes 1572868
  79.8 0.7 copy-start.7
  82.2 15.3 %all-to-all-start.2 = ((bf16[8,1,64,256]{3,2,1,0:T(8,128)(2,1)}), bf16[8,1,64,256]{3,2,1,0:T(8,128)(2,1)S(1)}, u32[]{:S(2)}, u32[]{:S(2)}) async-start(bf16[8,1,64,256]{3,2,1,0:T(8,128)(2,1)} %sum_parts.1), calls=%async_computation.2 | async-start | bytes 524288 | tf_op jit(solution)/shard_map/all_to_all | solution.py:727
  86.8 5.1 %collective-permute-start.16 = (bf16[1056,128]{1,0:T(8,128)(2,1)}, bf16[1056,128]{1,0:T(8,128)(2,1)S(1)}, u32[]{:S(2)}, u32[]{:S(2)}) collective-permute-start(bf16[1056,128]{1,0:T(8,128)(2,1)} %get-tuple-element.191), channel_id=1, source_target_pairs={{7,5},{6,4},{15,13},{14,12},{23,21},{22,20},{31,29},{30,28}} | collective-permute-start | bytes 811016 | tf_op jit(solution)/shard_map/ppermute | solution.py:332
  87.5 10.0 %collective-permute-start.15 = (bf16[1056,128]{1,0:T(8,128)(2,1)}, bf16[1056,128]{1,0:T(8,128)(2,1)}, u32[]{:S(2)}, u32[]{:S(2)}) collective-permute-start(bf16[1056,128]{1,0:T(8,128)(2,1)} %get-tuple-element.185.rest_1_), channel_id=1, source_target_pairs={{0,2},{1,3},{8,10},{9,11},{16,18},{17,19},{24,26},{25,27}} | collective-permute-start | bytes 811016 | tf_op jit(solution)/shard_map/ppermute | solution.py:328
  88.8 19.1 %collective-permute-start.13 = (bf16[4,64,1024]{2,1,0:T(8,128)(2,1)}, bf16[4,64,1024]{2,1,0:T(8,128)(2,1)S(1)}, u32[]{:S(2)}, u32[]{:S(2)}) collective-permute-start(bf16[4,64,1024]{2,1,0:T(8,128)(2,1)} %get-tuple-element.189), channel_id=1, source_target_pairs={{0,8},{8,0},{16,24},{24,16},{1,9},{9,1},{17,25},{25,17},{2,10},{10... | collective-permute-start | bytes 1572872 | tf_op jit(solution)/shard_map/ppermute | solution.py:168
  88.9 22.0 %collective-permute-start.14 = (bf16[4,64,1024]{2,1,0:T(8,128)(2,1)}, bf16[4,64,1024]{2,1,0:T(8,128)(2,1)}, u32[]{:S(2)}, u32[]{:S(2)}) collective-permute-start(bf16[4,64,1024]{2,1,0:T(8,128)(2,1)} %get-tuple-element.190), channel_id=1, source_target_pairs={{0,24},{8,16},{16,8},{24,0},{1,25},{9,17},{17,9},{25,1},{2,26},{10... | collective-permute-start | bytes 1572872 | tf_op jit(solution)/shard_map/ppermute | solution.py:168
  90.5 17.4 %collective-permute-start.19 = (bf16[1056,128]{1,0:T(8,128)(2,1)}, bf16[1056,128]{1,0:T(8,128)(2,1)}, u32[]{:S(2)}, u32[]{:S(2)}) collective-permute-start(bf16[1056,128]{1,0:T(8,128)(2,1)} %get-tuple-element.195), channel_id=1, source_target_pairs={{0,1},{1,0},{2,3},{3,2},{4,5},{5,4},{6,7},{7,6},{8,9},{9,8},{10,11... | collective-permute-start | bytes 811016 | tf_op jit(solution)/shard_map/ppermute | solution.py:666
  91.9 0.7 copy-start.8
  97.5 0.7 copy-start.5
  100.7 24.5 %collective-permute-start.18 = (bf16[1056,128]{1,0:T(8,128)(2,1)}, bf16[1056,128]{1,0:T(8,128)(2,1)}, u32[]{:S(2)}, u32[]{:S(2)}) collective-permute-start(bf16[1056,128]{1,0:T(8,128)(2,1)} %get-tuple-element.193), channel_id=1, source_target_pairs={{7,5},{6,4},{5,3},{4,2},{15,13},{14,12},{13,11},{12,10},{23,21},{2... | collective-permute-start | bytes 811016 | tf_op jit(solution)/shard_map/ppermute | solution.py:332
  102.0 24.6 %collective-permute-start.17 = (bf16[1056,128]{1,0:T(8,128)(2,1)}, bf16[1056,128]{1,0:T(8,128)(2,1)}, u32[]{:S(2)}, u32[]{:S(2)}) collective-permute-start(bf16[1056,128]{1,0:T(8,128)(2,1)} %get-tuple-element.192.rest_8_), channel_id=1, source_target_pairs={{0,2},{1,3},{2,4},{3,5},{8,10},{9,11},{10,12},{11,13},{16,18},{17,... | collective-permute-start | bytes 811016 | tf_op jit(solution)/shard_map/ppermute | solution.py:328
  107.8 27.9 %collective-permute-start.22 = (bf16[1056,128]{1,0:T(8,128)(2,1)}, bf16[1056,128]{1,0:T(8,128)(2,1)}, u32[]{:S(2)}, u32[]{:S(2)}) collective-permute-start(bf16[1056,128]{1,0:T(8,128)(2,1)} %get-tuple-element.201), channel_id=1, source_target_pairs={{0,6},{1,7},{2,4},{3,5},{4,2},{5,3},{6,0},{7,1},{8,14},{9,15},{10,... | collective-permute-start | bytes 811016 | tf_op jit(solution)/shard_map/ppermute | solution.py:732
  107.9 2.9 %copy-start.6 = (bf16[4,64,1024]{2,1,0:T(8,128)(2,1)}, bf16[4,64,1024]{2,1,0:T(8,128)(2,1)S(1)}, u32[]{:S(2)}) copy-start(bf16[4,64,1024]{2,1,0:T(8,128)(2,1)S(1)} %collective-permute-done.13.rest_1_) | copy-start | bytes 1572868
  107.9 30.3 %collective-permute-start.23 = (bf16[1056,128]{1,0:T(8,128)(2,1)}, bf16[1056,128]{1,0:T(8,128)(2,1)}, u32[]{:S(2)}, u32[]{:S(2)}) collective-permute-start(bf16[1056,128]{1,0:T(8,128)(2,1)} %get-tuple-element.202), channel_id=1, source_target_pairs={{0,7},{1,6},{2,5},{3,4},{4,3},{5,2},{6,1},{7,0},{8,15},{9,14},{10,... | collective-permute-start | bytes 811016 | tf_op jit(solution)/shard_map/ppermute | solution.py:732
  129.2 24.9 %collective-permute-start.21 = (bf16[1056,128]{1,0:T(8,128)(2,1)}, bf16[1056,128]{1,0:T(8,128)(2,1)}, u32[]{:S(2)}, u32[]{:S(2)}) collective-permute-start(bf16[1056,128]{1,0:T(8,128)(2,1)} %get-tuple-element.198), channel_id=1, source_target_pairs={{7,5},{6,4},{5,3},{4,2},{3,1},{2,0},{15,13},{14,12},{13,11},{12,10... | collective-permute-start | bytes 811016 | tf_op jit(solution)/shard_map/ppermute | solution.py:332
  131.1 23.0 %collective-permute-start.20 = (bf16[1056,128]{1,0:T(8,128)(2,1)}, bf16[1056,128]{1,0:T(8,128)(2,1)}, u32[]{:S(2)}, u32[]{:S(2)}) collective-permute-start(bf16[1056,128]{1,0:T(8,128)(2,1)} %get-tuple-element.197.rest_8_), channel_id=1, source_target_pairs={{0,2},{1,3},{2,4},{3,5},{4,6},{5,7},{8,10},{9,11},{10,12},{11,13},... | collective-permute-start | bytes 811016 | tf_op jit(solution)/shard_map/ppermute | solution.py:328
  138.2 15.9 %copy-start.2 = (bf16[3,1056,128]{2,1,0:T(8,128)(2,1)S(1)}, bf16[3,1056,128]{2,1,0:T(8,128)(2,1)}, u32[]{:S(2)}) copy-start(bf16[3,1056,128]{2,1,0:T(8,128)(2,1)} %copy-done.1) | copy-start | bytes 2433028
Sparse Core Ops, SparseCore 0:
  23.4 55.2 all-gather.1

commit v11 on v9

--- a/solution.py
+++ b/solution.py
@@ -650,7 +650,7 @@
 
     spread_others = spread_rest(meta, cache, conv, devices, width, limit)
 
-    up_send, _ = lax.optimization_barrier((packed[1:groups], got[2]))
+    up_send, _ = lax.optimization_barrier((packed[1:groups], got[lines]))
     up_got = swap(up_send, groups)
 
     rows_decay, column_decay, channel = pl.pallas_call(
@@ -671,14 +671,13 @@
     )
 
     each = per_group // 2
-    early = got[2:lines + 2]
     partial_down = pl.pallas_call(
         functools.partial(shrink_kernel, per_group),
         grid_spec=pltpu.PrefetchScalarGridSpec(
             num_scalar_prefetch=1,
             grid=(per_group // each,),
             in_specs=[pl.BlockSpec((each * T_REQ, hidden.shape[1]), lambda g, meta: (g, 0))]
-            + anywhere(3 + len(early)),
+            + anywhere(4),
             out_specs=pl.BlockSpec((each, rank, T_REQ), lambda g, meta: (g, 0, 0)),
             scratch_shapes=[
                 pltpu.VMEM((per_group,) + adapter_down_weight.shape[1:], bf16),
@@ -689,22 +688,22 @@
         cost_estimate=cost(),
         compiler_params=params(),
         name="shrink",
-    )(meta, hidden, down_got, channel, spread_others, *early)
+    )(meta, hidden, down_got, channel, got[lines], spread_others)
 
     parts = lax.all_to_all(partial_down, "dev", split_axis=0, concat_axis=0, tiled=True)
     summed = pl.pallas_call(
         sum_kernel,
         out_shape=jax.ShapeDtypeStruct((devices, 1, rank, T_REQ), bf16),
-        in_specs=vmem(1) + anywhere(1),
+        in_specs=vmem(1),
         out_specs=vmem(1)[0],
         cost_estimate=cost(),
         compiler_params=params(),
         name="sum_parts",
-    )(parts.reshape(devices, 1, rank, T_REQ), up_got[groups // 2 - 1])
+    )(parts.reshape(devices, 1, rank, T_REQ))
     shrunk = lax.all_to_all(summed, "dev", split_axis=0, concat_axis=0, tiled=True)
     shrunk = shrunk.reshape(per_group, rank, T_REQ)
 
-    befores = [[partial_down], [summed], [rows_all, up_got[-1]]]
+    befores = [[partial_down, got[lines + 1]], [summed, up_got[groups // 2 - 1]], [rows_all, up_got[-1]]]
     spread = spread_steps(zero, meta, packed[-2:], devices)
     next(spread)
     for step in range(1, lines):

time: 171 us -> 164 us (0.959); the launches traced: 171 us -> 161 us
  waiting for transfers between devices: 51.5 us -> 45.6 us
  starting transfers between devices: 45.4 us -> 41 us
    ppermute x7, starting transfers between devices: 12.1 us -> 7.59 us  [body(): lax.ppermute(chunks[d], 'dev', [(s, s ^ d) for s in range(devices)])]
    ppermute x3, waiting for transfers between devices: 11.5 us -> 7.78 us  [spread_steps(): lax.ppermute(to_right, 'dev', [(2 * i + x, 2 * i + 2 + x) for i in range(...]
    ppermute x7, waiting for transfers between devices: 29.1 us -> 26.4 us  [body(): lax.ppermute(chunks[d], 'dev', [(s, s ^ d) for s in range(devices)])]
  transfers between devices with their start and end apart: 21 -> 21, of which waited for: 9 -> 6; matrix products, arithmetic and copies ran while one was open for 0% -> 0% of each run, Pallas kernels for 18% -> 20%
where the time goes in v11:
time: 164 us; the launch traced here: 161 us
  Pallas kernels  59.1 us (36%)
  waiting for transfers between devices  45.6 us (28%)
  starting transfers between devices  41 us (25%)
  between operations  14.2 us (9%)
    pallas_call x2, Pallas kernels, body(): pl.pallas_call(functools.partial(mix_kernel, groups, taps, begin, steps,...  33.5 us
    ppermute x7, waiting for transfers between devices, body(): lax.ppermute(chunks[d], 'dev', [(s, s ^ d) for s in range(devices)])  26.4 us
    ppermute x3, starting transfers between devices, spread_steps(): lax.ppermute(to_right, 'dev', [(2 * i + x, 2 * i + 2 + x) for i in range(...  9.47 us
    pallas_call x1, Pallas kernels, body(): pl.pallas_call(functools.partial(pack_kernel, groups, devices, per_group,...  8.06 us
    ppermute x3, waiting for transfers between devices, spread_steps(): lax.ppermute(to_right, 'dev', [(2 * i + x, 2 * i + 2 + x) for i in range(...  7.78 us
    pallas_call x3, Pallas kernels, spread_steps(): pl.pallas_call(functools.partial(pick_kernel, step, lines), in_specs=smem...  7.6 us
    ppermute x7, starting transfers between devices, body(): lax.ppermute(chunks[d], 'dev', [(s, s ^ d) for s in range(devices)])  7.59 us
    all_to_all x1, starting transfers between devices, body(): lax.all_to_all(partial_down, 'dev', split_axis=0, concat_axis=0, tiled=True)  6.5 us
  transfers between devices with their start and end apart: 21, of which 6 were waited for; matrix products, arithmetic and copies ran while one was open for 0% of the time, Pallas kernels for 20%

profile of v11, /device:TPU:8, one launch (start us, length us, event | category | flops | bytes accessed | tf_op | source)
XLA Modules:
  0.0 161.2 jit_solution(17322243241374679106)
XLA Ops:
  7.2 8.1 %pack.1 = (s32[16,64]{1,0:T(8,128)S(1)}, bf16[256,256]{1,0:T(8,128)(2,1)}, bf16[4,4,64,1024]{3,2,1,0:T(8,128)(2,1)}, bf16[4,64,1024]{2,1,0:T(8,128)(2,1)}, bf16[...) custom-call(s32[32]{0:T(128)} %bitcast.22, ...), custom_call_target="tpu_custom_call" | custom-call | bytes 65536 | tf_op jit(solution)/shard_map/pack/pallas_call | solution.py:615
  15.2 4.6 %all-to-all-start = ((bf16[4,4,64,1024]{3,2,1,0:T(8,128)(2,1)}), bf16[4,4,64,1024]{3,2,1,0:T(8,128)(2,1)}, u32[]{:S(2)}, u32[]{:S(2)}) async-start(bf16[4,4,64,1024]{3,2,1,0:T(8,128)(2,1)} %get-tuple-element.167), calls=%async_computation | async-start | bytes 4194304 | tf_op jit(solution)/shard_map/all_to_all | solution.py:642
  19.9 0.0 all-gather.2.cloned.1.call-start
  19.9 0.7 all-gather.2.cloned.1.call-update
  20.6 1.6 collective-permute-start.14
  22.2 2.6 %collective-permute-start.7 = (bf16[1056,128]{1,0:T(8,128)(2,1)S(1)}, bf16[1056,128]{1,0:T(8,128)(2,1)S(1)}, u32[]{:S(2)}, u32[]{:S(2)}) collective-permute-start(bf16[1056,128]{1,0:T(8,128)(2,1)S(1)} %copy-done.3), channel_id=1, source_target_pairs={{0,4},{1,5},{2,6},{3,7},{4,0},{5,1},{6,2},{7,3},{8,12},{9,13},{10,... | collective-permute-start | bytes 811016 | tf_op jit(solution)/shard_map/ppermute | solution.py:647
  24.8 0.3 collective-permute-start.11
  25.1 21.3 %collective-permute-done.7.rest_1_.rest_4_ = bf16[1056,128]{1,0:T(8,128)(2,1)S(1)} collective-permute-done((bf16[1056,128]{1,0:T(8,128)(2,1)S(1)}, bf16[1056,128]{1,0:T(8,128)(2,1)S(1)}, u32[]{:S(2)}, u32[]{:S(2)}) %collective-permute-start.7) | collective-permute-done | bytes 270368 | tf_op jit(solution)/shard_map/ppermute | solution.py:647
  46.4 1.7 %collective-permute-start.9 = (bf16[4,64,1024]{2,1,0:T(8,128)(2,1)}, bf16[4,64,1024]{2,1,0:T(8,128)(2,1)}, u32[]{:S(2)}, u32[]{:S(2)}) collective-permute-start(bf16[4,64,1024]{2,1,0:T(8,128)(2,1)} %get-tuple-element.178), channel_id=1, source_target_pairs={{0,16},{8,24},{16,0},{24,8},{1,17},{9,25},{17,1},{25,9},{2,18},{10... | collective-permute-start | bytes 1572872 | tf_op jit(solution)/shard_map/ppermute | solution.py:157
  48.1 0.6 slice.3
  48.6 0.1 broadcast_in_dim.12
  48.8 0.6 while.14
  49.4 0.1 collective-permute-start.10
  49.5 2.5 %prep.1 = (f32[32,2048]{1,0:T(8,128)}, f32[8,256,16]{2,1,0:T(8,128)}, f32[8,1024]{1,0:T(8,128)}) custom-call(f32[16]{0:T(128)} %rates.1, f32[16]{0:T(128)} %skips.1, f32[16,2048]{1,0:T(8,128)} %steps.1, f32[4,1024]{1,0:T(4,128)} %taps_in.1, f32[1,1024]{1,0:T(1,128)} %bitcast.21, s32[16,64]{1,0:T(8,128)S(1)} %get-tuple-element.297), custom_call_target="tpu_custom_call" | custom-call | bytes 65536 | tf_op jit(solution)/shard_map/prep/pallas_call | solution.py:656
  52.0 0.0 all-to-all-done.table
  52.0 5.7 %shrink.1.rest_0_ = bf16[8,64,256]{2,1,0:T(8,128)(2,1)} custom-call(s32[16,64]{1,0:T(8,128)S(1)} %get-tuple-element.297, bf16[2048,1024]{1,0:T(8,128)(2,1)} %hidden.1, bf16[4,4,64,1024]{3,2,1,0:T(8,128)(2,1)} %all-to-all-done.table, f32[8,1024]{1,0:T(8,128)} %get-tuple-element.168.rest_0_.channel, bf16[1056,128]{1,0:T(8,128)(2,1)} %copy-done.2, ...), custom_call_target="tpu_custom_call" | custom-call | bytes 65536 | tf_op jit(solution)/shard_map/shrink/pallas_call | solution.py:674
  57.7 6.5 %all-to-all-start.1 = ((bf16[8,64,256]{2,1,0:T(8,128)(2,1)}), bf16[8,64,256]{2,1,0:T(8,128)(2,1)}, u32[]{:S(2)}, u32[]{:S(2)}) async-start(bf16[8,64,256]{2,1,0:T(8,128)(2,1)} %shrink.1.rest_0_), calls=%async_computation.1 | async-start | bytes 524288 | tf_op jit(solution)/shard_map/all_to_all | solution.py:693
  64.2 0.0 collective-permute-done.14.over.rest_9_
  64.2 2.5 %pick_1.8 = (bf16[1056,128]{1,0:T(8,128)(2,1)}, bf16[1056,128]{1,0:T(8,128)(2,1)}) custom-call(s32[1]{0:T(128)} %constant.34.clone.1.j, s32[16,64]{1,0:T(8,128)S(1)} %get-tuple-element.297, bf16[4,1056,128]{2,1,0:T(8,128)(2,1)} %get-tuple-element.183.own.rest_8_, bf16[4,1056,128]{2,1,0:T(8,128)(2,1)} %collective-permute-done.14.over.rest_9_, ...), custom_call_target="tpu_custom_call" | custom-call | bytes 65536 | tf_op jit(solution)/shard_map/pick_1/pallas_call | solution.py:307
  66.7 1.3 collective-permute-start.15
  68.0 1.4 collective-permute-start.16
  69.4 0.5 collective-permute-start.12
  69.9 6.4 %all-to-all-done.1 = bf16[8,64,256]{2,1,0:T(8,128)(2,1)} async-done(((bf16[8,64,256]{2,1,0:T(8,128)(2,1)}), bf16[8,64,256]{2,1,0:T(8,128)(2,1)}, u32[]{:S(2)}, u32[]{:S(2)}) %all-to-all-start.1) | async-done | bytes 262176 | tf_op jit(solution)/shard_map/all_to_all | solution.py:693
  76.3 1.7 %sum_parts.1.rest_2_ = bf16[8,1,64,256]{3,2,1,0:T(8,128)(2,1)} custom-call(bf16[8,1,64,256]{3,2,1,0:T(8,128)(2,1)} %bitcast.8.parts), custom_call_target="tpu_custom_call" | custom-call | bytes 65536 | tf_op jit(solution)/shard_map/sum_parts/pallas_call | solution.py:694
  78.0 0.0 collective-permute-done.9.rest_3_.rest_2_
  78.0 2.5 %collective-permute-done.15.rest_0_ = bf16[1056,128]{1,0:T(8,128)(2,1)} collective-permute-done((bf16[1056,128]{1,0:T(8,128)(2,1)}, bf16[1056,128]{1,0:T(8,128)(2,1)}, u32[]{:S(2)}, u32[]{:S(2)}) %collective-permute-start.15) | collective-permute-done | bytes 270368 | tf_op jit(solution)/shard_map/ppermute | solution.py:317
  80.5 0.0 collective-permute-done.16.rest_1_
  80.5 2.5 %pick_2.8 = (bf16[1056,128]{1,0:T(8,128)(2,1)}, bf16[1056,128]{1,0:T(8,128)(2,1)}) custom-call(s32[1]{0:T(128)} %constant.34.clone.1.j, s32[16,64]{1,0:T(8,128)S(1)} %get-tuple-element.297, bf16[4,1056,128]{2,1,0:T(8,128)(2,1)} %get-tuple-element.183.own.rest_8_, bf16[4,1056,128]{2,1,0:T(8,128)(2,1)} %collective-permute-done.14.over.rest_9_, ...), custom_call_target="tpu_custom_call" | custom-call | bytes 65536 | tf_op jit(solution)/shard_map/pick_2/pallas_call | solution.py:307
  83.1 4.3 %collective-permute-start.17 = (bf16[1056,128]{1,0:T(8,128)(2,1)}, bf16[1056,128]{1,0:T(8,128)(2,1)}, u32[]{:S(2)}, u32[]{:S(2)}) collective-permute-start(bf16[1056,128]{1,0:T(8,128)(2,1)} %get-tuple-element.187), channel_id=1, source_target_pairs={{0,2},{1,3},{2,4},{3,5},{8,10},{9,11},{10,12},{11,13},{16,18},{17,... | collective-permute-start | bytes 811016 | tf_op jit(solution)/shard_map/ppermute | solution.py:317
  87.3 1.3 collective-permute-start.18
  88.6 3.4 %collective-permute-start.13 = (bf16[1056,128]{1,0:T(8,128)(2,1)}, bf16[1056,128]{1,0:T(8,128)(2,1)}, u32[]{:S(2)}, u32[]{:S(2)}) collective-permute-start(bf16[1056,128]{1,0:T(8,128)(2,1)} %get-tuple-element.182), channel_id=1, source_target_pairs={{0,7},{1,6},{2,5},{3,4},{4,3},{5,2},{6,1},{7,0},{8,15},{9,14},{10,... | collective-permute-start | bytes 811016 | tf_op jit(solution)/shard_map/ppermute | solution.py:647
  92.0 0.0 collective-permute-done.12.rest_9_.rest_6_
  92.0 0.8 collective-permute-start.21
  92.8 0.0 collective-permute-start.8
  92.8 4.8 %all-to-all-start.2 = ((bf16[8,1,64,256]{3,2,1,0:T(8,128)(2,1)}), bf16[8,1,64,256]{3,2,1,0:T(8,128)(2,1)}, u32[]{:S(2)}, u32[]{:S(2)}) async-start(bf16[8,1,64,256]{3,2,1,0:T(8,128)(2,1)} %sum_parts.1.rest_2_), calls=%async_computation.2 | async-start | bytes 524288 | tf_op jit(solution)/shard_map/all_to_all | solution.py:703
  97.7 5.3 %collective-permute-done.17.rest_0_ = bf16[1056,128]{1,0:T(8,128)(2,1)} collective-permute-done((bf16[1056,128]{1,0:T(8,128)(2,1)}, bf16[1056,128]{1,0:T(8,128)(2,1)}, u32[]{:S(2)}, u32[]{:S(2)}) %collective-permute-start.17) | collective-permute-done | bytes 270368 | tf_op jit(solution)/shard_map/ppermute | solution.py:317
  102.9 0.0 collective-permute-start.22
  103.0 4.4 %collective-permute-done.18.rest_1_ = bf16[1056,128]{1,0:T(8,128)(2,1)} collective-permute-done((bf16[1056,128]{1,0:T(8,128)(2,1)}, bf16[1056,128]{1,0:T(8,128)(2,1)}, u32[]{:S(2)}, u32[]{:S(2)}) %collective-permute-start.18) | collective-permute-done | bytes 270368 | tf_op jit(solution)/shard_map/ppermute | solution.py:321
  107.3 2.5 %pick_3.8 = (bf16[1056,128]{1,0:T(8,128)(2,1)}, bf16[1056,128]{1,0:T(8,128)(2,1)}) custom-call(s32[1]{0:T(128)} %constant.34.clone.1.j, s32[16,64]{1,0:T(8,128)S(1)} %get-tuple-element.297, bf16[4,1056,128]{2,1,0:T(8,128)(2,1)} %get-tuple-element.183.own.rest_8_, bf16[4,1056,128]{2,1,0:T(8,128)(2,1)} %collective-permute-done.14.over.rest_9_, ...), custom_call_target="tpu_custom_call" | custom-call | bytes 65536 | tf_op jit(solution)/shard_map/pick_3/pallas_call | solution.py:307
  109.9 5.1 %collective-permute-done.13.rest_10_.rest_7_ = bf16[1056,128]{1,0:T(8,128)(2,1)} collective-permute-done((bf16[1056,128]{1,0:T(8,128)(2,1)}, bf16[1056,128]{1,0:T(8,128)(2,1)}, u32[]{:S(2)}, u32[]{:S(2)}) %collective-permute-start.13) | collective-permute-done | bytes 270368 | tf_op jit(solution)/shard_map/ppermute | solution.py:647
  114.9 1.9 %collective-permute-start.20 = (bf16[1056,128]{1,0:T(8,128)(2,1)}, bf16[1056,128]{1,0:T(8,128)(2,1)}, u32[]{:S(2)}, u32[]{:S(2)}) collective-permute-start(bf16[1056,128]{1,0:T(8,128)(2,1)} %get-tuple-element.190), channel_id=1, source_target_pairs={{7,5},{6,4},{5,3},{4,2},{3,1},{2,0},{15,13},{14,12},{13,11},{12,10... | collective-permute-start | bytes 811016 | tf_op jit(solution)/shard_map/ppermute | solution.py:321
  116.8 0.0 collective-permute-done.21.rest_5_
  116.8 3.9 %collective-permute-start.19 = (bf16[1056,128]{1,0:T(8,128)(2,1)}, bf16[1056,128]{1,0:T(8,128)(2,1)}, u32[]{:S(2)}, u32[]{:S(2)}) collective-permute-start(bf16[1056,128]{1,0:T(8,128)(2,1)} %get-tuple-element.189.rest_8_), channel_id=1, source_target_pairs={{0,2},{1,3},{2,4},{3,5},{4,6},{5,7},{8,10},{9,11},{10,12},{11,13},... | collective-permute-start | bytes 811016 | tf_op jit(solution)/shard_map/ppermute | solution.py:317
  120.8 0.0 collective-permute-done.22.rest_6_
  120.8 0.0 collective-permute-done.23.rest_7_
  120.8 0.0 all-to-all-done.2
  120.8 14.1 %mix_0.1 = (bf16[2048,1024]{1,0:T(8,128)(2,1)}, bf16[8,1024,128]{2,1,0:T(8,128)(2,1)}) custom-call(s32[16,64]{1,0:T(8,128)S(1)} %get-tuple-element.297, bf16[2048,1024]{1,0:T(8,128)(2,1)} %base.3, bf16[8,64,256]{2,1,0:T(8,128)(2,1)} %bitcast.9.shrunk, f32[8,1024]{1,0:T(8,128)} %get-tuple-element.168.rest_0_.channel, ...), custom_call_target="tpu_custom_call" | custom-call | bytes 65536 | tf_op jit(solution)/shard_map/mix_0/pallas_call | solution.py:740
  134.9 19.4 %mix_4.1 = (bf16[2048,1024]{1,0:T(8,128)(2,1)}, bf16[8,1024,128]{2,1,0:T(8,128)(2,1)}) custom-call(s32[16,64]{1,0:T(8,128)S(1)} %get-tuple-element.297, bf16[2048,1024]{1,0:T(8,128)(2,1)} %base.3, bf16[8,64,256]{2,1,0:T(8,128)(2,1)} %bitcast.9.shrunk, f32[8,1024]{1,0:T(8,128)} %get-tuple-element.168.rest_0_.channel, ...), custom_call_target="tpu_custom_call", output_to_operand_aliasing={{0}: (20, {}), {1}: (21, {})} | custom-call | bytes 65536 | tf_op jit(solution)/shard_map/mix_4/pallas_call | solution.py:740
  (11 shorter events, 0.0 us)
Async XLA Ops:
  15.2 7.0 %copy-start.3 = (bf16[1056,128]{1,0:T(8,128)(2,1)S(1)}, bf16[1056,128]{1,0:T(8,128)(2,1)}, u32[]{:S(2)}) copy-start(bf16[1056,128]{1,0:T(8,128)(2,1)} %get-tuple-element.169) | copy-start | bytes 811012
  15.2 36.7 %all-to-all-start = ((bf16[4,4,64,1024]{3,2,1,0:T(8,128)(2,1)}), bf16[4,4,64,1024]{3,2,1,0:T(8,128)(2,1)}, u32[]{:S(2)}, u32[]{:S(2)}) async-start(bf16[4,4,64,1024]{3,2,1,0:T(8,128)(2,1)} %get-tuple-element.167), calls=%async_computation | async-start | bytes 4194304 | tf_op jit(solution)/shard_map/all_to_all | solution.py:642
  19.9 87.4 %all-gather.2.cloned.1.call-start = ((), (), s32[]{:S(2)}) async-start(), calls=%async_computation.3 | async-start | bytes 1179648 | tf_op jit(solution)/shard_map/all_gather | solution.py:644
  20.6 43.5 %collective-permute-start.14 = (bf16[4,1056,128]{2,1,0:T(8,128)(2,1)}, bf16[4,1056,128]{2,1,0:T(8,128)(2,1)}, u32[]{:S(2)}, u32[]{:S(2)}) collective-permute-start(bf16[4,1056,128]{2,1,0:T(8,128)(2,1)} %get-tuple-element.184), channel_id=1, source_target_pairs={{0,1},{1,0},{2,3},{3,2},{4,5},{5,4},{6,7},{7,6},{8,9},{9,8},{10,11... | collective-permute-start | bytes 3244040 | tf_op jit(solution)/shard_map/ppermute | solution.py:299
  22.2 24.2 %collective-permute-start.7 = (bf16[1056,128]{1,0:T(8,128)(2,1)S(1)}, bf16[1056,128]{1,0:T(8,128)(2,1)S(1)}, u32[]{:S(2)}, u32[]{:S(2)}) collective-permute-start(bf16[1056,128]{1,0:T(8,128)(2,1)S(1)} %copy-done.3), channel_id=1, source_target_pairs={{0,4},{1,5},{2,6},{3,7},{4,0},{5,1},{6,2},{7,3},{8,12},{9,13},{10,... | collective-permute-start | bytes 811016 | tf_op jit(solution)/shard_map/ppermute | solution.py:647
  24.8 39.4 %collective-permute-start.11 = (bf16[1056,128]{1,0:T(8,128)(2,1)}, bf16[1056,128]{1,0:T(8,128)(2,1)}, u32[]{:S(2)}, u32[]{:S(2)}) collective-permute-start(bf16[1056,128]{1,0:T(8,128)(2,1)} %get-tuple-element.180), channel_id=1, source_target_pairs={{0,5},{1,4},{2,7},{3,6},{4,1},{5,0},{6,3},{7,2},{8,13},{9,12},{10,... | collective-permute-start | bytes 811016 | tf_op jit(solution)/shard_map/ppermute | solution.py:647
  46.4 2.3 %copy-start.2 = (bf16[1056,128]{1,0:T(8,128)(2,1)}, bf16[1056,128]{1,0:T(8,128)(2,1)S(1)}, u32[]{:S(2)}) copy-start(bf16[1056,128]{1,0:T(8,128)(2,1)S(1)} %collective-permute-done.7.rest_1_.rest_4_) | copy-start | bytes 811012
  46.4 31.7 %collective-permute-start.9 = (bf16[4,64,1024]{2,1,0:T(8,128)(2,1)}, bf16[4,64,1024]{2,1,0:T(8,128)(2,1)}, u32[]{:S(2)}, u32[]{:S(2)}) collective-permute-start(bf16[4,64,1024]{2,1,0:T(8,128)(2,1)} %get-tuple-element.178), channel_id=1, source_target_pairs={{0,16},{8,24},{16,0},{24,8},{1,17},{9,25},{17,1},{25,9},{2,18},{10... | collective-permute-start | bytes 1572872 | tf_op jit(solution)/shard_map/ppermute | solution.py:157
  49.4 43.4 %collective-permute-start.10 = (bf16[4,64,1024]{2,1,0:T(8,128)(2,1)}, bf16[4,64,1024]{2,1,0:T(8,128)(2,1)}, u32[]{:S(2)}, u32[]{:S(2)}) collective-permute-start(bf16[4,64,1024]{2,1,0:T(8,128)(2,1)} %get-tuple-element.179), channel_id=1, source_target_pairs={{0,24},{8,16},{16,8},{24,0},{1,25},{9,17},{17,9},{25,1},{2,26},{10... | collective-permute-start | bytes 1572872 | tf_op jit(solution)/shard_map/ppermute | solution.py:157
  57.7 18.7 %all-to-all-start.1 = ((bf16[8,64,256]{2,1,0:T(8,128)(2,1)}), bf16[8,64,256]{2,1,0:T(8,128)(2,1)}, u32[]{:S(2)}, u32[]{:S(2)}) async-start(bf16[8,64,256]{2,1,0:T(8,128)(2,1)} %shrink.1.rest_0_), calls=%async_computation.1 | async-start | bytes 524288 | tf_op jit(solution)/shard_map/all_to_all | solution.py:693
  66.7 13.8 %collective-permute-start.15 = (bf16[1056,128]{1,0:T(8,128)(2,1)}, bf16[1056,128]{1,0:T(8,128)(2,1)}, u32[]{:S(2)}, u32[]{:S(2)}) collective-permute-start(bf16[1056,128]{1,0:T(8,128)(2,1)} %get-tuple-element.185), channel_id=1, source_target_pairs={{0,2},{1,3},{8,10},{9,11},{16,18},{17,19},{24,26},{25,27}} | collective-permute-start | bytes 811016 | tf_op jit(solution)/shard_map/ppermute | solution.py:317
  68.0 12.5 %collective-permute-start.16 = (bf16[1056,128]{1,0:T(8,128)(2,1)}, bf16[1056,128]{1,0:T(8,128)(2,1)}, u32[]{:S(2)}, u32[]{:S(2)}) collective-permute-start(bf16[1056,128]{1,0:T(8,128)(2,1)} %get-tuple-element.186), channel_id=1, source_target_pairs={{7,5},{6,4},{15,13},{14,12},{23,21},{22,20},{31,29},{30,28}} | collective-permute-start | bytes 811016 | tf_op jit(solution)/shard_map/ppermute | solution.py:321
  69.4 22.6 %collective-permute-start.12 = (bf16[1056,128]{1,0:T(8,128)(2,1)}, bf16[1056,128]{1,0:T(8,128)(2,1)}, u32[]{:S(2)}, u32[]{:S(2)}) collective-permute-start(bf16[1056,128]{1,0:T(8,128)(2,1)} %get-tuple-element.181), channel_id=1, source_target_pairs={{0,6},{1,7},{2,4},{3,5},{4,2},{5,3},{6,0},{7,1},{8,14},{9,15},{10,... | collective-permute-start | bytes 811016 | tf_op jit(solution)/shard_map/ppermute | solution.py:647
  83.1 19.9 %collective-permute-start.17 = (bf16[1056,128]{1,0:T(8,128)(2,1)}, bf16[1056,128]{1,0:T(8,128)(2,1)}, u32[]{:S(2)}, u32[]{:S(2)}) collective-permute-start(bf16[1056,128]{1,0:T(8,128)(2,1)} %get-tuple-element.187), channel_id=1, source_target_pairs={{0,2},{1,3},{2,4},{3,5},{8,10},{9,11},{10,12},{11,13},{16,18},{17,... | collective-permute-start | bytes 811016 | tf_op jit(solution)/shard_map/ppermute | solution.py:317
  87.3 20.0 %collective-permute-start.18 = (bf16[1056,128]{1,0:T(8,128)(2,1)}, bf16[1056,128]{1,0:T(8,128)(2,1)}, u32[]{:S(2)}, u32[]{:S(2)}) collective-permute-start(bf16[1056,128]{1,0:T(8,128)(2,1)} %get-tuple-element.188), channel_id=1, source_target_pairs={{7,5},{6,4},{5,3},{4,2},{15,13},{14,12},{13,11},{12,10},{23,21},{2... | collective-permute-start | bytes 811016 | tf_op jit(solution)/shard_map/ppermute | solution.py:321
  88.6 26.3 %collective-permute-start.13 = (bf16[1056,128]{1,0:T(8,128)(2,1)}, bf16[1056,128]{1,0:T(8,128)(2,1)}, u32[]{:S(2)}, u32[]{:S(2)}) collective-permute-start(bf16[1056,128]{1,0:T(8,128)(2,1)} %get-tuple-element.182), channel_id=1, source_target_pairs={{0,7},{1,6},{2,5},{3,4},{4,3},{5,2},{6,1},{7,0},{8,15},{9,14},{10,... | collective-permute-start | bytes 811016 | tf_op jit(solution)/shard_map/ppermute | solution.py:647
  92.0 24.8 %collective-permute-start.21 = (bf16[1056,128]{1,0:T(8,128)(2,1)}, bf16[1056,128]{1,0:T(8,128)(2,1)}, u32[]{:S(2)}, u32[]{:S(2)}) collective-permute-start(bf16[1056,128]{1,0:T(8,128)(2,1)} %get-tuple-element.192), channel_id=1, source_target_pairs={{0,1},{1,0},{2,3},{3,2},{4,5},{5,4},{6,7},{7,6},{8,9},{9,8},{10,11... | collective-permute-start | bytes 811016 | tf_op jit(solution)/shard_map/ppermute | solution.py:647
  92.8 28.0 %collective-permute-start.8 = (bf16[4,64,1024]{2,1,0:T(8,128)(2,1)}, bf16[4,64,1024]{2,1,0:T(8,128)(2,1)}, u32[]{:S(2)}, u32[]{:S(2)}) collective-permute-start(bf16[4,64,1024]{2,1,0:T(8,128)(2,1)} %get-tuple-element.177), channel_id=1, source_target_pairs={{0,8},{8,0},{16,24},{24,16},{1,9},{9,1},{17,25},{25,17},{2,10},{10... | collective-permute-start | bytes 1572872 | tf_op jit(solution)/shard_map/ppermute | solution.py:157
  92.8 28.0 %all-to-all-start.2 = ((bf16[8,1,64,256]{3,2,1,0:T(8,128)(2,1)}), bf16[8,1,64,256]{3,2,1,0:T(8,128)(2,1)}, u32[]{:S(2)}, u32[]{:S(2)}) async-start(bf16[8,1,64,256]{3,2,1,0:T(8,128)(2,1)} %sum_parts.1.rest_2_), calls=%async_computation.2 | async-start | bytes 524288 | tf_op jit(solution)/shard_map/all_to_all | solution.py:703
  102.9 17.8 %collective-permute-start.22 = (bf16[1056,128]{1,0:T(8,128)(2,1)}, bf16[1056,128]{1,0:T(8,128)(2,1)}, u32[]{:S(2)}, u32[]{:S(2)}) collective-permute-start(bf16[1056,128]{1,0:T(8,128)(2,1)} %get-tuple-element.193), channel_id=1, source_target_pairs={{0,2},{1,3},{2,0},{3,1},{4,6},{5,7},{6,4},{7,5},{8,10},{9,11},{10,... | collective-permute-start | bytes 811016 | tf_op jit(solution)/shard_map/ppermute | solution.py:647
  107.3 13.5 %collective-permute-start.23 = (bf16[1056,128]{1,0:T(8,128)(2,1)}, bf16[1056,128]{1,0:T(8,128)(2,1)}, u32[]{:S(2)}, u32[]{:S(2)}) collective-permute-start(bf16[1056,128]{1,0:T(8,128)(2,1)} %get-tuple-element.194), channel_id=1, source_target_pairs={{0,3},{1,2},{2,1},{3,0},{4,7},{5,6},{6,5},{7,4},{8,11},{9,10},{10,... | collective-permute-start | bytes 811016 | tf_op jit(solution)/shard_map/ppermute | solution.py:647
  114.9 20.0 %collective-permute-start.20 = (bf16[1056,128]{1,0:T(8,128)(2,1)}, bf16[1056,128]{1,0:T(8,128)(2,1)}, u32[]{:S(2)}, u32[]{:S(2)}) collective-permute-start(bf16[1056,128]{1,0:T(8,128)(2,1)} %get-tuple-element.190), channel_id=1, source_target_pairs={{7,5},{6,4},{5,3},{4,2},{3,1},{2,0},{15,13},{14,12},{13,11},{12,10... | collective-permute-start | bytes 811016 | tf_op jit(solution)/shard_map/ppermute | solution.py:321
  116.8 18.1 %collective-permute-start.19 = (bf16[1056,128]{1,0:T(8,128)(2,1)}, bf16[1056,128]{1,0:T(8,128)(2,1)}, u32[]{:S(2)}, u32[]{:S(2)}) collective-permute-start(bf16[1056,128]{1,0:T(8,128)(2,1)} %get-tuple-element.189.rest_8_), channel_id=1, source_target_pairs={{0,2},{1,3},{2,4},{3,5},{4,6},{5,7},{8,10},{9,11},{10,12},{11,13},... | collective-permute-start | bytes 811016 | tf_op jit(solution)/shard_map/ppermute | solution.py:317
Sparse Core Ops, SparseCore 0:
  22.9 54.6 all-gather.1
